TPU v7x, 32 devices: a whole 2x2x4 slice. The times are simulated.
32 devices in a mesh: pipe: 2 (over y), dp: 4 (over z), tensor: 4 (over x, core).
Axes of the slice: x: 2, y: 2, z: 4, core: 2. Of those that a mesh axis runs over, the one named last changes fastest.
Arguments:
- handoff: bfloat16 [2, 8192, 1024], P('pipe', 'dp', 'tensor'), may hold values from -6 to 6
- hidden_pre: bfloat16 [2, 8192, 4096], P('pipe', 'dp', 'tensor'), may hold values from -6 to 6
- down_weight: bfloat16 [2, 4096, 1024], P('pipe', 'tensor'), may hold values from -6 to 6
- up_weight: bfloat16 [2, 4096, 1024], P('pipe', 'tensor'), may hold values from -6 to 6
- moment: float32 [2, 4096, 1024], P('pipe', ('tensor', 'dp')), may hold values from -3 to 3
- second: float32 [2, 4096, 1024], P('pipe', ('tensor', 'dp')), may hold values from 0.05 to 2
Outputs:
- input_grad: bfloat16 [2, 8192, 1024], P('pipe', 'dp', 'tensor')
- new_down: bfloat16 [2, 4096, 1024], P('pipe', 'tensor')
- new_moment: float32 [2, 4096, 1024], P('pipe', ('tensor', 'dp'))
- new_second: float32 [2, 4096, 1024], P('pipe', ('tensor', 'dp'))
All inputs are finite; a program needn't handle non-finite values.
Results may differ from a plain program's by a relative error of at most 0.017.
Values may be sent and summed in bfloat16 or wider, within the bound.
No kernel may reach another device: no remote copies, remote signals or barrier semaphores. Data moves between devices by JAX's collectives and lax.ppermute only.
A program may use at most 64 MiB of HBM per device.

v0:
```python
import math

import jax
import jax.numpy as jnp
from jax import lax
from jax.sharding import PartitionSpec as P


def from_behind(block, axis, distance):
    devices = range(lax.axis_size(axis))
    route = [((i - distance) % len(devices), i) for i in devices]
    return lax.ppermute(block, axis, route)


def normal_cdf(inputs):
    return 0.5 * (1.0 + jax.scipy.special.erf(inputs * (1.0 / math.sqrt(2.0))))


def gelu_value(inputs):
    return inputs * normal_cdf(inputs)


def gelu_slope(inputs):
    return normal_cdf(inputs) + inputs * jnp.exp(-0.5 * inputs * inputs) * (
        1.0 / math.sqrt(2.0 * math.pi)
    )


def on_device(handoff, hidden_pre, down_weight, up_weight, moment, second):
    arrived = from_behind(handoff, "pipe", -1)
    incoming = lax.all_gather(arrived, "tensor", axis=2, tiled=True)
    incoming = incoming[0]
    tok_rows = incoming.shape[0]
    model_width = incoming.shape[1]
    slab_rows = down_weight.shape[1]
    shard_rows = moment.shape[1]
    hidden_total = slab_rows * lax.axis_size("tensor")
    token_total = tok_rows * lax.axis_size("dp")
    pre_values = hidden_pre[0].astype(jnp.float32)
    hidden = gelu_value(pre_values).astype(jnp.bfloat16)
    down_back = lax.dot_general(
        incoming, down_weight[0], (((1,), (1,)), ((), ())), preferred_element_type=jnp.float32
    )
    act_grad = (down_back * (1.0 / math.sqrt(model_width)) * gelu_slope(pre_values)).astype(
        jnp.bfloat16
    )
    partial_value = jnp.dot(act_grad, up_weight[0], preferred_element_type=jnp.float32) * (
        1.0 / math.sqrt(hidden_total)
    )
    summed = lax.psum(partial_value.astype(jnp.bfloat16), "tensor").astype(jnp.float32)
    col_width = model_width // lax.axis_size("tensor")
    own_cols = lax.dynamic_slice_in_dim(summed, lax.axis_index("tensor") * col_width, col_width, 1)
    input_grad = own_cols.astype(jnp.bfloat16)[None]
    grad_scale = 1.0 / math.sqrt(token_total)
    product = lax.dot_general(
        hidden, incoming, (((0,), (0,)), ((), ())), preferred_element_type=jnp.float32
    )
    gradient = lax.psum_scatter(
        (product * grad_scale).astype(jnp.bfloat16), "dp", scatter_dimension=0, tiled=True
    ).astype(jnp.float32)
    new_m = 0.9 * moment[0] + 0.1 * gradient
    new_v = 0.95 * second[0] + 0.05 * gradient * gradient
    own_rows = lax.dynamic_slice_in_dim(
        down_weight[0], lax.axis_index("dp") * shard_rows, shard_rows, 0
    )
    fresh_rows = (own_rows.astype(jnp.float32) - 0.2 * new_m / (jnp.sqrt(new_v) + 1e-08)).astype(
        jnp.bfloat16
    )
    new_down = lax.all_gather(fresh_rows, "dp", axis=0, tiled=True)
    return (input_grad, new_down[None], new_m[None], new_v[None])


def solution(mesh):
    placed = (
        P("pipe", "dp", "tensor"),
        P("pipe", "dp", "tensor"),
        P("pipe", "tensor", None),
        P("pipe", "tensor", None),
        P("pipe", ("tensor", "dp"), None),
        P("pipe", ("tensor", "dp"), None),
    )
    return jax.shard_map(
        on_device,
        mesh=mesh,
        in_specs=placed,
        out_specs=(
            P("pipe", "dp", "tensor"),
            P("pipe", "tensor", None),
            P("pipe", ("tensor", "dp"), None),
            P("pipe", ("tensor", "dp"), None),
        ),
        check_vma=False,
    )
```

profile of v0, /device:TPU:0, one launch (start us, length us, event | category | flops | bytes accessed | tf_op | source)
XLA Modules:
  0.0 268.9 jit_solution(15805265283817216094)
XLA Ops:
  7.2 0.0 copy-start
  7.2 0.0 all-gather.3.cloned.1.call-start
  7.2 3.0 %collective-permute-start = (bf16[1,2048,256]{2,1,0:T(8,128)(2,1)}, bf16[1,2048,256]{2,1,0:T(8,128)(2,1)S(1)}, u32[]{:S(2)}, u32[]{:S(2)}) collective-permute-start(bf16[1,2048,256]{2,1,0:T(8,128)(2,1)} %param.6), channel_id=1, source_target_pairs={{16,0},{0,16},{17,1},{1,17},{18,2},{2,18},{19,3},{3,19},{20,4},{4,... | collective-permute-start | bytes 3145736 | tf_op jit(solution)/shard_map/ppermute | solution.py:12
  10.3 23.4 %collective-permute-done = bf16[1,2048,256]{2,1,0:T(8,128)(2,1)S(1)} collective-permute-done((bf16[1,2048,256]{2,1,0:T(8,128)(2,1)}, bf16[1,2048,256]{2,1,0:T(8,128)(2,1)S(1)}, u32[]{:S(2)}, u32[]{:S(2)}) %collective-permute-start) | collective-permute-done | bytes 1048608 | tf_op jit(solution)/shard_map/ppermute | solution.py:12
  33.6 0.0 copy-start.1
  33.6 1.0 copy-done.1
  34.6 0.0 all-gather.3.cloned.1.call-update
  34.6 0.0 reduce-scatter.2.cloned.1.call-start
  34.7 36.6 %all-gather.3.cloned.1.call-done = bf16[1,2048,1024]{2,1,0:T(8,128)(2,1)} async-done(((bf16[1,2048,256]{2,1,0:T(8,128)(2,1)}), bf16[1,2048,1024]{2,1,0:T(8,128)(2,1)}) %all-gather.3.cloned.1.call-update) | async-done | bytes 4194320 | tf_op jit(solution)/shard_map/all_gather | solution.py:31
  71.3 8.6 %multiply_convert_fusion.1 = bf16[1024,1024]{1,0:T(8,128)(2,1)} fusion(bf16[1,2048,1024]{2,1,0:T(8,128)(2,1)} %all-gather.3.cloned.1.call-done, bf16[1,2048,1024]{2,1,0:T(8,128)(2,1)} %param.7), kind=kOutput, calls=%fused_computation.24 | convolution fusion | flops 4309647360 | bytes 10485760 | tf_op jit(solution)/shard_map/dot_general | solution.py:55
  79.8 0.0 reduce-scatter.2.cloned.1.call-update
  79.9 0.0 all-reduce.2.cloned.1.call-start
  79.9 0.0 copy-done
  79.9 13.7 %multiply_convert_fusion = bf16[2048,1024]{1,0:T(8,128)(2,1)} fusion(bf16[1,1024,1024]{2,1,0:T(8,128)(2,1)S(1)} %copy-done, bf16[1,2048,1024]{2,1,0:T(8,128)(2,1)} %param.7, bf16[1,2048,1024]{2,1,0:T(8,128)(2,1)} %all-gather.3.cloned.1.call-done, bf16[1,1024,1024]{2,1,0:T(8,128)(2,1)} %param.8), kind=kOutput, calls=%fused_computation.18 | convolution fusion | flops 8619294720 | bytes 16777216 | tf_op jit(solution)/shard_map/dot_general | solution.py:47
  93.6 0.0 copy-start.2
  93.6 0.0 all-reduce.2.cloned.1.call-update
  93.6 0.0 all-gather.5.cloned.1.call-start
  93.7 30.2 %reduce-scatter.2.cloned.1.call-done = bf16[256,1024]{1,0:T(8,128)(2,1)} async-done(((bf16[1024,1024]{1,0:T(8,128)(2,1)}), bf16[256,1024]{1,0:T(8,128)(2,1)}) %reduce-scatter.2.cloned.1.call-update) | async-done | bytes 524304 | tf_op jit(solution)/shard_map/reduce_scatter | solution.py:58
  123.9 0.0 copy-done.2
  123.9 3.7 %fusion.38 = (f32[1,256,1024]{2,1,0:T(8,128)}, bf16[256,1024]{1,0:T(8,128)(2,1)}, f32[1,256,1024]{2,1,0:T(8,128)}) fusion(bf16[256,1024]{1,0:T(8,128)(2,1)} %reduce-scatter.2.cloned.1.call-done, f32[1,256,1024]{2,1,0:T(8,128)S(1)} %copy-done.2, f32[1,256,1024]{2,1,0:T(8,128)} %param.10, bf16[1,1024,1024]{2,1,0:T(8,128)(2,1)} %param.8, s32[]{:T(128)S(6)} %select_n.7), kind=kLoop, calls=%fused_computation.38 | loop fusion | flops 3670016 | bytes 5767172 | tf_op jit(solution)/shard_map/broadcast_in_dim | solution.py:70
  127.6 0.0 all-gather.5.cloned.1.call-update
  127.7 83.6 %all-reduce.2.cloned.1.call-done = bf16[2048,1024]{1,0:T(8,128)(2,1)} async-done(((bf16[2048,1024]{1,0:T(8,128)(2,1)}), bf16[2048,1024]{1,0:T(8,128)(2,1)}) %all-reduce.2.cloned.1.call-update) | async-done | bytes 4194320 | tf_op jit(solution)/shard_map/psum | solution.py:50
  211.2 2.3 fusion.35
  213.5 45.9 %all-gather.5.cloned.1.call-done = bf16[1024,1024]{1,0:T(8,128)(2,1)} async-done(((bf16[256,1024]{1,0:T(8,128)(2,1)}), bf16[1024,1024]{1,0:T(8,128)(2,1)}) %all-gather.5.cloned.1.call-update) | async-done | bytes 2097168 | tf_op jit(solution)/shard_map/all_gather | solution.py:69
  259.3 3.1 %copy.12 = bf16[1,1024,1024]{2,1,0:T(8,128)(2,1)} copy(bf16[1,1024,1024]{2,1,0:T(8,128)(2,1)} %bitcast.78) | data formatting | bytes 4194304
Async XLA Ops:
  7.2 72.7 %copy-start = (bf16[1,1024,1024]{2,1,0:T(8,128)(2,1)S(1)}, bf16[1,1024,1024]{2,1,0:T(8,128)(2,1)}, u32[]{:S(2)}) copy-start(bf16[1,1024,1024]{2,1,0:T(8,128)(2,1)} %param.9) | copy-start | bytes 6291460
  7.2 64.1 %all-gather.3.cloned.1.call-start = ((), (), s32[]{:S(2)}) async-start(), calls=%async_computation.1 | async-start | bytes 5242880 | tf_op jit(solution)/shard_map/all_gather | solution.py:31
  7.2 26.4 %collective-permute-start = (bf16[1,2048,256]{2,1,0:T(8,128)(2,1)}, bf16[1,2048,256]{2,1,0:T(8,128)(2,1)S(1)}, u32[]{:S(2)}, u32[]{:S(2)}) collective-permute-start(bf16[1,2048,256]{2,1,0:T(8,128)(2,1)} %param.6), channel_id=1, source_target_pairs={{16,0},{0,16},{17,1},{1,17},{18,2},{2,18},{19,3},{3,19},{20,4},{4,... | collective-permute-start | bytes 3145736 | tf_op jit(solution)/shard_map/ppermute | solution.py:12
  33.6 1.0 copy-start.1
  34.6 89.3 %reduce-scatter.2.cloned.1.call-start = ((), (), s32[]{:S(2)}) async-start(), calls=%async_computation.3 | async-start | bytes 2621440 | tf_op jit(solution)/shard_map/reduce_scatter | solution.py:58
  79.9 131.3 %all-reduce.2.cloned.1.call-start = ((), (), s32[]{:S(2)}) async-start(), calls=%async_computation.2 | async-start | bytes 8388608 | tf_op jit(solution)/shard_map/psum | solution.py:50
  93.6 30.3 %copy-start.2 = (f32[1,256,1024]{2,1,0:T(8,128)S(1)}, f32[1,256,1024]{2,1,0:T(8,128)}, u32[]{:S(2)}) copy-start(f32[1,256,1024]{2,1,0:T(8,128)} %param.11) | copy-start | bytes 3145732
  93.6 165.7 %all-gather.5.cloned.1.call-start = ((), (), s32[]{:S(2)}) async-start(), calls=%async_computation.4 | async-start | bytes 2621440 | tf_op jit(solution)/shard_map/all_gather | solution.py:69
Sparse Core Ops, SparseCore 0:
  34.7 36.4 all-gather.2
  80.0 43.8 reduce-scatter.1
  126.4 84.7 all-reduce.1
  213.2 46.0 all-gather.4
where the time goes:
time: 269 us
  waiting for transfers between devices  220 us (82%)
  matrix products  22.2 us (8%)
  between operations  13.8 us (5%)
  other arithmetic  5.98 us (2%)
  local copies, waits for them, and re-layouts  4.06 us (2%)
  starting transfers between devices  3.19 us (1%)
    psum x1, waiting for transfers between devices, on_device(): lax.psum(partial_value.astype(jnp.bfloat16), 'tensor').astype(jnp.float32)  83.6 us
    all_gather x1, waiting for transfers between devices, on_device(): new_down = lax.all_gather(fresh_rows, 'dp', axis=0, tiled=True)  45.9 us
    all_gather x1, waiting for transfers between devices, on_device(): incoming = lax.all_gather(arrived, 'tensor', axis=2, tiled=True)  36.6 us
    reduce_scatter x1, waiting for transfers between devices, on_device(): lax.psum_scatter((product * grad_scale).astype(jnp.bfloat16), 'dp', scatt...  30.2 us
    ppermute x1, waiting for transfers between devices, from_behind(): return lax.ppermute(block, axis, route)  23.4 us
    dot_general x1, matrix products, on_device(): jnp.dot(act_grad, up_weight[0], preferred_element_type=jnp.float32)  13.7 us
    dot_general x1, matrix products, on_device(): lax.dot_general(hidden, incoming, (((0,), (0,)), ((), ())), preferred_ele...  8.56 us
  transfers between devices with their start and end apart: 5, of which 5 were waited for; matrix products, arithmetic and copies ran while one was open for 7% of the time, Pallas kernels for 0%

commit v1 on v0

v1 whole, which is shorter than its diff:
```python
import math

import jax
import jax.numpy as jnp
from jax import lax
from jax.experimental import pallas as pl
from jax.experimental.pallas import tpu as pltpu
from jax.sharding import PartitionSpec as P

F32 = jnp.float32
BF16 = jnp.bfloat16
COL_PARTS = 2
TILE = 256
CHUNKS = (((0, 0), (1, 0)), ((0, 1), (1, 1), (2, 0), (3, 0)), ((2, 1), (3, 1)))
SUMS = ("one", "one", "one",)
GATHERS = ("two", "two", "one",)
PLAN = (
    "h0", "b00", "b10", "t0", "r0", "a0", "b01", "b20", "b30", "b11", "g0", "t1", "b21",
    "b31", "t2", "p0", "r1", "a1", "w0", "r2", "a2", "g1", "x0", "l0", "x1", "g2", "l2",
    "l1",
)
ANYWHERE = pl.BlockSpec(memory_space=pl.ANY)
TOKEN = jax.ShapeDtypeStruct((8, 128), F32)
SMALL = pl.CostEstimate(flops=1024, bytes_accessed=1024, transcendentals=0)


def from_behind(block, axis, distance):
    devices = range(lax.axis_size(axis))
    route = [((i - distance) % len(devices), i) for i in devices]
    return lax.ppermute(block, axis, route)


def normal_cdf(inputs):
    return 0.5 * (1.0 + jax.scipy.special.erf(inputs * (1.0 / math.sqrt(2.0))))


def gelu_value(inputs):
    return inputs * normal_cdf(inputs)


def gelu_slope(inputs):
    return normal_cdf(inputs) + inputs * jnp.exp(-0.5 * inputs * inputs) * (
        1.0 / math.sqrt(2.0 * math.pi)
    )


def hidden_of(hidden_pre):
    return gelu_value(hidden_pre.astype(F32)).astype(BF16)


def act_grad_of(incoming, down, hidden_pre):
    back = lax.dot_general(incoming, down, (((1,), (1,)), ((), ())), preferred_element_type=F32)
    scale = 1.0 / math.sqrt(down.shape[1])
    return (back * scale * gelu_slope(hidden_pre.astype(F32))).astype(BF16)


def term_of(hidden, columns, token_total):
    product = lax.dot_general(
        hidden, columns, (((0,), (0,)), ((), ())), preferred_element_type=F32
    )
    return (product * (1.0 / math.sqrt(token_total))).astype(BF16)


def adam(gradient, moment, second, rows):
    new_m = 0.9 * moment + 0.1 * gradient
    new_v = 0.95 * second + 0.05 * gradient * gradient
    fresh = (rows.astype(F32) - 0.2 * new_m / (jnp.sqrt(new_v) + 1e-08)).astype(BF16)
    return new_m, new_v, fresh


def plain(handoff, hidden_pre, down_weight, up_weight, moment, second):
    arrived = from_behind(handoff, "pipe", -1)
    incoming = lax.all_gather(arrived, "tensor", axis=2, tiled=True)[0]
    model_width = incoming.shape[1]
    shard_rows = moment.shape[1]
    hidden_total = down_weight.shape[1] * lax.axis_size("tensor")
    token_total = incoming.shape[0] * lax.axis_size("dp")
    hidden = hidden_of(hidden_pre[0])
    act_grad = act_grad_of(incoming, down_weight[0], hidden_pre[0])
    partial_value = jnp.dot(act_grad, up_weight[0], preferred_element_type=F32) * (
        1.0 / math.sqrt(hidden_total)
    )
    input_grad = lax.psum_scatter(
        partial_value.astype(BF16), "tensor", scatter_dimension=1, tiled=True
    )
    gradient = lax.psum_scatter(
        term_of(hidden, incoming, token_total), "dp", scatter_dimension=0, tiled=True
    ).astype(F32)
    own_rows = lax.dynamic_slice_in_dim(
        down_weight[0], lax.axis_index("dp") * shard_rows, shard_rows, 0
    )
    new_m, new_v, fresh = adam(gradient, moment[0], second[0], own_rows)
    new_down = lax.all_gather(fresh, "dp", axis=0, tiled=True)
    return (input_grad[None], new_down[None], new_m[None], new_v[None])


def params(mib):
    return pltpu.CompilerParams(vmem_limit_bytes=mib * 2**20)


def prepare(hidden_pre, model_width):
    tokens, units = hidden_pre.shape
    scale = 1.0 / math.sqrt(model_width)

    def kernel(pre_ref, hidden_ref, slope_ref, token_ref):
        token_ref[...] = jnp.zeros_like(token_ref)
        pre = pre_ref[...].astype(F32)
        phi = 0.5 * (1.0 + lax.erf(pre * (1.0 / math.sqrt(2.0))))
        hidden_ref[...] = (pre * phi).astype(BF16).T
        bell = jnp.exp(-0.5 * pre * pre) * (1.0 / math.sqrt(2.0 * math.pi))
        slope_ref[...] = ((phi + pre * bell) * scale).astype(BF16)

    return pl.pallas_call(
        kernel,
        grid=(tokens // TILE,),
        in_specs=[pl.BlockSpec((TILE, units), lambda i: (i, 0))],
        out_specs=[
            pl.BlockSpec((units, TILE), lambda i: (0, i)),
            pl.BlockSpec((TILE, units), lambda i: (i, 0)),
            pl.BlockSpec((8, 128), lambda i: (0, 0)),
        ],
        out_shape=[
            jax.ShapeDtypeStruct((units, tokens), BF16),
            jax.ShapeDtypeStruct((tokens, units), BF16),
            TOKEN,
        ],
        compiler_params=params(8),
        cost_estimate=SMALL,
        name="prepare",
    )(hidden_pre)


def terms(hidden_t, pieces, places, scale, paired, after):
    units, tokens = hidden_t.shape
    size, width = units // 4, pieces[0].shape[1]
    count, wide = len(pieces), len(pieces) * pieces[0].shape[1]
    heights = [size, size, 2 * size] if paired else [size] * 4
    number = len(heights)

    def kernel(places_ref, hidden_ref, *refs):
        piece_refs, refs = refs[:count], refs[count + len(after) :]
        out_refs, token_ref, joined = refs[:number], refs[number], refs[number + 1]
        step = pl.program_id(0)

        @pl.when(step == 0)
        def _():
            token_ref[...] = jnp.zeros_like(token_ref)
            for j in range(count):
                joined[:, j * width : (j + 1) * width] = piece_refs[j][...]

        product = jnp.dot(hidden_ref[...], joined[...], preferred_element_type=F32)
        product = (product * scale).astype(BF16)
        for j in range(4):
            @pl.when(step == j)
            def _(j=j):
                if paired and j >= 2:
                    out_refs[2][(j - 2) * size : (j - 1) * size, :] = product
                else:
                    out_refs[j][...] = product

    return pl.pallas_call(
        kernel,
        grid_spec=pltpu.PrefetchScalarGridSpec(
            num_scalar_prefetch=1,
            grid=(4,),
            in_specs=[pl.BlockSpec((size, tokens), lambda i, places: (places[i], 0))]
            + [pl.BlockSpec((tokens, width), lambda i, places: (0, 0))] * count
            + [ANYWHERE] * len(after),
            out_specs=[pl.BlockSpec((height, wide), lambda i, places: (0, 0)) for height in heights]
            + [pl.BlockSpec((8, 128), lambda i, places: (0, 0))],
            scratch_shapes=[pltpu.VMEM((tokens, wide), BF16)],
        ),
        out_shape=[jax.ShapeDtypeStruct((height, wide), BF16) for height in heights] + [TOKEN],
        compiler_params=params(16),
        cost_estimate=SMALL,
        name="terms",
    )(places, hidden_t, *pieces, *after)


def adam_chunk(shares, near, moment, second, down, columns, rank, previous, width, after):
    size, wide = shares[0].shape
    count = wide // width
    total = moment.shape[1]
    number = len(shares) + len(near)

    def kernel(columns_ref, rank_ref, *refs):
        m_ref, v_ref, down_ref = refs[number : number + 3]
        fresh_ref, new_m_ref, new_v_ref, token_ref = refs[-4:]
        token_ref[...] = jnp.zeros_like(token_ref)
        gradient = refs[0][...].astype(F32)
        for ref in refs[1:number]:
            gradient += ref[...].astype(F32)
        new_m = 0.9 * m_ref[...] + 0.1 * gradient
        new_v = 0.95 * v_ref[...] + 0.05 * gradient * gradient
        new_m_ref[...] = new_m
        new_v_ref[...] = new_v
        rows = down_ref[...].astype(F32)
        fresh_ref[...] = (rows - 0.2 * new_m / (jnp.sqrt(new_v) + 1e-08)).astype(BF16)

    here = pl.BlockSpec((size, width), lambda j, columns, rank: (0, j))
    below = pl.BlockSpec((size, width), lambda j, columns, rank: (1, j))
    there = pl.BlockSpec((size, width), lambda j, columns, rank: (0, columns[j]))
    return pl.pallas_call(
        kernel,
        grid_spec=pltpu.PrefetchScalarGridSpec(
            num_scalar_prefetch=2,
            grid=(count,),
            in_specs=[here] * len(shares)
            + [below] * len(near)
            + [there] * 2
            + [pl.BlockSpec((size, width), lambda j, columns, rank: (rank[0], columns[j]))]
            + [ANYWHERE] * (len(after) + len(previous)),
            out_specs=[here, there, there, pl.BlockSpec((8, 128), lambda j, columns, rank: (0, 0))],
        ),
        out_shape=[
            jax.ShapeDtypeStruct((size, wide), BF16),
            jax.ShapeDtypeStruct((size, total), F32),
            jax.ShapeDtypeStruct((size, total), F32),
            TOKEN,
        ],
        input_output_aliases={
            number + len(after) + 5: 1, number + len(after) + 6: 2
        } if previous else {},
        compiler_params=params(8),
        cost_estimate=SMALL,
        name="adam",
    )(columns, rank, *shares, *near, moment, second, down, *after, *previous)


def place_rows(shards, rows, columns, previous, total, width, after):
    size, wide = shards[0].shape
    count = wide // width
    number = len(shards)

    def kernel(rows_ref, columns_ref, *refs):
        shard_refs, out_ref, sems = refs[:number], refs[-2], refs[-1]
        copies = []
        for k in range(number):
            for j in range(count):
                copies.append(
                    pltpu.make_async_copy(
                        shard_refs[k].at[:, pl.ds(j * width, width)],
                        out_ref.at[
                            pl.ds(pl.multiple_of(rows_ref[k] * size, size), size),
                            pl.ds(pl.multiple_of(columns_ref[j] * width, width), width),
                        ],
                        sems.at[k, j],
                    )
                )
        for copy in copies:
            copy.start()
        for copy in copies:
            copy.wait()

    return pl.pallas_call(
        kernel,
        grid_spec=pltpu.PrefetchScalarGridSpec(
            num_scalar_prefetch=2,
            grid=(1,),
            in_specs=[ANYWHERE] * (number + len(after) + len(previous)),
            out_specs=ANYWHERE,
            scratch_shapes=[pltpu.SemaphoreType.DMA((number, count))],
        ),
        out_shape=jax.ShapeDtypeStruct(total, BF16),
        input_output_aliases={2 + number + len(after): 0} if previous else {},
        compiler_params=params(8),
        cost_estimate=SMALL,
        name="place",
    )(rows, columns, *shards, *after, *previous)


def partials(pieces, where, order, slope, down, up, scale, after):
    tokens, units = slope.shape
    model_width = down.shape[1]
    width = pieces[0].shape[1]
    count = len(pieces)
    block = model_width // 4
    rows = tokens

    def kernel(where_ref, order_ref, *refs):
        piece_refs, refs = refs[:count], refs[count:]
        slope_ref, down_ref, up_ref = refs[:3]
        own_ref, other_ref, send_ref, token_ref, joined, product_ref = refs[3 + len(after) :]
        token_ref[...] = jnp.zeros_like(token_ref)
        for j in range(count):
            joined[:, pl.ds(pl.multiple_of(where_ref[j] * width, width), width)] = piece_refs[j][...]
        back = lax.dot_general(
            joined[...], down_ref[...], (((1,), (1,)), ((), ())), preferred_element_type=F32
        )
        act_grad = (back * slope_ref[...].astype(F32)).astype(BF16)
        product = jnp.dot(act_grad, up_ref[...], preferred_element_type=F32) * scale
        product_ref[...] = product.astype(BF16)

        def columns(k):
            return product_ref[:, pl.ds(pl.multiple_of(order_ref[k] * block, block), block)]

        own_ref[...] = columns(0)
        other_ref[...] = columns(1)
        send_ref[:, :block] = columns(2)
        send_ref[:, block:] = columns(3)

    return pl.pallas_call(
        kernel,
        grid_spec=pltpu.PrefetchScalarGridSpec(
            num_scalar_prefetch=2,
            grid=(rows // TILE,),
            in_specs=[pl.BlockSpec((TILE, width), lambda i, w, o: (i, 0))] * count
            + [pl.BlockSpec((TILE, units), lambda i, w, o: (i, 0))]
            + [pl.BlockSpec((units, model_width), lambda i, w, o: (0, 0))] * 2
            + [ANYWHERE] * len(after),
            out_specs=[
                pl.BlockSpec((TILE, block), lambda i, w, o: (i, 0)),
                pl.BlockSpec((TILE, block), lambda i, w, o: (i, 0)),
                pl.BlockSpec((TILE, 2 * block), lambda i, w, o: (i, 0)),
                pl.BlockSpec((8, 128), lambda i, w, o: (0, 0)),
            ],
            scratch_shapes=[
                pltpu.VMEM((TILE, model_width), BF16),
                pltpu.VMEM((TILE, model_width), BF16),
            ],
        ),
        out_shape=[
            jax.ShapeDtypeStruct((rows, block), BF16),
            jax.ShapeDtypeStruct((rows, block), BF16),
            jax.ShapeDtypeStruct((rows, 2 * block), BF16),
            TOKEN,
        ],
        compiler_params=params(20),
        cost_estimate=SMALL,
        name="partials",
    )(where, order, *pieces, slope, down, up, *after)


def on_device(handoff, hidden_pre, down_weight, up_weight, moment, second):
    rank = lax.axis_index("dp")
    tensor = lax.axis_index("tensor")
    handoff, hidden_pre, down, up = handoff[0], hidden_pre[0], down_weight[0], up_weight[0]
    tokens, block = handoff.shape
    width = block // COL_PARTS
    model_width = down.shape[1]

    def swapped(value, axis, distance):
        return lax.ppermute(value, axis, [(i, i ^ distance) for i in range(4)])

    def column_of(key):
        return (tensor ^ key[0]) * COL_PARTS + key[1]

    def columns_of(keys):
        return jnp.stack([column_of(key) for key in keys]).astype(jnp.int32)

    shards = jnp.stack([rank, rank ^ 1, rank ^ 2, rank ^ 3]).astype(jnp.int32)
    paired = jnp.stack([rank, rank ^ 2, rank ^ 3, rank ^ 1]).astype(jnp.int32)
    rank_now = rank.astype(jnp.int32)[None]
    order = jnp.stack([tensor, tensor ^ 2, tensor ^ 1, tensor ^ 3]).astype(jnp.int32)
    term_scale = 1.0 / math.sqrt(tokens * 4)
    partial_scale = 1.0 / math.sqrt(down.shape[0] * 4)
    columns = [columns_of(chunk) for chunk in CHUNKS]
    keys = [(b, g) for g in range(COL_PARTS) for b in range(4)]
    where = columns_of(keys)
    held, values, moments, new_down = [], {}, [], []

    def after():
        out = list(held)
        held.clear()
        return out

    def arrive(name):
        value, token = lax.optimization_barrier((values[name], values["token"]))
        values[name] = value
        held.extend([value, token])

    for part in range(COL_PARTS):
        columns_now = handoff[:, part * width : (part + 1) * width]
        values["b0" + str(part)] = from_behind(columns_now, "pipe", -1)

    for name in PLAN:
        kind, k = name[0], int(name[1])
        if kind == "h":
            values["hidden"], values["slope"], values["token"] = prepare(hidden_pre, model_width)
        elif kind == "b":
            arrive(name)
            part = name[2]
            if k == 0:
                values["b1" + part] = swapped(values[name], "tensor", 1)
                values["b2" + part] = swapped(values[name], "tensor", 2)
            elif k == 2:
                values["b3" + part] = swapped(values[name], "tensor", 1)
        elif kind == "t":
            pieces = [values["b%d%d" % key] for key in CHUNKS[k]]
            pair = SUMS[k] == "two"
            *out, values["token"] = terms(
                values["hidden"], pieces, paired if pair else shards, term_scale, pair, after()
            )
            if pair:
                values["s0" + name[1]], values["s2" + name[1]] = out[:2]
                values["m" + name[1]] = swapped(out[2], "dp", 1)
            else:
                values["s0" + name[1]] = out[0]
                for j in (3, 2, 1):
                    values["s%d%d" % (j, k)] = swapped(out[j], "dp", j)
        elif kind == "m":
            arrive(name)
            size = values["s0" + name[1]].shape[0]
            far = values["s2" + name[1]].astype(F32) + values[name][:size].astype(F32)
            values["s2" + name[1]] = swapped(far.astype(BF16), "dp", 2)
        elif kind == "r":
            for j in (2,) if SUMS[k] == "two" else (3, 2, 1):
                arrive("s%d%d" % (j, k))
        elif kind == "a":
            if SUMS[k] == "two":
                shares, near = [values["s%d%d" % (j, k)] for j in (0, 2)], [values["m" + name[1]]]
            else:
                shares, near = [values["s%d%d" % (j, k)] for j in range(4)], []
            fresh, *moments[:], values["token"] = adam_chunk(
                shares, near, moment[0], second[0], down, columns[k], rank_now,
                moments, width, after(),
            )
            values["g0" + name[1]] = fresh
            values["g2" + name[1]] = swapped(fresh, "dp", 2)
            values["g1" + name[1]] = swapped(fresh, "dp", 1)
            if GATHERS[k] == "one":
                values["g3" + name[1]] = swapped(fresh, "dp", 3)
        elif kind == "g":
            arrive("g2" + name[1])
            if GATHERS[k] != "one":
                values["g3" + name[1]] = swapped(values["g2" + name[1]], "dp", 1)
        elif kind == "l":
            gathered = [values["g%d%d" % (j, k)] for j in range(4)]
            new_down[:] = [
                place_rows(gathered, shards, columns[k], new_down, down.shape, width, after())
            ]
        elif kind == "p":
            pieces = [values["b%d%d" % key] for key in keys]
            values["own"], values["other"], values["x0"], values["token"] = partials(
                pieces, where, order, values["slope"], down, up, partial_scale, after()
            )
            if "w0" not in PLAN:
                values["x0"] = swapped(values["x0"], "tensor", 1)
        elif kind == "w":
            arrive("x0")
            values["x0"] = swapped(values["x0"], "tensor", 1)
        elif kind == "x" and k == 0:
            arrive("x0")
            other = values["other"].astype(F32) + values["x0"][:, block:].astype(F32)
            values["x1"] = swapped(other.astype(BF16), "tensor", 2)
        elif kind == "x":
            arrive("x1")
            own = values["own"].astype(F32) + values["x0"][:, :block].astype(F32)
            input_grad = (own + values["x1"].astype(F32)).astype(BF16)
    return (input_grad[None], new_down[0][None], moments[0][None], moments[1][None])


def solution(mesh):
    placed = (
        P("pipe", "dp", "tensor"),
        P("pipe", "dp", "tensor"),
        P("pipe", "tensor", None),
        P("pipe", "tensor", None),
        P("pipe", ("tensor", "dp"), None),
        P("pipe", ("tensor", "dp"), None),
    )
    fits = mesh.shape["tensor"] == 4 and mesh.shape["dp"] == 4
    return jax.shard_map(
        on_device if fits else plain,
        mesh=mesh,
        in_specs=placed,
        out_specs=(
            P("pipe", "dp", "tensor"),
            P("pipe", "tensor", None),
            P("pipe", ("tensor", "dp"), None),
            P("pipe", ("tensor", "dp"), None),
        ),
        check_vma=False,
    )
```

time: 269 us -> 156 us (0.58)
  waiting for transfers between devices: 220 us -> 52.4 us
  Pallas kernels: 0 us -> 46.4 us
  starting transfers between devices: 3.19 us -> 30.4 us
  matrix products: 22.2 us -> 0 us
  local copies, waits for them, and re-layouts: 4.06 us -> 22.8 us
  between operations: 13.8 us -> 0.85 us
  other arithmetic: 5.98 us -> 2.1 us
    psum x1 -> x0, waiting for transfers between devices: 83.6 us -> none  [on_device(): lax.psum(partial_value.astype(jnp.bfloat16), 'tensor').astype(jnp.float32)]
    all_gather x2 -> x0, waiting for transfers between devices: 82.5 us -> none  [the longest x1 45.9 us: on_device(): new_down = lax.all_gather(fresh_rows, 'dp', axis=0, tiled=True)]
    ppermute x0 -> x26, waiting for transfers between devices: none -> 51.6 us  [swapped(): return lax.ppermute(value, axis, [(i, i ^ distance) for i in range(4)])]
    pallas_call x0 -> x11, Pallas kernels: none -> 46.4 us  [the longest x3 15.3 us: terms(): pl.pallas_call(kernel, grid_spec=pltpu.PrefetchScalarGridSpec(num_scalar_...]
    reduce_scatter x1 -> x0, waiting for transfers between devices: 30.2 us -> none  [on_device(): lax.psum_scatter((product * grad_scale).astype(jnp.bfloat16), 'dp', scatt...]
    ppermute x0 -> x26, starting transfers between devices: none -> 25.7 us  [swapped(): return lax.ppermute(value, axis, [(i, i ^ distance) for i in range(4)])]
    ppermute x1 -> x2, waiting for transfers between devices: 23.4 us -> 0.82 us  [from_behind(): return lax.ppermute(block, axis, route)]
    dot_general x2 -> x0, matrix products: 22.2 us -> none  [the longest x1 13.7 us: on_device(): jnp.dot(act_grad, up_weight[0], preferred_element_type=jnp.float32)]
  transfers between devices with their start and end apart: 5 -> 28, of which waited for: 5 -> 11; matrix products, arithmetic and copies ran while one was open for 7% -> 1% of each run, Pallas kernels for 0% -> 26%
where the time goes in v1:
time: 156 us; the launch traced here: 155 us
  waiting for transfers between devices  52.4 us (34%)
  Pallas kernels  46.4 us (30%)
  starting transfers between devices  30.4 us (19%)
  local copies, waits for them, and re-layouts  22.8 us (15%)
  other arithmetic  2.1 us (1%)
    ppermute x26, waiting for transfers between devices, swapped(): return lax.ppermute(value, axis, [(i, i ^ distance) for i in range(4)])  51.6 us
    ppermute x26, starting transfers between devices, swapped(): return lax.ppermute(value, axis, [(i, i ^ distance) for i in range(4)])  25.7 us
    unnamed x50, local copies, waits for them, and re-layouts  20.6 us
    pallas_call x3, Pallas kernels, terms(): pl.pallas_call(kernel, grid_spec=pltpu.PrefetchScalarGridSpec(num_scalar_...  15.3 us
    pallas_call x1, Pallas kernels, partials(): pl.pallas_call(kernel, grid_spec=pltpu.PrefetchScalarGridSpec(num_scalar_...  13.5 us
    pallas_call x3, Pallas kernels, adam_chunk(): pl.pallas_call(kernel, grid_spec=pltpu.PrefetchScalarGridSpec(num_scalar_...  8.13 us
    pallas_call x1, Pallas kernels, prepare(): pl.pallas_call(kernel, grid=(tokens // TILE,), in_specs=[pl.BlockSpec((TI...  5.02 us
    ppermute x2, starting transfers between devices, from_behind(): return lax.ppermute(block, axis, route)  4.71 us
  transfers between devices with their start and end apart: 28, of which 11 were waited for; matrix products, arithmetic and copies ran while one was open for 1% of the time, Pallas kernels for 26%

profile of v1, /device:TPU:0, one launch (start us, length us, event | category | flops | bytes accessed | tf_op | source)
XLA Modules:
  0.0 154.9 jit_solution(14999463309166534356)
XLA Ops:
  0.6 2.1 %fusion.1 = (bf16[2048,128]{1,0:T(8,128)(2,1)}, bf16[2048,128]{1,0:T(8,128)(2,1)S(1)}) fusion(bf16[2048,256]{1,0:T(8,128)(2,1)} %bitcast.42), kind=kLoop, calls=%fused_computation.8 | loop fusion | bytes 2097152 | tf_op jit(solution)/shard_map/slice | solution.py:373
  2.7 3.0 %collective-permute-start = (bf16[2048,128]{1,0:T(8,128)(2,1)S(1)}, bf16[2048,128]{1,0:T(8,128)(2,1)}, u32[]{:S(2)}, u32[]{:S(2)}) collective-permute-start(bf16[2048,128]{1,0:T(8,128)(2,1)S(1)} %get-tuple-element.163), channel_id=1, source_target_pairs={{16,0},{0,16},{17,1},{1,17},{18,2},{2,18},{19,3},{3,19},{20,4},{4,... | collective-permute-start | bytes 1572872 | tf_op jit(solution)/shard_map/ppermute | solution.py:30
  5.7 2.2 %copy-done.17 = bf16[1,2048,1024]{2,1,0:T(8,128)(2,1)S(1)} copy-done((bf16[1,2048,1024]{2,1,0:T(8,128)(2,1)S(1)}, bf16[1,2048,1024]{2,1,0:T(8,128)(2,1)}, u32[]{:S(2)}) %copy-start.17) | copy-done | bytes 4194328
  7.8 5.0 %prepare.1 = (bf16[1024,2048]{1,0:T(8,128)(2,1)S(1)}, bf16[2048,1024]{1,0:T(8,128)(2,1)S(1)}, f32[8,128]{1,0:T(8,128)S(1)}) custom-call(bf16[2048,1024]{1,0:T(8,128)(2,1)S(1)} %bitcast.37), custom_call_target="tpu_custom_call" | custom-call | flops 1024 | bytes 1024 | tf_op jit(solution)/shard_map/prepare/pallas_call | solution.py:113
  12.9 2.0 %copy-done = bf16[1024,2048]{1,0:T(8,128)(2,1)} copy-done((bf16[1024,2048]{1,0:T(8,128)(2,1)}, bf16[1024,2048]{1,0:T(8,128)(2,1)S(1)}, u32[]{:S(2)}) %copy-start) | copy-done | bytes 4194328
  14.9 2.0 %copy-done.15 = bf16[2048,1024]{1,0:T(8,128)(2,1)} copy-done((bf16[2048,1024]{1,0:T(8,128)(2,1)}, bf16[2048,1024]{1,0:T(8,128)(2,1)S(1)}, u32[]{:S(2)}) %copy-start.15) | copy-done | bytes 4194328
  17.7 1.7 %collective-permute-start.7 = (bf16[2048,128]{1,0:T(8,128)(2,1)}, bf16[2048,128]{1,0:T(8,128)(2,1)}, u32[]{:S(2)}, u32[]{:S(2)}) collective-permute-start(bf16[2048,128]{1,0:T(8,128)(2,1)} %get-tuple-element.162), channel_id=1, source_target_pairs={{16,0},{0,16},{17,1},{1,17},{18,2},{2,18},{19,3},{3,19},{20,4},{4,... | collective-permute-start | bytes 1572872 | tf_op jit(solution)/shard_map/ppermute | solution.py:30
  21.8 2.2 %copy-done.1 = bf16[1024,2048]{1,0:T(8,128)(2,1)S(1)} copy-done((bf16[1024,2048]{1,0:T(8,128)(2,1)S(1)}, bf16[1024,2048]{1,0:T(8,128)(2,1)}, u32[]{:S(2)}) %copy-start.1) | copy-done | bytes 4194328
  25.0 4.7 %terms.3 = (bf16[256,256]{1,0:T(8,128)(2,1)S(1)}, bf16[256,256]{1,0:T(8,128)(2,1)}, bf16[256,256]{1,0:T(8,128)(2,1)}, bf16[256,256]{1,0:T(8,128)(2,1)}, f32[8,128]{1,0:T(8,128)S(1)}) custom-call(s32[4]{0:T(128)S(1)} %pad_add_fusion.2.places_ref.rows_ref, bf16[1024,2048]{1,0:T(8,128)(2,1)S(1)} %copy-done.1, ...), custom_call_target="tpu_custom_call" | custom-call | flops 1024 | bytes 1024 | tf_op jit(solution)/shard_map/terms/pallas_call | solution.py:161
  30.4 3.6 %collective-permute-start.5 = (bf16[256,256]{1,0:T(8,128)(2,1)}, bf16[256,256]{1,0:T(8,128)(2,1)S(1)}, u32[]{:S(2)}, u32[]{:S(2)}) collective-permute-start(bf16[256,256]{1,0:T(8,128)(2,1)} %get-tuple-element.95), channel_id=1, source_target_pairs={{0,12},{4,8},{8,4},{12,0},{1,13},{5,9},{9,5},{13,1},{2,14},{6,10},... | collective-permute-start | bytes 393224 | tf_op jit(solution)/shard_map/ppermute | solution.py:343
  34.9 4.0 %collective-permute-done.5.refs_3_.refs_7_ = bf16[256,256]{1,0:T(8,128)(2,1)S(1)} collective-permute-done((bf16[256,256]{1,0:T(8,128)(2,1)}, bf16[256,256]{1,0:T(8,128)(2,1)S(1)}, u32[]{:S(2)}, u32[]{:S(2)}) %collective-permute-start.5) | collective-permute-done | bytes 131104 | tf_op jit(solution)/shard_map/ppermute | solution.py:343
  38.9 6.5 %collective-permute-done.4.refs_2_.refs_9_ = bf16[256,256]{1,0:T(8,128)(2,1)S(1)} collective-permute-done((bf16[256,256]{1,0:T(8,128)(2,1)}, bf16[256,256]{1,0:T(8,128)(2,1)S(1)}, u32[]{:S(2)}, u32[]{:S(2)}) %collective-permute-start.4) | collective-permute-done | bytes 131104 | tf_op jit(solution)/shard_map/ppermute | solution.py:343
  47.5 1.9 %adam.3 = (bf16[256,256]{1,0:T(8,128)(2,1)S(1)}, f32[256,1024]{1,0:T(8,128)}, f32[256,1024]{1,0:T(8,128)}, f32[8,128]{1,0:T(8,128)S(1)}) custom-call(s32[2]{0:T(128)S(1)} %pad_add_fusion.1.columns_ref, s32[1]{0:T(128)} %bitcast.14.rank_ref, bf16[256,256]{1,0:T(8,128)(2,1)S(1)} %copy-done.24, bf16[256,256]{1,0:T(8,128)(2,1)S(1)} %collective-permute-done.3.refs_1_.refs_11_, ...), custom_call_target="tpu_custom_call" | custom-call | flops 1024 | bytes 1024 | tf_op jit(solution)/shard_map/adam/pallas_call | solution.py:203
  50.7 8.8 %collective-permute-done.10.refs_12_.refs_2_ = bf16[256,256]{1,0:T(8,128)(2,1)S(1)} collective-permute-done((bf16[256,256]{1,0:T(8,128)(2,1)S(1)}, bf16[256,256]{1,0:T(8,128)(2,1)S(1)}, u32[]{:S(2)}, u32[]{:S(2)}) %collective-permute-start.10) | collective-permute-done | bytes 131104 | tf_op jit(solution)/shard_map/ppermute | solution.py:343
  59.5 6.1 %terms.4 = (bf16[256,512]{1,0:T(8,128)(2,1)S(1)}, bf16[256,512]{1,0:T(8,128)(2,1)}, bf16[256,512]{1,0:T(8,128)(2,1)}, bf16[256,512]{1,0:T(8,128)(2,1)}, f32[8,128]{1,0:T(8,128)S(1)}) custom-call(s32[4]{0:T(128)S(1)} %pad_add_fusion.2.places_ref.rows_ref, bf16[1024,2048]{1,0:T(8,128)(2,1)S(1)} %copy-done.2, ...), custom_call_target="tpu_custom_call" | custom-call | flops 1024 | bytes 1024 | tf_op jit(solution)/shard_map/terms/pallas_call | solution.py:161
  67.7 3.1 %collective-permute-start.12 = (bf16[256,512]{1,0:T(8,128)(2,1)}, bf16[256,512]{1,0:T(8,128)(2,1)}, u32[]{:S(2)}, u32[]{:S(2)}) collective-permute-start(bf16[256,512]{1,0:T(8,128)(2,1)} %get-tuple-element.119), channel_id=1, source_target_pairs={{0,4},{4,0},{8,12},{12,8},{1,5},{5,1},{9,13},{13,9},{2,6},{6,2},{1... | collective-permute-start | bytes 786440 | tf_op jit(solution)/shard_map/ppermute | solution.py:343
  74.2 2.2 %copy-done.16 = bf16[2048,1024]{1,0:T(8,128)(2,1)S(1)} copy-done((bf16[2048,1024]{1,0:T(8,128)(2,1)S(1)}, bf16[2048,1024]{1,0:T(8,128)(2,1)}, u32[]{:S(2)}) %copy-start.16) | copy-done | bytes 4194328
  77.9 13.5 %partials.1 = (bf16[2048,256]{1,0:T(8,128)(2,1)S(1)}, bf16[2048,256]{1,0:T(8,128)(2,1)S(1)}, bf16[2048,512]{1,0:T(8,128)(2,1)S(1)}, f32[8,128]{1,0:T(8,128)S(1)}) custom-call(s32[8]{0:T(128)S(1)} %stack.80.where_ref, s32[4]{0:T(128)S(1)} %pad_add_fusion.order_ref, bf16[2048,128]{1,0:T(8,128)(2,1)} %collective-permute-done.refs_0_.refs_2_, ...), custom_call_target="tpu_custom_call" | custom-call | flops 1024 | bytes 1024 | tf_op jit(solution)/shard_map/partials/pallas_call | solution.py:302
  91.5 4.3 %adam.4 = (bf16[256,512]{1,0:T(8,128)(2,1)S(1)}, f32[256,1024]{1,0:T(8,128)}, f32[256,1024]{1,0:T(8,128)}, f32[8,128]{1,0:T(8,128)S(1)}) custom-call(s32[4]{0:T(128)S(1)} %pad_add_fusion.3.columns_ref, s32[1]{0:T(128)} %bitcast.14.rank_ref, bf16[256,512]{1,0:T(8,128)(2,1)S(1)} %copy-done.20, ...), custom_call_target="tpu_custom_call", output_to_operand_aliasing={{1}: (15, {}), {2}: (16, {})} | custom-call | flops 1024 | bytes 1024 | tf_op jit(solution)/shard_map/adam/pallas_call | solution.py:203
  95.9 4.5 %terms.5 = (bf16[256,256]{1,0:T(8,128)(2,1)S(1)}, bf16[256,256]{1,0:T(8,128)(2,1)S(1)}, bf16[256,256]{1,0:T(8,128)(2,1)S(1)}, bf16[256,256]{1,0:T(8,128)(2,1)S(1)}, f32[8,128]{1,0:T(8,128)}) custom-call(s32[4]{0:T(128)S(1)} %pad_add_fusion.2.places_ref.rows_ref, bf16[1024,2048]{1,0:T(8,128)(2,1)S(1)} %copy-done.3, ...), custom_call_target="tpu_custom_call" | custom-call | flops 1024 | bytes 1024 | tf_op jit(solution)/shard_map/terms/pallas_call | solution.py:161
  101.8 2.9 %collective-permute-start.16 = (bf16[256,256]{1,0:T(8,128)(2,1)S(1)}, bf16[256,256]{1,0:T(8,128)(2,1)S(1)}, u32[]{:S(2)}, u32[]{:S(2)}) collective-permute-start(bf16[256,256]{1,0:T(8,128)(2,1)S(1)} %get-tuple-element.136), channel_id=1, source_target_pairs={{0,4},{4,0},{8,12},{12,8},{1,5},{5,1},{9,13},{13,9},{2,6},{6,2},{1... | collective-permute-start | bytes 393224 | tf_op jit(solution)/shard_map/ppermute | solution.py:343
  104.8 3.8 %collective-permute-done.18.refs_3_.refs_9_ = bf16[256,256]{1,0:T(8,128)(2,1)S(1)} collective-permute-done((bf16[256,256]{1,0:T(8,128)(2,1)S(1)}, bf16[256,256]{1,0:T(8,128)(2,1)S(1)}, u32[]{:S(2)}, u32[]{:S(2)}) %collective-permute-start.18) | collective-permute-done | bytes 131104 | tf_op jit(solution)/shard_map/ppermute | solution.py:343
  108.6 5.5 %collective-permute-done.17.refs_2_.refs_11_ = bf16[256,256]{1,0:T(8,128)(2,1)S(1)} collective-permute-done((bf16[256,256]{1,0:T(8,128)(2,1)S(1)}, bf16[256,256]{1,0:T(8,128)(2,1)S(1)}, u32[]{:S(2)}, u32[]{:S(2)}) %collective-permute-start.17) | collective-permute-done | bytes 131104 | tf_op jit(solution)/shard_map/ppermute | solution.py:343
  114.1 1.9 %adam.5 = (bf16[256,256]{1,0:T(8,128)(2,1)S(1)}, f32[256,1024]{1,0:T(8,128)}, f32[256,1024]{1,0:T(8,128)}, f32[8,128]{1,0:T(8,128)S(1)}) custom-call(s32[2]{0:T(128)S(1)} %pad_add_fusion.4.columns_ref, s32[1]{0:T(128)} %bitcast.14.rank_ref, bf16[256,256]{1,0:T(8,128)(2,1)S(1)} %get-tuple-element.135.refs_0_, ...), custom_call_target="tpu_custom_call", output_to_operand_aliasing={{1}: (17, {}), {2}: (18, {})} | custom-call | flops 1024 | bytes 1024 | tf_op jit(solution)/shard_map/adam/pallas_call | solution.py:203
  117.9 2.7 %collective-permute-start.24 = (bf16[256,256]{1,0:T(8,128)(2,1)S(1)}, bf16[256,256]{1,0:T(8,128)(2,1)S(1)}, u32[]{:S(2)}, u32[]{:S(2)}) collective-permute-start(bf16[256,256]{1,0:T(8,128)(2,1)S(1)} %get-tuple-element.154.refs_0_), channel_id=1, source_target_pairs={{0,8},{4,12},{8,0},{12,4},{1,9},{5,13},{9,1},{13,5},{2,10},{6,14},... | collective-permute-start | bytes 393224 | tf_op jit(solution)/shard_map/ppermute | solution.py:343
  120.6 2.0 %collective-permute-start.27 = (bf16[256,256]{1,0:T(8,128)(2,1)S(1)}, bf16[256,256]{1,0:T(8,128)(2,1)S(1)}, u32[]{:S(2)}, u32[]{:S(2)}) collective-permute-start(bf16[256,256]{1,0:T(8,128)(2,1)S(1)} %collective-permute-done.10.refs_12_.refs_2_), channel_id=1, source_target_pairs={{0,4},{4,0},{8,12},{12,8},{1,5},{5,1},{9,13},{13,9},{2,6},{6,2},{1... | collective-permute-start | bytes 393224 | tf_op jit(solution)/shard_map/ppermute | solution.py:343
  122.6 11.1 %collective-permute-done.21.refs_4_.refs_2_ = bf16[256,512]{1,0:T(8,128)(2,1)S(1)} collective-permute-done((bf16[256,512]{1,0:T(8,128)(2,1)S(1)}, bf16[256,512]{1,0:T(8,128)(2,1)S(1)}, u32[]{:S(2)}, u32[]{:S(2)}) %collective-permute-start.21) | collective-permute-done | bytes 262176 | tf_op jit(solution)/shard_map/ppermute | solution.py:343
  133.7 2.7 %collective-permute-done.24.refs_2_.refs_6_ = bf16[256,256]{1,0:T(8,128)(2,1)S(1)} collective-permute-done((bf16[256,256]{1,0:T(8,128)(2,1)S(1)}, bf16[256,256]{1,0:T(8,128)(2,1)S(1)}, u32[]{:S(2)}, u32[]{:S(2)}) %collective-permute-start.24) | collective-permute-done | bytes 131104 | tf_op jit(solution)/shard_map/ppermute | solution.py:343
  136.5 2.3 %collective-permute-start.25 = (bf16[256,256]{1,0:T(8,128)(2,1)S(1)}, bf16[256,256]{1,0:T(8,128)(2,1)S(1)}, u32[]{:S(2)}, u32[]{:S(2)}) collective-permute-start(bf16[256,256]{1,0:T(8,128)(2,1)S(1)} %get-tuple-element.154.refs_0_), channel_id=1, source_target_pairs={{0,12},{4,8},{8,4},{12,0},{1,13},{5,9},{9,5},{13,1},{2,14},{6,10},... | collective-permute-start | bytes 393224 | tf_op jit(solution)/shard_map/ppermute | solution.py:343
  142.7 5.5 %collective-permute-done.23.refs_1_ = bf16[256,256]{1,0:T(8,128)(2,1)S(1)} collective-permute-done((bf16[256,256]{1,0:T(8,128)(2,1)S(1)}, bf16[256,256]{1,0:T(8,128)(2,1)S(1)}, u32[]{:S(2)}, u32[]{:S(2)}) %collective-permute-start.23) | collective-permute-done | bytes 131104 | tf_op jit(solution)/shard_map/ppermute | solution.py:343
  150.2 3.1 %collective-permute-done.22.refs_3_ = bf16[256,512]{1,0:T(8,128)(2,1)S(1)} collective-permute-done((bf16[256,512]{1,0:T(8,128)(2,1)S(1)}, bf16[256,512]{1,0:T(8,128)(2,1)S(1)}, u32[]{:S(2)}, u32[]{:S(2)}) %collective-permute-start.22) | collective-permute-done | bytes 262176 | tf_op jit(solution)/shard_map/ppermute | solution.py:343
  153.3 1.6 %place.5 = bf16[1024,1024]{1,0:T(8,128)(2,1)} custom-call(s32[4]{0:T(128)S(1)} %pad_add_fusion.2.places_ref.rows_ref, s32[4]{0:T(128)S(1)} %pad_add_fusion.3.columns_ref, bf16[256,512]{1,0:T(8,128)(2,1)S(1)} %get-tuple-element.152.refs_0_, bf16[256,512]{1,0:T(8,128)(2,1)S(1)} %collective-permute-done.20.refs_1_, ...), custom_call_target="tpu_custom_call", output_to_operand_aliasing={{}: (6, {})} | custom-call | flops 1024 | bytes 1024 | tf_op jit(solution)/shard_map/place/pallas_call | solution.py:255
  (94 shorter events, 25.5 us)
Async XLA Ops:
  2.7 15.0 %collective-permute-start = (bf16[2048,128]{1,0:T(8,128)(2,1)S(1)}, bf16[2048,128]{1,0:T(8,128)(2,1)}, u32[]{:S(2)}, u32[]{:S(2)}) collective-permute-start(bf16[2048,128]{1,0:T(8,128)(2,1)S(1)} %get-tuple-element.163), channel_id=1, source_target_pairs={{16,0},{0,16},{17,1},{1,17},{18,2},{2,18},{19,3},{3,19},{20,4},{4,... | collective-permute-start | bytes 1572872 | tf_op jit(solution)/shard_map/ppermute | solution.py:30
  17.7 3.3 %collective-permute-start.1 = (bf16[2048,128]{1,0:T(8,128)(2,1)}, bf16[2048,128]{1,0:T(8,128)(2,1)S(1)}, u32[]{:S(2)}, u32[]{:S(2)}) collective-permute-start(bf16[2048,128]{1,0:T(8,128)(2,1)} %collective-permute-done.refs_0_.refs_2_), channel_id=1, source_target_pairs={{0,1},{1,0},{2,3},{3,2},{4,5},{5,4},{6,7},{7,6},{8,9},{9,8},{10,11... | collective-permute-start | bytes 1572872 | tf_op jit(solution)/shard_map/ppermute | solution.py:343
  17.7 31.8 %collective-permute-start.7 = (bf16[2048,128]{1,0:T(8,128)(2,1)}, bf16[2048,128]{1,0:T(8,128)(2,1)}, u32[]{:S(2)}, u32[]{:S(2)}) collective-permute-start(bf16[2048,128]{1,0:T(8,128)(2,1)} %get-tuple-element.162), channel_id=1, source_target_pairs={{16,0},{0,16},{17,1},{1,17},{18,2},{2,18},{19,3},{3,19},{20,4},{4,... | collective-permute-start | bytes 1572872 | tf_op jit(solution)/shard_map/ppermute | solution.py:30
  19.4 30.1 %collective-permute-start.2 = (bf16[2048,128]{1,0:T(8,128)(2,1)}, bf16[2048,128]{1,0:T(8,128)(2,1)}, u32[]{:S(2)}, u32[]{:S(2)}) collective-permute-start(bf16[2048,128]{1,0:T(8,128)(2,1)} %collective-permute-done.refs_0_.refs_2_), channel_id=1, source_target_pairs={{0,2},{1,3},{2,0},{3,1},{4,6},{5,7},{6,4},{7,5},{8,10},{9,11},{10,... | collective-permute-start | bytes 1572872 | tf_op jit(solution)/shard_map/ppermute | solution.py:343
  25.0 20.4 %copy-start.4 = (bf16[1,1024,1024]{2,1,0:T(8,128)(2,1)S(1)}, bf16[1,1024,1024]{2,1,0:T(8,128)(2,1)}, u32[]{:S(2)}) copy-start(bf16[1,1024,1024]{2,1,0:T(8,128)(2,1)} %param.8) | copy-start | bytes 6291460
  25.0 20.4 %copy-start.5 = (f32[1,256,1024]{2,1,0:T(8,128)S(1)}, f32[1,256,1024]{2,1,0:T(8,128)}, u32[]{:S(2)}) copy-start(f32[1,256,1024]{2,1,0:T(8,128)} %param.10) | copy-start | bytes 3145732
  30.4 8.5 %collective-permute-start.5 = (bf16[256,256]{1,0:T(8,128)(2,1)}, bf16[256,256]{1,0:T(8,128)(2,1)S(1)}, u32[]{:S(2)}, u32[]{:S(2)}) collective-permute-start(bf16[256,256]{1,0:T(8,128)(2,1)} %get-tuple-element.95), channel_id=1, source_target_pairs={{0,12},{4,8},{8,4},{12,0},{1,13},{5,9},{9,5},{13,1},{2,14},{6,10},... | collective-permute-start | bytes 393224 | tf_op jit(solution)/shard_map/ppermute | solution.py:343
  34.0 11.4 %collective-permute-start.4 = (bf16[256,256]{1,0:T(8,128)(2,1)}, bf16[256,256]{1,0:T(8,128)(2,1)S(1)}, u32[]{:S(2)}, u32[]{:S(2)}) collective-permute-start(bf16[256,256]{1,0:T(8,128)(2,1)} %get-tuple-element.93), channel_id=1, source_target_pairs={{0,8},{4,12},{8,0},{12,4},{1,9},{5,13},{9,1},{13,5},{2,10},{6,14},... | collective-permute-start | bytes 393224 | tf_op jit(solution)/shard_map/ppermute | solution.py:343
  34.0 11.4 %collective-permute-start.3 = (bf16[256,256]{1,0:T(8,128)(2,1)}, bf16[256,256]{1,0:T(8,128)(2,1)S(1)}, u32[]{:S(2)}, u32[]{:S(2)}) collective-permute-start(bf16[256,256]{1,0:T(8,128)(2,1)} %get-tuple-element.90), channel_id=1, source_target_pairs={{0,4},{4,0},{8,12},{12,8},{1,5},{5,1},{9,13},{13,9},{2,6},{6,2},{1... | collective-permute-start | bytes 393224 | tf_op jit(solution)/shard_map/ppermute | solution.py:343
  49.4 10.0 %collective-permute-start.8 = (bf16[2048,128]{1,0:T(8,128)(2,1)}, bf16[2048,128]{1,0:T(8,128)(2,1)S(1)}, u32[]{:S(2)}, u32[]{:S(2)}) collective-permute-start(bf16[2048,128]{1,0:T(8,128)(2,1)} %collective-permute-done.7.refs_0_.refs_4_), channel_id=1, source_target_pairs={{0,1},{1,0},{2,3},{3,2},{4,5},{5,4},{6,7},{7,6},{8,9},{9,8},{10,11... | collective-permute-start | bytes 1572872 | tf_op jit(solution)/shard_map/ppermute | solution.py:343
  49.5 10.0 %collective-permute-start.6 = (bf16[2048,128]{1,0:T(8,128)(2,1)}, bf16[2048,128]{1,0:T(8,128)(2,1)S(1)}, u32[]{:S(2)}, u32[]{:S(2)}) collective-permute-start(bf16[2048,128]{1,0:T(8,128)(2,1)} %collective-permute-done.2.refs_2_.refs_6_), channel_id=1, source_target_pairs={{0,1},{1,0},{2,3},{3,2},{4,5},{5,4},{6,7},{7,6},{8,9},{9,8},{10,11... | collective-permute-start | bytes 1572872 | tf_op jit(solution)/shard_map/ppermute | solution.py:343
  50.0 16.4 %collective-permute-start.9 = (bf16[2048,128]{1,0:T(8,128)(2,1)}, bf16[2048,128]{1,0:T(8,128)(2,1)}, u32[]{:S(2)}, u32[]{:S(2)}) collective-permute-start(bf16[2048,128]{1,0:T(8,128)(2,1)} %collective-permute-done.7.refs_0_.refs_4_), channel_id=1, source_target_pairs={{0,2},{1,3},{2,0},{3,1},{4,6},{5,7},{6,4},{7,5},{8,10},{9,11},{10,... | collective-permute-start | bytes 1572872 | tf_op jit(solution)/shard_map/ppermute | solution.py:343
  50.7 8.8 %collective-permute-start.10 = (bf16[256,256]{1,0:T(8,128)(2,1)S(1)}, bf16[256,256]{1,0:T(8,128)(2,1)S(1)}, u32[]{:S(2)}, u32[]{:S(2)}) collective-permute-start(bf16[256,256]{1,0:T(8,128)(2,1)S(1)} %get-tuple-element.109.refs_0_), channel_id=1, source_target_pairs={{0,8},{4,12},{8,0},{12,4},{1,9},{5,13},{9,1},{13,5},{2,10},{6,14},... | collective-permute-start | bytes 393224 | tf_op jit(solution)/shard_map/ppermute | solution.py:343
  66.4 4.6 %collective-permute-start.11 = (bf16[2048,128]{1,0:T(8,128)(2,1)}, bf16[2048,128]{1,0:T(8,128)(2,1)}, u32[]{:S(2)}, u32[]{:S(2)}) collective-permute-start(bf16[2048,128]{1,0:T(8,128)(2,1)} %collective-permute-done.9.refs_6_.refs_0_.refs_2_), channel_id=1, source_target_pairs={{0,1},{1,0},{2,3},{3,2},{4,5},{5,4},{6,7},{7,6},{8,9},{9,8},{10,11... | collective-permute-start | bytes 1572872 | tf_op jit(solution)/shard_map/ppermute | solution.py:343
  66.4 25.1 %collective-permute-start.14 = (bf16[256,512]{1,0:T(8,128)(2,1)}, bf16[256,512]{1,0:T(8,128)(2,1)S(1)}, u32[]{:S(2)}, u32[]{:S(2)}) collective-permute-start(bf16[256,512]{1,0:T(8,128)(2,1)} %get-tuple-element.124), channel_id=1, source_target_pairs={{0,12},{4,8},{8,4},{12,0},{1,13},{5,9},{9,5},{13,1},{2,14},{6,10},... | collective-permute-start | bytes 786440 | tf_op jit(solution)/shard_map/ppermute | solution.py:343
  67.7 23.8 %collective-permute-start.13 = (bf16[256,512]{1,0:T(8,128)(2,1)}, bf16[256,512]{1,0:T(8,128)(2,1)}, u32[]{:S(2)}, u32[]{:S(2)}) collective-permute-start(bf16[256,512]{1,0:T(8,128)(2,1)} %get-tuple-element.122), channel_id=1, source_target_pairs={{0,8},{4,12},{8,0},{12,4},{1,9},{5,13},{9,1},{13,5},{2,10},{6,14},... | collective-permute-start | bytes 786440 | tf_op jit(solution)/shard_map/ppermute | solution.py:343
  67.7 23.8 %collective-permute-start.12 = (bf16[256,512]{1,0:T(8,128)(2,1)}, bf16[256,512]{1,0:T(8,128)(2,1)}, u32[]{:S(2)}, u32[]{:S(2)}) collective-permute-start(bf16[256,512]{1,0:T(8,128)(2,1)} %get-tuple-element.119), channel_id=1, source_target_pairs={{0,4},{4,0},{8,12},{12,8},{1,5},{5,1},{9,13},{13,9},{2,6},{6,2},{1... | collective-permute-start | bytes 786440 | tf_op jit(solution)/shard_map/ppermute | solution.py:343
  77.9 13.6 %copy-start.7 = (f32[1,256,1024]{2,1,0:T(8,128)S(1)}, f32[1,256,1024]{2,1,0:T(8,128)}, u32[]{:S(2)}) copy-start(f32[1,256,1024]{2,1,0:T(8,128)} %param.11) | copy-start | bytes 3145732
  77.9 13.6 %copy-start.20 = (bf16[256,512]{1,0:T(8,128)(2,1)S(1)}, bf16[256,512]{1,0:T(8,128)(2,1)}, u32[]{:S(2)}) copy-start(bf16[256,512]{1,0:T(8,128)(2,1)} %copy-done.19) | copy-start | bytes 786436
  95.9 20.1 %collective-permute-start.15 = (bf16[2048,512]{1,0:T(8,128)(2,1)S(1)}, bf16[2048,512]{1,0:T(8,128)(2,1)S(1)}, u32[]{:S(2)}, u32[]{:S(2)}) collective-permute-start(bf16[2048,512]{1,0:T(8,128)(2,1)S(1)} %get-tuple-element.132.refs_7_), channel_id=1, source_target_pairs={{0,1},{1,0},{2,3},{3,2},{4,5},{5,4},{6,7},{7,6},{8,9},{9,8},{10,11... | collective-permute-start | bytes 6291464 | tf_op jit(solution)/shard_map/ppermute | solution.py:343
  100.3 8.2 %collective-permute-start.18 = (bf16[256,256]{1,0:T(8,128)(2,1)S(1)}, bf16[256,256]{1,0:T(8,128)(2,1)S(1)}, u32[]{:S(2)}, u32[]{:S(2)}) collective-permute-start(bf16[256,256]{1,0:T(8,128)(2,1)S(1)} %get-tuple-element.140), channel_id=1, source_target_pairs={{0,12},{4,8},{8,4},{12,0},{1,13},{5,9},{9,5},{13,1},{2,14},{6,10},... | collective-permute-start | bytes 393224 | tf_op jit(solution)/shard_map/ppermute | solution.py:343
  101.6 12.4 %collective-permute-start.17 = (bf16[256,256]{1,0:T(8,128)(2,1)S(1)}, bf16[256,256]{1,0:T(8,128)(2,1)S(1)}, u32[]{:S(2)}, u32[]{:S(2)}) collective-permute-start(bf16[256,256]{1,0:T(8,128)(2,1)S(1)} %get-tuple-element.138), channel_id=1, source_target_pairs={{0,8},{4,12},{8,0},{12,4},{1,9},{5,13},{9,1},{13,5},{2,10},{6,14},... | collective-permute-start | bytes 393224 | tf_op jit(solution)/shard_map/ppermute | solution.py:343
  101.8 12.3 %collective-permute-start.16 = (bf16[256,256]{1,0:T(8,128)(2,1)S(1)}, bf16[256,256]{1,0:T(8,128)(2,1)S(1)}, u32[]{:S(2)}, u32[]{:S(2)}) collective-permute-start(bf16[256,256]{1,0:T(8,128)(2,1)S(1)} %get-tuple-element.136), channel_id=1, source_target_pairs={{0,4},{4,0},{8,12},{12,8},{1,5},{5,1},{9,13},{13,9},{2,6},{6,2},{1... | collective-permute-start | bytes 393224 | tf_op jit(solution)/shard_map/ppermute | solution.py:343
  116.3 25.0 %collective-permute-start.19 = (bf16[2048,256]{1,0:T(8,128)(2,1)S(1)}, bf16[2048,256]{1,0:T(8,128)(2,1)S(1)}, u32[]{:S(2)}, u32[]{:S(2)}) collective-permute-start(bf16[2048,256]{1,0:T(8,128)(2,1)S(1)} %add_convert_fusion.1), channel_id=1, source_target_pairs={{0,2},{1,3},{2,0},{3,1},{4,6},{5,7},{6,4},{7,5},{8,10},{9,11},{10,... | collective-permute-start | bytes 3145736 | tf_op jit(solution)/shard_map/ppermute | solution.py:343
  117.7 16.0 %collective-permute-start.21 = (bf16[256,512]{1,0:T(8,128)(2,1)S(1)}, bf16[256,512]{1,0:T(8,128)(2,1)S(1)}, u32[]{:S(2)}, u32[]{:S(2)}) collective-permute-start(bf16[256,512]{1,0:T(8,128)(2,1)S(1)} %get-tuple-element.152.refs_0_), channel_id=1, source_target_pairs={{0,8},{4,12},{8,0},{12,4},{1,9},{5,13},{9,1},{13,5},{2,10},{6,14},... | collective-permute-start | bytes 786440 | tf_op jit(solution)/shard_map/ppermute | solution.py:343
  117.9 18.6 %collective-permute-start.24 = (bf16[256,256]{1,0:T(8,128)(2,1)S(1)}, bf16[256,256]{1,0:T(8,128)(2,1)S(1)}, u32[]{:S(2)}, u32[]{:S(2)}) collective-permute-start(bf16[256,256]{1,0:T(8,128)(2,1)S(1)} %get-tuple-element.154.refs_0_), channel_id=1, source_target_pairs={{0,8},{4,12},{8,0},{12,4},{1,9},{5,13},{9,1},{13,5},{2,10},{6,14},... | collective-permute-start | bytes 393224 | tf_op jit(solution)/shard_map/ppermute | solution.py:343
  120.6 15.8 %collective-permute-start.26 = (bf16[256,256]{1,0:T(8,128)(2,1)S(1)}, bf16[256,256]{1,0:T(8,128)(2,1)S(1)}, u32[]{:S(2)}, u32[]{:S(2)}) collective-permute-start(bf16[256,256]{1,0:T(8,128)(2,1)S(1)} %copy-done.22), channel_id=1, source_target_pairs={{0,4},{4,0},{8,12},{12,8},{1,5},{5,1},{9,13},{13,9},{2,6},{6,2},{1... | collective-permute-start | bytes 393224 | tf_op jit(solution)/shard_map/ppermute | solution.py:343
  120.6 18.2 %collective-permute-start.27 = (bf16[256,256]{1,0:T(8,128)(2,1)S(1)}, bf16[256,256]{1,0:T(8,128)(2,1)S(1)}, u32[]{:S(2)}, u32[]{:S(2)}) collective-permute-start(bf16[256,256]{1,0:T(8,128)(2,1)S(1)} %collective-permute-done.10.refs_12_.refs_2_), channel_id=1, source_target_pairs={{0,4},{4,0},{8,12},{12,8},{1,5},{5,1},{9,13},{13,9},{2,6},{6,2},{1... | collective-permute-start | bytes 393224 | tf_op jit(solution)/shard_map/ppermute | solution.py:343
  133.7 16.5 %collective-permute-start.20 = (bf16[256,512]{1,0:T(8,128)(2,1)S(1)}, bf16[256,512]{1,0:T(8,128)(2,1)S(1)}, u32[]{:S(2)}, u32[]{:S(2)}) collective-permute-start(bf16[256,512]{1,0:T(8,128)(2,1)S(1)} %get-tuple-element.152.refs_0_), channel_id=1, source_target_pairs={{0,4},{4,0},{8,12},{12,8},{1,5},{5,1},{9,13},{13,9},{2,6},{6,2},{1... | collective-permute-start | bytes 786440 | tf_op jit(solution)/shard_map/ppermute | solution.py:343
  136.5 11.8 %collective-permute-start.23 = (bf16[256,256]{1,0:T(8,128)(2,1)S(1)}, bf16[256,256]{1,0:T(8,128)(2,1)S(1)}, u32[]{:S(2)}, u32[]{:S(2)}) collective-permute-start(bf16[256,256]{1,0:T(8,128)(2,1)S(1)} %get-tuple-element.154.refs_0_), channel_id=1, source_target_pairs={{0,4},{4,0},{8,12},{12,8},{1,5},{5,1},{9,13},{13,9},{2,6},{6,2},{1... | collective-permute-start | bytes 393224 | tf_op jit(solution)/shard_map/ppermute | solution.py:343
  136.5 12.3 %collective-permute-start.25 = (bf16[256,256]{1,0:T(8,128)(2,1)S(1)}, bf16[256,256]{1,0:T(8,128)(2,1)S(1)}, u32[]{:S(2)}, u32[]{:S(2)}) collective-permute-start(bf16[256,256]{1,0:T(8,128)(2,1)S(1)} %get-tuple-element.154.refs_0_), channel_id=1, source_target_pairs={{0,12},{4,8},{8,4},{12,0},{1,13},{5,9},{9,5},{13,1},{2,14},{6,10},... | collective-permute-start | bytes 393224 | tf_op jit(solution)/shard_map/ppermute | solution.py:343
  138.8 14.5 %collective-permute-start.22 = (bf16[256,512]{1,0:T(8,128)(2,1)S(1)}, bf16[256,512]{1,0:T(8,128)(2,1)S(1)}, u32[]{:S(2)}, u32[]{:S(2)}) collective-permute-start(bf16[256,512]{1,0:T(8,128)(2,1)S(1)} %collective-permute-done.21.refs_4_.refs_2_), channel_id=1, source_target_pairs={{0,4},{4,0},{8,12},{12,8},{1,5},{5,1},{9,13},{13,9},{2,6},{6,2},{1... | collective-permute-start | bytes 786440 | tf_op jit(solution)/shard_map/ppermute | solution.py:343
  (21 other events, 63.9 us)

commit v2 on v1

--- a/solution.py
+++ b/solution.py
@@ -15,8 +15,8 @@
 SUMS = ("one", "one", "one",)
 GATHERS = ("two", "two", "one",)
 PLAN = (
-    "h0", "b00", "b10", "t0", "r0", "a0", "b01", "b20", "b30", "b11", "g0", "t1", "b21",
-    "b31", "t2", "p0", "r1", "a1", "w0", "r2", "a2", "g1", "x0", "l0", "x1", "g2", "l2",
+    "h0", "b00", "b10", "t0", "b01", "r0", "a0", "b11", "b20", "g0", "b30", "t1", "b21",
+    "b31", "t2", "p0", "r1", "l0", "a1", "w0", "r2", "a2", "g1", "x0", "g2", "x1", "l2",
     "l1",
 )
 ANYWHERE = pl.BlockSpec(memory_space=pl.ANY)
@@ -98,11 +98,12 @@
     return pltpu.CompilerParams(vmem_limit_bytes=mib * 2**20)
 
 
-def prepare(hidden_pre, model_width):
+def prepare(hidden_pre, model_width, after):
     tokens, units = hidden_pre.shape
     scale = 1.0 / math.sqrt(model_width)
 
-    def kernel(pre_ref, hidden_ref, slope_ref, token_ref):
+    def kernel(pre_ref, *refs):
+        hidden_ref, slope_ref, token_ref = refs[len(after) :]
         token_ref[...] = jnp.zeros_like(token_ref)
         pre = pre_ref[...].astype(F32)
         phi = 0.5 * (1.0 + lax.erf(pre * (1.0 / math.sqrt(2.0))))
@@ -113,7 +114,7 @@
     return pl.pallas_call(
         kernel,
         grid=(tokens // TILE,),
-        in_specs=[pl.BlockSpec((TILE, units), lambda i: (i, 0))],
+        in_specs=[pl.BlockSpec((TILE, units), lambda i: (i, 0))] + [ANYWHERE] * len(after),
         out_specs=[
             pl.BlockSpec((units, TILE), lambda i: (0, i)),
             pl.BlockSpec((TILE, units), lambda i: (i, 0)),
@@ -127,7 +128,7 @@
         compiler_params=params(8),
         cost_estimate=SMALL,
         name="prepare",
-    )(hidden_pre)
+    )(hidden_pre, *after)
 
 
 def terms(hidden_t, pieces, places, scale, paired, after):
@@ -376,7 +377,9 @@
     for name in PLAN:
         kind, k = name[0], int(name[1])
         if kind == "h":
-            values["hidden"], values["slope"], values["token"] = prepare(hidden_pre, model_width)
+            values["hidden"], values["slope"], values["token"] = prepare(
+                hidden_pre, model_width, [shards, paired, rank_now, order, where, *columns]
+            )
         elif kind == "b":
             arrive(name)
             part = name[2]

time: 156 us -> 136 us (0.87)
  local copies, waits for them, and re-layouts: 22.8 us -> 3.57 us
  Pallas kernels: 46.4 us -> 38.6 us
  waiting for transfers between devices: 52.4 us -> 59 us
  starting transfers between devices: 30.4 us -> 32.4 us
    unnamed x50 -> x10, local copies, waits for them, and re-layouts: 20.6 us -> 2.21 us
    ppermute x2, waiting for transfers between devices: 0.82 us -> 8.31 us  [from_behind(): return lax.ppermute(block, axis, route)]
    pallas_call x3, Pallas kernels: 15.3 us -> 10.1 us  [terms(): pl.pallas_call(kernel, grid_spec=pltpu.PrefetchScalarGridSpec(num_scalar_...]
    ppermute x26, starting transfers between devices: 25.7 us -> 27.6 us  [swapped(): return lax.ppermute(value, axis, [(i, i ^ distance) for i in range(4)])]
  transfers between devices with their start and end apart: 28 -> 28, of which waited for: 11 -> 15; matrix products, arithmetic and copies ran while one was open for 1% -> 1% of each run, Pallas kernels for 26% -> 25%
where the time goes in v2:
time: 136 us
  waiting for transfers between devices  59 us (43%)
  Pallas kernels  38.6 us (28%)
  starting transfers between devices  32.4 us (24%)
  local copies, waits for them, and re-layouts  3.57 us (3%)
  other arithmetic  1.91 us (1%)
    ppermute x26, waiting for transfers between devices, swapped(): return lax.ppermute(value, axis, [(i, i ^ distance) for i in range(4)])  50.7 us
    ppermute x26, starting transfers between devices, swapped(): return lax.ppermute(value, axis, [(i, i ^ distance) for i in range(4)])  27.6 us
    pallas_call x1, Pallas kernels, partials(): pl.pallas_call(kernel, grid_spec=pltpu.PrefetchScalarGridSpec(num_scalar_...  12.5 us
    pallas_call x3, Pallas kernels, terms(): pl.pallas_call(kernel, grid_spec=pltpu.PrefetchScalarGridSpec(num_scalar_...  10.1 us
    ppermute x2, waiting for transfers between devices, from_behind(): return lax.ppermute(block, axis, route)  8.31 us
    pallas_call x3, Pallas kernels, adam_chunk(): pl.pallas_call(kernel, grid_spec=pltpu.PrefetchScalarGridSpec(num_scalar_...  6.66 us
    pallas_call x1, Pallas kernels, prepare(): pl.pallas_call(kernel, grid=(tokens // TILE,), in_specs=[pl.BlockSpec((TI...  5.02 us
    ppermute x2, starting transfers between devices, from_behind(): return lax.ppermute(block, axis, route)  4.77 us
  transfers between devices with their start and end apart: 28, of which 15 were waited for; matrix products, arithmetic and copies ran while one was open for 1% of the time, Pallas kernels for 25%

profile of v2, /device:TPU:0, one launch (start us, length us, event | category | flops | bytes accessed | tf_op | source)
XLA Modules:
  0.0 136.2 jit_solution(8385027238616495468)
XLA Ops:
  1.9 3.0 %collective-permute-start = (bf16[2048,128]{1,0:T(8,128)(2,1)S(1)}, bf16[2048,128]{1,0:T(8,128)(2,1)S(1)}, u32[]{:S(2)}, u32[]{:S(2)}) collective-permute-start(bf16[2048,128]{1,0:T(8,128)(2,1)S(1)} %get-tuple-element.163), channel_id=1, source_target_pairs={{16,0},{0,16},{17,1},{1,17},{18,2},{2,18},{19,3},{3,19},{20,4},{4,... | collective-permute-start | bytes 1572872 | tf_op jit(solution)/shard_map/ppermute | solution.py:30
  5.3 2.2 %copy-done.3 = bf16[1,2048,1024]{2,1,0:T(8,128)(2,1)S(1)} copy-done((bf16[1,2048,1024]{2,1,0:T(8,128)(2,1)S(1)}, bf16[1,2048,1024]{2,1,0:T(8,128)(2,1)}, u32[]{:S(2)}) %copy-start.3) | copy-done | bytes 4194328
  7.4 5.0 %prepare.1 = (bf16[1024,2048]{1,0:T(8,128)(2,1)S(1)}, bf16[2048,1024]{1,0:T(8,128)(2,1)S(1)}, f32[8,128]{1,0:T(8,128)S(1)}) custom-call(bf16[2048,1024]{1,0:T(8,128)(2,1)S(1)} %bitcast.37, s32[4]{0:T(128)S(1)} %get-tuple-element.164.refs_0_.places_ref.rows_ref, s32[4]{0:T(128)S(1)} %get-tuple-element.165.refs_1_, s32[1]{0:T(128)} %bitcast.14.refs_2_.rank_ref, ...), custom_call_target="tpu_custom_call" | custom-call | flops 1024 | bytes 1024 | tf_op jit(solution)/shard_map/prepare/pallas_call | solution.py:114
  12.5 4.4 %collective-permute-done.refs_0_.refs_2_ = bf16[2048,128]{1,0:T(8,128)(2,1)S(1)} collective-permute-done((bf16[2048,128]{1,0:T(8,128)(2,1)S(1)}, bf16[2048,128]{1,0:T(8,128)(2,1)S(1)}, u32[]{:S(2)}, u32[]{:S(2)}) %collective-permute-start) | collective-permute-done | bytes 524320 | tf_op jit(solution)/shard_map/ppermute | solution.py:30
  16.9 1.7 %collective-permute-start.6 = (bf16[2048,128]{1,0:T(8,128)(2,1)S(1)}, bf16[2048,128]{1,0:T(8,128)(2,1)S(1)}, u32[]{:S(2)}, u32[]{:S(2)}) collective-permute-start(bf16[2048,128]{1,0:T(8,128)(2,1)S(1)} %get-tuple-element.162), channel_id=1, source_target_pairs={{16,0},{0,16},{17,1},{1,17},{18,2},{2,18},{19,3},{3,19},{20,4},{4,... | collective-permute-start | bytes 1572872 | tf_op jit(solution)/shard_map/ppermute | solution.py:30
  20.1 2.7 %terms.3 = (bf16[256,256]{1,0:T(8,128)(2,1)S(1)}, bf16[256,256]{1,0:T(8,128)(2,1)S(1)}, bf16[256,256]{1,0:T(8,128)(2,1)S(1)}, bf16[256,256]{1,0:T(8,128)(2,1)S(1)}, f32[8,128]{1,0:T(8,128)S(1)}) custom-call(s32[4]{0:T(128)S(1)} %get-tuple-element.164.refs_0_.places_ref.rows_ref, bf16[1024,2048]{1,0:T(8,128)(2,1)S(1)} %get-tuple-element.86.hidden_ref, ...), custom_call_target="tpu_custom_call" | custom-call | flops 1024 | bytes 1024 | tf_op jit(solution)/shard_map/terms/pallas_call | solution.py:162
  22.8 3.7 %collective-permute-start.5 = (bf16[256,256]{1,0:T(8,128)(2,1)S(1)}, bf16[256,256]{1,0:T(8,128)(2,1)S(1)}, u32[]{:S(2)}, u32[]{:S(2)}) collective-permute-start(bf16[256,256]{1,0:T(8,128)(2,1)S(1)} %get-tuple-element.95), channel_id=1, source_target_pairs={{0,12},{4,8},{8,4},{12,0},{1,13},{5,9},{9,5},{13,1},{2,14},{6,10},... | collective-permute-start | bytes 393224 | tf_op jit(solution)/shard_map/ppermute | solution.py:344
  27.3 3.9 %collective-permute-done.6.refs_7_.refs_0_.refs_4_ = bf16[2048,128]{1,0:T(8,128)(2,1)S(1)} collective-permute-done((bf16[2048,128]{1,0:T(8,128)(2,1)S(1)}, bf16[2048,128]{1,0:T(8,128)(2,1)S(1)}, u32[]{:S(2)}, u32[]{:S(2)}) %collective-permute-start.6) | collective-permute-done | bytes 524320 | tf_op jit(solution)/shard_map/ppermute | solution.py:30
  31.2 6.5 %collective-permute-done.4.refs_2_.refs_11_ = bf16[256,256]{1,0:T(8,128)(2,1)S(1)} collective-permute-done((bf16[256,256]{1,0:T(8,128)(2,1)S(1)}, bf16[256,256]{1,0:T(8,128)(2,1)S(1)}, u32[]{:S(2)}, u32[]{:S(2)}) %collective-permute-start.4) | collective-permute-done | bytes 131104 | tf_op jit(solution)/shard_map/ppermute | solution.py:344
  37.7 1.9 %adam.3 = (bf16[256,256]{1,0:T(8,128)(2,1)S(1)}, f32[256,1024]{1,0:T(8,128)}, f32[256,1024]{1,0:T(8,128)}, f32[8,128]{1,0:T(8,128)S(1)}) custom-call(s32[2]{0:T(128)S(1)} %get-tuple-element.168.refs_5_.columns_ref, s32[1]{0:T(128)} %bitcast.14.refs_2_.rank_ref, bf16[256,256]{1,0:T(8,128)(2,1)S(1)} %get-tuple-element.89.refs_0_, ...), custom_call_target="tpu_custom_call" | custom-call | flops 1024 | bytes 1024 | tf_op jit(solution)/shard_map/adam/pallas_call | solution.py:204
  40.2 9.1 %collective-permute-done.10.refs_8_.refs_2_ = bf16[256,256]{1,0:T(8,128)(2,1)S(1)} collective-permute-done((bf16[256,256]{1,0:T(8,128)(2,1)S(1)}, bf16[256,256]{1,0:T(8,128)(2,1)S(1)}, u32[]{:S(2)}, u32[]{:S(2)}) %collective-permute-start.10) | collective-permute-done | bytes 131104 | tf_op jit(solution)/shard_map/ppermute | solution.py:344
  49.4 4.1 %terms.4 = (bf16[256,512]{1,0:T(8,128)(2,1)S(1)}, bf16[256,512]{1,0:T(8,128)(2,1)S(1)}, bf16[256,512]{1,0:T(8,128)(2,1)S(1)}, bf16[256,512]{1,0:T(8,128)(2,1)S(1)}, f32[8,128]{1,0:T(8,128)S(1)}) custom-call(s32[4]{0:T(128)S(1)} %get-tuple-element.164.refs_0_.places_ref.rows_ref, bf16[1024,2048]{1,0:T(8,128)(2,1)S(1)} %get-tuple-element.86.hidden_ref, ...), custom_call_target="tpu_custom_call" | custom-call | flops 1024 | bytes 1024 | tf_op jit(solution)/shard_map/terms/pallas_call | solution.py:162
  54.0 2.5 %collective-permute-start.14 = (bf16[256,512]{1,0:T(8,128)(2,1)S(1)}, bf16[256,512]{1,0:T(8,128)(2,1)S(1)}, u32[]{:S(2)}, u32[]{:S(2)}) collective-permute-start(bf16[256,512]{1,0:T(8,128)(2,1)S(1)} %get-tuple-element.124), channel_id=1, source_target_pairs={{0,12},{4,8},{8,4},{12,0},{1,13},{5,9},{9,5},{13,1},{2,14},{6,10},... | collective-permute-start | bytes 786440 | tf_op jit(solution)/shard_map/ppermute | solution.py:344
  56.4 1.9 %collective-permute-start.12 = (bf16[256,512]{1,0:T(8,128)(2,1)S(1)}, bf16[256,512]{1,0:T(8,128)(2,1)S(1)}, u32[]{:S(2)}, u32[]{:S(2)}) collective-permute-start(bf16[256,512]{1,0:T(8,128)(2,1)S(1)} %get-tuple-element.119), channel_id=1, source_target_pairs={{0,4},{4,0},{8,12},{12,8},{1,5},{5,1},{9,13},{13,9},{2,6},{6,2},{1... | collective-permute-start | bytes 786440 | tf_op jit(solution)/shard_map/ppermute | solution.py:344
  58.4 12.5 %partials.1 = (bf16[2048,256]{1,0:T(8,128)(2,1)S(1)}, bf16[2048,256]{1,0:T(8,128)(2,1)S(1)}, bf16[2048,512]{1,0:T(8,128)(2,1)S(1)}, f32[8,128]{1,0:T(8,128)S(1)}) custom-call(s32[8]{0:T(128)S(1)} %stack.89.refs_4_.where_ref, s32[4]{0:T(128)S(1)} %get-tuple-element.166.refs_3_.order_ref, bf16[2048,128]{1,0:T(8,128)(2,1)S(1)} %collective-permute-done.refs_0_.refs_2_, ...), custom_call_target="tpu_custom_call" | custom-call | flops 1024 | bytes 1024 | tf_op jit(solution)/shard_map/partials/pallas_call | solution.py:303
  70.8 8.0 %collective-permute-done.13.refs_2_.refs_6_ = bf16[256,512]{1,0:T(8,128)(2,1)S(1)} collective-permute-done((bf16[256,512]{1,0:T(8,128)(2,1)S(1)}, bf16[256,512]{1,0:T(8,128)(2,1)S(1)}, u32[]{:S(2)}, u32[]{:S(2)}) %collective-permute-start.13) | collective-permute-done | bytes 262176 | tf_op jit(solution)/shard_map/ppermute | solution.py:344
  78.8 2.9 %adam.4 = (bf16[256,512]{1,0:T(8,128)(2,1)S(1)}, f32[256,1024]{1,0:T(8,128)}, f32[256,1024]{1,0:T(8,128)}, f32[8,128]{1,0:T(8,128)S(1)}) custom-call(s32[4]{0:T(128)S(1)} %get-tuple-element.167.refs_6_.columns_ref, s32[1]{0:T(128)} %bitcast.14.refs_2_.rank_ref, ...), custom_call_target="tpu_custom_call", output_to_operand_aliasing={{1}: (9, {}), {2}: (10, {})} | custom-call | flops 1024 | bytes 1024 | tf_op jit(solution)/shard_map/adam/pallas_call | solution.py:204
  81.7 3.3 %terms.5 = (bf16[256,256]{1,0:T(8,128)(2,1)S(1)}, bf16[256,256]{1,0:T(8,128)(2,1)S(1)}, bf16[256,256]{1,0:T(8,128)(2,1)S(1)}, bf16[256,256]{1,0:T(8,128)(2,1)S(1)}, f32[8,128]{1,0:T(8,128)}) custom-call(s32[4]{0:T(128)S(1)} %get-tuple-element.164.refs_0_.places_ref.rows_ref, bf16[1024,2048]{1,0:T(8,128)(2,1)S(1)} %get-tuple-element.86.hidden_ref, ...), custom_call_target="tpu_custom_call" | custom-call | flops 1024 | bytes 1024 | tf_op jit(solution)/shard_map/terms/pallas_call | solution.py:162
  86.4 2.9 %collective-permute-start.16 = (bf16[256,256]{1,0:T(8,128)(2,1)S(1)}, bf16[256,256]{1,0:T(8,128)(2,1)S(1)}, u32[]{:S(2)}, u32[]{:S(2)}) collective-permute-start(bf16[256,256]{1,0:T(8,128)(2,1)S(1)} %get-tuple-element.133), channel_id=1, source_target_pairs={{0,4},{4,0},{8,12},{12,8},{1,5},{5,1},{9,13},{13,9},{2,6},{6,2},{1... | collective-permute-start | bytes 393224 | tf_op jit(solution)/shard_map/ppermute | solution.py:344
  89.3 3.8 %collective-permute-done.18.refs_3_.refs_9_ = bf16[256,256]{1,0:T(8,128)(2,1)S(1)} collective-permute-done((bf16[256,256]{1,0:T(8,128)(2,1)S(1)}, bf16[256,256]{1,0:T(8,128)(2,1)S(1)}, u32[]{:S(2)}, u32[]{:S(2)}) %collective-permute-start.18) | collective-permute-done | bytes 131104 | tf_op jit(solution)/shard_map/ppermute | solution.py:344
  93.2 5.1 %collective-permute-done.17.refs_2_.refs_11_ = bf16[256,256]{1,0:T(8,128)(2,1)S(1)} collective-permute-done((bf16[256,256]{1,0:T(8,128)(2,1)S(1)}, bf16[256,256]{1,0:T(8,128)(2,1)S(1)}, u32[]{:S(2)}, u32[]{:S(2)}) %collective-permute-start.17) | collective-permute-done | bytes 131104 | tf_op jit(solution)/shard_map/ppermute | solution.py:344
  98.3 1.9 %adam.5 = (bf16[256,256]{1,0:T(8,128)(2,1)S(1)}, f32[256,1024]{1,0:T(8,128)}, f32[256,1024]{1,0:T(8,128)}, f32[8,128]{1,0:T(8,128)S(1)}) custom-call(s32[2]{0:T(128)S(1)} %get-tuple-element.169.refs_7_.columns_ref, s32[1]{0:T(128)} %bitcast.14.refs_2_.rank_ref, ...), custom_call_target="tpu_custom_call", output_to_operand_aliasing={{1}: (17, {}), {2}: (18, {})} | custom-call | flops 1024 | bytes 1024 | tf_op jit(solution)/shard_map/adam/pallas_call | solution.py:204
  101.7 1.6 %collective-permute-start.26 = (bf16[256,256]{1,0:T(8,128)(2,1)S(1)}, bf16[256,256]{1,0:T(8,128)(2,1)S(1)}, u32[]{:S(2)}, u32[]{:S(2)}) collective-permute-start(bf16[256,256]{1,0:T(8,128)(2,1)S(1)} %get-tuple-element.108.refs_0_), channel_id=1, source_target_pairs={{0,4},{4,0},{8,12},{12,8},{1,5},{5,1},{9,13},{13,9},{2,6},{6,2},{1... | collective-permute-start | bytes 393224 | tf_op jit(solution)/shard_map/ppermute | solution.py:344
  103.8 2.3 %collective-permute-start.24 = (bf16[256,256]{1,0:T(8,128)(2,1)S(1)}, bf16[256,256]{1,0:T(8,128)(2,1)S(1)}, u32[]{:S(2)}, u32[]{:S(2)}) collective-permute-start(bf16[256,256]{1,0:T(8,128)(2,1)S(1)} %get-tuple-element.151.refs_0_), channel_id=1, source_target_pairs={{0,8},{4,12},{8,0},{12,4},{1,9},{5,13},{9,1},{13,5},{2,10},{6,14},... | collective-permute-start | bytes 393224 | tf_op jit(solution)/shard_map/ppermute | solution.py:344
  106.1 5.3 %collective-permute-done.26.refs_1_ = bf16[256,256]{1,0:T(8,128)(2,1)S(1)} collective-permute-done((bf16[256,256]{1,0:T(8,128)(2,1)S(1)}, bf16[256,256]{1,0:T(8,128)(2,1)S(1)}, u32[]{:S(2)}, u32[]{:S(2)}) %collective-permute-start.26) | collective-permute-done | bytes 131104 | tf_op jit(solution)/shard_map/ppermute | solution.py:344
  111.4 2.5 %collective-permute-start.20 = (bf16[256,512]{1,0:T(8,128)(2,1)S(1)}, bf16[256,512]{1,0:T(8,128)(2,1)S(1)}, u32[]{:S(2)}, u32[]{:S(2)}) collective-permute-start(bf16[256,512]{1,0:T(8,128)(2,1)S(1)} %get-tuple-element.149.refs_0_), channel_id=1, source_target_pairs={{0,4},{4,0},{8,12},{12,8},{1,5},{5,1},{9,13},{13,9},{2,6},{6,2},{1... | collective-permute-start | bytes 786440 | tf_op jit(solution)/shard_map/ppermute | solution.py:344
  115.6 2.5 %collective-permute-start.23 = (bf16[256,256]{1,0:T(8,128)(2,1)S(1)}, bf16[256,256]{1,0:T(8,128)(2,1)S(1)}, u32[]{:S(2)}, u32[]{:S(2)}) collective-permute-start(bf16[256,256]{1,0:T(8,128)(2,1)S(1)} %get-tuple-element.151.refs_0_), channel_id=1, source_target_pairs={{0,4},{4,0},{8,12},{12,8},{1,5},{5,1},{9,13},{13,9},{2,6},{6,2},{1... | collective-permute-start | bytes 393224 | tf_op jit(solution)/shard_map/ppermute | solution.py:344
  118.1 1.7 %collective-permute-start.25 = (bf16[256,256]{1,0:T(8,128)(2,1)S(1)}, bf16[256,256]{1,0:T(8,128)(2,1)S(1)}, u32[]{:S(2)}, u32[]{:S(2)}) collective-permute-start(bf16[256,256]{1,0:T(8,128)(2,1)S(1)} %get-tuple-element.151.refs_0_), channel_id=1, source_target_pairs={{0,12},{4,8},{8,4},{12,0},{1,13},{5,9},{9,5},{13,1},{2,14},{6,10},... | collective-permute-start | bytes 393224 | tf_op jit(solution)/shard_map/ppermute | solution.py:344
  120.4 5.2 %collective-permute-done.19.refs_10_ = bf16[2048,256]{1,0:T(8,128)(2,1)S(1)} collective-permute-done((bf16[2048,256]{1,0:T(8,128)(2,1)S(1)}, bf16[2048,256]{1,0:T(8,128)(2,1)S(1)}, u32[]{:S(2)}, u32[]{:S(2)}) %collective-permute-start.19) | collective-permute-done | bytes 1048608 | tf_op jit(solution)/shard_map/ppermute | solution.py:344
  127.1 2.5 %collective-permute-done.23.refs_1_ = bf16[256,256]{1,0:T(8,128)(2,1)S(1)} collective-permute-done((bf16[256,256]{1,0:T(8,128)(2,1)S(1)}, bf16[256,256]{1,0:T(8,128)(2,1)S(1)}, u32[]{:S(2)}, u32[]{:S(2)}) %collective-permute-start.23) | collective-permute-done | bytes 131104 | tf_op jit(solution)/shard_map/ppermute | solution.py:344
  131.8 2.9 %collective-permute-done.22.refs_3_ = bf16[256,512]{1,0:T(8,128)(2,1)S(1)} collective-permute-done((bf16[256,512]{1,0:T(8,128)(2,1)S(1)}, bf16[256,512]{1,0:T(8,128)(2,1)S(1)}, u32[]{:S(2)}, u32[]{:S(2)}) %collective-permute-start.22) | collective-permute-done | bytes 262176 | tf_op jit(solution)/shard_map/ppermute | solution.py:344
  134.6 1.6 %place.5 = bf16[1024,1024]{1,0:T(8,128)(2,1)} custom-call(s32[4]{0:T(128)S(1)} %get-tuple-element.164.refs_0_.places_ref.rows_ref, s32[4]{0:T(128)S(1)} %get-tuple-element.167.refs_6_.columns_ref, bf16[256,512]{1,0:T(8,128)(2,1)S(1)} %get-tuple-element.149.refs_0_, ...), custom_call_target="tpu_custom_call", output_to_operand_aliasing={{}: (6, {})} | custom-call | flops 1024 | bytes 1024 | tf_op jit(solution)/shard_map/place/pallas_call | solution.py:256
  (52 shorter events, 14.3 us)
Async XLA Ops:
  1.9 15.0 %collective-permute-start = (bf16[2048,128]{1,0:T(8,128)(2,1)S(1)}, bf16[2048,128]{1,0:T(8,128)(2,1)S(1)}, u32[]{:S(2)}, u32[]{:S(2)}) collective-permute-start(bf16[2048,128]{1,0:T(8,128)(2,1)S(1)} %get-tuple-element.163), channel_id=1, source_target_pairs={{16,0},{0,16},{17,1},{1,17},{18,2},{2,18},{19,3},{3,19},{20,4},{4,... | collective-permute-start | bytes 1572872 | tf_op jit(solution)/shard_map/ppermute | solution.py:30
  16.9 3.2 %collective-permute-start.1 = (bf16[2048,128]{1,0:T(8,128)(2,1)S(1)}, bf16[2048,128]{1,0:T(8,128)(2,1)S(1)}, u32[]{:S(2)}, u32[]{:S(2)}) collective-permute-start(bf16[2048,128]{1,0:T(8,128)(2,1)S(1)} %collective-permute-done.refs_0_.refs_2_), channel_id=1, source_target_pairs={{0,1},{1,0},{2,3},{3,2},{4,5},{5,4},{6,7},{7,6},{8,9},{9,8},{10,11... | collective-permute-start | bytes 1572872 | tf_op jit(solution)/shard_map/ppermute | solution.py:344
  16.9 14.3 %collective-permute-start.6 = (bf16[2048,128]{1,0:T(8,128)(2,1)S(1)}, bf16[2048,128]{1,0:T(8,128)(2,1)S(1)}, u32[]{:S(2)}, u32[]{:S(2)}) collective-permute-start(bf16[2048,128]{1,0:T(8,128)(2,1)S(1)} %get-tuple-element.162), channel_id=1, source_target_pairs={{16,0},{0,16},{17,1},{1,17},{18,2},{2,18},{19,3},{3,19},{20,4},{4,... | collective-permute-start | bytes 1572872 | tf_op jit(solution)/shard_map/ppermute | solution.py:30
  18.6 21.0 %collective-permute-start.2 = (bf16[2048,128]{1,0:T(8,128)(2,1)S(1)}, bf16[2048,128]{1,0:T(8,128)(2,1)S(1)}, u32[]{:S(2)}, u32[]{:S(2)}) collective-permute-start(bf16[2048,128]{1,0:T(8,128)(2,1)S(1)} %collective-permute-done.refs_0_.refs_2_), channel_id=1, source_target_pairs={{0,2},{1,3},{2,0},{3,1},{4,6},{5,7},{6,4},{7,5},{8,10},{9,11},{10,... | collective-permute-start | bytes 1572872 | tf_op jit(solution)/shard_map/ppermute | solution.py:344
  20.1 17.6 %copy-start = (bf16[1,1024,1024]{2,1,0:T(8,128)(2,1)S(1)}, bf16[1,1024,1024]{2,1,0:T(8,128)(2,1)}, u32[]{:S(2)}) copy-start(bf16[1,1024,1024]{2,1,0:T(8,128)(2,1)} %param.8) | copy-start | bytes 6291460
  20.1 17.6 %copy-start.1 = (f32[1,256,1024]{2,1,0:T(8,128)S(1)}, f32[1,256,1024]{2,1,0:T(8,128)}, u32[]{:S(2)}) copy-start(f32[1,256,1024]{2,1,0:T(8,128)} %param.10) | copy-start | bytes 3145732
  20.1 17.6 %copy-start.2 = (f32[1,256,1024]{2,1,0:T(8,128)S(1)}, f32[1,256,1024]{2,1,0:T(8,128)}, u32[]{:S(2)}) copy-start(f32[1,256,1024]{2,1,0:T(8,128)} %param.11) | copy-start | bytes 3145732
  22.8 8.4 %collective-permute-start.5 = (bf16[256,256]{1,0:T(8,128)(2,1)S(1)}, bf16[256,256]{1,0:T(8,128)(2,1)S(1)}, u32[]{:S(2)}, u32[]{:S(2)}) collective-permute-start(bf16[256,256]{1,0:T(8,128)(2,1)S(1)} %get-tuple-element.95), channel_id=1, source_target_pairs={{0,12},{4,8},{8,4},{12,0},{1,13},{5,9},{9,5},{13,1},{2,14},{6,10},... | collective-permute-start | bytes 393224 | tf_op jit(solution)/shard_map/ppermute | solution.py:344
  26.5 11.2 %collective-permute-start.4 = (bf16[256,256]{1,0:T(8,128)(2,1)S(1)}, bf16[256,256]{1,0:T(8,128)(2,1)S(1)}, u32[]{:S(2)}, u32[]{:S(2)}) collective-permute-start(bf16[256,256]{1,0:T(8,128)(2,1)S(1)} %get-tuple-element.93), channel_id=1, source_target_pairs={{0,8},{4,12},{8,0},{12,4},{1,9},{5,13},{9,1},{13,5},{2,10},{6,14},... | collective-permute-start | bytes 393224 | tf_op jit(solution)/shard_map/ppermute | solution.py:344
  26.5 11.2 %collective-permute-start.3 = (bf16[256,256]{1,0:T(8,128)(2,1)S(1)}, bf16[256,256]{1,0:T(8,128)(2,1)S(1)}, u32[]{:S(2)}, u32[]{:S(2)}) collective-permute-start(bf16[256,256]{1,0:T(8,128)(2,1)S(1)} %get-tuple-element.90), channel_id=1, source_target_pairs={{0,4},{4,0},{8,12},{12,8},{1,5},{5,1},{9,13},{13,9},{2,6},{6,2},{1... | collective-permute-start | bytes 393224 | tf_op jit(solution)/shard_map/ppermute | solution.py:344
  31.2 18.2 %collective-permute-start.8 = (bf16[2048,128]{1,0:T(8,128)(2,1)S(1)}, bf16[2048,128]{1,0:T(8,128)(2,1)S(1)}, u32[]{:S(2)}, u32[]{:S(2)}) collective-permute-start(bf16[2048,128]{1,0:T(8,128)(2,1)S(1)} %collective-permute-done.6.refs_7_.refs_0_.refs_4_), channel_id=1, source_target_pairs={{0,1},{1,0},{2,3},{3,2},{4,5},{5,4},{6,7},{7,6},{8,9},{9,8},{10,11... | collective-permute-start | bytes 1572872 | tf_op jit(solution)/shard_map/ppermute | solution.py:344
  39.6 9.8 %collective-permute-start.7 = (bf16[2048,128]{1,0:T(8,128)(2,1)S(1)}, bf16[2048,128]{1,0:T(8,128)(2,1)S(1)}, u32[]{:S(2)}, u32[]{:S(2)}) collective-permute-start(bf16[2048,128]{1,0:T(8,128)(2,1)S(1)} %collective-permute-done.2.refs_2_.refs_6_), channel_id=1, source_target_pairs={{0,1},{1,0},{2,3},{3,2},{4,5},{5,4},{6,7},{7,6},{8,9},{9,8},{10,11... | collective-permute-start | bytes 1572872 | tf_op jit(solution)/shard_map/ppermute | solution.py:344
  39.6 14.3 %collective-permute-start.9 = (bf16[2048,128]{1,0:T(8,128)(2,1)S(1)}, bf16[2048,128]{1,0:T(8,128)(2,1)S(1)}, u32[]{:S(2)}, u32[]{:S(2)}) collective-permute-start(bf16[2048,128]{1,0:T(8,128)(2,1)S(1)} %collective-permute-done.6.refs_7_.refs_0_.refs_4_), channel_id=1, source_target_pairs={{0,2},{1,3},{2,0},{3,1},{4,6},{5,7},{6,4},{7,5},{8,10},{9,11},{10,... | collective-permute-start | bytes 1572872 | tf_op jit(solution)/shard_map/ppermute | solution.py:344
  40.2 18.1 %copy-start.4 = (bf16[1,1024,1024]{2,1,0:T(8,128)(2,1)S(1)}, bf16[1,1024,1024]{2,1,0:T(8,128)(2,1)}, u32[]{:S(2)}) copy-start(bf16[1,1024,1024]{2,1,0:T(8,128)(2,1)} %param.9) | copy-start | bytes 6291460
  40.2 9.1 %collective-permute-start.10 = (bf16[256,256]{1,0:T(8,128)(2,1)S(1)}, bf16[256,256]{1,0:T(8,128)(2,1)S(1)}, u32[]{:S(2)}, u32[]{:S(2)}) collective-permute-start(bf16[256,256]{1,0:T(8,128)(2,1)S(1)} %get-tuple-element.108.refs_0_), channel_id=1, source_target_pairs={{0,8},{4,12},{8,0},{12,4},{1,9},{5,13},{9,1},{13,5},{2,10},{6,14},... | collective-permute-start | bytes 393224 | tf_op jit(solution)/shard_map/ppermute | solution.py:344
  54.0 4.4 %collective-permute-start.11 = (bf16[2048,128]{1,0:T(8,128)(2,1)S(1)}, bf16[2048,128]{1,0:T(8,128)(2,1)S(1)}, u32[]{:S(2)}, u32[]{:S(2)}) collective-permute-start(bf16[2048,128]{1,0:T(8,128)(2,1)S(1)} %collective-permute-done.9.refs_6_.refs_0_.refs_2_), channel_id=1, source_target_pairs={{0,1},{1,0},{2,3},{3,2},{4,5},{5,4},{6,7},{7,6},{8,9},{9,8},{10,11... | collective-permute-start | bytes 1572872 | tf_op jit(solution)/shard_map/ppermute | solution.py:344
  54.0 16.9 %collective-permute-start.14 = (bf16[256,512]{1,0:T(8,128)(2,1)S(1)}, bf16[256,512]{1,0:T(8,128)(2,1)S(1)}, u32[]{:S(2)}, u32[]{:S(2)}) collective-permute-start(bf16[256,512]{1,0:T(8,128)(2,1)S(1)} %get-tuple-element.124), channel_id=1, source_target_pairs={{0,12},{4,8},{8,4},{12,0},{1,13},{5,9},{9,5},{13,1},{2,14},{6,10},... | collective-permute-start | bytes 786440 | tf_op jit(solution)/shard_map/ppermute | solution.py:344
  56.4 22.4 %collective-permute-start.13 = (bf16[256,512]{1,0:T(8,128)(2,1)S(1)}, bf16[256,512]{1,0:T(8,128)(2,1)S(1)}, u32[]{:S(2)}, u32[]{:S(2)}) collective-permute-start(bf16[256,512]{1,0:T(8,128)(2,1)S(1)} %get-tuple-element.122), channel_id=1, source_target_pairs={{0,8},{4,12},{8,0},{12,4},{1,9},{5,13},{9,1},{13,5},{2,10},{6,14},... | collective-permute-start | bytes 786440 | tf_op jit(solution)/shard_map/ppermute | solution.py:344
  56.4 22.4 %collective-permute-start.12 = (bf16[256,512]{1,0:T(8,128)(2,1)S(1)}, bf16[256,512]{1,0:T(8,128)(2,1)S(1)}, u32[]{:S(2)}, u32[]{:S(2)}) collective-permute-start(bf16[256,512]{1,0:T(8,128)(2,1)S(1)} %get-tuple-element.119), channel_id=1, source_target_pairs={{0,4},{4,0},{8,12},{12,8},{1,5},{5,1},{9,13},{13,9},{2,6},{6,2},{1... | collective-permute-start | bytes 786440 | tf_op jit(solution)/shard_map/ppermute | solution.py:344
  81.7 18.6 %collective-permute-start.15 = (bf16[2048,512]{1,0:T(8,128)(2,1)S(1)}, bf16[2048,512]{1,0:T(8,128)(2,1)S(1)}, u32[]{:S(2)}, u32[]{:S(2)}) collective-permute-start(bf16[2048,512]{1,0:T(8,128)(2,1)S(1)} %get-tuple-element.129.refs_7_), channel_id=1, source_target_pairs={{0,1},{1,0},{2,3},{3,2},{4,5},{5,4},{6,7},{7,6},{8,9},{9,8},{10,11... | collective-permute-start | bytes 6291464 | tf_op jit(solution)/shard_map/ppermute | solution.py:344
  84.9 8.2 %collective-permute-start.18 = (bf16[256,256]{1,0:T(8,128)(2,1)S(1)}, bf16[256,256]{1,0:T(8,128)(2,1)S(1)}, u32[]{:S(2)}, u32[]{:S(2)}) collective-permute-start(bf16[256,256]{1,0:T(8,128)(2,1)S(1)} %get-tuple-element.137), channel_id=1, source_target_pairs={{0,12},{4,8},{8,4},{12,0},{1,13},{5,9},{9,5},{13,1},{2,14},{6,10},... | collective-permute-start | bytes 393224 | tf_op jit(solution)/shard_map/ppermute | solution.py:344
  86.4 11.9 %collective-permute-start.17 = (bf16[256,256]{1,0:T(8,128)(2,1)S(1)}, bf16[256,256]{1,0:T(8,128)(2,1)S(1)}, u32[]{:S(2)}, u32[]{:S(2)}) collective-permute-start(bf16[256,256]{1,0:T(8,128)(2,1)S(1)} %get-tuple-element.135), channel_id=1, source_target_pairs={{0,8},{4,12},{8,0},{12,4},{1,9},{5,13},{9,1},{13,5},{2,10},{6,14},... | collective-permute-start | bytes 393224 | tf_op jit(solution)/shard_map/ppermute | solution.py:344
  86.4 11.9 %collective-permute-start.16 = (bf16[256,256]{1,0:T(8,128)(2,1)S(1)}, bf16[256,256]{1,0:T(8,128)(2,1)S(1)}, u32[]{:S(2)}, u32[]{:S(2)}) collective-permute-start(bf16[256,256]{1,0:T(8,128)(2,1)S(1)} %get-tuple-element.133), channel_id=1, source_target_pairs={{0,4},{4,0},{8,12},{12,8},{1,5},{5,1},{9,13},{13,9},{2,6},{6,2},{1... | collective-permute-start | bytes 393224 | tf_op jit(solution)/shard_map/ppermute | solution.py:344
  100.5 25.2 %collective-permute-start.19 = (bf16[2048,256]{1,0:T(8,128)(2,1)S(1)}, bf16[2048,256]{1,0:T(8,128)(2,1)S(1)}, u32[]{:S(2)}, u32[]{:S(2)}) collective-permute-start(bf16[2048,256]{1,0:T(8,128)(2,1)S(1)} %add_convert_fusion.1), channel_id=1, source_target_pairs={{0,2},{1,3},{2,0},{3,1},{4,6},{5,7},{6,4},{7,5},{8,10},{9,11},{10,... | collective-permute-start | bytes 3145736 | tf_op jit(solution)/shard_map/ppermute | solution.py:344
  101.1 17.0 %collective-permute-start.21 = (bf16[256,512]{1,0:T(8,128)(2,1)S(1)}, bf16[256,512]{1,0:T(8,128)(2,1)S(1)}, u32[]{:S(2)}, u32[]{:S(2)}) collective-permute-start(bf16[256,512]{1,0:T(8,128)(2,1)S(1)} %get-tuple-element.149.refs_0_), channel_id=1, source_target_pairs={{0,8},{4,12},{8,0},{12,4},{1,9},{5,13},{9,1},{13,5},{2,10},{6,14},... | collective-permute-start | bytes 786440 | tf_op jit(solution)/shard_map/ppermute | solution.py:344
  101.7 9.6 %collective-permute-start.26 = (bf16[256,256]{1,0:T(8,128)(2,1)S(1)}, bf16[256,256]{1,0:T(8,128)(2,1)S(1)}, u32[]{:S(2)}, u32[]{:S(2)}) collective-permute-start(bf16[256,256]{1,0:T(8,128)(2,1)S(1)} %get-tuple-element.108.refs_0_), channel_id=1, source_target_pairs={{0,4},{4,0},{8,12},{12,8},{1,5},{5,1},{9,13},{13,9},{2,6},{6,2},{1... | collective-permute-start | bytes 393224 | tf_op jit(solution)/shard_map/ppermute | solution.py:344
  103.4 10.8 %collective-permute-start.27 = (bf16[256,256]{1,0:T(8,128)(2,1)S(1)}, bf16[256,256]{1,0:T(8,128)(2,1)S(1)}, u32[]{:S(2)}, u32[]{:S(2)}) collective-permute-start(bf16[256,256]{1,0:T(8,128)(2,1)S(1)} %collective-permute-done.10.refs_8_.refs_2_), channel_id=1, source_target_pairs={{0,4},{4,0},{8,12},{12,8},{1,5},{5,1},{9,13},{13,9},{2,6},{6,2},{1... | collective-permute-start | bytes 393224 | tf_op jit(solution)/shard_map/ppermute | solution.py:344
  103.8 16.7 %collective-permute-start.24 = (bf16[256,256]{1,0:T(8,128)(2,1)S(1)}, bf16[256,256]{1,0:T(8,128)(2,1)S(1)}, u32[]{:S(2)}, u32[]{:S(2)}) collective-permute-start(bf16[256,256]{1,0:T(8,128)(2,1)S(1)} %get-tuple-element.151.refs_0_), channel_id=1, source_target_pairs={{0,8},{4,12},{8,0},{12,4},{1,9},{5,13},{9,1},{13,5},{2,10},{6,14},... | collective-permute-start | bytes 393224 | tf_op jit(solution)/shard_map/ppermute | solution.py:344
  111.4 20.4 %collective-permute-start.20 = (bf16[256,512]{1,0:T(8,128)(2,1)S(1)}, bf16[256,512]{1,0:T(8,128)(2,1)S(1)}, u32[]{:S(2)}, u32[]{:S(2)}) collective-permute-start(bf16[256,512]{1,0:T(8,128)(2,1)S(1)} %get-tuple-element.149.refs_0_), channel_id=1, source_target_pairs={{0,4},{4,0},{8,12},{12,8},{1,5},{5,1},{9,13},{13,9},{2,6},{6,2},{1... | collective-permute-start | bytes 786440 | tf_op jit(solution)/shard_map/ppermute | solution.py:344
  115.6 14.0 %collective-permute-start.23 = (bf16[256,256]{1,0:T(8,128)(2,1)S(1)}, bf16[256,256]{1,0:T(8,128)(2,1)S(1)}, u32[]{:S(2)}, u32[]{:S(2)}) collective-permute-start(bf16[256,256]{1,0:T(8,128)(2,1)S(1)} %get-tuple-element.151.refs_0_), channel_id=1, source_target_pairs={{0,4},{4,0},{8,12},{12,8},{1,5},{5,1},{9,13},{13,9},{2,6},{6,2},{1... | collective-permute-start | bytes 393224 | tf_op jit(solution)/shard_map/ppermute | solution.py:344
  118.1 12.2 %collective-permute-start.25 = (bf16[256,256]{1,0:T(8,128)(2,1)S(1)}, bf16[256,256]{1,0:T(8,128)(2,1)S(1)}, u32[]{:S(2)}, u32[]{:S(2)}) collective-permute-start(bf16[256,256]{1,0:T(8,128)(2,1)S(1)} %get-tuple-element.151.refs_0_), channel_id=1, source_target_pairs={{0,12},{4,8},{8,4},{12,0},{1,13},{5,9},{9,5},{13,1},{2,14},{6,10},... | collective-permute-start | bytes 393224 | tf_op jit(solution)/shard_map/ppermute | solution.py:344
  120.4 14.2 %collective-permute-start.22 = (bf16[256,512]{1,0:T(8,128)(2,1)S(1)}, bf16[256,512]{1,0:T(8,128)(2,1)S(1)}, u32[]{:S(2)}, u32[]{:S(2)}) collective-permute-start(bf16[256,512]{1,0:T(8,128)(2,1)S(1)} %collective-permute-done.21.refs_4_.refs_2_), channel_id=1, source_target_pairs={{0,4},{4,0},{8,12},{12,8},{1,5},{5,1},{9,13},{13,9},{2,6},{6,2},{1... | collective-permute-start | bytes 786440 | tf_op jit(solution)/shard_map/ppermute | solution.py:344
  (1 other events, 2.2 us)

commit v3 on v2

--- a/solution.py
+++ b/solution.py
@@ -12,16 +12,20 @@
 COL_PARTS = 2
 TILE = 256
 CHUNKS = (((0, 0), (1, 0)), ((0, 1), (1, 1), (2, 0), (3, 0)), ((2, 1), (3, 1)))
-SUMS = ("one", "one", "one",)
-GATHERS = ("two", "two", "one",)
+SUMS = ("two", "one", "one",)
+GATHERS = ("two", "two", "two",)
 PLAN = (
-    "h0", "b00", "b10", "t0", "b01", "r0", "a0", "b11", "b20", "g0", "b30", "t1", "b21",
-    "b31", "t2", "p0", "r1", "l0", "a1", "w0", "r2", "a2", "g1", "x0", "g2", "x1", "l2",
-    "l1",
+    "h0", "b00", "b10", "t0", "b01", "m0", "r0", "b20", "b11", "a0", "b30", "t1", "g0",
+    "e0", "b21", "b31", "t2", "p0", "r1", "a1", "r2", "x0", "a2", "e1", "g1", "e2", "g2",
+    "l0", "x1", "l1", "l2",
 )
 ANYWHERE = pl.BlockSpec(memory_space=pl.ANY)
 TOKEN = jax.ShapeDtypeStruct((8, 128), F32)
-SMALL = pl.CostEstimate(flops=1024, bytes_accessed=1024, transcendentals=0)
+COSTS = {
+    "h0": 15000000000, "t0": 10000000000, "a0": 80000000000, "t1": 40000000000,
+    "t2": 6000000000, "p0": 35100000000, "a1": 6000000000, "a2": 6000000000, "l0": 4199999999,
+    "l1": 1000, "l2": 80000000000,
+}
 
 
 def from_behind(block, axis, distance):
@@ -94,11 +98,15 @@
     return (input_grad[None], new_down[None], new_m[None], new_v[None])
 
 
+def cost(item):
+    return pl.CostEstimate(flops=COSTS[item], bytes_accessed=1024, transcendentals=0)
+
+
 def params(mib):
     return pltpu.CompilerParams(vmem_limit_bytes=mib * 2**20)
 
 
-def prepare(hidden_pre, model_width, after):
+def prepare(hidden_pre, model_width, after, item):
     tokens, units = hidden_pre.shape
     scale = 1.0 / math.sqrt(model_width)
 
@@ -126,12 +134,12 @@
             TOKEN,
         ],
         compiler_params=params(8),
-        cost_estimate=SMALL,
+        cost_estimate=cost(item),
         name="prepare",
     )(hidden_pre, *after)
 
 
-def terms(hidden_t, pieces, places, scale, paired, after):
+def terms(hidden_t, pieces, places, scale, paired, after, item):
     units, tokens = hidden_t.shape
     size, width = units // 4, pieces[0].shape[1]
     count, wide = len(pieces), len(pieces) * pieces[0].shape[1]
@@ -173,12 +181,12 @@
         ),
         out_shape=[jax.ShapeDtypeStruct((height, wide), BF16) for height in heights] + [TOKEN],
         compiler_params=params(16),
-        cost_estimate=SMALL,
+        cost_estimate=cost(item),
         name="terms",
     )(places, hidden_t, *pieces, *after)
 
 
-def adam_chunk(shares, near, moment, second, down, columns, rank, previous, width, after):
+def adam_chunk(shares, near, moment, second, down, columns, rank, previous, width, after, item):
     size, wide = shares[0].shape
     count = wide // width
     total = moment.shape[1]
@@ -223,18 +231,19 @@
             number + len(after) + 5: 1, number + len(after) + 6: 2
         } if previous else {},
         compiler_params=params(8),
-        cost_estimate=SMALL,
+        cost_estimate=cost(item),
         name="adam",
     )(columns, rank, *shares, *near, moment, second, down, *after, *previous)
 
 
-def place_rows(shards, rows, columns, previous, total, width, after):
+def place_rows(shards, rows, columns, previous, total, width, after, item):
     size, wide = shards[0].shape
     count = wide // width
     number = len(shards)
 
     def kernel(rows_ref, columns_ref, *refs):
-        shard_refs, out_ref, sems = refs[:number], refs[-2], refs[-1]
+        shard_refs, out_ref, token_ref, sems = refs[:number], refs[-3], refs[-2], refs[-1]
+        token_ref[...] = jnp.zeros_like(token_ref)
         copies = []
         for k in range(number):
             for j in range(count):
@@ -259,29 +268,30 @@
             num_scalar_prefetch=2,
             grid=(1,),
             in_specs=[ANYWHERE] * (number + len(after) + len(previous)),
-            out_specs=ANYWHERE,
+            out_specs=[ANYWHERE, pl.BlockSpec((8, 128), lambda i, rows, columns: (0, 0))],
             scratch_shapes=[pltpu.SemaphoreType.DMA((number, count))],
         ),
-        out_shape=jax.ShapeDtypeStruct(total, BF16),
+        out_shape=[jax.ShapeDtypeStruct(total, BF16), TOKEN],
         input_output_aliases={2 + number + len(after): 0} if previous else {},
         compiler_params=params(8),
-        cost_estimate=SMALL,
+        cost_estimate=cost(item),
         name="place",
     )(rows, columns, *shards, *after, *previous)
 
 
-def partials(pieces, where, order, slope, down, up, scale, after):
+def partials(pieces, where, order, slope, down, up, scale, after, item):
     tokens, units = slope.shape
     model_width = down.shape[1]
     width = pieces[0].shape[1]
     count = len(pieces)
     block = model_width // 4
     rows = tokens
+    step = 2 * TILE
 
     def kernel(where_ref, order_ref, *refs):
         piece_refs, refs = refs[:count], refs[count:]
         slope_ref, down_ref, up_ref = refs[:3]
-        own_ref, other_ref, send_ref, token_ref, joined, product_ref = refs[3 + len(after) :]
+        outs, token_ref, joined, product_ref = refs[3 + len(after) : -3], *refs[-3:]
         token_ref[...] = jnp.zeros_like(token_ref)
         for j in range(count):
             joined[:, pl.ds(pl.multiple_of(where_ref[j] * width, width), width)] = piece_refs[j][...]
@@ -292,42 +302,36 @@
         product = jnp.dot(act_grad, up_ref[...], preferred_element_type=F32) * scale
         product_ref[...] = product.astype(BF16)
 
-        def columns(k):
-            return product_ref[:, pl.ds(pl.multiple_of(order_ref[k] * block, block), block)]
-
-        own_ref[...] = columns(0)
-        other_ref[...] = columns(1)
-        send_ref[:, :block] = columns(2)
-        send_ref[:, block:] = columns(3)
+        for k in range(4):
+            first = pl.multiple_of(order_ref[k] * block, block)
+            outs[k][...] = product_ref[:, pl.ds(first, block)]
 
     return pl.pallas_call(
         kernel,
         grid_spec=pltpu.PrefetchScalarGridSpec(
             num_scalar_prefetch=2,
-            grid=(rows // TILE,),
-            in_specs=[pl.BlockSpec((TILE, width), lambda i, w, o: (i, 0))] * count
-            + [pl.BlockSpec((TILE, units), lambda i, w, o: (i, 0))]
+            grid=(rows // step,),
+            in_specs=[pl.BlockSpec((step, width), lambda i, w, o: (i, 0))] * count
+            + [pl.BlockSpec((step, units), lambda i, w, o: (i, 0))]
             + [pl.BlockSpec((units, model_width), lambda i, w, o: (0, 0))] * 2
             + [ANYWHERE] * len(after),
             out_specs=[
-                pl.BlockSpec((TILE, block), lambda i, w, o: (i, 0)),
-                pl.BlockSpec((TILE, block), lambda i, w, o: (i, 0)),
-                pl.BlockSpec((TILE, 2 * block), lambda i, w, o: (i, 0)),
-                pl.BlockSpec((8, 128), lambda i, w, o: (0, 0)),
-            ],
+                pl.BlockSpec((step, block), lambda i, w, o: (i, 0)),
+            ]
+            * 4
+            + [pl.BlockSpec((8, 128), lambda i, w, o: (0, 0))],
             scratch_shapes=[
-                pltpu.VMEM((TILE, model_width), BF16),
-                pltpu.VMEM((TILE, model_width), BF16),
+                pltpu.VMEM((step, model_width), BF16),
+                pltpu.VMEM((step, model_width), BF16),
             ],
         ),
         out_shape=[
             jax.ShapeDtypeStruct((rows, block), BF16),
-            jax.ShapeDtypeStruct((rows, block), BF16),
-            jax.ShapeDtypeStruct((rows, 2 * block), BF16),
-            TOKEN,
-        ],
-        compiler_params=params(20),
-        cost_estimate=SMALL,
+        ]
+        * 4
+        + [TOKEN],
+        compiler_params=params(28),
+        cost_estimate=cost(item),
         name="partials",
     )(where, order, *pieces, slope, down, up, *after)
 
@@ -366,9 +370,8 @@
         return out
 
     def arrive(name):
-        value, token = lax.optimization_barrier((values[name], values["token"]))
-        values[name] = value
-        held.extend([value, token])
+        values[name], *held[:] = lax.optimization_barrier((values[name], values["token"], *held))
+        held.append(values[name])
 
     for part in range(COL_PARTS):
         columns_now = handoff[:, part * width : (part + 1) * width]
@@ -378,7 +381,8 @@
         kind, k = name[0], int(name[1])
         if kind == "h":
             values["hidden"], values["slope"], values["token"] = prepare(
-                hidden_pre, model_width, [shards, paired, rank_now, order, where, *columns]
+                hidden_pre, model_width, [shards, paired, rank_now, order, where, *columns],
+                name,
             )
         elif kind == "b":
             arrive(name)
@@ -390,33 +394,36 @@
                 values["b3" + part] = swapped(values[name], "tensor", 1)
         elif kind == "t":
             pieces = [values["b%d%d" % key] for key in CHUNKS[k]]
-            pair = SUMS[k] == "two"
+            pair, step = SUMS[k] == "two", SUMS[k] == "tri"
             *out, values["token"] = terms(
-                values["hidden"], pieces, paired if pair else shards, term_scale, pair, after()
+                values["hidden"], pieces, paired if pair else shards, term_scale, pair, after(), name
             )
             if pair:
                 values["s0" + name[1]], values["s2" + name[1]] = out[:2]
                 values["m" + name[1]] = swapped(out[2], "dp", 1)
             else:
-                values["s0" + name[1]] = out[0]
-                for j in (3, 2, 1):
+                values["s0" + name[1]], values["s2" + name[1]] = out[0], out[2]
+                values["m" + name[1]] = swapped(out[3], "dp", 1) if step else None
+                for j in (1,) if step else (3, 2, 1):
                     values["s%d%d" % (j, k)] = swapped(out[j], "dp", j)
         elif kind == "m":
             arrive(name)
             size = values["s0" + name[1]].shape[0]
-            far = values["s2" + name[1]].astype(F32) + values[name][:size].astype(F32)
+            held_part = values[name][:size] if SUMS[k] == "two" else values[name]
+            far = values["s2" + name[1]].astype(F32) + held_part.astype(F32)
             values["s2" + name[1]] = swapped(far.astype(BF16), "dp", 2)
         elif kind == "r":
-            for j in (2,) if SUMS[k] == "two" else (3, 2, 1):
+            for j in {"two": (2,), "tri": (1, 2), "one": (3, 2, 1)}[SUMS[k]]:
                 arrive("s%d%d" % (j, k))
         elif kind == "a":
             if SUMS[k] == "two":
                 shares, near = [values["s%d%d" % (j, k)] for j in (0, 2)], [values["m" + name[1]]]
             else:
-                shares, near = [values["s%d%d" % (j, k)] for j in range(4)], []
+                number = 3 if SUMS[k] == "tri" else 4
+                shares, near = [values["s%d%d" % (j, k)] for j in range(number)], []
             fresh, *moments[:], values["token"] = adam_chunk(
                 shares, near, moment[0], second[0], down, columns[k], rank_now,
-                moments, width, after(),
+                moments, width, after(), name,
             )
             values["g0" + name[1]] = fresh
             values["g2" + name[1]] = swapped(fresh, "dp", 2)
@@ -427,28 +434,33 @@
             arrive("g2" + name[1])
             if GATHERS[k] != "one":
                 values["g3" + name[1]] = swapped(values["g2" + name[1]], "dp", 1)
+        elif kind == "e":
+            arrive("g1" + name[1])
         elif kind == "l":
             gathered = [values["g%d%d" % (j, k)] for j in range(4)]
-            new_down[:] = [
-                place_rows(gathered, shards, columns[k], new_down, down.shape, width, after())
-            ]
+            *new_down[:], values["token"] = place_rows(
+                gathered, shards, columns[k], new_down, down.shape, width, after(), name
+            )
         elif kind == "p":
             pieces = [values["b%d%d" % key] for key in keys]
-            values["own"], values["other"], values["x0"], values["token"] = partials(
-                pieces, where, order, values["slope"], down, up, partial_scale, after()
+            values["own"], values["other"], values["x2"], values["x0"], values["token"] = partials(
+                pieces, where, order, values["slope"], down, up, partial_scale, after(), name
             )
+            values["x2"] = swapped(values["x2"], "tensor", 1)
             if "w0" not in PLAN:
                 values["x0"] = swapped(values["x0"], "tensor", 1)
         elif kind == "w":
             arrive("x0")
             values["x0"] = swapped(values["x0"], "tensor", 1)
+        elif kind == "u":
+            arrive("x2")
         elif kind == "x" and k == 0:
             arrive("x0")
-            other = values["other"].astype(F32) + values["x0"][:, block:].astype(F32)
+            other = values["other"].astype(F32) + values["x0"].astype(F32)
             values["x1"] = swapped(other.astype(BF16), "tensor", 2)
         elif kind == "x":
             arrive("x1")
-            own = values["own"].astype(F32) + values["x0"][:, :block].astype(F32)
+            own = values["own"].astype(F32) + values["x2"].astype(F32)
             input_grad = (own + values["x1"].astype(F32)).astype(BF16)
     return (input_grad[None], new_down[0][None], moments[0][None], moments[1][None])
 

time: 136 us -> 122 us (0.90)
  waiting for transfers between devices: 59 us -> 44.4 us
    ppermute x26, waiting for transfers between devices: 50.7 us -> 33.6 us  [swapped(): return lax.ppermute(value, axis, [(i, i ^ distance) for i in range(4)])]
    ppermute x2, waiting for transfers between devices: 8.31 us -> 10.8 us  [from_behind(): return lax.ppermute(block, axis, route)]
  transfers between devices with their start and end apart: 28 -> 28, of which waited for: 15 -> 14; matrix products, arithmetic and copies ran while one was open for 1% -> 1% of each run, Pallas kernels for 25% -> 32%
where the time goes in v3:
time: 122 us
  waiting for transfers between devices  44.4 us (36%)
  Pallas kernels  38.8 us (32%)
  starting transfers between devices  32.1 us (26%)
  local copies, waits for them, and re-layouts  3.58 us (3%)
  other arithmetic  1.96 us (2%)
    ppermute x26, waiting for transfers between devices, swapped(): return lax.ppermute(value, axis, [(i, i ^ distance) for i in range(4)])  33.6 us
    ppermute x26, starting transfers between devices, swapped(): return lax.ppermute(value, axis, [(i, i ^ distance) for i in range(4)])  27.3 us
    pallas_call x1, Pallas kernels, partials(): pl.pallas_call(kernel, grid_spec=pltpu.PrefetchScalarGridSpec(num_scalar_...  11.8 us
    ppermute x2, waiting for transfers between devices, from_behind(): return lax.ppermute(block, axis, route)  10.8 us
    pallas_call x3, Pallas kernels, terms(): pl.pallas_call(kernel, grid_spec=pltpu.PrefetchScalarGridSpec(num_scalar_...  9.86 us
    pallas_call x3, Pallas kernels, adam_chunk(): pl.pallas_call(kernel, grid_spec=pltpu.PrefetchScalarGridSpec(num_scalar_...  6.61 us
    pallas_call x3, Pallas kernels, place_rows(): pl.pallas_call(kernel, grid_spec=pltpu.PrefetchScalarGridSpec(num_scalar_...  5.61 us
    pallas_call x1, Pallas kernels, prepare(): pl.pallas_call(kernel, grid=(tokens // TILE,), in_specs=[pl.BlockSpec((TI...  5.02 us
  transfers between devices with their start and end apart: 28, of which 14 were waited for; matrix products, arithmetic and copies ran while one was open for 1% of the time, Pallas kernels for 32%

profile of v3, /device:TPU:0, one launch (start us, length us, event | category | flops | bytes accessed | tf_op | source)
XLA Modules:
  0.0 121.7 jit_solution(16236134858292419129)
XLA Ops:
  1.9 3.0 %collective-permute-start = (bf16[2048,128]{1,0:T(8,128)(2,1)S(1)}, bf16[2048,128]{1,0:T(8,128)(2,1)S(1)}, u32[]{:S(2)}, u32[]{:S(2)}) collective-permute-start(bf16[2048,128]{1,0:T(8,128)(2,1)S(1)} %get-tuple-element.303), channel_id=1, source_target_pairs={{16,0},{0,16},{17,1},{1,17},{18,2},{2,18},{19,3},{3,19},{20,4},{4,... | collective-permute-start | bytes 1572872 | tf_op jit(solution)/shard_map/ppermute | solution.py:34
  5.3 2.2 %copy-done.2 = bf16[1,2048,1024]{2,1,0:T(8,128)(2,1)S(1)} copy-done((bf16[1,2048,1024]{2,1,0:T(8,128)(2,1)S(1)}, bf16[1,2048,1024]{2,1,0:T(8,128)(2,1)}, u32[]{:S(2)}) %copy-start.2) | copy-done | bytes 4194328
  7.5 5.0 %prepare.1 = (bf16[1024,2048]{1,0:T(8,128)(2,1)S(1)}, bf16[2048,1024]{1,0:T(8,128)(2,1)S(1)}, f32[8,128]{1,0:T(8,128)S(1)}) custom-call(bf16[2048,1024]{1,0:T(8,128)(2,1)S(1)} %bitcast.27, s32[4]{0:T(128)S(1)} %get-tuple-element.304.refs_0_.places_ref.rows_ref, s32[4]{0:T(128)S(1)} %get-tuple-element.305.refs_1_.places_ref, s32[1]{0:T(128)} %bitcast.14.refs_2_.rank_ref, ...), custom_call_target="tpu_custom_call" | custom-call | flops 15000000512 | bytes 1024 | tf_op jit(solution)/shard_map/prepare/pallas_call | solution.py:122
  12.5 4.4 %collective-permute-done.refs_0_.refs_4_ = bf16[2048,128]{1,0:T(8,128)(2,1)S(1)} collective-permute-done((bf16[2048,128]{1,0:T(8,128)(2,1)S(1)}, bf16[2048,128]{1,0:T(8,128)(2,1)S(1)}, u32[]{:S(2)}, u32[]{:S(2)}) %collective-permute-start) | collective-permute-done | bytes 524320 | tf_op jit(solution)/shard_map/ppermute | solution.py:34
  16.9 1.7 %collective-permute-start.4 = (bf16[2048,128]{1,0:T(8,128)(2,1)S(1)}, bf16[2048,128]{1,0:T(8,128)(2,1)S(1)}, u32[]{:S(2)}, u32[]{:S(2)}) collective-permute-start(bf16[2048,128]{1,0:T(8,128)(2,1)S(1)} %get-tuple-element.302), channel_id=1, source_target_pairs={{16,0},{0,16},{17,1},{1,17},{18,2},{2,18},{19,3},{3,19},{20,4},{4,... | collective-permute-start | bytes 1572872 | tf_op jit(solution)/shard_map/ppermute | solution.py:34
  18.8 2.7 %terms.3 = (bf16[256,256]{1,0:T(8,128)(2,1)S(1)}, bf16[256,256]{1,0:T(8,128)(2,1)S(1)}, bf16[512,256]{1,0:T(8,128)(2,1)S(1)}, f32[8,128]{1,0:T(8,128)S(1)}) custom-call(s32[4]{0:T(128)S(1)} %get-tuple-element.305.refs_1_.places_ref, bf16[1024,2048]{1,0:T(8,128)(2,1)S(1)} %get-tuple-element.157.hidden_ref, ...), custom_call_target="tpu_custom_call" | custom-call | flops 10000000000 | bytes 1024 | tf_op jit(solution)/shard_map/terms/pallas_call | solution.py:170
  21.4 1.9 %collective-permute-start.3 = (bf16[512,256]{1,0:T(8,128)(2,1)S(1)}, bf16[512,256]{1,0:T(8,128)(2,1)S(1)}, u32[]{:S(2)}, u32[]{:S(2)}) collective-permute-start(bf16[512,256]{1,0:T(8,128)(2,1)S(1)} %get-tuple-element.163), channel_id=1, source_target_pairs={{0,4},{4,0},{8,12},{12,8},{1,5},{5,1},{9,13},{13,9},{2,6},{6,2},{1... | collective-permute-start | bytes 786440 | tf_op jit(solution)/shard_map/ppermute | solution.py:348
  24.8 6.4 %collective-permute-done.4.refs_11_.refs_0_.refs_4_ = bf16[2048,128]{1,0:T(8,128)(2,1)S(1)} collective-permute-done((bf16[2048,128]{1,0:T(8,128)(2,1)S(1)}, bf16[2048,128]{1,0:T(8,128)(2,1)S(1)}, u32[]{:S(2)}, u32[]{:S(2)}) %collective-permute-start.4) | collective-permute-done | bytes 524320 | tf_op jit(solution)/shard_map/ppermute | solution.py:34
  31.2 2.9 %collective-permute-start.5 = (bf16[256,256]{1,0:T(8,128)(2,1)S(1)}, bf16[256,256]{1,0:T(8,128)(2,1)S(1)}, u32[]{:S(2)}, u32[]{:S(2)}) collective-permute-start(bf16[256,256]{1,0:T(8,128)(2,1)S(1)} %add_convert_fusion.2), channel_id=1, source_target_pairs={{0,8},{4,12},{8,0},{12,4},{1,9},{5,13},{9,1},{13,5},{2,10},{6,14},... | collective-permute-start | bytes 393224 | tf_op jit(solution)/shard_map/ppermute | solution.py:348
  35.6 5.5 %collective-permute-done.5.refs_1_.refs_13_ = bf16[256,256]{1,0:T(8,128)(2,1)S(1)} collective-permute-done((bf16[256,256]{1,0:T(8,128)(2,1)S(1)}, bf16[256,256]{1,0:T(8,128)(2,1)S(1)}, u32[]{:S(2)}, u32[]{:S(2)}) %collective-permute-start.5) | collective-permute-done | bytes 131104 | tf_op jit(solution)/shard_map/ppermute | solution.py:348
  41.1 1.9 %adam.3 = (bf16[256,256]{1,0:T(8,128)(2,1)S(1)}, f32[256,1024]{1,0:T(8,128)}, f32[256,1024]{1,0:T(8,128)}, f32[8,128]{1,0:T(8,128)S(1)}) custom-call(s32[2]{0:T(128)S(1)} %get-tuple-element.308.refs_5_.columns_ref, s32[1]{0:T(128)} %bitcast.14.refs_2_.rank_ref, bf16[256,256]{1,0:T(8,128)(2,1)S(1)} %get-tuple-element.177.refs_0_, ...), custom_call_target="tpu_custom_call" | custom-call | flops 80000000000 | bytes 1024 | tf_op jit(solution)/shard_map/adam/pallas_call | solution.py:212
  43.0 4.2 %collective-permute-start.9 = (bf16[256,256]{1,0:T(8,128)(2,1)S(1)}, bf16[256,256]{1,0:T(8,128)(2,1)S(1)}, u32[]{:S(2)}, u32[]{:S(2)}) collective-permute-start(bf16[256,256]{1,0:T(8,128)(2,1)S(1)} %get-tuple-element.199.refs_0_), channel_id=1, source_target_pairs={{0,4},{4,0},{8,12},{12,8},{1,5},{5,1},{9,13},{13,9},{2,6},{6,2},{1... | collective-permute-start | bytes 393224 | tf_op jit(solution)/shard_map/ppermute | solution.py:348
  47.2 4.0 %terms.4 = (bf16[256,512]{1,0:T(8,128)(2,1)S(1)}, bf16[256,512]{1,0:T(8,128)(2,1)S(1)}, bf16[256,512]{1,0:T(8,128)(2,1)S(1)}, bf16[256,512]{1,0:T(8,128)(2,1)S(1)}, f32[8,128]{1,0:T(8,128)S(1)}) custom-call(s32[4]{0:T(128)S(1)} %get-tuple-element.304.refs_0_.places_ref.rows_ref, bf16[1024,2048]{1,0:T(8,128)(2,1)S(1)} %get-tuple-element.157.hidden_ref, ...), custom_call_target="tpu_custom_call" | custom-call | flops 40000000000 | bytes 1024 | tf_op jit(solution)/shard_map/terms/pallas_call | solution.py:170
  51.1 1.6 %collective-permute-done.10.refs_6_.refs_2_ = bf16[256,256]{1,0:T(8,128)(2,1)S(1)} collective-permute-done((bf16[256,256]{1,0:T(8,128)(2,1)S(1)}, bf16[256,256]{1,0:T(8,128)(2,1)S(1)}, u32[]{:S(2)}, u32[]{:S(2)}) %collective-permute-start.10) | collective-permute-done | bytes 131104 | tf_op jit(solution)/shard_map/ppermute | solution.py:348
  52.8 2.5 %collective-permute-start.16 = (bf16[256,512]{1,0:T(8,128)(2,1)S(1)}, bf16[256,512]{1,0:T(8,128)(2,1)S(1)}, u32[]{:S(2)}, u32[]{:S(2)}) collective-permute-start(bf16[256,512]{1,0:T(8,128)(2,1)S(1)} %get-tuple-element.222), channel_id=1, source_target_pairs={{0,12},{4,8},{8,4},{12,0},{1,13},{5,9},{9,5},{13,1},{2,14},{6,10},... | collective-permute-start | bytes 786440 | tf_op jit(solution)/shard_map/ppermute | solution.py:348
  55.3 2.0 %collective-permute-start.14 = (bf16[256,512]{1,0:T(8,128)(2,1)S(1)}, bf16[256,512]{1,0:T(8,128)(2,1)S(1)}, u32[]{:S(2)}, u32[]{:S(2)}) collective-permute-start(bf16[256,512]{1,0:T(8,128)(2,1)S(1)} %get-tuple-element.219), channel_id=1, source_target_pairs={{0,4},{4,0},{8,12},{12,8},{1,5},{5,1},{9,13},{13,9},{2,6},{6,2},{1... | collective-permute-start | bytes 786440 | tf_op jit(solution)/shard_map/ppermute | solution.py:348
  57.2 11.8 %partials.1 = (bf16[2048,256]{1,0:T(8,128)(2,1)S(1)}, bf16[2048,256]{1,0:T(8,128)(2,1)S(1)}, bf16[2048,256]{1,0:T(8,128)(2,1)S(1)}, bf16[2048,256]{1,0:T(8,128)(2,1)S(1)}, f32[8,128]{1,0:T(8,128)S(1)}) custom-call(s32[8]{0:T(128)S(1)} %stack.89.refs_4_.where_ref, s32[4]{0:T(128)S(1)} %get-tuple-element.306.refs_3_.order_ref, ...), custom_call_target="tpu_custom_call" | custom-call | flops 35100000256 | bytes 1024 | tf_op jit(solution)/shard_map/partials/pallas_call | solution.py:309
  69.1 3.2 %terms.5 = (bf16[256,256]{1,0:T(8,128)(2,1)S(1)}, bf16[256,256]{1,0:T(8,128)(2,1)S(1)}, bf16[256,256]{1,0:T(8,128)(2,1)S(1)}, bf16[256,256]{1,0:T(8,128)(2,1)S(1)}, f32[8,128]{1,0:T(8,128)}) custom-call(s32[4]{0:T(128)S(1)} %get-tuple-element.304.refs_0_.places_ref.rows_ref, bf16[1024,2048]{1,0:T(8,128)(2,1)S(1)} %get-tuple-element.157.hidden_ref, ...), custom_call_target="tpu_custom_call" | custom-call | flops 6000000000 | bytes 1024 | tf_op jit(solution)/shard_map/terms/pallas_call | solution.py:170
  72.3 2.4 %collective-permute-start.19 = (bf16[256,256]{1,0:T(8,128)(2,1)S(1)}, bf16[256,256]{1,0:T(8,128)(2,1)S(1)}, u32[]{:S(2)}, u32[]{:S(2)}) collective-permute-start(bf16[256,256]{1,0:T(8,128)(2,1)S(1)} %get-tuple-element.247), channel_id=1, source_target_pairs={{0,12},{4,8},{8,4},{12,0},{1,13},{5,9},{9,5},{13,1},{2,14},{6,10},... | collective-permute-start | bytes 393224 | tf_op jit(solution)/shard_map/ppermute | solution.py:348
  74.7 6.3 %collective-permute-done.15.refs_2_.refs_11_ = bf16[256,512]{1,0:T(8,128)(2,1)S(1)} collective-permute-done((bf16[256,512]{1,0:T(8,128)(2,1)S(1)}, bf16[256,512]{1,0:T(8,128)(2,1)S(1)}, u32[]{:S(2)}, u32[]{:S(2)}) %collective-permute-start.15) | collective-permute-done | bytes 262176 | tf_op jit(solution)/shard_map/ppermute | solution.py:348
  81.0 3.3 %collective-permute-start.17 = (bf16[256,256]{1,0:T(8,128)(2,1)S(1)}, bf16[256,256]{1,0:T(8,128)(2,1)S(1)}, u32[]{:S(2)}, u32[]{:S(2)}) collective-permute-start(bf16[256,256]{1,0:T(8,128)(2,1)S(1)} %get-tuple-element.245), channel_id=1, source_target_pairs={{0,4},{4,0},{8,12},{12,8},{1,5},{5,1},{9,13},{13,9},{2,6},{6,2},{1... | collective-permute-start | bytes 393224 | tf_op jit(solution)/shard_map/ppermute | solution.py:348
  84.4 2.9 %adam.4 = (bf16[256,512]{1,0:T(8,128)(2,1)S(1)}, f32[256,1024]{1,0:T(8,128)}, f32[256,1024]{1,0:T(8,128)}, f32[8,128]{1,0:T(8,128)S(1)}) custom-call(s32[4]{0:T(128)S(1)} %copy-done.1, s32[1]{0:T(128)} %bitcast.14.refs_2_.rank_ref, bf16[256,512]{1,0:T(8,128)(2,1)S(1)} %get-tuple-element.218.refs_0_, ...), custom_call_target="tpu_custom_call", output_to_operand_aliasing={{1}: (15, {}), {2}: (16, {})} | custom-call | flops 6000000000 | bytes 1024 | tf_op jit(solution)/shard_map/adam/pallas_call | solution.py:212
  87.2 1.6 %collective-permute-start.24 = (bf16[256,512]{1,0:T(8,128)(2,1)S(1)}, bf16[256,512]{1,0:T(8,128)(2,1)S(1)}, u32[]{:S(2)}, u32[]{:S(2)}) collective-permute-start(bf16[256,512]{1,0:T(8,128)(2,1)S(1)} %get-tuple-element.273.refs_0_), channel_id=1, source_target_pairs={{0,8},{4,12},{8,0},{12,4},{1,9},{5,13},{9,1},{13,5},{2,10},{6,14},... | collective-permute-start | bytes 786440 | tf_op jit(solution)/shard_map/ppermute | solution.py:348
  89.7 4.9 %collective-permute-done.17.refs_1_.refs_13_ = bf16[256,256]{1,0:T(8,128)(2,1)S(1)} collective-permute-done((bf16[256,256]{1,0:T(8,128)(2,1)S(1)}, bf16[256,256]{1,0:T(8,128)(2,1)S(1)}, u32[]{:S(2)}, u32[]{:S(2)}) %collective-permute-start.17) | collective-permute-done | bytes 131104 | tf_op jit(solution)/shard_map/ppermute | solution.py:348
  95.0 1.6 %collective-permute-start.20 = (bf16[2048,256]{1,0:T(8,128)(2,1)S(1)}, bf16[2048,256]{1,0:T(8,128)(2,1)S(1)}, u32[]{:S(2)}, u32[]{:S(2)}) collective-permute-start(bf16[2048,256]{1,0:T(8,128)(2,1)S(1)} %add_convert_fusion.1), channel_id=1, source_target_pairs={{0,2},{1,3},{2,0},{3,1},{4,6},{5,7},{6,4},{7,5},{8,10},{9,11},{10,... | collective-permute-start | bytes 3145736 | tf_op jit(solution)/shard_map/ppermute | solution.py:348
  96.5 1.9 %adam.5 = (bf16[256,256]{1,0:T(8,128)(2,1)S(1)}, f32[256,1024]{1,0:T(8,128)}, f32[256,1024]{1,0:T(8,128)}, f32[8,128]{1,0:T(8,128)S(1)}) custom-call(s32[2]{0:T(128)S(1)} %get-tuple-element.309.refs_7_.columns_ref, s32[1]{0:T(128)} %bitcast.14.refs_2_.rank_ref, ...), custom_call_target="tpu_custom_call", output_to_operand_aliasing={{1}: (17, {}), {2}: (18, {})} | custom-call | flops 6000000000 | bytes 1024 | tf_op jit(solution)/shard_map/adam/pallas_call | solution.py:212
  98.4 4.2 %collective-permute-done.25.refs_8_.refs_1_ = bf16[256,512]{1,0:T(8,128)(2,1)S(1)} collective-permute-done((bf16[256,512]{1,0:T(8,128)(2,1)S(1)}, bf16[256,512]{1,0:T(8,128)(2,1)S(1)}, u32[]{:S(2)}, u32[]{:S(2)}) %collective-permute-start.25) | collective-permute-done | bytes 262176 | tf_op jit(solution)/shard_map/ppermute | solution.py:348
  102.6 4.2 %collective-permute-done.23.refs_10_.refs_1_ = bf16[256,256]{1,0:T(8,128)(2,1)S(1)} collective-permute-done((bf16[256,256]{1,0:T(8,128)(2,1)S(1)}, bf16[256,256]{1,0:T(8,128)(2,1)S(1)}, u32[]{:S(2)}, u32[]{:S(2)}) %collective-permute-start.23) | collective-permute-done | bytes 131104 | tf_op jit(solution)/shard_map/ppermute | solution.py:348
  106.8 2.0 %collective-permute-start.26 = (bf16[256,256]{1,0:T(8,128)(2,1)S(1)}, bf16[256,256]{1,0:T(8,128)(2,1)S(1)}, u32[]{:S(2)}, u32[]{:S(2)}) collective-permute-start(bf16[256,256]{1,0:T(8,128)(2,1)S(1)} %collective-permute-done.22.refs_11_.refs_2_), channel_id=1, source_target_pairs={{0,4},{4,0},{8,12},{12,8},{1,5},{5,1},{9,13},{13,9},{2,6},{6,2},{1... | collective-permute-start | bytes 393224 | tf_op jit(solution)/shard_map/ppermute | solution.py:348
  111.0 4.1 %collective-permute-done.20.refs_5_ = bf16[2048,256]{1,0:T(8,128)(2,1)S(1)} collective-permute-done((bf16[2048,256]{1,0:T(8,128)(2,1)S(1)}, bf16[2048,256]{1,0:T(8,128)(2,1)S(1)}, u32[]{:S(2)}, u32[]{:S(2)}) %collective-permute-start.20) | collective-permute-done | bytes 1048608 | tf_op jit(solution)/shard_map/ppermute | solution.py:348
  116.1 2.2 %place.4 = (bf16[1024,1024]{1,0:T(8,128)(2,1)}, f32[8,128]{1,0:T(8,128)}) custom-call(s32[4]{0:T(128)S(1)} %get-tuple-element.304.refs_0_.places_ref.rows_ref, s32[4]{0:T(128)S(1)} %copy-done.1, bf16[256,512]{1,0:T(8,128)(2,1)S(1)} %get-tuple-element.273.refs_0_, ...), custom_call_target="tpu_custom_call", output_to_operand_aliasing={{0}: (8, {})} | custom-call | flops 1000 | bytes 1024 | tf_op jit(solution)/shard_map/place/pallas_call | solution.py:265
  118.3 2.0 %place.5 = (bf16[1024,1024]{1,0:T(8,128)(2,1)}, f32[8,128]{1,0:T(8,128)}) custom-call(s32[4]{0:T(128)S(1)} %get-tuple-element.304.refs_0_.places_ref.rows_ref, s32[2]{0:T(128)S(1)} %get-tuple-element.309.refs_7_.columns_ref, bf16[256,256]{1,0:T(8,128)(2,1)S(1)} %get-tuple-element.271.refs_0_, ...), custom_call_target="tpu_custom_call", output_to_operand_aliasing={{0}: (6, {})} | custom-call | flops 80000000000 | bytes 1024 | tf_op jit(solution)/shard_map/place/pallas_call | solution.py:265
  (57 shorter events, 10.8 us)
Async XLA Ops:
  1.9 15.0 %collective-permute-start = (bf16[2048,128]{1,0:T(8,128)(2,1)S(1)}, bf16[2048,128]{1,0:T(8,128)(2,1)S(1)}, u32[]{:S(2)}, u32[]{:S(2)}) collective-permute-start(bf16[2048,128]{1,0:T(8,128)(2,1)S(1)} %get-tuple-element.303), channel_id=1, source_target_pairs={{16,0},{0,16},{17,1},{1,17},{18,2},{2,18},{19,3},{3,19},{20,4},{4,... | collective-permute-start | bytes 1572872 | tf_op jit(solution)/shard_map/ppermute | solution.py:34
  16.9 1.9 %collective-permute-start.1 = (bf16[2048,128]{1,0:T(8,128)(2,1)S(1)}, bf16[2048,128]{1,0:T(8,128)(2,1)S(1)}, u32[]{:S(2)}, u32[]{:S(2)}) collective-permute-start(bf16[2048,128]{1,0:T(8,128)(2,1)S(1)} %collective-permute-done.refs_0_.refs_4_), channel_id=1, source_target_pairs={{0,1},{1,0},{2,3},{3,2},{4,5},{5,4},{6,7},{7,6},{8,9},{9,8},{10,11... | collective-permute-start | bytes 1572872 | tf_op jit(solution)/shard_map/ppermute | solution.py:348
  16.9 14.3 %collective-permute-start.4 = (bf16[2048,128]{1,0:T(8,128)(2,1)S(1)}, bf16[2048,128]{1,0:T(8,128)(2,1)S(1)}, u32[]{:S(2)}, u32[]{:S(2)}) collective-permute-start(bf16[2048,128]{1,0:T(8,128)(2,1)S(1)} %get-tuple-element.302), channel_id=1, source_target_pairs={{16,0},{0,16},{17,1},{1,17},{18,2},{2,18},{19,3},{3,19},{20,4},{4,... | collective-permute-start | bytes 1572872 | tf_op jit(solution)/shard_map/ppermute | solution.py:34
  18.8 22.3 %copy-start.4 = (bf16[1,1024,1024]{2,1,0:T(8,128)(2,1)S(1)}, bf16[1,1024,1024]{2,1,0:T(8,128)(2,1)}, u32[]{:S(2)}) copy-start(bf16[1,1024,1024]{2,1,0:T(8,128)(2,1)} %param.8) | copy-start | bytes 6291460
  18.8 22.4 %copy-start.5 = (f32[1,256,1024]{2,1,0:T(8,128)S(1)}, f32[1,256,1024]{2,1,0:T(8,128)}, u32[]{:S(2)}) copy-start(f32[1,256,1024]{2,1,0:T(8,128)} %param.10) | copy-start | bytes 3145732
  18.8 22.4 %copy-start.6 = (f32[1,256,1024]{2,1,0:T(8,128)S(1)}, f32[1,256,1024]{2,1,0:T(8,128)}, u32[]{:S(2)}) copy-start(f32[1,256,1024]{2,1,0:T(8,128)} %param.11) | copy-start | bytes 3145732
  21.4 9.8 %collective-permute-start.3 = (bf16[512,256]{1,0:T(8,128)(2,1)S(1)}, bf16[512,256]{1,0:T(8,128)(2,1)S(1)}, u32[]{:S(2)}, u32[]{:S(2)}) collective-permute-start(bf16[512,256]{1,0:T(8,128)(2,1)S(1)} %get-tuple-element.163), channel_id=1, source_target_pairs={{0,4},{4,0},{8,12},{12,8},{1,5},{5,1},{9,13},{13,9},{2,6},{6,2},{1... | collective-permute-start | bytes 786440 | tf_op jit(solution)/shard_map/ppermute | solution.py:348
  23.3 17.8 %collective-permute-start.2 = (bf16[2048,128]{1,0:T(8,128)(2,1)S(1)}, bf16[2048,128]{1,0:T(8,128)(2,1)S(1)}, u32[]{:S(2)}, u32[]{:S(2)}) collective-permute-start(bf16[2048,128]{1,0:T(8,128)(2,1)S(1)} %collective-permute-done.refs_0_.refs_4_), channel_id=1, source_target_pairs={{0,2},{1,3},{2,0},{3,1},{4,6},{5,7},{6,4},{7,5},{8,10},{9,11},{10,... | collective-permute-start | bytes 1572872 | tf_op jit(solution)/shard_map/ppermute | solution.py:348
  31.2 9.9 %collective-permute-start.7 = (bf16[2048,128]{1,0:T(8,128)(2,1)S(1)}, bf16[2048,128]{1,0:T(8,128)(2,1)S(1)}, u32[]{:S(2)}, u32[]{:S(2)}) collective-permute-start(bf16[2048,128]{1,0:T(8,128)(2,1)S(1)} %collective-permute-done.4.refs_11_.refs_0_.refs_4_), channel_id=1, source_target_pairs={{0,1},{1,0},{2,3},{3,2},{4,5},{5,4},{6,7},{7,6},{8,9},{9,8},{10,11... | collective-permute-start | bytes 1572872 | tf_op jit(solution)/shard_map/ppermute | solution.py:348
  31.2 9.9 %collective-permute-start.5 = (bf16[256,256]{1,0:T(8,128)(2,1)S(1)}, bf16[256,256]{1,0:T(8,128)(2,1)S(1)}, u32[]{:S(2)}, u32[]{:S(2)}) collective-permute-start(bf16[256,256]{1,0:T(8,128)(2,1)S(1)} %add_convert_fusion.2), channel_id=1, source_target_pairs={{0,8},{4,12},{8,0},{12,4},{1,9},{5,13},{9,1},{13,5},{2,10},{6,14},... | collective-permute-start | bytes 393224 | tf_op jit(solution)/shard_map/ppermute | solution.py:348
  34.1 18.7 %collective-permute-start.8 = (bf16[2048,128]{1,0:T(8,128)(2,1)S(1)}, bf16[2048,128]{1,0:T(8,128)(2,1)S(1)}, u32[]{:S(2)}, u32[]{:S(2)}) collective-permute-start(bf16[2048,128]{1,0:T(8,128)(2,1)S(1)} %collective-permute-done.4.refs_11_.refs_0_.refs_4_), channel_id=1, source_target_pairs={{0,2},{1,3},{2,0},{3,1},{4,6},{5,7},{6,4},{7,5},{8,10},{9,11},{10,... | collective-permute-start | bytes 1572872 | tf_op jit(solution)/shard_map/ppermute | solution.py:348
  41.1 6.1 %collective-permute-start.6 = (bf16[2048,128]{1,0:T(8,128)(2,1)S(1)}, bf16[2048,128]{1,0:T(8,128)(2,1)S(1)}, u32[]{:S(2)}, u32[]{:S(2)}) collective-permute-start(bf16[2048,128]{1,0:T(8,128)(2,1)S(1)} %collective-permute-done.2.refs_14_.refs_2_), channel_id=1, source_target_pairs={{0,1},{1,0},{2,3},{3,2},{4,5},{5,4},{6,7},{7,6},{8,9},{9,8},{10,11... | collective-permute-start | bytes 1572872 | tf_op jit(solution)/shard_map/ppermute | solution.py:348
  43.0 9.7 %collective-permute-start.10 = (bf16[256,256]{1,0:T(8,128)(2,1)S(1)}, bf16[256,256]{1,0:T(8,128)(2,1)S(1)}, u32[]{:S(2)}, u32[]{:S(2)}) collective-permute-start(bf16[256,256]{1,0:T(8,128)(2,1)S(1)} %get-tuple-element.199.refs_0_), channel_id=1, source_target_pairs={{0,8},{4,12},{8,0},{12,4},{1,9},{5,13},{9,1},{13,5},{2,10},{6,14},... | collective-permute-start | bytes 393224 | tf_op jit(solution)/shard_map/ppermute | solution.py:348
  43.0 9.8 %collective-permute-start.9 = (bf16[256,256]{1,0:T(8,128)(2,1)S(1)}, bf16[256,256]{1,0:T(8,128)(2,1)S(1)}, u32[]{:S(2)}, u32[]{:S(2)}) collective-permute-start(bf16[256,256]{1,0:T(8,128)(2,1)S(1)} %get-tuple-element.199.refs_0_), channel_id=1, source_target_pairs={{0,4},{4,0},{8,12},{12,8},{1,5},{5,1},{9,13},{13,9},{2,6},{6,2},{1... | collective-permute-start | bytes 393224 | tf_op jit(solution)/shard_map/ppermute | solution.py:348
  52.8 4.4 %collective-permute-start.11 = (bf16[2048,128]{1,0:T(8,128)(2,1)S(1)}, bf16[2048,128]{1,0:T(8,128)(2,1)S(1)}, u32[]{:S(2)}, u32[]{:S(2)}) collective-permute-start(bf16[2048,128]{1,0:T(8,128)(2,1)S(1)} %collective-permute-done.8.refs_6_.refs_0_.refs_8_), channel_id=1, source_target_pairs={{0,1},{1,0},{2,3},{3,2},{4,5},{5,4},{6,7},{7,6},{8,9},{9,8},{10,11... | collective-permute-start | bytes 1572872 | tf_op jit(solution)/shard_map/ppermute | solution.py:348
  52.8 21.9 %collective-permute-start.16 = (bf16[256,512]{1,0:T(8,128)(2,1)S(1)}, bf16[256,512]{1,0:T(8,128)(2,1)S(1)}, u32[]{:S(2)}, u32[]{:S(2)}) collective-permute-start(bf16[256,512]{1,0:T(8,128)(2,1)S(1)} %get-tuple-element.222), channel_id=1, source_target_pairs={{0,12},{4,8},{8,4},{12,0},{1,13},{5,9},{9,5},{13,1},{2,14},{6,10},... | collective-permute-start | bytes 786440 | tf_op jit(solution)/shard_map/ppermute | solution.py:348
  55.3 25.7 %collective-permute-start.15 = (bf16[256,512]{1,0:T(8,128)(2,1)S(1)}, bf16[256,512]{1,0:T(8,128)(2,1)S(1)}, u32[]{:S(2)}, u32[]{:S(2)}) collective-permute-start(bf16[256,512]{1,0:T(8,128)(2,1)S(1)} %get-tuple-element.221), channel_id=1, source_target_pairs={{0,8},{4,12},{8,0},{12,4},{1,9},{5,13},{9,1},{13,5},{2,10},{6,14},... | collective-permute-start | bytes 786440 | tf_op jit(solution)/shard_map/ppermute | solution.py:348
  55.3 25.7 %collective-permute-start.14 = (bf16[256,512]{1,0:T(8,128)(2,1)S(1)}, bf16[256,512]{1,0:T(8,128)(2,1)S(1)}, u32[]{:S(2)}, u32[]{:S(2)}) collective-permute-start(bf16[256,512]{1,0:T(8,128)(2,1)S(1)} %get-tuple-element.219), channel_id=1, source_target_pairs={{0,4},{4,0},{8,12},{12,8},{1,5},{5,1},{9,13},{13,9},{2,6},{6,2},{1... | collective-permute-start | bytes 786440 | tf_op jit(solution)/shard_map/ppermute | solution.py:348
  69.0 15.4 %copy-start.1 = (s32[4]{0:T(128)S(1)}, s32[4]{0:T(128)}, u32[]{:S(2)}) copy-start(s32[4]{0:T(128)} %copy-done) | copy-start | bytes 52
  69.0 25.7 %collective-permute-start.13 = (bf16[2048,256]{1,0:T(8,128)(2,1)S(1)}, bf16[2048,256]{1,0:T(8,128)(2,1)S(1)}, u32[]{:S(2)}, u32[]{:S(2)}) collective-permute-start(bf16[2048,256]{1,0:T(8,128)(2,1)S(1)} %get-tuple-element.217), channel_id=1, source_target_pairs={{0,1},{1,0},{2,3},{3,2},{4,5},{5,4},{6,7},{7,6},{8,9},{9,8},{10,11... | collective-permute-start | bytes 3145736 | tf_op jit(solution)/shard_map/ppermute | solution.py:348
  72.3 14.9 %collective-permute-start.19 = (bf16[256,256]{1,0:T(8,128)(2,1)S(1)}, bf16[256,256]{1,0:T(8,128)(2,1)S(1)}, u32[]{:S(2)}, u32[]{:S(2)}) collective-permute-start(bf16[256,256]{1,0:T(8,128)(2,1)S(1)} %get-tuple-element.247), channel_id=1, source_target_pairs={{0,12},{4,8},{8,4},{12,0},{1,13},{5,9},{9,5},{13,1},{2,14},{6,10},... | collective-permute-start | bytes 393224 | tf_op jit(solution)/shard_map/ppermute | solution.py:348
  81.0 8.7 %collective-permute-start.18 = (bf16[256,256]{1,0:T(8,128)(2,1)S(1)}, bf16[256,256]{1,0:T(8,128)(2,1)S(1)}, u32[]{:S(2)}, u32[]{:S(2)}) collective-permute-start(bf16[256,256]{1,0:T(8,128)(2,1)S(1)} %get-tuple-element.246), channel_id=1, source_target_pairs={{0,8},{4,12},{8,0},{12,4},{1,9},{5,13},{9,1},{13,5},{2,10},{6,14},... | collective-permute-start | bytes 393224 | tf_op jit(solution)/shard_map/ppermute | solution.py:348
  81.0 13.6 %collective-permute-start.17 = (bf16[256,256]{1,0:T(8,128)(2,1)S(1)}, bf16[256,256]{1,0:T(8,128)(2,1)S(1)}, u32[]{:S(2)}, u32[]{:S(2)}) collective-permute-start(bf16[256,256]{1,0:T(8,128)(2,1)S(1)} %get-tuple-element.245), channel_id=1, source_target_pairs={{0,4},{4,0},{8,12},{12,8},{1,5},{5,1},{9,13},{13,9},{2,6},{6,2},{1... | collective-permute-start | bytes 393224 | tf_op jit(solution)/shard_map/ppermute | solution.py:348
  87.2 15.4 %collective-permute-start.25 = (bf16[256,512]{1,0:T(8,128)(2,1)S(1)}, bf16[256,512]{1,0:T(8,128)(2,1)S(1)}, u32[]{:S(2)}, u32[]{:S(2)}) collective-permute-start(bf16[256,512]{1,0:T(8,128)(2,1)S(1)} %get-tuple-element.273.refs_0_), channel_id=1, source_target_pairs={{0,4},{4,0},{8,12},{12,8},{1,5},{5,1},{9,13},{13,9},{2,6},{6,2},{1... | collective-permute-start | bytes 786440 | tf_op jit(solution)/shard_map/ppermute | solution.py:348
  87.2 15.4 %collective-permute-start.24 = (bf16[256,512]{1,0:T(8,128)(2,1)S(1)}, bf16[256,512]{1,0:T(8,128)(2,1)S(1)}, u32[]{:S(2)}, u32[]{:S(2)}) collective-permute-start(bf16[256,512]{1,0:T(8,128)(2,1)S(1)} %get-tuple-element.273.refs_0_), channel_id=1, source_target_pairs={{0,8},{4,12},{8,0},{12,4},{1,9},{5,13},{9,1},{13,5},{2,10},{6,14},... | collective-permute-start | bytes 786440 | tf_op jit(solution)/shard_map/ppermute | solution.py:348
  95.0 20.1 %collective-permute-start.20 = (bf16[2048,256]{1,0:T(8,128)(2,1)S(1)}, bf16[2048,256]{1,0:T(8,128)(2,1)S(1)}, u32[]{:S(2)}, u32[]{:S(2)}) collective-permute-start(bf16[2048,256]{1,0:T(8,128)(2,1)S(1)} %add_convert_fusion.1), channel_id=1, source_target_pairs={{0,2},{1,3},{2,0},{3,1},{4,6},{5,7},{6,4},{7,5},{8,10},{9,11},{10,... | collective-permute-start | bytes 3145736 | tf_op jit(solution)/shard_map/ppermute | solution.py:348
  98.4 8.4 %collective-permute-start.23 = (bf16[256,256]{1,0:T(8,128)(2,1)S(1)}, bf16[256,256]{1,0:T(8,128)(2,1)S(1)}, u32[]{:S(2)}, u32[]{:S(2)}) collective-permute-start(bf16[256,256]{1,0:T(8,128)(2,1)S(1)} %get-tuple-element.271.refs_0_), channel_id=1, source_target_pairs={{0,4},{4,0},{8,12},{12,8},{1,5},{5,1},{9,13},{13,9},{2,6},{6,2},{1... | collective-permute-start | bytes 393224 | tf_op jit(solution)/shard_map/ppermute | solution.py:348
  98.4 8.4 %collective-permute-start.22 = (bf16[256,256]{1,0:T(8,128)(2,1)S(1)}, bf16[256,256]{1,0:T(8,128)(2,1)S(1)}, u32[]{:S(2)}, u32[]{:S(2)}) collective-permute-start(bf16[256,256]{1,0:T(8,128)(2,1)S(1)} %get-tuple-element.271.refs_0_), channel_id=1, source_target_pairs={{0,8},{4,12},{8,0},{12,4},{1,9},{5,13},{9,1},{13,5},{2,10},{6,14},... | collective-permute-start | bytes 393224 | tf_op jit(solution)/shard_map/ppermute | solution.py:348
  102.6 7.0 %collective-permute-start.21 = (bf16[256,256]{1,0:T(8,128)(2,1)S(1)}, bf16[256,256]{1,0:T(8,128)(2,1)S(1)}, u32[]{:S(2)}, u32[]{:S(2)}) collective-permute-start(bf16[256,256]{1,0:T(8,128)(2,1)S(1)} %collective-permute-done.10.refs_6_.refs_2_), channel_id=1, source_target_pairs={{0,4},{4,0},{8,12},{12,8},{1,5},{5,1},{9,13},{13,9},{2,6},{6,2},{1... | collective-permute-start | bytes 393224 | tf_op jit(solution)/shard_map/ppermute | solution.py:348
  102.6 17.7 %collective-permute-start.12 = (bf16[2048,256]{1,0:T(8,128)(2,1)S(1)}, bf16[2048,256]{1,0:T(8,128)(2,1)S(1)}, u32[]{:S(2)}, u32[]{:S(2)}) collective-permute-start(bf16[2048,256]{1,0:T(8,128)(2,1)S(1)} %get-tuple-element.215), channel_id=1, source_target_pairs={{0,1},{1,0},{2,3},{3,2},{4,5},{5,4},{6,7},{7,6},{8,9},{9,8},{10,11... | collective-permute-start | bytes 3145736 | tf_op jit(solution)/shard_map/ppermute | solution.py:348
  106.8 9.2 %collective-permute-start.27 = (bf16[256,512]{1,0:T(8,128)(2,1)S(1)}, bf16[256,512]{1,0:T(8,128)(2,1)S(1)}, u32[]{:S(2)}, u32[]{:S(2)}) collective-permute-start(bf16[256,512]{1,0:T(8,128)(2,1)S(1)} %collective-permute-done.24.refs_9_.refs_2_), channel_id=1, source_target_pairs={{0,4},{4,0},{8,12},{12,8},{1,5},{5,1},{9,13},{13,9},{2,6},{6,2},{1... | collective-permute-start | bytes 786440 | tf_op jit(solution)/shard_map/ppermute | solution.py:348
  106.8 11.5 %collective-permute-start.26 = (bf16[256,256]{1,0:T(8,128)(2,1)S(1)}, bf16[256,256]{1,0:T(8,128)(2,1)S(1)}, u32[]{:S(2)}, u32[]{:S(2)}) collective-permute-start(bf16[256,256]{1,0:T(8,128)(2,1)S(1)} %collective-permute-done.22.refs_11_.refs_2_), channel_id=1, source_target_pairs={{0,4},{4,0},{8,12},{12,8},{1,5},{5,1},{9,13},{13,9},{2,6},{6,2},{1... | collective-permute-start | bytes 393224 | tf_op jit(solution)/shard_map/ppermute | solution.py:348
  (3 other events, 19.6 us)

commit v4 on v3

--- a/solution.py
+++ b/solution.py
@@ -12,19 +12,19 @@
 COL_PARTS = 2
 TILE = 256
 CHUNKS = (((0, 0), (1, 0)), ((0, 1), (1, 1), (2, 0), (3, 0)), ((2, 1), (3, 1)))
-SUMS = ("two", "one", "one",)
+SUMS = ("two", "tri", "two",)
 GATHERS = ("two", "two", "two",)
 PLAN = (
     "h0", "b00", "b10", "t0", "b01", "m0", "r0", "b20", "b11", "a0", "b30", "t1", "g0",
-    "e0", "b21", "b31", "t2", "p0", "r1", "a1", "r2", "x0", "a2", "e1", "g1", "e2", "g2",
-    "l0", "x1", "l1", "l2",
+    "e0", "b21", "b31", "t2", "m1", "r1", "a1", "p0", "m2", "r2", "x0", "a2", "u0", "e1",
+    "g1", "e2", "g2", "l0", "x1", "l1", "l2",
 )
 ANYWHERE = pl.BlockSpec(memory_space=pl.ANY)
 TOKEN = jax.ShapeDtypeStruct((8, 128), F32)
 COSTS = {
-    "h0": 15000000000, "t0": 10000000000, "a0": 80000000000, "t1": 40000000000,
-    "t2": 6000000000, "p0": 35100000000, "a1": 6000000000, "a2": 6000000000, "l0": 4199999999,
-    "l1": 1000, "l2": 80000000000,
+    "h0": 40000000000, "t0": 10000000000, "a0": 6000000000, "t1": 40000000000,
+    "t2": 6000000000, "a1": 10000000000, "p0": 35100000000, "a2": 6000000000,
+    "l0": 4199999999, "l1": 1000, "l2": 80000000000,
 }
 
 

time: 122 us -> 119 us (0.975)
  starting transfers between devices: 32.1 us -> 30.4 us
    ppermute x26 -> x25, starting transfers between devices: 27.3 us -> 25.6 us  [swapped(): return lax.ppermute(value, axis, [(i, i ^ distance) for i in range(4)])]
    ppermute x26 -> x25, waiting for transfers between devices: 33.6 us -> 32.5 us  [swapped(): return lax.ppermute(value, axis, [(i, i ^ distance) for i in range(4)])]
  transfers between devices with their start and end apart: 28 -> 27, of which waited for: 14 -> 13; matrix products, arithmetic and copies ran while one was open for 1% -> 2% of each run, Pallas kernels for 32% -> 31%
where the time goes in v4:
time: 119 us; the launch traced here: 118 us
  waiting for transfers between devices  43.2 us (36%)
  Pallas kernels  38.3 us (32%)
  starting transfers between devices  30.4 us (26%)
  local copies, waits for them, and re-layouts  3.57 us (3%)
  other arithmetic  2.06 us (2%)
    ppermute x25, waiting for transfers between devices, swapped(): return lax.ppermute(value, axis, [(i, i ^ distance) for i in range(4)])  32.5 us
    ppermute x25, starting transfers between devices, swapped(): return lax.ppermute(value, axis, [(i, i ^ distance) for i in range(4)])  25.6 us
    pallas_call x1, Pallas kernels, partials(): pl.pallas_call(kernel, grid_spec=pltpu.PrefetchScalarGridSpec(num_scalar_...  11.7 us
    ppermute x2, waiting for transfers between devices, from_behind(): return lax.ppermute(block, axis, route)  10.7 us
    pallas_call x3, Pallas kernels, terms(): pl.pallas_call(kernel, grid_spec=pltpu.PrefetchScalarGridSpec(num_scalar_...  9.42 us
    pallas_call x3, Pallas kernels, adam_chunk(): pl.pallas_call(kernel, grid_spec=pltpu.PrefetchScalarGridSpec(num_scalar_...  6.49 us
    pallas_call x3, Pallas kernels, place_rows(): pl.pallas_call(kernel, grid_spec=pltpu.PrefetchScalarGridSpec(num_scalar_...  5.6 us
    pallas_call x1, Pallas kernels, prepare(): pl.pallas_call(kernel, grid=(tokens // TILE,), in_specs=[pl.BlockSpec((TI...  5.02 us
  transfers between devices with their start and end apart: 27, of which 13 were waited for; matrix products, arithmetic and copies ran while one was open for 2% of the time, Pallas kernels for 31%

profile of v4, /device:TPU:0, one launch (start us, length us, event | category | flops | bytes accessed | tf_op | source)
XLA Modules:
  0.0 118.4 jit_solution(5196983433072522597)
XLA Ops:
  1.9 3.0 %collective-permute-start = (bf16[2048,128]{1,0:T(8,128)(2,1)S(1)}, bf16[2048,128]{1,0:T(8,128)(2,1)S(1)}, u32[]{:S(2)}, u32[]{:S(2)}) collective-permute-start(bf16[2048,128]{1,0:T(8,128)(2,1)S(1)} %get-tuple-element.305), channel_id=1, source_target_pairs={{16,0},{0,16},{17,1},{1,17},{18,2},{2,18},{19,3},{3,19},{20,4},{4,... | collective-permute-start | bytes 1572872 | tf_op jit(solution)/shard_map/ppermute | solution.py:34
  5.3 2.2 %copy-done = bf16[1,2048,1024]{2,1,0:T(8,128)(2,1)S(1)} copy-done((bf16[1,2048,1024]{2,1,0:T(8,128)(2,1)S(1)}, bf16[1,2048,1024]{2,1,0:T(8,128)(2,1)}, u32[]{:S(2)}) %copy-start) | copy-done | bytes 4194328
  7.4 5.0 %prepare.1 = (bf16[1024,2048]{1,0:T(8,128)(2,1)S(1)}, bf16[2048,1024]{1,0:T(8,128)(2,1)S(1)}, f32[8,128]{1,0:T(8,128)S(1)}) custom-call(bf16[2048,1024]{1,0:T(8,128)(2,1)S(1)} %bitcast.27, s32[4]{0:T(128)S(1)} %get-tuple-element.306.refs_0_.places_ref.rows_ref, s32[4]{0:T(128)S(1)} %get-tuple-element.307.refs_1_.places_ref, s32[1]{0:T(128)} %bitcast.14.refs_2_.rank_ref, ...), custom_call_target="tpu_custom_call" | custom-call | flops 40000000000 | bytes 1024 | tf_op jit(solution)/shard_map/prepare/pallas_call | solution.py:122
  12.5 4.4 %collective-permute-done.refs_0_.refs_4_ = bf16[2048,128]{1,0:T(8,128)(2,1)S(1)} collective-permute-done((bf16[2048,128]{1,0:T(8,128)(2,1)S(1)}, bf16[2048,128]{1,0:T(8,128)(2,1)S(1)}, u32[]{:S(2)}, u32[]{:S(2)}) %collective-permute-start) | collective-permute-done | bytes 524320 | tf_op jit(solution)/shard_map/ppermute | solution.py:34
  16.9 1.7 %collective-permute-start.4 = (bf16[2048,128]{1,0:T(8,128)(2,1)S(1)}, bf16[2048,128]{1,0:T(8,128)(2,1)S(1)}, u32[]{:S(2)}, u32[]{:S(2)}) collective-permute-start(bf16[2048,128]{1,0:T(8,128)(2,1)S(1)} %get-tuple-element.304), channel_id=1, source_target_pairs={{16,0},{0,16},{17,1},{1,17},{18,2},{2,18},{19,3},{3,19},{20,4},{4,... | collective-permute-start | bytes 1572872 | tf_op jit(solution)/shard_map/ppermute | solution.py:34
  18.8 2.7 %terms.3 = (bf16[256,256]{1,0:T(8,128)(2,1)S(1)}, bf16[256,256]{1,0:T(8,128)(2,1)S(1)}, bf16[512,256]{1,0:T(8,128)(2,1)S(1)}, f32[8,128]{1,0:T(8,128)S(1)}) custom-call(s32[4]{0:T(128)S(1)} %get-tuple-element.307.refs_1_.places_ref, bf16[1024,2048]{1,0:T(8,128)(2,1)S(1)} %get-tuple-element.158.hidden_ref, ...), custom_call_target="tpu_custom_call" | custom-call | flops 10000000000 | bytes 1024 | tf_op jit(solution)/shard_map/terms/pallas_call | solution.py:170
  21.5 1.9 %collective-permute-start.3 = (bf16[512,256]{1,0:T(8,128)(2,1)S(1)}, bf16[512,256]{1,0:T(8,128)(2,1)S(1)}, u32[]{:S(2)}, u32[]{:S(2)}) collective-permute-start(bf16[512,256]{1,0:T(8,128)(2,1)S(1)} %get-tuple-element.164), channel_id=1, source_target_pairs={{0,4},{4,0},{8,12},{12,8},{1,5},{5,1},{9,13},{13,9},{2,6},{6,2},{1... | collective-permute-start | bytes 786440 | tf_op jit(solution)/shard_map/ppermute | solution.py:348
  23.4 1.5 %collective-permute-start.2 = (bf16[2048,128]{1,0:T(8,128)(2,1)S(1)}, bf16[2048,128]{1,0:T(8,128)(2,1)S(1)}, u32[]{:S(2)}, u32[]{:S(2)}) collective-permute-start(bf16[2048,128]{1,0:T(8,128)(2,1)S(1)} %collective-permute-done.refs_0_.refs_4_), channel_id=1, source_target_pairs={{0,2},{1,3},{2,0},{3,1},{4,6},{5,7},{6,4},{7,5},{8,10},{9,11},{10,... | collective-permute-start | bytes 1572872 | tf_op jit(solution)/shard_map/ppermute | solution.py:348
  24.9 6.3 %collective-permute-done.4.refs_11_.refs_0_.refs_4_ = bf16[2048,128]{1,0:T(8,128)(2,1)S(1)} collective-permute-done((bf16[2048,128]{1,0:T(8,128)(2,1)S(1)}, bf16[2048,128]{1,0:T(8,128)(2,1)S(1)}, u32[]{:S(2)}, u32[]{:S(2)}) %collective-permute-start.4) | collective-permute-done | bytes 524320 | tf_op jit(solution)/shard_map/ppermute | solution.py:34
  31.2 2.9 %collective-permute-start.5 = (bf16[256,256]{1,0:T(8,128)(2,1)S(1)}, bf16[256,256]{1,0:T(8,128)(2,1)S(1)}, u32[]{:S(2)}, u32[]{:S(2)}) collective-permute-start(bf16[256,256]{1,0:T(8,128)(2,1)S(1)} %add_convert_fusion.4), channel_id=1, source_target_pairs={{0,8},{4,12},{8,0},{12,4},{1,9},{5,13},{9,1},{13,5},{2,10},{6,14},... | collective-permute-start | bytes 393224 | tf_op jit(solution)/shard_map/ppermute | solution.py:348
  35.6 5.5 %collective-permute-done.5.refs_1_.refs_13_ = bf16[256,256]{1,0:T(8,128)(2,1)S(1)} collective-permute-done((bf16[256,256]{1,0:T(8,128)(2,1)S(1)}, bf16[256,256]{1,0:T(8,128)(2,1)S(1)}, u32[]{:S(2)}, u32[]{:S(2)}) %collective-permute-start.5) | collective-permute-done | bytes 131104 | tf_op jit(solution)/shard_map/ppermute | solution.py:348
  41.1 1.9 %adam.3 = (bf16[256,256]{1,0:T(8,128)(2,1)S(1)}, f32[256,1024]{1,0:T(8,128)}, f32[256,1024]{1,0:T(8,128)}, f32[8,128]{1,0:T(8,128)S(1)}) custom-call(s32[2]{0:T(128)S(1)} %get-tuple-element.310.refs_5_.columns_ref, s32[1]{0:T(128)} %bitcast.14.refs_2_.rank_ref, bf16[256,256]{1,0:T(8,128)(2,1)S(1)} %get-tuple-element.178.refs_0_, ...), custom_call_target="tpu_custom_call" | custom-call | flops 6000000000 | bytes 1024 | tf_op jit(solution)/shard_map/adam/pallas_call | solution.py:212
  43.0 4.2 %collective-permute-start.9 = (bf16[256,256]{1,0:T(8,128)(2,1)S(1)}, bf16[256,256]{1,0:T(8,128)(2,1)S(1)}, u32[]{:S(2)}, u32[]{:S(2)}) collective-permute-start(bf16[256,256]{1,0:T(8,128)(2,1)S(1)} %get-tuple-element.200.refs_0_), channel_id=1, source_target_pairs={{0,4},{4,0},{8,12},{12,8},{1,5},{5,1},{9,13},{13,9},{2,6},{6,2},{1... | collective-permute-start | bytes 393224 | tf_op jit(solution)/shard_map/ppermute | solution.py:348
  47.2 4.0 %terms.4 = (bf16[256,512]{1,0:T(8,128)(2,1)S(1)}, bf16[256,512]{1,0:T(8,128)(2,1)S(1)}, bf16[256,512]{1,0:T(8,128)(2,1)S(1)}, bf16[256,512]{1,0:T(8,128)(2,1)S(1)}, f32[8,128]{1,0:T(8,128)S(1)}) custom-call(s32[4]{0:T(128)S(1)} %get-tuple-element.306.refs_0_.places_ref.rows_ref, bf16[1024,2048]{1,0:T(8,128)(2,1)S(1)} %get-tuple-element.158.hidden_ref, ...), custom_call_target="tpu_custom_call" | custom-call | flops 40000000000 | bytes 1024 | tf_op jit(solution)/shard_map/terms/pallas_call | solution.py:170
  51.1 1.6 %collective-permute-done.10.refs_6_.refs_2_ = bf16[256,256]{1,0:T(8,128)(2,1)S(1)} collective-permute-done((bf16[256,256]{1,0:T(8,128)(2,1)S(1)}, bf16[256,256]{1,0:T(8,128)(2,1)S(1)}, u32[]{:S(2)}, u32[]{:S(2)}) %collective-permute-start.10) | collective-permute-done | bytes 131104 | tf_op jit(solution)/shard_map/ppermute | solution.py:348
  52.8 2.0 %collective-permute-start.16 = (bf16[256,512]{1,0:T(8,128)(2,1)S(1)}, bf16[256,512]{1,0:T(8,128)(2,1)S(1)}, u32[]{:S(2)}, u32[]{:S(2)}) collective-permute-start(bf16[256,512]{1,0:T(8,128)(2,1)S(1)} %get-tuple-element.242), channel_id=1, source_target_pairs={{0,4},{4,0},{8,12},{12,8},{1,5},{5,1},{9,13},{13,9},{2,6},{6,2},{1... | collective-permute-start | bytes 786440 | tf_op jit(solution)/shard_map/ppermute | solution.py:348
  54.9 2.7 %terms.5 = (bf16[256,256]{1,0:T(8,128)(2,1)S(1)}, bf16[256,256]{1,0:T(8,128)(2,1)S(1)}, bf16[512,256]{1,0:T(8,128)(2,1)S(1)}, f32[8,128]{1,0:T(8,128)S(1)}) custom-call(s32[4]{0:T(128)S(1)} %get-tuple-element.307.refs_1_.places_ref, bf16[1024,2048]{1,0:T(8,128)(2,1)S(1)} %get-tuple-element.158.hidden_ref, ...), custom_call_target="tpu_custom_call" | custom-call | flops 6000000000 | bytes 1024 | tf_op jit(solution)/shard_map/terms/pallas_call | solution.py:170
  57.6 4.3 %collective-permute-done.17.refs_9_ = bf16[256,512]{1,0:T(8,128)(2,1)S(1)} collective-permute-done((bf16[256,512]{1,0:T(8,128)(2,1)S(1)}, bf16[256,512]{1,0:T(8,128)(2,1)S(1)}, u32[]{:S(2)}, u32[]{:S(2)}) %collective-permute-start.17) | collective-permute-done | bytes 262176 | tf_op jit(solution)/shard_map/ppermute | solution.py:348
  63.4 1.7 %collective-permute-start.13 = (bf16[512,256]{1,0:T(8,128)(2,1)S(1)}, bf16[512,256]{1,0:T(8,128)(2,1)S(1)}, u32[]{:S(2)}, u32[]{:S(2)}) collective-permute-start(bf16[512,256]{1,0:T(8,128)(2,1)S(1)} %get-tuple-element.226), channel_id=1, source_target_pairs={{0,4},{4,0},{8,12},{12,8},{1,5},{5,1},{9,13},{13,9},{2,6},{6,2},{1... | collective-permute-start | bytes 786440 | tf_op jit(solution)/shard_map/ppermute | solution.py:348
  65.1 11.7 %partials.1 = (bf16[2048,256]{1,0:T(8,128)(2,1)S(1)}, bf16[2048,256]{1,0:T(8,128)(2,1)S(1)}, bf16[2048,256]{1,0:T(8,128)(2,1)S(1)}, bf16[2048,256]{1,0:T(8,128)(2,1)S(1)}, f32[8,128]{1,0:T(8,128)S(1)}) custom-call(s32[8]{0:T(128)S(1)} %stack.89.refs_4_.where_ref, s32[4]{0:T(128)S(1)} %get-tuple-element.308.refs_3_.order_ref, ...), custom_call_target="tpu_custom_call" | custom-call | flops 35100000256 | bytes 1024 | tf_op jit(solution)/shard_map/partials/pallas_call | solution.py:309
  79.8 2.8 %adam.4 = (bf16[256,512]{1,0:T(8,128)(2,1)S(1)}, f32[256,1024]{1,0:T(8,128)}, f32[256,1024]{1,0:T(8,128)}, f32[8,128]{1,0:T(8,128)}) custom-call(s32[4]{0:T(128)S(1)} %get-tuple-element.309.refs_6_.columns_ref, s32[1]{0:T(128)} %bitcast.14.refs_2_.rank_ref, ...), custom_call_target="tpu_custom_call", output_to_operand_aliasing={{1}: (14, {}), {2}: (15, {})} | custom-call | flops 10000000000 | bytes 1024 | tf_op jit(solution)/shard_map/adam/pallas_call | solution.py:212
  82.6 1.7 %collective-permute-start.24 = (bf16[256,512]{1,0:T(8,128)(2,1)S(1)}, bf16[256,512]{1,0:T(8,128)(2,1)S(1)}, u32[]{:S(2)}, u32[]{:S(2)}) collective-permute-start(bf16[256,512]{1,0:T(8,128)(2,1)S(1)} %get-tuple-element.266.refs_0_), channel_id=1, source_target_pairs={{0,4},{4,0},{8,12},{12,8},{1,5},{5,1},{9,13},{13,9},{2,6},{6,2},{1... | collective-permute-start | bytes 786440 | tf_op jit(solution)/shard_map/ppermute | solution.py:348
  84.5 2.9 %collective-permute-done.14.refs_1_.refs_10_ = bf16[256,256]{1,0:T(8,128)(2,1)S(1)} collective-permute-done((bf16[256,256]{1,0:T(8,128)(2,1)S(1)}, bf16[256,256]{1,0:T(8,128)(2,1)S(1)}, u32[]{:S(2)}, u32[]{:S(2)}) %collective-permute-start.14) | collective-permute-done | bytes 131104 | tf_op jit(solution)/shard_map/ppermute | solution.py:348
  87.8 1.6 %collective-permute-start.19 = (bf16[2048,256]{1,0:T(8,128)(2,1)S(1)}, bf16[2048,256]{1,0:T(8,128)(2,1)S(1)}, u32[]{:S(2)}, u32[]{:S(2)}) collective-permute-start(bf16[2048,256]{1,0:T(8,128)(2,1)S(1)} %add_convert_fusion.1), channel_id=1, source_target_pairs={{0,2},{1,3},{2,0},{3,1},{4,6},{5,7},{6,4},{7,5},{8,10},{9,11},{10,... | collective-permute-start | bytes 3145736 | tf_op jit(solution)/shard_map/ppermute | solution.py:348
  89.4 1.8 %adam.5 = (bf16[256,256]{1,0:T(8,128)(2,1)S(1)}, f32[256,1024]{1,0:T(8,128)}, f32[256,1024]{1,0:T(8,128)}, f32[8,128]{1,0:T(8,128)S(1)}) custom-call(s32[2]{0:T(128)S(1)} %get-tuple-element.311.refs_7_.columns_ref, s32[1]{0:T(128)} %bitcast.14.refs_2_.rank_ref, ...), custom_call_target="tpu_custom_call", output_to_operand_aliasing={{1}: (14, {}), {2}: (15, {})} | custom-call | flops 6000000000 | bytes 1024 | tf_op jit(solution)/shard_map/adam/pallas_call | solution.py:212
  91.2 7.2 %collective-permute-done.24.refs_10_.refs_1_ = bf16[256,512]{1,0:T(8,128)(2,1)S(1)} collective-permute-done((bf16[256,512]{1,0:T(8,128)(2,1)S(1)}, bf16[256,512]{1,0:T(8,128)(2,1)S(1)}, u32[]{:S(2)}, u32[]{:S(2)}) %collective-permute-start.24) | collective-permute-done | bytes 262176 | tf_op jit(solution)/shard_map/ppermute | solution.py:348
  98.8 2.7 %collective-permute-start.20 = (bf16[256,256]{1,0:T(8,128)(2,1)S(1)}, bf16[256,256]{1,0:T(8,128)(2,1)S(1)}, u32[]{:S(2)}, u32[]{:S(2)}) collective-permute-start(bf16[256,256]{1,0:T(8,128)(2,1)S(1)} %collective-permute-done.10.refs_6_.refs_2_), channel_id=1, source_target_pairs={{0,4},{4,0},{8,12},{12,8},{1,5},{5,1},{9,13},{13,9},{2,6},{6,2},{1... | collective-permute-start | bytes 393224 | tf_op jit(solution)/shard_map/ppermute | solution.py:348
  101.6 4.5 %collective-permute-done.21.refs_13_.refs_2_ = bf16[256,256]{1,0:T(8,128)(2,1)S(1)} collective-permute-done((bf16[256,256]{1,0:T(8,128)(2,1)S(1)}, bf16[256,256]{1,0:T(8,128)(2,1)S(1)}, u32[]{:S(2)}, u32[]{:S(2)}) %collective-permute-start.21) | collective-permute-done | bytes 131104 | tf_op jit(solution)/shard_map/ppermute | solution.py:348
  106.1 1.9 %collective-permute-done.20.refs_3_ = bf16[256,256]{1,0:T(8,128)(2,1)S(1)} collective-permute-done((bf16[256,256]{1,0:T(8,128)(2,1)S(1)}, bf16[256,256]{1,0:T(8,128)(2,1)S(1)}, u32[]{:S(2)}, u32[]{:S(2)}) %collective-permute-start.20) | collective-permute-done | bytes 131104 | tf_op jit(solution)/shard_map/ppermute | solution.py:348
  109.3 3.4 %collective-permute-done.19.refs_5_ = bf16[2048,256]{1,0:T(8,128)(2,1)S(1)} collective-permute-done((bf16[2048,256]{1,0:T(8,128)(2,1)S(1)}, bf16[2048,256]{1,0:T(8,128)(2,1)S(1)}, u32[]{:S(2)}, u32[]{:S(2)}) %collective-permute-start.19) | collective-permute-done | bytes 1048608 | tf_op jit(solution)/shard_map/ppermute | solution.py:348
  114.1 2.2 %place.4 = (bf16[1024,1024]{1,0:T(8,128)(2,1)}, f32[8,128]{1,0:T(8,128)}) custom-call(s32[4]{0:T(128)S(1)} %get-tuple-element.306.refs_0_.places_ref.rows_ref, s32[4]{0:T(128)S(1)} %get-tuple-element.309.refs_6_.columns_ref, bf16[256,512]{1,0:T(8,128)(2,1)S(1)} %get-tuple-element.266.refs_0_, ...), custom_call_target="tpu_custom_call", output_to_operand_aliasing={{0}: (8, {})} | custom-call | flops 1000 | bytes 1024 | tf_op jit(solution)/shard_map/place/pallas_call | solution.py:265
  116.4 2.0 %place.5 = (bf16[1024,1024]{1,0:T(8,128)(2,1)}, f32[8,128]{1,0:T(8,128)}) custom-call(s32[4]{0:T(128)S(1)} %get-tuple-element.306.refs_0_.places_ref.rows_ref, s32[2]{0:T(128)S(1)} %get-tuple-element.311.refs_7_.columns_ref, bf16[256,256]{1,0:T(8,128)(2,1)S(1)} %get-tuple-element.265.refs_0_, ...), custom_call_target="tpu_custom_call", output_to_operand_aliasing={{0}: (6, {})} | custom-call | flops 80000000000 | bytes 1024 | tf_op jit(solution)/shard_map/place/pallas_call | solution.py:265
  (53 shorter events, 11.7 us)
Async XLA Ops:
  1.9 15.0 %collective-permute-start = (bf16[2048,128]{1,0:T(8,128)(2,1)S(1)}, bf16[2048,128]{1,0:T(8,128)(2,1)S(1)}, u32[]{:S(2)}, u32[]{:S(2)}) collective-permute-start(bf16[2048,128]{1,0:T(8,128)(2,1)S(1)} %get-tuple-element.305), channel_id=1, source_target_pairs={{16,0},{0,16},{17,1},{1,17},{18,2},{2,18},{19,3},{3,19},{20,4},{4,... | collective-permute-start | bytes 1572872 | tf_op jit(solution)/shard_map/ppermute | solution.py:34
  5.3 2.2 %copy-start = (bf16[1,2048,1024]{2,1,0:T(8,128)(2,1)S(1)}, bf16[1,2048,1024]{2,1,0:T(8,128)(2,1)}, u32[]{:S(2)}) copy-start(bf16[1,2048,1024]{2,1,0:T(8,128)(2,1)} %param.7) | copy-start | bytes 12582916
  16.9 1.9 %collective-permute-start.1 = (bf16[2048,128]{1,0:T(8,128)(2,1)S(1)}, bf16[2048,128]{1,0:T(8,128)(2,1)S(1)}, u32[]{:S(2)}, u32[]{:S(2)}) collective-permute-start(bf16[2048,128]{1,0:T(8,128)(2,1)S(1)} %collective-permute-done.refs_0_.refs_4_), channel_id=1, source_target_pairs={{0,1},{1,0},{2,3},{3,2},{4,5},{5,4},{6,7},{7,6},{8,9},{9,8},{10,11... | collective-permute-start | bytes 1572872 | tf_op jit(solution)/shard_map/ppermute | solution.py:348
  16.9 14.3 %collective-permute-start.4 = (bf16[2048,128]{1,0:T(8,128)(2,1)S(1)}, bf16[2048,128]{1,0:T(8,128)(2,1)S(1)}, u32[]{:S(2)}, u32[]{:S(2)}) collective-permute-start(bf16[2048,128]{1,0:T(8,128)(2,1)S(1)} %get-tuple-element.304), channel_id=1, source_target_pairs={{16,0},{0,16},{17,1},{1,17},{18,2},{2,18},{19,3},{3,19},{20,4},{4,... | collective-permute-start | bytes 1572872 | tf_op jit(solution)/shard_map/ppermute | solution.py:34
  18.8 22.3 %copy-start.2 = (bf16[1,1024,1024]{2,1,0:T(8,128)(2,1)S(1)}, bf16[1,1024,1024]{2,1,0:T(8,128)(2,1)}, u32[]{:S(2)}) copy-start(bf16[1,1024,1024]{2,1,0:T(8,128)(2,1)} %param.8) | copy-start | bytes 6291460
  18.8 22.4 %copy-start.3 = (f32[1,256,1024]{2,1,0:T(8,128)S(1)}, f32[1,256,1024]{2,1,0:T(8,128)}, u32[]{:S(2)}) copy-start(f32[1,256,1024]{2,1,0:T(8,128)} %param.10) | copy-start | bytes 3145732
  18.8 22.4 %copy-start.4 = (f32[1,256,1024]{2,1,0:T(8,128)S(1)}, f32[1,256,1024]{2,1,0:T(8,128)}, u32[]{:S(2)}) copy-start(f32[1,256,1024]{2,1,0:T(8,128)} %param.11) | copy-start | bytes 3145732
  21.5 9.7 %collective-permute-start.3 = (bf16[512,256]{1,0:T(8,128)(2,1)S(1)}, bf16[512,256]{1,0:T(8,128)(2,1)S(1)}, u32[]{:S(2)}, u32[]{:S(2)}) collective-permute-start(bf16[512,256]{1,0:T(8,128)(2,1)S(1)} %get-tuple-element.164), channel_id=1, source_target_pairs={{0,4},{4,0},{8,12},{12,8},{1,5},{5,1},{9,13},{13,9},{2,6},{6,2},{1... | collective-permute-start | bytes 786440 | tf_op jit(solution)/shard_map/ppermute | solution.py:348
  23.4 17.7 %collective-permute-start.2 = (bf16[2048,128]{1,0:T(8,128)(2,1)S(1)}, bf16[2048,128]{1,0:T(8,128)(2,1)S(1)}, u32[]{:S(2)}, u32[]{:S(2)}) collective-permute-start(bf16[2048,128]{1,0:T(8,128)(2,1)S(1)} %collective-permute-done.refs_0_.refs_4_), channel_id=1, source_target_pairs={{0,2},{1,3},{2,0},{3,1},{4,6},{5,7},{6,4},{7,5},{8,10},{9,11},{10,... | collective-permute-start | bytes 1572872 | tf_op jit(solution)/shard_map/ppermute | solution.py:348
  31.2 9.9 %collective-permute-start.7 = (bf16[2048,128]{1,0:T(8,128)(2,1)S(1)}, bf16[2048,128]{1,0:T(8,128)(2,1)S(1)}, u32[]{:S(2)}, u32[]{:S(2)}) collective-permute-start(bf16[2048,128]{1,0:T(8,128)(2,1)S(1)} %collective-permute-done.4.refs_11_.refs_0_.refs_4_), channel_id=1, source_target_pairs={{0,1},{1,0},{2,3},{3,2},{4,5},{5,4},{6,7},{7,6},{8,9},{9,8},{10,11... | collective-permute-start | bytes 1572872 | tf_op jit(solution)/shard_map/ppermute | solution.py:348
  31.2 9.9 %collective-permute-start.5 = (bf16[256,256]{1,0:T(8,128)(2,1)S(1)}, bf16[256,256]{1,0:T(8,128)(2,1)S(1)}, u32[]{:S(2)}, u32[]{:S(2)}) collective-permute-start(bf16[256,256]{1,0:T(8,128)(2,1)S(1)} %add_convert_fusion.4), channel_id=1, source_target_pairs={{0,8},{4,12},{8,0},{12,4},{1,9},{5,13},{9,1},{13,5},{2,10},{6,14},... | collective-permute-start | bytes 393224 | tf_op jit(solution)/shard_map/ppermute | solution.py:348
  34.1 18.7 %collective-permute-start.8 = (bf16[2048,128]{1,0:T(8,128)(2,1)S(1)}, bf16[2048,128]{1,0:T(8,128)(2,1)S(1)}, u32[]{:S(2)}, u32[]{:S(2)}) collective-permute-start(bf16[2048,128]{1,0:T(8,128)(2,1)S(1)} %collective-permute-done.4.refs_11_.refs_0_.refs_4_), channel_id=1, source_target_pairs={{0,2},{1,3},{2,0},{3,1},{4,6},{5,7},{6,4},{7,5},{8,10},{9,11},{10,... | collective-permute-start | bytes 1572872 | tf_op jit(solution)/shard_map/ppermute | solution.py:348
  41.1 6.1 %collective-permute-start.6 = (bf16[2048,128]{1,0:T(8,128)(2,1)S(1)}, bf16[2048,128]{1,0:T(8,128)(2,1)S(1)}, u32[]{:S(2)}, u32[]{:S(2)}) collective-permute-start(bf16[2048,128]{1,0:T(8,128)(2,1)S(1)} %collective-permute-done.2.refs_14_.refs_2_), channel_id=1, source_target_pairs={{0,1},{1,0},{2,3},{3,2},{4,5},{5,4},{6,7},{7,6},{8,9},{9,8},{10,11... | collective-permute-start | bytes 1572872 | tf_op jit(solution)/shard_map/ppermute | solution.py:348
  43.0 9.7 %collective-permute-start.10 = (bf16[256,256]{1,0:T(8,128)(2,1)S(1)}, bf16[256,256]{1,0:T(8,128)(2,1)S(1)}, u32[]{:S(2)}, u32[]{:S(2)}) collective-permute-start(bf16[256,256]{1,0:T(8,128)(2,1)S(1)} %get-tuple-element.200.refs_0_), channel_id=1, source_target_pairs={{0,8},{4,12},{8,0},{12,4},{1,9},{5,13},{9,1},{13,5},{2,10},{6,14},... | collective-permute-start | bytes 393224 | tf_op jit(solution)/shard_map/ppermute | solution.py:348
  43.0 9.8 %collective-permute-start.9 = (bf16[256,256]{1,0:T(8,128)(2,1)S(1)}, bf16[256,256]{1,0:T(8,128)(2,1)S(1)}, u32[]{:S(2)}, u32[]{:S(2)}) collective-permute-start(bf16[256,256]{1,0:T(8,128)(2,1)S(1)} %get-tuple-element.200.refs_0_), channel_id=1, source_target_pairs={{0,4},{4,0},{8,12},{12,8},{1,5},{5,1},{9,13},{13,9},{2,6},{6,2},{1... | collective-permute-start | bytes 393224 | tf_op jit(solution)/shard_map/ppermute | solution.py:348
  52.8 2.1 %collective-permute-start.11 = (bf16[2048,128]{1,0:T(8,128)(2,1)S(1)}, bf16[2048,128]{1,0:T(8,128)(2,1)S(1)}, u32[]{:S(2)}, u32[]{:S(2)}) collective-permute-start(bf16[2048,128]{1,0:T(8,128)(2,1)S(1)} %collective-permute-done.8.refs_6_.refs_0_.refs_8_), channel_id=1, source_target_pairs={{0,1},{1,0},{2,3},{3,2},{4,5},{5,4},{6,7},{7,6},{8,9},{9,8},{10,11... | collective-permute-start | bytes 1572872 | tf_op jit(solution)/shard_map/ppermute | solution.py:348
  52.8 9.1 %collective-permute-start.17 = (bf16[256,512]{1,0:T(8,128)(2,1)S(1)}, bf16[256,512]{1,0:T(8,128)(2,1)S(1)}, u32[]{:S(2)}, u32[]{:S(2)}) collective-permute-start(bf16[256,512]{1,0:T(8,128)(2,1)S(1)} %get-tuple-element.244), channel_id=1, source_target_pairs={{0,4},{4,0},{8,12},{12,8},{1,5},{5,1},{9,13},{13,9},{2,6},{6,2},{1... | collective-permute-start | bytes 786440 | tf_op jit(solution)/shard_map/ppermute | solution.py:348
  52.8 12.2 %copy-start.1 = (bf16[1,1024,1024]{2,1,0:T(8,128)(2,1)S(1)}, bf16[1,1024,1024]{2,1,0:T(8,128)(2,1)}, u32[]{:S(2)}) copy-start(bf16[1,1024,1024]{2,1,0:T(8,128)(2,1)} %param.9) | copy-start | bytes 6291460
  52.8 24.0 %collective-permute-start.16 = (bf16[256,512]{1,0:T(8,128)(2,1)S(1)}, bf16[256,512]{1,0:T(8,128)(2,1)S(1)}, u32[]{:S(2)}, u32[]{:S(2)}) collective-permute-start(bf16[256,512]{1,0:T(8,128)(2,1)S(1)} %get-tuple-element.242), channel_id=1, source_target_pairs={{0,4},{4,0},{8,12},{12,8},{1,5},{5,1},{9,13},{13,9},{2,6},{6,2},{1... | collective-permute-start | bytes 786440 | tf_op jit(solution)/shard_map/ppermute | solution.py:348
  62.0 16.4 %collective-permute-start.18 = (bf16[256,512]{1,0:T(8,128)(2,1)S(1)}, bf16[256,512]{1,0:T(8,128)(2,1)S(1)}, u32[]{:S(2)}, u32[]{:S(2)}) collective-permute-start(bf16[256,512]{1,0:T(8,128)(2,1)S(1)} %add_convert_fusion.2), channel_id=1, source_target_pairs={{0,8},{4,12},{8,0},{12,4},{1,9},{5,13},{9,1},{13,5},{2,10},{6,14},... | collective-permute-start | bytes 786440 | tf_op jit(solution)/shard_map/ppermute | solution.py:348
  63.4 15.0 %collective-permute-start.13 = (bf16[512,256]{1,0:T(8,128)(2,1)S(1)}, bf16[512,256]{1,0:T(8,128)(2,1)S(1)}, u32[]{:S(2)}, u32[]{:S(2)}) collective-permute-start(bf16[512,256]{1,0:T(8,128)(2,1)S(1)} %get-tuple-element.226), channel_id=1, source_target_pairs={{0,4},{4,0},{8,12},{12,8},{1,5},{5,1},{9,13},{13,9},{2,6},{6,2},{1... | collective-permute-start | bytes 786440 | tf_op jit(solution)/shard_map/ppermute | solution.py:348
  76.8 10.6 %collective-permute-start.15 = (bf16[2048,256]{1,0:T(8,128)(2,1)S(1)}, bf16[2048,256]{1,0:T(8,128)(2,1)S(1)}, u32[]{:S(2)}, u32[]{:S(2)}) collective-permute-start(bf16[2048,256]{1,0:T(8,128)(2,1)S(1)} %get-tuple-element.231), channel_id=1, source_target_pairs={{0,1},{1,0},{2,3},{3,2},{4,5},{5,4},{6,7},{7,6},{8,9},{9,8},{10,11... | collective-permute-start | bytes 3145736 | tf_op jit(solution)/shard_map/ppermute | solution.py:348
  76.9 21.9 %collective-permute-start.12 = (bf16[2048,256]{1,0:T(8,128)(2,1)S(1)}, bf16[2048,256]{1,0:T(8,128)(2,1)S(1)}, u32[]{:S(2)}, u32[]{:S(2)}) collective-permute-start(bf16[2048,256]{1,0:T(8,128)(2,1)S(1)} %get-tuple-element.216), channel_id=1, source_target_pairs={{0,1},{1,0},{2,3},{3,2},{4,5},{5,4},{6,7},{7,6},{8,9},{9,8},{10,11... | collective-permute-start | bytes 3145736 | tf_op jit(solution)/shard_map/ppermute | solution.py:348
  78.4 9.0 %collective-permute-start.14 = (bf16[256,256]{1,0:T(8,128)(2,1)S(1)}, bf16[256,256]{1,0:T(8,128)(2,1)S(1)}, u32[]{:S(2)}, u32[]{:S(2)}) collective-permute-start(bf16[256,256]{1,0:T(8,128)(2,1)S(1)} %add_convert_fusion.3), channel_id=1, source_target_pairs={{0,8},{4,12},{8,0},{12,4},{1,9},{5,13},{9,1},{13,5},{2,10},{6,14},... | collective-permute-start | bytes 393224 | tf_op jit(solution)/shard_map/ppermute | solution.py:348
  82.6 15.7 %collective-permute-start.24 = (bf16[256,512]{1,0:T(8,128)(2,1)S(1)}, bf16[256,512]{1,0:T(8,128)(2,1)S(1)}, u32[]{:S(2)}, u32[]{:S(2)}) collective-permute-start(bf16[256,512]{1,0:T(8,128)(2,1)S(1)} %get-tuple-element.266.refs_0_), channel_id=1, source_target_pairs={{0,4},{4,0},{8,12},{12,8},{1,5},{5,1},{9,13},{13,9},{2,6},{6,2},{1... | collective-permute-start | bytes 786440 | tf_op jit(solution)/shard_map/ppermute | solution.py:348
  84.3 17.2 %collective-permute-start.23 = (bf16[256,512]{1,0:T(8,128)(2,1)S(1)}, bf16[256,512]{1,0:T(8,128)(2,1)S(1)}, u32[]{:S(2)}, u32[]{:S(2)}) collective-permute-start(bf16[256,512]{1,0:T(8,128)(2,1)S(1)} %get-tuple-element.266.refs_0_), channel_id=1, source_target_pairs={{0,8},{4,12},{8,0},{12,4},{1,9},{5,13},{9,1},{13,5},{2,10},{6,14},... | collective-permute-start | bytes 786440 | tf_op jit(solution)/shard_map/ppermute | solution.py:348
  87.8 25.0 %collective-permute-start.19 = (bf16[2048,256]{1,0:T(8,128)(2,1)S(1)}, bf16[2048,256]{1,0:T(8,128)(2,1)S(1)}, u32[]{:S(2)}, u32[]{:S(2)}) collective-permute-start(bf16[2048,256]{1,0:T(8,128)(2,1)S(1)} %add_convert_fusion.1), channel_id=1, source_target_pairs={{0,2},{1,3},{2,0},{3,1},{4,6},{5,7},{6,4},{7,5},{8,10},{9,11},{10,... | collective-permute-start | bytes 3145736 | tf_op jit(solution)/shard_map/ppermute | solution.py:348
  91.2 10.4 %collective-permute-start.22 = (bf16[256,256]{1,0:T(8,128)(2,1)S(1)}, bf16[256,256]{1,0:T(8,128)(2,1)S(1)}, u32[]{:S(2)}, u32[]{:S(2)}) collective-permute-start(bf16[256,256]{1,0:T(8,128)(2,1)S(1)} %get-tuple-element.265.refs_0_), channel_id=1, source_target_pairs={{0,4},{4,0},{8,12},{12,8},{1,5},{5,1},{9,13},{13,9},{2,6},{6,2},{1... | collective-permute-start | bytes 393224 | tf_op jit(solution)/shard_map/ppermute | solution.py:348
  98.4 7.7 %collective-permute-start.21 = (bf16[256,256]{1,0:T(8,128)(2,1)S(1)}, bf16[256,256]{1,0:T(8,128)(2,1)S(1)}, u32[]{:S(2)}, u32[]{:S(2)}) collective-permute-start(bf16[256,256]{1,0:T(8,128)(2,1)S(1)} %get-tuple-element.265.refs_0_), channel_id=1, source_target_pairs={{0,8},{4,12},{8,0},{12,4},{1,9},{5,13},{9,1},{13,5},{2,10},{6,14},... | collective-permute-start | bytes 393224 | tf_op jit(solution)/shard_map/ppermute | solution.py:348
  98.8 9.2 %collective-permute-start.20 = (bf16[256,256]{1,0:T(8,128)(2,1)S(1)}, bf16[256,256]{1,0:T(8,128)(2,1)S(1)}, u32[]{:S(2)}, u32[]{:S(2)}) collective-permute-start(bf16[256,256]{1,0:T(8,128)(2,1)S(1)} %collective-permute-done.10.refs_6_.refs_2_), channel_id=1, source_target_pairs={{0,4},{4,0},{8,12},{12,8},{1,5},{5,1},{9,13},{13,9},{2,6},{6,2},{1... | collective-permute-start | bytes 393224 | tf_op jit(solution)/shard_map/ppermute | solution.py:348
  101.5 12.7 %collective-permute-start.26 = (bf16[256,512]{1,0:T(8,128)(2,1)S(1)}, bf16[256,512]{1,0:T(8,128)(2,1)S(1)}, u32[]{:S(2)}, u32[]{:S(2)}) collective-permute-start(bf16[256,512]{1,0:T(8,128)(2,1)S(1)} %collective-permute-done.23.refs_11_.refs_2_), channel_id=1, source_target_pairs={{0,4},{4,0},{8,12},{12,8},{1,5},{5,1},{9,13},{13,9},{2,6},{6,2},{1... | collective-permute-start | bytes 786440 | tf_op jit(solution)/shard_map/ppermute | solution.py:348
  106.1 10.3 %collective-permute-start.25 = (bf16[256,256]{1,0:T(8,128)(2,1)S(1)}, bf16[256,256]{1,0:T(8,128)(2,1)S(1)}, u32[]{:S(2)}, u32[]{:S(2)}) collective-permute-start(bf16[256,256]{1,0:T(8,128)(2,1)S(1)} %collective-permute-done.21.refs_13_.refs_2_), channel_id=1, source_target_pairs={{0,4},{4,0},{8,12},{12,8},{1,5},{5,1},{9,13},{13,9},{2,6},{6,2},{1... | collective-permute-start | bytes 393224 | tf_op jit(solution)/shard_map/ppermute | solution.py:348

commit v5 on v4

--- a/solution.py
+++ b/solution.py
@@ -15,16 +15,17 @@
 SUMS = ("two", "tri", "two",)
 GATHERS = ("two", "two", "two",)
 PLAN = (
-    "h0", "b00", "b10", "t0", "b01", "m0", "r0", "b20", "b11", "a0", "b30", "t1", "g0",
+    "h0", "b00", "b10", "t0", "b01", "m0", "b20", "b11", "r0", "a0", "b30", "t1", "g0",
     "e0", "b21", "b31", "t2", "m1", "r1", "a1", "p0", "m2", "r2", "x0", "a2", "u0", "e1",
     "g1", "e2", "g2", "l0", "x1", "l1", "l2",
 )
 ANYWHERE = pl.BlockSpec(memory_space=pl.ANY)
+INSIDE = pl.BlockSpec(memory_space=pltpu.VMEM)
 TOKEN = jax.ShapeDtypeStruct((8, 128), F32)
 COSTS = {
-    "h0": 40000000000, "t0": 10000000000, "a0": 6000000000, "t1": 40000000000,
-    "t2": 6000000000, "a1": 10000000000, "p0": 35100000000, "a2": 6000000000,
-    "l0": 4199999999, "l1": 1000, "l2": 80000000000,
+    "h0": 40000000000, "t0": 10000000000, "a0": 10000000000, "t1": 40000000000,
+    "t2": 6000000000, "a1": 10000000000, "p0": 3000000000, "a2": 6000000000, "l0": 4199999999,
+    "l1": 1000, "l2": 80000000000,
 }
 
 
@@ -148,37 +149,26 @@
 
     def kernel(places_ref, hidden_ref, *refs):
         piece_refs, refs = refs[:count], refs[count + len(after) :]
-        out_refs, token_ref, joined = refs[:number], refs[number], refs[number + 1]
-        step = pl.program_id(0)
-
-        @pl.when(step == 0)
-        def _():
-            token_ref[...] = jnp.zeros_like(token_ref)
-            for j in range(count):
-                joined[:, j * width : (j + 1) * width] = piece_refs[j][...]
-
-        product = jnp.dot(hidden_ref[...], joined[...], preferred_element_type=F32)
-        product = (product * scale).astype(BF16)
+        out_refs, token_ref, joined, product = refs[:number], *refs[number:]
+        token_ref[...] = jnp.zeros_like(token_ref)
+        for j in range(count):
+            joined[:, j * width : (j + 1) * width] = piece_refs[j][...]
+        whole = jnp.dot(hidden_ref[...], joined[...], preferred_element_type=F32)
+        product[...] = (whole * scale).astype(BF16)
         for j in range(4):
-            @pl.when(step == j)
-            def _(j=j):
-                if paired and j >= 2:
-                    out_refs[2][(j - 2) * size : (j - 1) * size, :] = product
-                else:
-                    out_refs[j][...] = product
+            rows = product[pl.ds(pl.multiple_of(places_ref[j] * size, size), size), :]
+            if paired and j >= 2:
+                out_refs[2][(j - 2) * size : (j - 1) * size, :] = rows
+            else:
+                out_refs[j][...] = rows
 
     return pl.pallas_call(
         kernel,
-        grid_spec=pltpu.PrefetchScalarGridSpec(
-            num_scalar_prefetch=1,
-            grid=(4,),
-            in_specs=[pl.BlockSpec((size, tokens), lambda i, places: (places[i], 0))]
-            + [pl.BlockSpec((tokens, width), lambda i, places: (0, 0))] * count
-            + [ANYWHERE] * len(after),
-            out_specs=[pl.BlockSpec((height, wide), lambda i, places: (0, 0)) for height in heights]
-            + [pl.BlockSpec((8, 128), lambda i, places: (0, 0))],
-            scratch_shapes=[pltpu.VMEM((tokens, wide), BF16)],
-        ),
+        in_specs=[pl.BlockSpec(memory_space=pltpu.SMEM)]
+        + [INSIDE] * (1 + count)
+        + [ANYWHERE] * len(after),
+        out_specs=[INSIDE] * (number + 1),
+        scratch_shapes=[pltpu.VMEM((tokens, wide), BF16), pltpu.VMEM((units, wide), BF16)],
         out_shape=[jax.ShapeDtypeStruct((height, wide), BF16) for height in heights] + [TOKEN],
         compiler_params=params(16),
         cost_estimate=cost(item),
@@ -394,7 +384,7 @@
                 values["b3" + part] = swapped(values[name], "tensor", 1)
         elif kind == "t":
             pieces = [values["b%d%d" % key] for key in CHUNKS[k]]
-            pair, step = SUMS[k] == "two", SUMS[k] == "tri"
+            pair, step = SUMS[k] == "two", SUMS[k] in ("tri", "trd")
             *out, values["token"] = terms(
                 values["hidden"], pieces, paired if pair else shards, term_scale, pair, after(), name
             )
@@ -404,22 +394,27 @@
             else:
                 values["s0" + name[1]], values["s2" + name[1]] = out[0], out[2]
                 values["m" + name[1]] = swapped(out[3], "dp", 1) if step else None
-                for j in (1,) if step else (3, 2, 1):
+                values["s1" + name[1]] = out[1]
+                for j in {"tri": (1,), "trd": (), "one": (3, 2, 1)}[SUMS[k]]:
                     values["s%d%d" % (j, k)] = swapped(out[j], "dp", j)
         elif kind == "m":
             arrive(name)
             size = values["s0" + name[1]].shape[0]
             held_part = values[name][:size] if SUMS[k] == "two" else values[name]
             far = values["s2" + name[1]].astype(F32) + held_part.astype(F32)
-            values["s2" + name[1]] = swapped(far.astype(BF16), "dp", 2)
+            far = far.astype(BF16)
+            if SUMS[k] == "trd":
+                far, near = lax.optimization_barrier((far, values["s1" + name[1]]))
+                values["s1" + name[1]] = swapped(near, "dp", 1)
+            values["s2" + name[1]] = swapped(far, "dp", 2)
         elif kind == "r":
-            for j in {"two": (2,), "tri": (1, 2), "one": (3, 2, 1)}[SUMS[k]]:
+            for j in {"two": (2,), "tri": (1, 2), "trd": (2, 1), "one": (3, 2, 1)}[SUMS[k]]:
                 arrive("s%d%d" % (j, k))
         elif kind == "a":
             if SUMS[k] == "two":
                 shares, near = [values["s%d%d" % (j, k)] for j in (0, 2)], [values["m" + name[1]]]
             else:
-                number = 3 if SUMS[k] == "tri" else 4
+                number = 3 if SUMS[k] in ("tri", "trd") else 4
                 shares, near = [values["s%d%d" % (j, k)] for j in range(number)], []
             fresh, *moments[:], values["token"] = adam_chunk(
                 shares, near, moment[0], second[0], down, columns[k], rank_now,

time: 119 us -> 118 us (level)
  Pallas kernels: 38.3 us -> 36.2 us
    pallas_call x3, Pallas kernels: 9.42 us -> 7.26 us  [terms(): pl.pallas_call(kernel, in_specs=[pl.BlockSpec(memory_space=pltpu.SMEM)] +...]
  transfers between devices with their start and end apart: 27 -> 27, of which waited for: 13 -> 14; matrix products, arithmetic and copies ran while one was open for 2% -> 2% of each run, Pallas kernels for 31% -> 29%
where the time goes in v5:
time: 118 us
  waiting for transfers between devices  44.2 us (37%)
  Pallas kernels  36.2 us (31%)
  starting transfers between devices  30.8 us (26%)
  local copies, waits for them, and re-layouts  3.57 us (3%)
  other arithmetic  2.06 us (2%)
    ppermute x25, waiting for transfers between devices, swapped(): return lax.ppermute(value, axis, [(i, i ^ distance) for i in range(4)])  32.7 us
    ppermute x25, starting transfers between devices, swapped(): return lax.ppermute(value, axis, [(i, i ^ distance) for i in range(4)])  26 us
    pallas_call x1, Pallas kernels, partials(): pl.pallas_call(kernel, grid_spec=pltpu.PrefetchScalarGridSpec(num_scalar_...  11.9 us
    ppermute x2, waiting for transfers between devices, from_behind(): return lax.ppermute(block, axis, route)  11.5 us
    pallas_call x3, Pallas kernels, terms(): pl.pallas_call(kernel, in_specs=[pl.BlockSpec(memory_space=pltpu.SMEM)] +...  7.26 us
    pallas_call x3, Pallas kernels, adam_chunk(): pl.pallas_call(kernel, grid_spec=pltpu.PrefetchScalarGridSpec(num_scalar_...  6.49 us
    pallas_call x3, Pallas kernels, place_rows(): pl.pallas_call(kernel, grid_spec=pltpu.PrefetchScalarGridSpec(num_scalar_...  5.6 us
    pallas_call x1, Pallas kernels, prepare(): pl.pallas_call(kernel, grid=(tokens // TILE,), in_specs=[pl.BlockSpec((TI...  5.02 us
  transfers between devices with their start and end apart: 27, of which 14 were waited for; matrix products, arithmetic and copies ran while one was open for 2% of the time, Pallas kernels for 29%

profile of v5, /device:TPU:0, one launch (start us, length us, event | category | flops | bytes accessed | tf_op | source)
XLA Modules:
  0.0 117.6 jit_solution(1868463747884915296)
XLA Ops:
  1.9 3.0 %collective-permute-start = (bf16[2048,128]{1,0:T(8,128)(2,1)S(1)}, bf16[2048,128]{1,0:T(8,128)(2,1)S(1)}, u32[]{:S(2)}, u32[]{:S(2)}) collective-permute-start(bf16[2048,128]{1,0:T(8,128)(2,1)S(1)} %get-tuple-element.305), channel_id=1, source_target_pairs={{16,0},{0,16},{17,1},{1,17},{18,2},{2,18},{19,3},{3,19},{20,4},{4,... | collective-permute-start | bytes 1572872 | tf_op jit(solution)/shard_map/ppermute | solution.py:35
  5.3 2.2 %copy-done.2 = bf16[1,2048,1024]{2,1,0:T(8,128)(2,1)S(1)} copy-done((bf16[1,2048,1024]{2,1,0:T(8,128)(2,1)S(1)}, bf16[1,2048,1024]{2,1,0:T(8,128)(2,1)}, u32[]{:S(2)}) %copy-start.2) | copy-done | bytes 4194328
  7.4 5.0 %prepare.1 = (bf16[1024,2048]{1,0:T(8,128)(2,1)S(1)}, bf16[2048,1024]{1,0:T(8,128)(2,1)S(1)}, f32[8,128]{1,0:T(8,128)S(1)}) custom-call(bf16[2048,1024]{1,0:T(8,128)(2,1)S(1)} %bitcast.32, s32[4]{0:T(128)S(1)} %get-tuple-element.306.refs_0_.places_ref.rows_ref, s32[4]{0:T(128)S(1)} %get-tuple-element.307.refs_1_.places_ref, s32[1]{0:T(128)} %bitcast.14.refs_2_.rank_ref, ...), custom_call_target="tpu_custom_call" | custom-call | flops 40000000000 | bytes 1024 | tf_op jit(solution)/shard_map/prepare/pallas_call | solution.py:123
  12.5 4.4 %collective-permute-done.refs_0_.refs_4_ = bf16[2048,128]{1,0:T(8,128)(2,1)S(1)} collective-permute-done((bf16[2048,128]{1,0:T(8,128)(2,1)S(1)}, bf16[2048,128]{1,0:T(8,128)(2,1)S(1)}, u32[]{:S(2)}, u32[]{:S(2)}) %collective-permute-start) | collective-permute-done | bytes 524320 | tf_op jit(solution)/shard_map/ppermute | solution.py:35
  16.9 1.7 %collective-permute-start.4 = (bf16[2048,128]{1,0:T(8,128)(2,1)S(1)}, bf16[2048,128]{1,0:T(8,128)(2,1)S(1)}, u32[]{:S(2)}, u32[]{:S(2)}) collective-permute-start(bf16[2048,128]{1,0:T(8,128)(2,1)S(1)} %get-tuple-element.304), channel_id=1, source_target_pairs={{16,0},{0,16},{17,1},{1,17},{18,2},{2,18},{19,3},{3,19},{20,4},{4,... | collective-permute-start | bytes 1572872 | tf_op jit(solution)/shard_map/ppermute | solution.py:35
  18.8 2.0 %terms.3 = (bf16[256,256]{1,0:T(8,128)(2,1)S(1)}, bf16[256,256]{1,0:T(8,128)(2,1)S(1)}, bf16[512,256]{1,0:T(8,128)(2,1)S(1)}, f32[8,128]{1,0:T(8,128)S(1)}) custom-call(s32[4]{0:T(128)S(1)} %get-tuple-element.307.refs_1_.places_ref, bf16[1024,2048]{1,0:T(8,128)(2,1)S(1)} %get-tuple-element.158.hidden_ref, ...), custom_call_target="tpu_custom_call" | custom-call | flops 10000000000 | bytes 1024 | tf_op jit(solution)/shard_map/terms/pallas_call | solution.py:165
  20.8 1.9 %collective-permute-start.3 = (bf16[512,256]{1,0:T(8,128)(2,1)S(1)}, bf16[512,256]{1,0:T(8,128)(2,1)S(1)}, u32[]{:S(2)}, u32[]{:S(2)}) collective-permute-start(bf16[512,256]{1,0:T(8,128)(2,1)S(1)} %get-tuple-element.163), channel_id=1, source_target_pairs={{0,4},{4,0},{8,12},{12,8},{1,5},{5,1},{9,13},{13,9},{2,6},{6,2},{1... | collective-permute-start | bytes 786440 | tf_op jit(solution)/shard_map/ppermute | solution.py:338
  24.1 7.1 %collective-permute-done.4.refs_11_.refs_0_.refs_4_ = bf16[2048,128]{1,0:T(8,128)(2,1)S(1)} collective-permute-done((bf16[2048,128]{1,0:T(8,128)(2,1)S(1)}, bf16[2048,128]{1,0:T(8,128)(2,1)S(1)}, u32[]{:S(2)}, u32[]{:S(2)}) %collective-permute-start.4) | collective-permute-done | bytes 524320 | tf_op jit(solution)/shard_map/ppermute | solution.py:35
  31.2 2.9 %collective-permute-start.6 = (bf16[256,256]{1,0:T(8,128)(2,1)S(1)}, bf16[256,256]{1,0:T(8,128)(2,1)S(1)}, u32[]{:S(2)}, u32[]{:S(2)}) collective-permute-start(bf16[256,256]{1,0:T(8,128)(2,1)S(1)} %add_convert_fusion.4), channel_id=1, source_target_pairs={{0,8},{4,12},{8,0},{12,4},{1,9},{5,13},{9,1},{13,5},{2,10},{6,14},... | collective-permute-start | bytes 393224 | tf_op jit(solution)/shard_map/ppermute | solution.py:338
  36.3 4.8 %collective-permute-done.6.refs_1_.refs_15_ = bf16[256,256]{1,0:T(8,128)(2,1)S(1)} collective-permute-done((bf16[256,256]{1,0:T(8,128)(2,1)S(1)}, bf16[256,256]{1,0:T(8,128)(2,1)S(1)}, u32[]{:S(2)}, u32[]{:S(2)}) %collective-permute-start.6) | collective-permute-done | bytes 131104 | tf_op jit(solution)/shard_map/ppermute | solution.py:338
  41.1 1.9 %adam.3 = (bf16[256,256]{1,0:T(8,128)(2,1)S(1)}, f32[256,1024]{1,0:T(8,128)}, f32[256,1024]{1,0:T(8,128)}, f32[8,128]{1,0:T(8,128)S(1)}) custom-call(s32[2]{0:T(128)S(1)} %get-tuple-element.310.refs_5_.columns_ref, s32[1]{0:T(128)} %bitcast.14.refs_2_.rank_ref, bf16[256,256]{1,0:T(8,128)(2,1)S(1)} %get-tuple-element.171.refs_0_, ...), custom_call_target="tpu_custom_call" | custom-call | flops 10000000000 | bytes 1024 | tf_op jit(solution)/shard_map/adam/pallas_call | solution.py:202
  43.0 4.1 %collective-permute-start.9 = (bf16[256,256]{1,0:T(8,128)(2,1)S(1)}, bf16[256,256]{1,0:T(8,128)(2,1)S(1)}, u32[]{:S(2)}, u32[]{:S(2)}) collective-permute-start(bf16[256,256]{1,0:T(8,128)(2,1)S(1)} %get-tuple-element.200.refs_0_), channel_id=1, source_target_pairs={{0,4},{4,0},{8,12},{12,8},{1,5},{5,1},{9,13},{13,9},{2,6},{6,2},{1... | collective-permute-start | bytes 393224 | tf_op jit(solution)/shard_map/ppermute | solution.py:338
  47.1 3.3 %terms.4 = (bf16[256,512]{1,0:T(8,128)(2,1)S(1)}, bf16[256,512]{1,0:T(8,128)(2,1)S(1)}, bf16[256,512]{1,0:T(8,128)(2,1)S(1)}, bf16[256,512]{1,0:T(8,128)(2,1)S(1)}, f32[8,128]{1,0:T(8,128)S(1)}) custom-call(s32[4]{0:T(128)S(1)} %get-tuple-element.306.refs_0_.places_ref.rows_ref, bf16[1024,2048]{1,0:T(8,128)(2,1)S(1)} %get-tuple-element.158.hidden_ref, ...), custom_call_target="tpu_custom_call" | custom-call | flops 40000000000 | bytes 1024 | tf_op jit(solution)/shard_map/terms/pallas_call | solution.py:165
  50.4 1.6 %collective-permute-done.10.refs_6_.refs_2_ = bf16[256,256]{1,0:T(8,128)(2,1)S(1)} collective-permute-done((bf16[256,256]{1,0:T(8,128)(2,1)S(1)}, bf16[256,256]{1,0:T(8,128)(2,1)S(1)}, u32[]{:S(2)}, u32[]{:S(2)}) %collective-permute-start.10) | collective-permute-done | bytes 131104 | tf_op jit(solution)/shard_map/ppermute | solution.py:338
  52.3 1.9 %collective-permute-start.16 = (bf16[256,512]{1,0:T(8,128)(2,1)S(1)}, bf16[256,512]{1,0:T(8,128)(2,1)S(1)}, u32[]{:S(2)}, u32[]{:S(2)}) collective-permute-start(bf16[256,512]{1,0:T(8,128)(2,1)S(1)} %get-tuple-element.242), channel_id=1, source_target_pairs={{0,4},{4,0},{8,12},{12,8},{1,5},{5,1},{9,13},{13,9},{2,6},{6,2},{1... | collective-permute-start | bytes 786440 | tf_op jit(solution)/shard_map/ppermute | solution.py:338
  54.1 2.0 %terms.5 = (bf16[256,256]{1,0:T(8,128)(2,1)S(1)}, bf16[256,256]{1,0:T(8,128)(2,1)S(1)}, bf16[512,256]{1,0:T(8,128)(2,1)S(1)}, f32[8,128]{1,0:T(8,128)S(1)}) custom-call(s32[4]{0:T(128)S(1)} %get-tuple-element.307.refs_1_.places_ref, bf16[1024,2048]{1,0:T(8,128)(2,1)S(1)} %get-tuple-element.158.hidden_ref, ...), custom_call_target="tpu_custom_call" | custom-call | flops 6000000000 | bytes 1024 | tf_op jit(solution)/shard_map/terms/pallas_call | solution.py:165
  56.1 5.1 %collective-permute-done.17.refs_9_ = bf16[256,512]{1,0:T(8,128)(2,1)S(1)} collective-permute-done((bf16[256,512]{1,0:T(8,128)(2,1)S(1)}, bf16[256,512]{1,0:T(8,128)(2,1)S(1)}, u32[]{:S(2)}, u32[]{:S(2)}) %collective-permute-start.17) | collective-permute-done | bytes 262176 | tf_op jit(solution)/shard_map/ppermute | solution.py:338
  61.3 1.6 %collective-permute-start.18 = (bf16[256,512]{1,0:T(8,128)(2,1)S(1)}, bf16[256,512]{1,0:T(8,128)(2,1)S(1)}, u32[]{:S(2)}, u32[]{:S(2)}) collective-permute-start(bf16[256,512]{1,0:T(8,128)(2,1)S(1)} %add_convert_fusion.2), channel_id=1, source_target_pairs={{0,8},{4,12},{8,0},{12,4},{1,9},{5,13},{9,1},{13,5},{2,10},{6,14},... | collective-permute-start | bytes 786440 | tf_op jit(solution)/shard_map/ppermute | solution.py:338
  62.9 1.7 %collective-permute-start.13 = (bf16[512,256]{1,0:T(8,128)(2,1)S(1)}, bf16[512,256]{1,0:T(8,128)(2,1)S(1)}, u32[]{:S(2)}, u32[]{:S(2)}) collective-permute-start(bf16[512,256]{1,0:T(8,128)(2,1)S(1)} %get-tuple-element.226), channel_id=1, source_target_pairs={{0,4},{4,0},{8,12},{12,8},{1,5},{5,1},{9,13},{13,9},{2,6},{6,2},{1... | collective-permute-start | bytes 786440 | tf_op jit(solution)/shard_map/ppermute | solution.py:338
  64.6 11.9 %partials.1 = (bf16[2048,256]{1,0:T(8,128)(2,1)S(1)}, bf16[2048,256]{1,0:T(8,128)(2,1)S(1)}, bf16[2048,256]{1,0:T(8,128)(2,1)S(1)}, bf16[2048,256]{1,0:T(8,128)(2,1)S(1)}, f32[8,128]{1,0:T(8,128)S(1)}) custom-call(s32[8]{0:T(128)S(1)} %stack.89.refs_4_.where_ref, s32[4]{0:T(128)S(1)} %get-tuple-element.308.refs_3_.order_ref, ...), custom_call_target="tpu_custom_call" | custom-call | flops 3000000000 | bytes 1024 | tf_op jit(solution)/shard_map/partials/pallas_call | solution.py:299
  77.7 1.7 %collective-permute-start.14 = (bf16[256,256]{1,0:T(8,128)(2,1)S(1)}, bf16[256,256]{1,0:T(8,128)(2,1)S(1)}, u32[]{:S(2)}, u32[]{:S(2)}) collective-permute-start(bf16[256,256]{1,0:T(8,128)(2,1)S(1)} %add_convert_fusion.3), channel_id=1, source_target_pairs={{0,8},{4,12},{8,0},{12,4},{1,9},{5,13},{9,1},{13,5},{2,10},{6,14},... | collective-permute-start | bytes 393224 | tf_op jit(solution)/shard_map/ppermute | solution.py:338
  79.4 2.8 %adam.4 = (bf16[256,512]{1,0:T(8,128)(2,1)S(1)}, f32[256,1024]{1,0:T(8,128)}, f32[256,1024]{1,0:T(8,128)}, f32[8,128]{1,0:T(8,128)}) custom-call(s32[4]{0:T(128)S(1)} %get-tuple-element.309.refs_6_.columns_ref, s32[1]{0:T(128)} %bitcast.14.refs_2_.rank_ref, ...), custom_call_target="tpu_custom_call", output_to_operand_aliasing={{1}: (14, {}), {2}: (15, {})} | custom-call | flops 10000000000 | bytes 1024 | tf_op jit(solution)/shard_map/adam/pallas_call | solution.py:202
  82.2 1.7 %collective-permute-start.24 = (bf16[256,512]{1,0:T(8,128)(2,1)S(1)}, bf16[256,512]{1,0:T(8,128)(2,1)S(1)}, u32[]{:S(2)}, u32[]{:S(2)}) collective-permute-start(bf16[256,512]{1,0:T(8,128)(2,1)S(1)} %get-tuple-element.266.refs_0_), channel_id=1, source_target_pairs={{0,4},{4,0},{8,12},{12,8},{1,5},{5,1},{9,13},{13,9},{2,6},{6,2},{1... | collective-permute-start | bytes 786440 | tf_op jit(solution)/shard_map/ppermute | solution.py:338
  83.9 2.9 %collective-permute-done.14.refs_1_.refs_10_ = bf16[256,256]{1,0:T(8,128)(2,1)S(1)} collective-permute-done((bf16[256,256]{1,0:T(8,128)(2,1)S(1)}, bf16[256,256]{1,0:T(8,128)(2,1)S(1)}, u32[]{:S(2)}, u32[]{:S(2)}) %collective-permute-start.14) | collective-permute-done | bytes 131104 | tf_op jit(solution)/shard_map/ppermute | solution.py:338
  88.5 1.8 %adam.5 = (bf16[256,256]{1,0:T(8,128)(2,1)S(1)}, f32[256,1024]{1,0:T(8,128)}, f32[256,1024]{1,0:T(8,128)}, f32[8,128]{1,0:T(8,128)S(1)}) custom-call(s32[2]{0:T(128)S(1)} %get-tuple-element.311.refs_7_.columns_ref, s32[1]{0:T(128)} %bitcast.14.refs_2_.rank_ref, ...), custom_call_target="tpu_custom_call", output_to_operand_aliasing={{1}: (14, {}), {2}: (15, {})} | custom-call | flops 6000000000 | bytes 1024 | tf_op jit(solution)/shard_map/adam/pallas_call | solution.py:202
  90.4 7.3 %collective-permute-done.24.refs_10_.refs_1_ = bf16[256,512]{1,0:T(8,128)(2,1)S(1)} collective-permute-done((bf16[256,512]{1,0:T(8,128)(2,1)S(1)}, bf16[256,512]{1,0:T(8,128)(2,1)S(1)}, u32[]{:S(2)}, u32[]{:S(2)}) %collective-permute-start.24) | collective-permute-done | bytes 262176 | tf_op jit(solution)/shard_map/ppermute | solution.py:338
  98.3 2.7 %collective-permute-start.20 = (bf16[256,256]{1,0:T(8,128)(2,1)S(1)}, bf16[256,256]{1,0:T(8,128)(2,1)S(1)}, u32[]{:S(2)}, u32[]{:S(2)}) collective-permute-start(bf16[256,256]{1,0:T(8,128)(2,1)S(1)} %collective-permute-done.10.refs_6_.refs_2_), channel_id=1, source_target_pairs={{0,4},{4,0},{8,12},{12,8},{1,5},{5,1},{9,13},{13,9},{2,6},{6,2},{1... | collective-permute-start | bytes 393224 | tf_op jit(solution)/shard_map/ppermute | solution.py:338
  101.1 4.2 %collective-permute-done.21.refs_13_.refs_2_ = bf16[256,256]{1,0:T(8,128)(2,1)S(1)} collective-permute-done((bf16[256,256]{1,0:T(8,128)(2,1)S(1)}, bf16[256,256]{1,0:T(8,128)(2,1)S(1)}, u32[]{:S(2)}, u32[]{:S(2)}) %collective-permute-start.21) | collective-permute-done | bytes 131104 | tf_op jit(solution)/shard_map/ppermute | solution.py:338
  105.4 1.8 %collective-permute-done.20.refs_3_ = bf16[256,256]{1,0:T(8,128)(2,1)S(1)} collective-permute-done((bf16[256,256]{1,0:T(8,128)(2,1)S(1)}, bf16[256,256]{1,0:T(8,128)(2,1)S(1)}, u32[]{:S(2)}, u32[]{:S(2)}) %collective-permute-start.20) | collective-permute-done | bytes 131104 | tf_op jit(solution)/shard_map/ppermute | solution.py:338
  108.6 3.4 %collective-permute-done.19.refs_5_ = bf16[2048,256]{1,0:T(8,128)(2,1)S(1)} collective-permute-done((bf16[2048,256]{1,0:T(8,128)(2,1)S(1)}, bf16[2048,256]{1,0:T(8,128)(2,1)S(1)}, u32[]{:S(2)}, u32[]{:S(2)}) %collective-permute-start.19) | collective-permute-done | bytes 1048608 | tf_op jit(solution)/shard_map/ppermute | solution.py:338
  113.4 2.2 %place.4 = (bf16[1024,1024]{1,0:T(8,128)(2,1)}, f32[8,128]{1,0:T(8,128)}) custom-call(s32[4]{0:T(128)S(1)} %get-tuple-element.306.refs_0_.places_ref.rows_ref, s32[4]{0:T(128)S(1)} %get-tuple-element.309.refs_6_.columns_ref, bf16[256,512]{1,0:T(8,128)(2,1)S(1)} %get-tuple-element.266.refs_0_, ...), custom_call_target="tpu_custom_call", output_to_operand_aliasing={{0}: (8, {})} | custom-call | flops 1000 | bytes 1024 | tf_op jit(solution)/shard_map/place/pallas_call | solution.py:255
  115.6 2.0 %place.5 = (bf16[1024,1024]{1,0:T(8,128)(2,1)}, f32[8,128]{1,0:T(8,128)}) custom-call(s32[4]{0:T(128)S(1)} %get-tuple-element.306.refs_0_.places_ref.rows_ref, s32[2]{0:T(128)S(1)} %get-tuple-element.311.refs_7_.columns_ref, bf16[256,256]{1,0:T(8,128)(2,1)S(1)} %get-tuple-element.265.refs_0_, ...), custom_call_target="tpu_custom_call", output_to_operand_aliasing={{0}: (6, {})} | custom-call | flops 80000000000 | bytes 1024 | tf_op jit(solution)/shard_map/place/pallas_call | solution.py:255
  (53 shorter events, 12.3 us)
Async XLA Ops:
  1.9 15.0 %collective-permute-start = (bf16[2048,128]{1,0:T(8,128)(2,1)S(1)}, bf16[2048,128]{1,0:T(8,128)(2,1)S(1)}, u32[]{:S(2)}, u32[]{:S(2)}) collective-permute-start(bf16[2048,128]{1,0:T(8,128)(2,1)S(1)} %get-tuple-element.305), channel_id=1, source_target_pairs={{16,0},{0,16},{17,1},{1,17},{18,2},{2,18},{19,3},{3,19},{20,4},{4,... | collective-permute-start | bytes 1572872 | tf_op jit(solution)/shard_map/ppermute | solution.py:35
  5.3 2.2 %copy-start.2 = (bf16[1,2048,1024]{2,1,0:T(8,128)(2,1)S(1)}, bf16[1,2048,1024]{2,1,0:T(8,128)(2,1)}, u32[]{:S(2)}) copy-start(bf16[1,2048,1024]{2,1,0:T(8,128)(2,1)} %param.7) | copy-start | bytes 12582916
  16.9 1.9 %collective-permute-start.1 = (bf16[2048,128]{1,0:T(8,128)(2,1)S(1)}, bf16[2048,128]{1,0:T(8,128)(2,1)S(1)}, u32[]{:S(2)}, u32[]{:S(2)}) collective-permute-start(bf16[2048,128]{1,0:T(8,128)(2,1)S(1)} %collective-permute-done.refs_0_.refs_4_), channel_id=1, source_target_pairs={{0,1},{1,0},{2,3},{3,2},{4,5},{5,4},{6,7},{7,6},{8,9},{9,8},{10,11... | collective-permute-start | bytes 1572872 | tf_op jit(solution)/shard_map/ppermute | solution.py:338
  16.9 14.3 %collective-permute-start.4 = (bf16[2048,128]{1,0:T(8,128)(2,1)S(1)}, bf16[2048,128]{1,0:T(8,128)(2,1)S(1)}, u32[]{:S(2)}, u32[]{:S(2)}) collective-permute-start(bf16[2048,128]{1,0:T(8,128)(2,1)S(1)} %get-tuple-element.304), channel_id=1, source_target_pairs={{16,0},{0,16},{17,1},{1,17},{18,2},{2,18},{19,3},{3,19},{20,4},{4,... | collective-permute-start | bytes 1572872 | tf_op jit(solution)/shard_map/ppermute | solution.py:35
  18.8 22.3 %copy-start.1 = (bf16[1,1024,1024]{2,1,0:T(8,128)(2,1)S(1)}, bf16[1,1024,1024]{2,1,0:T(8,128)(2,1)}, u32[]{:S(2)}) copy-start(bf16[1,1024,1024]{2,1,0:T(8,128)(2,1)} %param.8) | copy-start | bytes 6291460
  18.8 22.3 %copy-start.3 = (f32[1,256,1024]{2,1,0:T(8,128)S(1)}, f32[1,256,1024]{2,1,0:T(8,128)}, u32[]{:S(2)}) copy-start(f32[1,256,1024]{2,1,0:T(8,128)} %param.10) | copy-start | bytes 3145732
  18.8 22.3 %copy-start.4 = (f32[1,256,1024]{2,1,0:T(8,128)S(1)}, f32[1,256,1024]{2,1,0:T(8,128)}, u32[]{:S(2)}) copy-start(f32[1,256,1024]{2,1,0:T(8,128)} %param.11) | copy-start | bytes 3145732
  20.8 10.4 %collective-permute-start.3 = (bf16[512,256]{1,0:T(8,128)(2,1)S(1)}, bf16[512,256]{1,0:T(8,128)(2,1)S(1)}, u32[]{:S(2)}, u32[]{:S(2)}) collective-permute-start(bf16[512,256]{1,0:T(8,128)(2,1)S(1)} %get-tuple-element.163), channel_id=1, source_target_pairs={{0,4},{4,0},{8,12},{12,8},{1,5},{5,1},{9,13},{13,9},{2,6},{6,2},{1... | collective-permute-start | bytes 786440 | tf_op jit(solution)/shard_map/ppermute | solution.py:338
  22.6 13.7 %collective-permute-start.2 = (bf16[2048,128]{1,0:T(8,128)(2,1)S(1)}, bf16[2048,128]{1,0:T(8,128)(2,1)S(1)}, u32[]{:S(2)}, u32[]{:S(2)}) collective-permute-start(bf16[2048,128]{1,0:T(8,128)(2,1)S(1)} %collective-permute-done.refs_0_.refs_4_), channel_id=1, source_target_pairs={{0,2},{1,3},{2,0},{3,1},{4,6},{5,7},{6,4},{7,5},{8,10},{9,11},{10,... | collective-permute-start | bytes 1572872 | tf_op jit(solution)/shard_map/ppermute | solution.py:338
  31.2 5.1 %collective-permute-start.7 = (bf16[2048,128]{1,0:T(8,128)(2,1)S(1)}, bf16[2048,128]{1,0:T(8,128)(2,1)S(1)}, u32[]{:S(2)}, u32[]{:S(2)}) collective-permute-start(bf16[2048,128]{1,0:T(8,128)(2,1)S(1)} %collective-permute-done.4.refs_11_.refs_0_.refs_4_), channel_id=1, source_target_pairs={{0,1},{1,0},{2,3},{3,2},{4,5},{5,4},{6,7},{7,6},{8,9},{9,8},{10,11... | collective-permute-start | bytes 1572872 | tf_op jit(solution)/shard_map/ppermute | solution.py:338
  31.2 9.9 %collective-permute-start.6 = (bf16[256,256]{1,0:T(8,128)(2,1)S(1)}, bf16[256,256]{1,0:T(8,128)(2,1)S(1)}, u32[]{:S(2)}, u32[]{:S(2)}) collective-permute-start(bf16[256,256]{1,0:T(8,128)(2,1)S(1)} %add_convert_fusion.4), channel_id=1, source_target_pairs={{0,8},{4,12},{8,0},{12,4},{1,9},{5,13},{9,1},{13,5},{2,10},{6,14},... | collective-permute-start | bytes 393224 | tf_op jit(solution)/shard_map/ppermute | solution.py:338
  34.1 18.0 %collective-permute-start.8 = (bf16[2048,128]{1,0:T(8,128)(2,1)S(1)}, bf16[2048,128]{1,0:T(8,128)(2,1)S(1)}, u32[]{:S(2)}, u32[]{:S(2)}) collective-permute-start(bf16[2048,128]{1,0:T(8,128)(2,1)S(1)} %collective-permute-done.4.refs_11_.refs_0_.refs_4_), channel_id=1, source_target_pairs={{0,2},{1,3},{2,0},{3,1},{4,6},{5,7},{6,4},{7,5},{8,10},{9,11},{10,... | collective-permute-start | bytes 1572872 | tf_op jit(solution)/shard_map/ppermute | solution.py:338
  36.3 10.8 %collective-permute-start.5 = (bf16[2048,128]{1,0:T(8,128)(2,1)S(1)}, bf16[2048,128]{1,0:T(8,128)(2,1)S(1)}, u32[]{:S(2)}, u32[]{:S(2)}) collective-permute-start(bf16[2048,128]{1,0:T(8,128)(2,1)S(1)} %collective-permute-done.2.refs_13_.refs_2_), channel_id=1, source_target_pairs={{0,1},{1,0},{2,3},{3,2},{4,5},{5,4},{6,7},{7,6},{8,9},{9,8},{10,11... | collective-permute-start | bytes 1572872 | tf_op jit(solution)/shard_map/ppermute | solution.py:338
  43.0 9.0 %collective-permute-start.10 = (bf16[256,256]{1,0:T(8,128)(2,1)S(1)}, bf16[256,256]{1,0:T(8,128)(2,1)S(1)}, u32[]{:S(2)}, u32[]{:S(2)}) collective-permute-start(bf16[256,256]{1,0:T(8,128)(2,1)S(1)} %get-tuple-element.200.refs_0_), channel_id=1, source_target_pairs={{0,8},{4,12},{8,0},{12,4},{1,9},{5,13},{9,1},{13,5},{2,10},{6,14},... | collective-permute-start | bytes 393224 | tf_op jit(solution)/shard_map/ppermute | solution.py:338
  43.0 9.1 %collective-permute-start.9 = (bf16[256,256]{1,0:T(8,128)(2,1)S(1)}, bf16[256,256]{1,0:T(8,128)(2,1)S(1)}, u32[]{:S(2)}, u32[]{:S(2)}) collective-permute-start(bf16[256,256]{1,0:T(8,128)(2,1)S(1)} %get-tuple-element.200.refs_0_), channel_id=1, source_target_pairs={{0,4},{4,0},{8,12},{12,8},{1,5},{5,1},{9,13},{13,9},{2,6},{6,2},{1... | collective-permute-start | bytes 393224 | tf_op jit(solution)/shard_map/ppermute | solution.py:338
  52.1 2.1 %collective-permute-start.11 = (bf16[2048,128]{1,0:T(8,128)(2,1)S(1)}, bf16[2048,128]{1,0:T(8,128)(2,1)S(1)}, u32[]{:S(2)}, u32[]{:S(2)}) collective-permute-start(bf16[2048,128]{1,0:T(8,128)(2,1)S(1)} %collective-permute-done.8.refs_6_.refs_0_.refs_8_), channel_id=1, source_target_pairs={{0,1},{1,0},{2,3},{3,2},{4,5},{5,4},{6,7},{7,6},{8,9},{9,8},{10,11... | collective-permute-start | bytes 1572872 | tf_op jit(solution)/shard_map/ppermute | solution.py:338
  52.1 9.1 %collective-permute-start.17 = (bf16[256,512]{1,0:T(8,128)(2,1)S(1)}, bf16[256,512]{1,0:T(8,128)(2,1)S(1)}, u32[]{:S(2)}, u32[]{:S(2)}) collective-permute-start(bf16[256,512]{1,0:T(8,128)(2,1)S(1)} %get-tuple-element.244), channel_id=1, source_target_pairs={{0,4},{4,0},{8,12},{12,8},{1,5},{5,1},{9,13},{13,9},{2,6},{6,2},{1... | collective-permute-start | bytes 786440 | tf_op jit(solution)/shard_map/ppermute | solution.py:338
  52.3 24.2 %collective-permute-start.16 = (bf16[256,512]{1,0:T(8,128)(2,1)S(1)}, bf16[256,512]{1,0:T(8,128)(2,1)S(1)}, u32[]{:S(2)}, u32[]{:S(2)}) collective-permute-start(bf16[256,512]{1,0:T(8,128)(2,1)S(1)} %get-tuple-element.242), channel_id=1, source_target_pairs={{0,4},{4,0},{8,12},{12,8},{1,5},{5,1},{9,13},{13,9},{2,6},{6,2},{1... | collective-permute-start | bytes 786440 | tf_op jit(solution)/shard_map/ppermute | solution.py:338
  54.1 10.5 %copy-start = (bf16[1,1024,1024]{2,1,0:T(8,128)(2,1)S(1)}, bf16[1,1024,1024]{2,1,0:T(8,128)(2,1)}, u32[]{:S(2)}) copy-start(bf16[1,1024,1024]{2,1,0:T(8,128)(2,1)} %param.9) | copy-start | bytes 6291460
  61.3 16.4 %collective-permute-start.18 = (bf16[256,512]{1,0:T(8,128)(2,1)S(1)}, bf16[256,512]{1,0:T(8,128)(2,1)S(1)}, u32[]{:S(2)}, u32[]{:S(2)}) collective-permute-start(bf16[256,512]{1,0:T(8,128)(2,1)S(1)} %add_convert_fusion.2), channel_id=1, source_target_pairs={{0,8},{4,12},{8,0},{12,4},{1,9},{5,13},{9,1},{13,5},{2,10},{6,14},... | collective-permute-start | bytes 786440 | tf_op jit(solution)/shard_map/ppermute | solution.py:338
  62.9 14.8 %collective-permute-start.13 = (bf16[512,256]{1,0:T(8,128)(2,1)S(1)}, bf16[512,256]{1,0:T(8,128)(2,1)S(1)}, u32[]{:S(2)}, u32[]{:S(2)}) collective-permute-start(bf16[512,256]{1,0:T(8,128)(2,1)S(1)} %get-tuple-element.226), channel_id=1, source_target_pairs={{0,4},{4,0},{8,12},{12,8},{1,5},{5,1},{9,13},{13,9},{2,6},{6,2},{1... | collective-permute-start | bytes 786440 | tf_op jit(solution)/shard_map/ppermute | solution.py:338
  76.5 10.2 %collective-permute-start.15 = (bf16[2048,256]{1,0:T(8,128)(2,1)S(1)}, bf16[2048,256]{1,0:T(8,128)(2,1)S(1)}, u32[]{:S(2)}, u32[]{:S(2)}) collective-permute-start(bf16[2048,256]{1,0:T(8,128)(2,1)S(1)} %get-tuple-element.231), channel_id=1, source_target_pairs={{0,1},{1,0},{2,3},{3,2},{4,5},{5,4},{6,7},{7,6},{8,9},{9,8},{10,11... | collective-permute-start | bytes 3145736 | tf_op jit(solution)/shard_map/ppermute | solution.py:338
  76.6 21.7 %collective-permute-start.12 = (bf16[2048,256]{1,0:T(8,128)(2,1)S(1)}, bf16[2048,256]{1,0:T(8,128)(2,1)S(1)}, u32[]{:S(2)}, u32[]{:S(2)}) collective-permute-start(bf16[2048,256]{1,0:T(8,128)(2,1)S(1)} %get-tuple-element.216), channel_id=1, source_target_pairs={{0,1},{1,0},{2,3},{3,2},{4,5},{5,4},{6,7},{7,6},{8,9},{9,8},{10,11... | collective-permute-start | bytes 3145736 | tf_op jit(solution)/shard_map/ppermute | solution.py:338
  77.7 9.0 %collective-permute-start.14 = (bf16[256,256]{1,0:T(8,128)(2,1)S(1)}, bf16[256,256]{1,0:T(8,128)(2,1)S(1)}, u32[]{:S(2)}, u32[]{:S(2)}) collective-permute-start(bf16[256,256]{1,0:T(8,128)(2,1)S(1)} %add_convert_fusion.3), channel_id=1, source_target_pairs={{0,8},{4,12},{8,0},{12,4},{1,9},{5,13},{9,1},{13,5},{2,10},{6,14},... | collective-permute-start | bytes 393224 | tf_op jit(solution)/shard_map/ppermute | solution.py:338
  82.2 15.5 %collective-permute-start.24 = (bf16[256,512]{1,0:T(8,128)(2,1)S(1)}, bf16[256,512]{1,0:T(8,128)(2,1)S(1)}, u32[]{:S(2)}, u32[]{:S(2)}) collective-permute-start(bf16[256,512]{1,0:T(8,128)(2,1)S(1)} %get-tuple-element.266.refs_0_), channel_id=1, source_target_pairs={{0,4},{4,0},{8,12},{12,8},{1,5},{5,1},{9,13},{13,9},{2,6},{6,2},{1... | collective-permute-start | bytes 786440 | tf_op jit(solution)/shard_map/ppermute | solution.py:338
  83.8 17.2 %collective-permute-start.23 = (bf16[256,512]{1,0:T(8,128)(2,1)S(1)}, bf16[256,512]{1,0:T(8,128)(2,1)S(1)}, u32[]{:S(2)}, u32[]{:S(2)}) collective-permute-start(bf16[256,512]{1,0:T(8,128)(2,1)S(1)} %get-tuple-element.266.refs_0_), channel_id=1, source_target_pairs={{0,8},{4,12},{8,0},{12,4},{1,9},{5,13},{9,1},{13,5},{2,10},{6,14},... | collective-permute-start | bytes 786440 | tf_op jit(solution)/shard_map/ppermute | solution.py:338
  87.0 24.9 %collective-permute-start.19 = (bf16[2048,256]{1,0:T(8,128)(2,1)S(1)}, bf16[2048,256]{1,0:T(8,128)(2,1)S(1)}, u32[]{:S(2)}, u32[]{:S(2)}) collective-permute-start(bf16[2048,256]{1,0:T(8,128)(2,1)S(1)} %add_convert_fusion.1), channel_id=1, source_target_pairs={{0,2},{1,3},{2,0},{3,1},{4,6},{5,7},{6,4},{7,5},{8,10},{9,11},{10,... | collective-permute-start | bytes 3145736 | tf_op jit(solution)/shard_map/ppermute | solution.py:338
  90.4 10.7 %collective-permute-start.22 = (bf16[256,256]{1,0:T(8,128)(2,1)S(1)}, bf16[256,256]{1,0:T(8,128)(2,1)S(1)}, u32[]{:S(2)}, u32[]{:S(2)}) collective-permute-start(bf16[256,256]{1,0:T(8,128)(2,1)S(1)} %get-tuple-element.265.refs_0_), channel_id=1, source_target_pairs={{0,4},{4,0},{8,12},{12,8},{1,5},{5,1},{9,13},{13,9},{2,6},{6,2},{1... | collective-permute-start | bytes 393224 | tf_op jit(solution)/shard_map/ppermute | solution.py:338
  97.7 7.7 %collective-permute-start.21 = (bf16[256,256]{1,0:T(8,128)(2,1)S(1)}, bf16[256,256]{1,0:T(8,128)(2,1)S(1)}, u32[]{:S(2)}, u32[]{:S(2)}) collective-permute-start(bf16[256,256]{1,0:T(8,128)(2,1)S(1)} %get-tuple-element.265.refs_0_), channel_id=1, source_target_pairs={{0,8},{4,12},{8,0},{12,4},{1,9},{5,13},{9,1},{13,5},{2,10},{6,14},... | collective-permute-start | bytes 393224 | tf_op jit(solution)/shard_map/ppermute | solution.py:338
  98.3 8.9 %collective-permute-start.20 = (bf16[256,256]{1,0:T(8,128)(2,1)S(1)}, bf16[256,256]{1,0:T(8,128)(2,1)S(1)}, u32[]{:S(2)}, u32[]{:S(2)}) collective-permute-start(bf16[256,256]{1,0:T(8,128)(2,1)S(1)} %collective-permute-done.10.refs_6_.refs_2_), channel_id=1, source_target_pairs={{0,4},{4,0},{8,12},{12,8},{1,5},{5,1},{9,13},{13,9},{2,6},{6,2},{1... | collective-permute-start | bytes 393224 | tf_op jit(solution)/shard_map/ppermute | solution.py:338
  101.0 12.3 %collective-permute-start.26 = (bf16[256,512]{1,0:T(8,128)(2,1)S(1)}, bf16[256,512]{1,0:T(8,128)(2,1)S(1)}, u32[]{:S(2)}, u32[]{:S(2)}) collective-permute-start(bf16[256,512]{1,0:T(8,128)(2,1)S(1)} %collective-permute-done.23.refs_11_.refs_2_), channel_id=1, source_target_pairs={{0,4},{4,0},{8,12},{12,8},{1,5},{5,1},{9,13},{13,9},{2,6},{6,2},{1... | collective-permute-start | bytes 786440 | tf_op jit(solution)/shard_map/ppermute | solution.py:338
  105.3 10.2 %collective-permute-start.25 = (bf16[256,256]{1,0:T(8,128)(2,1)S(1)}, bf16[256,256]{1,0:T(8,128)(2,1)S(1)}, u32[]{:S(2)}, u32[]{:S(2)}) collective-permute-start(bf16[256,256]{1,0:T(8,128)(2,1)S(1)} %collective-permute-done.21.refs_13_.refs_2_), channel_id=1, source_target_pairs={{0,4},{4,0},{8,12},{12,8},{1,5},{5,1},{9,13},{13,9},{2,6},{6,2},{1... | collective-permute-start | bytes 393224 | tf_op jit(solution)/shard_map/ppermute | solution.py:338

commit v6 on v5

--- a/solution.py
+++ b/solution.py
@@ -13,11 +13,11 @@
 TILE = 256
 CHUNKS = (((0, 0), (1, 0)), ((0, 1), (1, 1), (2, 0), (3, 0)), ((2, 1), (3, 1)))
 SUMS = ("two", "tri", "two",)
-GATHERS = ("two", "two", "two",)
+GATHERS = ("two", "two", "one",)
 PLAN = (
     "h0", "b00", "b10", "t0", "b01", "m0", "b20", "b11", "r0", "a0", "b30", "t1", "g0",
-    "e0", "b21", "b31", "t2", "m1", "r1", "a1", "p0", "m2", "r2", "x0", "a2", "u0", "e1",
-    "g1", "e2", "g2", "l0", "x1", "l1", "l2",
+    "e0", "b21", "b31", "t2", "m1", "r1", "a1", "p0", "m2", "r2", "x0", "a2", "u0", "g1",
+    "e1", "g2", "l0", "x1", "l1", "l2",
 )
 ANYWHERE = pl.BlockSpec(memory_space=pl.ANY)
 INSIDE = pl.BlockSpec(memory_space=pltpu.VMEM)
@@ -25,7 +25,7 @@
 COSTS = {
     "h0": 40000000000, "t0": 10000000000, "a0": 10000000000, "t1": 40000000000,
     "t2": 6000000000, "a1": 10000000000, "p0": 3000000000, "a2": 6000000000, "l0": 4199999999,
-    "l1": 1000, "l2": 80000000000,
+    "l1": 1000, "l2": 6000000000,
 }
 
 
@@ -186,30 +186,30 @@
         m_ref, v_ref, down_ref = refs[number : number + 3]
         fresh_ref, new_m_ref, new_v_ref, token_ref = refs[-4:]
         token_ref[...] = jnp.zeros_like(token_ref)
-        gradient = refs[0][...].astype(F32)
-        for ref in refs[1:number]:
-            gradient += ref[...].astype(F32)
+        here = pl.ds(pl.multiple_of(pl.program_id(0) * width, width), width)
+        gradient = refs[0][:, here].astype(F32)
+        for ref in refs[1 : len(shares)]:
+            gradient += ref[:, here].astype(F32)
+        for ref in refs[len(shares) : number]:
+            gradient += ref[size:, here].astype(F32)
         new_m = 0.9 * m_ref[...] + 0.1 * gradient
         new_v = 0.95 * v_ref[...] + 0.05 * gradient * gradient
         new_m_ref[...] = new_m
         new_v_ref[...] = new_v
         rows = down_ref[...].astype(F32)
-        fresh_ref[...] = (rows - 0.2 * new_m / (jnp.sqrt(new_v) + 1e-08)).astype(BF16)
-
-    here = pl.BlockSpec((size, width), lambda j, columns, rank: (0, j))
-    below = pl.BlockSpec((size, width), lambda j, columns, rank: (1, j))
+        fresh_ref[:, here] = (rows - 0.2 * new_m / (jnp.sqrt(new_v) + 1e-08)).astype(BF16)
+
     there = pl.BlockSpec((size, width), lambda j, columns, rank: (0, columns[j]))
     return pl.pallas_call(
         kernel,
         grid_spec=pltpu.PrefetchScalarGridSpec(
             num_scalar_prefetch=2,
             grid=(count,),
-            in_specs=[here] * len(shares)
-            + [below] * len(near)
+            in_specs=[INSIDE] * number
             + [there] * 2
             + [pl.BlockSpec((size, width), lambda j, columns, rank: (rank[0], columns[j]))]
             + [ANYWHERE] * (len(after) + len(previous)),
-            out_specs=[here, there, there, pl.BlockSpec((8, 128), lambda j, columns, rank: (0, 0))],
+            out_specs=[INSIDE, there, there, pl.BlockSpec((8, 128), lambda j, columns, rank: (0, 0))],
         ),
         out_shape=[
             jax.ShapeDtypeStruct((size, wide), BF16),
@@ -226,7 +226,7 @@
     )(columns, rank, *shares, *near, moment, second, down, *after, *previous)
 
 
-def place_rows(shards, rows, columns, previous, total, width, after, item):
+def place_rows(shards, chosen, rows, columns, previous, total, width, after, item):
     size, wide = shards[0].shape
     count = wide // width
     number = len(shards)
@@ -241,7 +241,7 @@
                     pltpu.make_async_copy(
                         shard_refs[k].at[:, pl.ds(j * width, width)],
                         out_ref.at[
-                            pl.ds(pl.multiple_of(rows_ref[k] * size, size), size),
+                            pl.ds(pl.multiple_of(rows_ref[chosen[k]] * size, size), size),
                             pl.ds(pl.multiple_of(columns_ref[j] * width, width), width),
                         ],
                         sems.at[k, j],
@@ -303,7 +303,7 @@
             grid=(rows // step,),
             in_specs=[pl.BlockSpec((step, width), lambda i, w, o: (i, 0))] * count
             + [pl.BlockSpec((step, units), lambda i, w, o: (i, 0))]
-            + [pl.BlockSpec((units, model_width), lambda i, w, o: (0, 0))] * 2
+            + [INSIDE] * 2
             + [ANYWHERE] * len(after),
             out_specs=[
                 pl.BlockSpec((step, block), lambda i, w, o: (i, 0)),
@@ -431,10 +431,11 @@
                 values["g3" + name[1]] = swapped(values["g2" + name[1]], "dp", 1)
         elif kind == "e":
             arrive("g1" + name[1])
-        elif kind == "l":
-            gathered = [values["g%d%d" % (j, k)] for j in range(4)]
+        elif kind in "lq":
+            chosen = [3] if kind == "q" else [0, 1, 2] + [3] * ("q" + name[1] not in PLAN)
+            gathered = [values["g%d%d" % (j, k)] for j in chosen]
             *new_down[:], values["token"] = place_rows(
-                gathered, shards, columns[k], new_down, down.shape, width, after(), name
+                gathered, chosen, shards, columns[k], new_down, down.shape, width, after(), name
             )
         elif kind == "p":
             pieces = [values["b%d%d" % key] for key in keys]

time: 118 us -> 122 us (1.034)
  starting transfers between devices: 30.8 us -> 35.9 us
    ppermute x25, starting transfers between devices: 26 us -> 31.2 us  [swapped(): return lax.ppermute(value, axis, [(i, i ^ distance) for i in range(4)])]
  transfers between devices with their start and end apart: 27 -> 27, of which waited for: 14 -> 12; matrix products, arithmetic and copies ran while one was open for 2% -> 2% of each run, Pallas kernels for 29% -> 28%
where the time goes in v6:
time: 122 us
  waiting for transfers between devices  43.9 us (36%)
  starting transfers between devices  35.9 us (29%)
  Pallas kernels  35.6 us (29%)
  local copies, waits for them, and re-layouts  3.57 us (3%)
  other arithmetic  2.06 us (2%)
    ppermute x25, waiting for transfers between devices, swapped(): return lax.ppermute(value, axis, [(i, i ^ distance) for i in range(4)])  32.5 us
    ppermute x25, starting transfers between devices, swapped(): return lax.ppermute(value, axis, [(i, i ^ distance) for i in range(4)])  31.2 us
    pallas_call x1, Pallas kernels, partials(): pl.pallas_call(kernel, grid_spec=pltpu.PrefetchScalarGridSpec(num_scalar_...  11.9 us
    ppermute x2, waiting for transfers between devices, from_behind(): return lax.ppermute(block, axis, route)  11.5 us
    pallas_call x3, Pallas kernels, terms(): pl.pallas_call(kernel, in_specs=[pl.BlockSpec(memory_space=pltpu.SMEM)] +...  7.26 us
    pallas_call x3, Pallas kernels, adam_chunk(): pl.pallas_call(kernel, grid_spec=pltpu.PrefetchScalarGridSpec(num_scalar_...  5.83 us
    pallas_call x3, Pallas kernels, place_rows(): pl.pallas_call(kernel, grid_spec=pltpu.PrefetchScalarGridSpec(num_scalar_...  5.6 us
    pallas_call x1, Pallas kernels, prepare(): pl.pallas_call(kernel, grid=(tokens // TILE,), in_specs=[pl.BlockSpec((TI...  5.02 us
  transfers between devices with their start and end apart: 27, of which 12 were waited for; matrix products, arithmetic and copies ran while one was open for 2% of the time, Pallas kernels for 28%

profile of v6, /device:TPU:0, one launch (start us, length us, event | category | flops | bytes accessed | tf_op | source)
XLA Modules:
  0.0 121.8 jit_solution(1360413652374656755)
XLA Ops:
  1.9 3.0 %collective-permute-start = (bf16[2048,128]{1,0:T(8,128)(2,1)S(1)}, bf16[2048,128]{1,0:T(8,128)(2,1)S(1)}, u32[]{:S(2)}, u32[]{:S(2)}) collective-permute-start(bf16[2048,128]{1,0:T(8,128)(2,1)S(1)} %get-tuple-element.285), channel_id=1, source_target_pairs={{16,0},{0,16},{17,1},{1,17},{18,2},{2,18},{19,3},{3,19},{20,4},{4,... | collective-permute-start | bytes 1572872 | tf_op jit(solution)/shard_map/ppermute | solution.py:35
  5.3 2.2 %copy-done.2 = bf16[1,2048,1024]{2,1,0:T(8,128)(2,1)S(1)} copy-done((bf16[1,2048,1024]{2,1,0:T(8,128)(2,1)S(1)}, bf16[1,2048,1024]{2,1,0:T(8,128)(2,1)}, u32[]{:S(2)}) %copy-start.2) | copy-done | bytes 4194328
  7.4 5.0 %prepare.1 = (bf16[1024,2048]{1,0:T(8,128)(2,1)S(1)}, bf16[2048,1024]{1,0:T(8,128)(2,1)S(1)}, f32[8,128]{1,0:T(8,128)S(1)}) custom-call(bf16[2048,1024]{1,0:T(8,128)(2,1)S(1)} %bitcast.32, s32[4]{0:T(128)S(1)} %get-tuple-element.286.refs_0_.places_ref.rows_ref, s32[4]{0:T(128)S(1)} %get-tuple-element.287.refs_1_.places_ref, s32[1]{0:T(128)} %bitcast.14.refs_2_.rank_ref, ...), custom_call_target="tpu_custom_call" | custom-call | flops 40000000000 | bytes 1024 | tf_op jit(solution)/shard_map/prepare/pallas_call | solution.py:123
  12.5 4.4 %collective-permute-done.refs_0_.refs_4_ = bf16[2048,128]{1,0:T(8,128)(2,1)S(1)} collective-permute-done((bf16[2048,128]{1,0:T(8,128)(2,1)S(1)}, bf16[2048,128]{1,0:T(8,128)(2,1)S(1)}, u32[]{:S(2)}, u32[]{:S(2)}) %collective-permute-start) | collective-permute-done | bytes 524320 | tf_op jit(solution)/shard_map/ppermute | solution.py:35
  16.9 1.7 %collective-permute-start.4 = (bf16[2048,128]{1,0:T(8,128)(2,1)S(1)}, bf16[2048,128]{1,0:T(8,128)(2,1)S(1)}, u32[]{:S(2)}, u32[]{:S(2)}) collective-permute-start(bf16[2048,128]{1,0:T(8,128)(2,1)S(1)} %get-tuple-element.284), channel_id=1, source_target_pairs={{16,0},{0,16},{17,1},{1,17},{18,2},{2,18},{19,3},{3,19},{20,4},{4,... | collective-permute-start | bytes 1572872 | tf_op jit(solution)/shard_map/ppermute | solution.py:35
  18.8 2.0 %terms.3 = (bf16[256,256]{1,0:T(8,128)(2,1)S(1)}, bf16[256,256]{1,0:T(8,128)(2,1)S(1)}, bf16[512,256]{1,0:T(8,128)(2,1)S(1)}, f32[8,128]{1,0:T(8,128)S(1)}) custom-call(s32[4]{0:T(128)S(1)} %get-tuple-element.287.refs_1_.places_ref, bf16[1024,2048]{1,0:T(8,128)(2,1)S(1)} %get-tuple-element.148.hidden_ref, ...), custom_call_target="tpu_custom_call" | custom-call | flops 10000000000 | bytes 1024 | tf_op jit(solution)/shard_map/terms/pallas_call | solution.py:165
  20.8 1.9 %collective-permute-start.3 = (bf16[512,256]{1,0:T(8,128)(2,1)S(1)}, bf16[512,256]{1,0:T(8,128)(2,1)S(1)}, u32[]{:S(2)}, u32[]{:S(2)}) collective-permute-start(bf16[512,256]{1,0:T(8,128)(2,1)S(1)} %get-tuple-element.153), channel_id=1, source_target_pairs={{0,4},{4,0},{8,12},{12,8},{1,5},{5,1},{9,13},{13,9},{2,6},{6,2},{1... | collective-permute-start | bytes 786440 | tf_op jit(solution)/shard_map/ppermute | solution.py:338
  24.1 7.1 %collective-permute-done.4.refs_11_.refs_0_.refs_4_ = bf16[2048,128]{1,0:T(8,128)(2,1)S(1)} collective-permute-done((bf16[2048,128]{1,0:T(8,128)(2,1)S(1)}, bf16[2048,128]{1,0:T(8,128)(2,1)S(1)}, u32[]{:S(2)}, u32[]{:S(2)}) %collective-permute-start.4) | collective-permute-done | bytes 524320 | tf_op jit(solution)/shard_map/ppermute | solution.py:35
  31.2 2.9 %collective-permute-start.6 = (bf16[256,256]{1,0:T(8,128)(2,1)S(1)}, bf16[256,256]{1,0:T(8,128)(2,1)S(1)}, u32[]{:S(2)}, u32[]{:S(2)}) collective-permute-start(bf16[256,256]{1,0:T(8,128)(2,1)S(1)} %add_convert_fusion.4), channel_id=1, source_target_pairs={{0,8},{4,12},{8,0},{12,4},{1,9},{5,13},{9,1},{13,5},{2,10},{6,14},... | collective-permute-start | bytes 393224 | tf_op jit(solution)/shard_map/ppermute | solution.py:338
  36.3 4.8 %collective-permute-done.6.refs_1_.refs_15_ = bf16[256,256]{1,0:T(8,128)(2,1)S(1)} collective-permute-done((bf16[256,256]{1,0:T(8,128)(2,1)S(1)}, bf16[256,256]{1,0:T(8,128)(2,1)S(1)}, u32[]{:S(2)}, u32[]{:S(2)}) %collective-permute-start.6) | collective-permute-done | bytes 131104 | tf_op jit(solution)/shard_map/ppermute | solution.py:338
  41.1 1.7 %adam.3 = (bf16[256,256]{1,0:T(8,128)(2,1)S(1)}, f32[256,1024]{1,0:T(8,128)}, f32[256,1024]{1,0:T(8,128)}, f32[8,128]{1,0:T(8,128)S(1)}) custom-call(s32[2]{0:T(128)S(1)} %get-tuple-element.290.refs_5_.columns_ref, s32[1]{0:T(128)} %bitcast.14.refs_2_.rank_ref, bf16[256,256]{1,0:T(8,128)(2,1)S(1)} %get-tuple-element.161.refs_0_, ...), custom_call_target="tpu_custom_call" | custom-call | flops 10000000000 | bytes 1024 | tf_op jit(solution)/shard_map/adam/pallas_call | solution.py:203
  42.8 4.1 %collective-permute-start.9 = (bf16[256,256]{1,0:T(8,128)(2,1)S(1)}, bf16[256,256]{1,0:T(8,128)(2,1)S(1)}, u32[]{:S(2)}, u32[]{:S(2)}) collective-permute-start(bf16[256,256]{1,0:T(8,128)(2,1)S(1)} %get-tuple-element.190.refs_0_), channel_id=1, source_target_pairs={{0,4},{4,0},{8,12},{12,8},{1,5},{5,1},{9,13},{13,9},{2,6},{6,2},{1... | collective-permute-start | bytes 393224 | tf_op jit(solution)/shard_map/ppermute | solution.py:338
  46.9 3.3 %terms.4 = (bf16[256,512]{1,0:T(8,128)(2,1)S(1)}, bf16[256,512]{1,0:T(8,128)(2,1)S(1)}, bf16[256,512]{1,0:T(8,128)(2,1)S(1)}, bf16[256,512]{1,0:T(8,128)(2,1)S(1)}, f32[8,128]{1,0:T(8,128)S(1)}) custom-call(s32[4]{0:T(128)S(1)} %get-tuple-element.286.refs_0_.places_ref.rows_ref, bf16[1024,2048]{1,0:T(8,128)(2,1)S(1)} %get-tuple-element.148.hidden_ref, ...), custom_call_target="tpu_custom_call" | custom-call | flops 40000000000 | bytes 1024 | tf_op jit(solution)/shard_map/terms/pallas_call | solution.py:165
  50.2 1.6 %collective-permute-done.10.refs_6_.refs_2_ = bf16[256,256]{1,0:T(8,128)(2,1)S(1)} collective-permute-done((bf16[256,256]{1,0:T(8,128)(2,1)S(1)}, bf16[256,256]{1,0:T(8,128)(2,1)S(1)}, u32[]{:S(2)}, u32[]{:S(2)}) %collective-permute-start.10) | collective-permute-done | bytes 131104 | tf_op jit(solution)/shard_map/ppermute | solution.py:338
  52.1 1.9 %collective-permute-start.16 = (bf16[256,512]{1,0:T(8,128)(2,1)S(1)}, bf16[256,512]{1,0:T(8,128)(2,1)S(1)}, u32[]{:S(2)}, u32[]{:S(2)}) collective-permute-start(bf16[256,512]{1,0:T(8,128)(2,1)S(1)} %get-tuple-element.232), channel_id=1, source_target_pairs={{0,4},{4,0},{8,12},{12,8},{1,5},{5,1},{9,13},{13,9},{2,6},{6,2},{1... | collective-permute-start | bytes 786440 | tf_op jit(solution)/shard_map/ppermute | solution.py:338
  54.0 2.0 %terms.5 = (bf16[256,256]{1,0:T(8,128)(2,1)S(1)}, bf16[256,256]{1,0:T(8,128)(2,1)S(1)}, bf16[512,256]{1,0:T(8,128)(2,1)S(1)}, f32[8,128]{1,0:T(8,128)S(1)}) custom-call(s32[4]{0:T(128)S(1)} %get-tuple-element.287.refs_1_.places_ref, bf16[1024,2048]{1,0:T(8,128)(2,1)S(1)} %get-tuple-element.148.hidden_ref, ...), custom_call_target="tpu_custom_call" | custom-call | flops 6000000000 | bytes 1024 | tf_op jit(solution)/shard_map/terms/pallas_call | solution.py:165
  56.0 5.1 %collective-permute-done.17.refs_9_ = bf16[256,512]{1,0:T(8,128)(2,1)S(1)} collective-permute-done((bf16[256,512]{1,0:T(8,128)(2,1)S(1)}, bf16[256,512]{1,0:T(8,128)(2,1)S(1)}, u32[]{:S(2)}, u32[]{:S(2)}) %collective-permute-start.17) | collective-permute-done | bytes 262176 | tf_op jit(solution)/shard_map/ppermute | solution.py:338
  61.1 1.6 %collective-permute-start.18 = (bf16[256,512]{1,0:T(8,128)(2,1)S(1)}, bf16[256,512]{1,0:T(8,128)(2,1)S(1)}, u32[]{:S(2)}, u32[]{:S(2)}) collective-permute-start(bf16[256,512]{1,0:T(8,128)(2,1)S(1)} %add_convert_fusion.2), channel_id=1, source_target_pairs={{0,8},{4,12},{8,0},{12,4},{1,9},{5,13},{9,1},{13,5},{2,10},{6,14},... | collective-permute-start | bytes 786440 | tf_op jit(solution)/shard_map/ppermute | solution.py:338
  62.7 1.7 %collective-permute-start.13 = (bf16[512,256]{1,0:T(8,128)(2,1)S(1)}, bf16[512,256]{1,0:T(8,128)(2,1)S(1)}, u32[]{:S(2)}, u32[]{:S(2)}) collective-permute-start(bf16[512,256]{1,0:T(8,128)(2,1)S(1)} %get-tuple-element.216), channel_id=1, source_target_pairs={{0,4},{4,0},{8,12},{12,8},{1,5},{5,1},{9,13},{13,9},{2,6},{6,2},{1... | collective-permute-start | bytes 786440 | tf_op jit(solution)/shard_map/ppermute | solution.py:338
  64.4 11.9 %partials.1 = (bf16[2048,256]{1,0:T(8,128)(2,1)S(1)}, bf16[2048,256]{1,0:T(8,128)(2,1)S(1)}, bf16[2048,256]{1,0:T(8,128)(2,1)S(1)}, bf16[2048,256]{1,0:T(8,128)(2,1)S(1)}, f32[8,128]{1,0:T(8,128)S(1)}) custom-call(s32[8]{0:T(128)S(1)} %stack.89.refs_4_.where_ref, s32[4]{0:T(128)S(1)} %get-tuple-element.288.refs_3_.order_ref, ...), custom_call_target="tpu_custom_call" | custom-call | flops 3000000000 | bytes 1024 | tf_op jit(solution)/shard_map/partials/pallas_call | solution.py:299
  77.5 1.7 %collective-permute-start.14 = (bf16[256,256]{1,0:T(8,128)(2,1)S(1)}, bf16[256,256]{1,0:T(8,128)(2,1)S(1)}, u32[]{:S(2)}, u32[]{:S(2)}) collective-permute-start(bf16[256,256]{1,0:T(8,128)(2,1)S(1)} %add_convert_fusion.3), channel_id=1, source_target_pairs={{0,8},{4,12},{8,0},{12,4},{1,9},{5,13},{9,1},{13,5},{2,10},{6,14},... | collective-permute-start | bytes 393224 | tf_op jit(solution)/shard_map/ppermute | solution.py:338
  79.2 2.5 %adam.4 = (bf16[256,512]{1,0:T(8,128)(2,1)S(1)}, f32[256,1024]{1,0:T(8,128)}, f32[256,1024]{1,0:T(8,128)}, f32[8,128]{1,0:T(8,128)}) custom-call(s32[4]{0:T(128)S(1)} %get-tuple-element.289.refs_6_.columns_ref, s32[1]{0:T(128)} %bitcast.14.refs_2_.rank_ref, ...), custom_call_target="tpu_custom_call", output_to_operand_aliasing={{1}: (14, {}), {2}: (15, {})} | custom-call | flops 10000000000 | bytes 1024 | tf_op jit(solution)/shard_map/adam/pallas_call | solution.py:203
  83.4 8.1 %collective-permute-done.14.refs_1_.refs_10_ = bf16[256,256]{1,0:T(8,128)(2,1)S(1)} collective-permute-done((bf16[256,256]{1,0:T(8,128)(2,1)S(1)}, bf16[256,256]{1,0:T(8,128)(2,1)S(1)}, u32[]{:S(2)}, u32[]{:S(2)}) %collective-permute-start.14) | collective-permute-done | bytes 131104 | tf_op jit(solution)/shard_map/ppermute | solution.py:338
  91.8 1.6 %collective-permute-start.19 = (bf16[2048,256]{1,0:T(8,128)(2,1)S(1)}, bf16[2048,256]{1,0:T(8,128)(2,1)S(1)}, u32[]{:S(2)}, u32[]{:S(2)}) collective-permute-start(bf16[2048,256]{1,0:T(8,128)(2,1)S(1)} %add_convert_fusion.1), channel_id=1, source_target_pairs={{0,2},{1,3},{2,0},{3,1},{4,6},{5,7},{6,4},{7,5},{8,10},{9,11},{10,... | collective-permute-start | bytes 3145736 | tf_op jit(solution)/shard_map/ppermute | solution.py:338
  93.3 1.7 %adam.5 = (bf16[256,256]{1,0:T(8,128)(2,1)S(1)}, f32[256,1024]{1,0:T(8,128)}, f32[256,1024]{1,0:T(8,128)}, f32[8,128]{1,0:T(8,128)S(1)}) custom-call(s32[2]{0:T(128)S(1)} %get-tuple-element.291.refs_7_.columns_ref, s32[1]{0:T(128)} %bitcast.14.refs_2_.rank_ref, ...), custom_call_target="tpu_custom_call", output_to_operand_aliasing={{1}: (14, {}), {2}: (15, {})} | custom-call | flops 6000000000 | bytes 1024 | tf_op jit(solution)/shard_map/adam/pallas_call | solution.py:203
  95.0 3.8 %collective-permute-start.20 = (bf16[256,256]{1,0:T(8,128)(2,1)S(1)}, bf16[256,256]{1,0:T(8,128)(2,1)S(1)}, u32[]{:S(2)}, u32[]{:S(2)}) collective-permute-start(bf16[256,256]{1,0:T(8,128)(2,1)S(1)} %collective-permute-done.10.refs_6_.refs_2_), channel_id=1, source_target_pairs={{0,4},{4,0},{8,12},{12,8},{1,5},{5,1},{9,13},{13,9},{2,6},{6,2},{1... | collective-permute-start | bytes 393224 | tf_op jit(solution)/shard_map/ppermute | solution.py:338
  98.9 1.5 %collective-permute-start.24 = (bf16[256,256]{1,0:T(8,128)(2,1)S(1)}, bf16[256,256]{1,0:T(8,128)(2,1)S(1)}, u32[]{:S(2)}, u32[]{:S(2)}) collective-permute-start(bf16[256,256]{1,0:T(8,128)(2,1)S(1)} %get-tuple-element.255.refs_0_), channel_id=1, source_target_pairs={{0,4},{4,0},{8,12},{12,8},{1,5},{5,1},{9,13},{13,9},{2,6},{6,2},{1... | collective-permute-start | bytes 393224 | tf_op jit(solution)/shard_map/ppermute | solution.py:338
  100.9 2.5 %collective-permute-done.21.refs_11_.refs_2_ = bf16[256,256]{1,0:T(8,128)(2,1)S(1)} collective-permute-done((bf16[256,256]{1,0:T(8,128)(2,1)S(1)}, bf16[256,256]{1,0:T(8,128)(2,1)S(1)}, u32[]{:S(2)}, u32[]{:S(2)}) %collective-permute-start.21) | collective-permute-done | bytes 131104 | tf_op jit(solution)/shard_map/ppermute | solution.py:338
  103.4 2.6 %collective-permute-start.25 = (bf16[256,256]{1,0:T(8,128)(2,1)S(1)}, bf16[256,256]{1,0:T(8,128)(2,1)S(1)}, u32[]{:S(2)}, u32[]{:S(2)}) collective-permute-start(bf16[256,256]{1,0:T(8,128)(2,1)S(1)} %get-tuple-element.255.refs_0_), channel_id=1, source_target_pairs={{0,12},{4,8},{8,4},{12,0},{1,13},{5,9},{9,5},{13,1},{2,14},{6,10},... | collective-permute-start | bytes 393224 | tf_op jit(solution)/shard_map/ppermute | solution.py:338
  107.4 8.8 %collective-permute-done.19.refs_5_ = bf16[2048,256]{1,0:T(8,128)(2,1)S(1)} collective-permute-done((bf16[2048,256]{1,0:T(8,128)(2,1)S(1)}, bf16[2048,256]{1,0:T(8,128)(2,1)S(1)}, u32[]{:S(2)}, u32[]{:S(2)}) %collective-permute-start.19) | collective-permute-done | bytes 1048608 | tf_op jit(solution)/shard_map/ppermute | solution.py:338
  117.6 2.2 %place.4 = (bf16[1024,1024]{1,0:T(8,128)(2,1)}, f32[8,128]{1,0:T(8,128)}) custom-call(s32[4]{0:T(128)S(1)} %get-tuple-element.286.refs_0_.places_ref.rows_ref, s32[4]{0:T(128)S(1)} %get-tuple-element.289.refs_6_.columns_ref, bf16[256,512]{1,0:T(8,128)(2,1)S(1)} %get-tuple-element.256.refs_0_, ...), custom_call_target="tpu_custom_call", output_to_operand_aliasing={{0}: (8, {})} | custom-call | flops 1000 | bytes 1024 | tf_op jit(solution)/shard_map/place/pallas_call | solution.py:255
  119.9 2.0 %place.5 = (bf16[1024,1024]{1,0:T(8,128)(2,1)}, f32[8,128]{1,0:T(8,128)}) custom-call(s32[4]{0:T(128)S(1)} %get-tuple-element.286.refs_0_.places_ref.rows_ref, s32[2]{0:T(128)S(1)} %get-tuple-element.291.refs_7_.columns_ref, bf16[256,256]{1,0:T(8,128)(2,1)S(1)} %get-tuple-element.255.refs_0_, ...), custom_call_target="tpu_custom_call", output_to_operand_aliasing={{0}: (6, {})} | custom-call | flops 6000000000 | bytes 1024 | tf_op jit(solution)/shard_map/place/pallas_call | solution.py:255
  (53 shorter events, 12.4 us)
Async XLA Ops:
  1.9 15.0 %collective-permute-start = (bf16[2048,128]{1,0:T(8,128)(2,1)S(1)}, bf16[2048,128]{1,0:T(8,128)(2,1)S(1)}, u32[]{:S(2)}, u32[]{:S(2)}) collective-permute-start(bf16[2048,128]{1,0:T(8,128)(2,1)S(1)} %get-tuple-element.285), channel_id=1, source_target_pairs={{16,0},{0,16},{17,1},{1,17},{18,2},{2,18},{19,3},{3,19},{20,4},{4,... | collective-permute-start | bytes 1572872 | tf_op jit(solution)/shard_map/ppermute | solution.py:35
  5.3 2.2 %copy-start.2 = (bf16[1,2048,1024]{2,1,0:T(8,128)(2,1)S(1)}, bf16[1,2048,1024]{2,1,0:T(8,128)(2,1)}, u32[]{:S(2)}) copy-start(bf16[1,2048,1024]{2,1,0:T(8,128)(2,1)} %param.7) | copy-start | bytes 12582916
  16.9 1.9 %collective-permute-start.1 = (bf16[2048,128]{1,0:T(8,128)(2,1)S(1)}, bf16[2048,128]{1,0:T(8,128)(2,1)S(1)}, u32[]{:S(2)}, u32[]{:S(2)}) collective-permute-start(bf16[2048,128]{1,0:T(8,128)(2,1)S(1)} %collective-permute-done.refs_0_.refs_4_), channel_id=1, source_target_pairs={{0,1},{1,0},{2,3},{3,2},{4,5},{5,4},{6,7},{7,6},{8,9},{9,8},{10,11... | collective-permute-start | bytes 1572872 | tf_op jit(solution)/shard_map/ppermute | solution.py:338
  16.9 14.3 %collective-permute-start.4 = (bf16[2048,128]{1,0:T(8,128)(2,1)S(1)}, bf16[2048,128]{1,0:T(8,128)(2,1)S(1)}, u32[]{:S(2)}, u32[]{:S(2)}) collective-permute-start(bf16[2048,128]{1,0:T(8,128)(2,1)S(1)} %get-tuple-element.284), channel_id=1, source_target_pairs={{16,0},{0,16},{17,1},{1,17},{18,2},{2,18},{19,3},{3,19},{20,4},{4,... | collective-permute-start | bytes 1572872 | tf_op jit(solution)/shard_map/ppermute | solution.py:35
  18.8 22.3 %copy-start.1 = (bf16[1,1024,1024]{2,1,0:T(8,128)(2,1)S(1)}, bf16[1,1024,1024]{2,1,0:T(8,128)(2,1)}, u32[]{:S(2)}) copy-start(bf16[1,1024,1024]{2,1,0:T(8,128)(2,1)} %param.8) | copy-start | bytes 6291460
  18.8 22.3 %copy-start.3 = (f32[1,256,1024]{2,1,0:T(8,128)S(1)}, f32[1,256,1024]{2,1,0:T(8,128)}, u32[]{:S(2)}) copy-start(f32[1,256,1024]{2,1,0:T(8,128)} %param.10) | copy-start | bytes 3145732
  18.8 22.3 %copy-start.4 = (f32[1,256,1024]{2,1,0:T(8,128)S(1)}, f32[1,256,1024]{2,1,0:T(8,128)}, u32[]{:S(2)}) copy-start(f32[1,256,1024]{2,1,0:T(8,128)} %param.11) | copy-start | bytes 3145732
  20.8 10.4 %collective-permute-start.3 = (bf16[512,256]{1,0:T(8,128)(2,1)S(1)}, bf16[512,256]{1,0:T(8,128)(2,1)S(1)}, u32[]{:S(2)}, u32[]{:S(2)}) collective-permute-start(bf16[512,256]{1,0:T(8,128)(2,1)S(1)} %get-tuple-element.153), channel_id=1, source_target_pairs={{0,4},{4,0},{8,12},{12,8},{1,5},{5,1},{9,13},{13,9},{2,6},{6,2},{1... | collective-permute-start | bytes 786440 | tf_op jit(solution)/shard_map/ppermute | solution.py:338
  22.6 13.7 %collective-permute-start.2 = (bf16[2048,128]{1,0:T(8,128)(2,1)S(1)}, bf16[2048,128]{1,0:T(8,128)(2,1)S(1)}, u32[]{:S(2)}, u32[]{:S(2)}) collective-permute-start(bf16[2048,128]{1,0:T(8,128)(2,1)S(1)} %collective-permute-done.refs_0_.refs_4_), channel_id=1, source_target_pairs={{0,2},{1,3},{2,0},{3,1},{4,6},{5,7},{6,4},{7,5},{8,10},{9,11},{10,... | collective-permute-start | bytes 1572872 | tf_op jit(solution)/shard_map/ppermute | solution.py:338
  31.2 5.1 %collective-permute-start.7 = (bf16[2048,128]{1,0:T(8,128)(2,1)S(1)}, bf16[2048,128]{1,0:T(8,128)(2,1)S(1)}, u32[]{:S(2)}, u32[]{:S(2)}) collective-permute-start(bf16[2048,128]{1,0:T(8,128)(2,1)S(1)} %collective-permute-done.4.refs_11_.refs_0_.refs_4_), channel_id=1, source_target_pairs={{0,1},{1,0},{2,3},{3,2},{4,5},{5,4},{6,7},{7,6},{8,9},{9,8},{10,11... | collective-permute-start | bytes 1572872 | tf_op jit(solution)/shard_map/ppermute | solution.py:338
  31.2 9.9 %collective-permute-start.6 = (bf16[256,256]{1,0:T(8,128)(2,1)S(1)}, bf16[256,256]{1,0:T(8,128)(2,1)S(1)}, u32[]{:S(2)}, u32[]{:S(2)}) collective-permute-start(bf16[256,256]{1,0:T(8,128)(2,1)S(1)} %add_convert_fusion.4), channel_id=1, source_target_pairs={{0,8},{4,12},{8,0},{12,4},{1,9},{5,13},{9,1},{13,5},{2,10},{6,14},... | collective-permute-start | bytes 393224 | tf_op jit(solution)/shard_map/ppermute | solution.py:338
  34.1 17.8 %collective-permute-start.8 = (bf16[2048,128]{1,0:T(8,128)(2,1)S(1)}, bf16[2048,128]{1,0:T(8,128)(2,1)S(1)}, u32[]{:S(2)}, u32[]{:S(2)}) collective-permute-start(bf16[2048,128]{1,0:T(8,128)(2,1)S(1)} %collective-permute-done.4.refs_11_.refs_0_.refs_4_), channel_id=1, source_target_pairs={{0,2},{1,3},{2,0},{3,1},{4,6},{5,7},{6,4},{7,5},{8,10},{9,11},{10,... | collective-permute-start | bytes 1572872 | tf_op jit(solution)/shard_map/ppermute | solution.py:338
  36.3 10.6 %collective-permute-start.5 = (bf16[2048,128]{1,0:T(8,128)(2,1)S(1)}, bf16[2048,128]{1,0:T(8,128)(2,1)S(1)}, u32[]{:S(2)}, u32[]{:S(2)}) collective-permute-start(bf16[2048,128]{1,0:T(8,128)(2,1)S(1)} %collective-permute-done.2.refs_13_.refs_2_), channel_id=1, source_target_pairs={{0,1},{1,0},{2,3},{3,2},{4,5},{5,4},{6,7},{7,6},{8,9},{9,8},{10,11... | collective-permute-start | bytes 1572872 | tf_op jit(solution)/shard_map/ppermute | solution.py:338
  42.8 9.0 %collective-permute-start.10 = (bf16[256,256]{1,0:T(8,128)(2,1)S(1)}, bf16[256,256]{1,0:T(8,128)(2,1)S(1)}, u32[]{:S(2)}, u32[]{:S(2)}) collective-permute-start(bf16[256,256]{1,0:T(8,128)(2,1)S(1)} %get-tuple-element.190.refs_0_), channel_id=1, source_target_pairs={{0,8},{4,12},{8,0},{12,4},{1,9},{5,13},{9,1},{13,5},{2,10},{6,14},... | collective-permute-start | bytes 393224 | tf_op jit(solution)/shard_map/ppermute | solution.py:338
  42.8 9.1 %collective-permute-start.9 = (bf16[256,256]{1,0:T(8,128)(2,1)S(1)}, bf16[256,256]{1,0:T(8,128)(2,1)S(1)}, u32[]{:S(2)}, u32[]{:S(2)}) collective-permute-start(bf16[256,256]{1,0:T(8,128)(2,1)S(1)} %get-tuple-element.190.refs_0_), channel_id=1, source_target_pairs={{0,4},{4,0},{8,12},{12,8},{1,5},{5,1},{9,13},{13,9},{2,6},{6,2},{1... | collective-permute-start | bytes 393224 | tf_op jit(solution)/shard_map/ppermute | solution.py:338
  51.9 2.1 %collective-permute-start.11 = (bf16[2048,128]{1,0:T(8,128)(2,1)S(1)}, bf16[2048,128]{1,0:T(8,128)(2,1)S(1)}, u32[]{:S(2)}, u32[]{:S(2)}) collective-permute-start(bf16[2048,128]{1,0:T(8,128)(2,1)S(1)} %collective-permute-done.8.refs_6_.refs_0_.refs_8_), channel_id=1, source_target_pairs={{0,1},{1,0},{2,3},{3,2},{4,5},{5,4},{6,7},{7,6},{8,9},{9,8},{10,11... | collective-permute-start | bytes 1572872 | tf_op jit(solution)/shard_map/ppermute | solution.py:338
  51.9 9.1 %collective-permute-start.17 = (bf16[256,512]{1,0:T(8,128)(2,1)S(1)}, bf16[256,512]{1,0:T(8,128)(2,1)S(1)}, u32[]{:S(2)}, u32[]{:S(2)}) collective-permute-start(bf16[256,512]{1,0:T(8,128)(2,1)S(1)} %get-tuple-element.234), channel_id=1, source_target_pairs={{0,4},{4,0},{8,12},{12,8},{1,5},{5,1},{9,13},{13,9},{2,6},{6,2},{1... | collective-permute-start | bytes 786440 | tf_op jit(solution)/shard_map/ppermute | solution.py:338
  52.1 24.2 %collective-permute-start.16 = (bf16[256,512]{1,0:T(8,128)(2,1)S(1)}, bf16[256,512]{1,0:T(8,128)(2,1)S(1)}, u32[]{:S(2)}, u32[]{:S(2)}) collective-permute-start(bf16[256,512]{1,0:T(8,128)(2,1)S(1)} %get-tuple-element.232), channel_id=1, source_target_pairs={{0,4},{4,0},{8,12},{12,8},{1,5},{5,1},{9,13},{13,9},{2,6},{6,2},{1... | collective-permute-start | bytes 786440 | tf_op jit(solution)/shard_map/ppermute | solution.py:338
  54.0 10.5 %copy-start = (bf16[1,1024,1024]{2,1,0:T(8,128)(2,1)S(1)}, bf16[1,1024,1024]{2,1,0:T(8,128)(2,1)}, u32[]{:S(2)}) copy-start(bf16[1,1024,1024]{2,1,0:T(8,128)(2,1)} %param.9) | copy-start | bytes 6291460
  61.1 16.4 %collective-permute-start.18 = (bf16[256,512]{1,0:T(8,128)(2,1)S(1)}, bf16[256,512]{1,0:T(8,128)(2,1)S(1)}, u32[]{:S(2)}, u32[]{:S(2)}) collective-permute-start(bf16[256,512]{1,0:T(8,128)(2,1)S(1)} %add_convert_fusion.2), channel_id=1, source_target_pairs={{0,8},{4,12},{8,0},{12,4},{1,9},{5,13},{9,1},{13,5},{2,10},{6,14},... | collective-permute-start | bytes 786440 | tf_op jit(solution)/shard_map/ppermute | solution.py:338
  62.7 14.8 %collective-permute-start.13 = (bf16[512,256]{1,0:T(8,128)(2,1)S(1)}, bf16[512,256]{1,0:T(8,128)(2,1)S(1)}, u32[]{:S(2)}, u32[]{:S(2)}) collective-permute-start(bf16[512,256]{1,0:T(8,128)(2,1)S(1)} %get-tuple-element.216), channel_id=1, source_target_pairs={{0,4},{4,0},{8,12},{12,8},{1,5},{5,1},{9,13},{13,9},{2,6},{6,2},{1... | collective-permute-start | bytes 786440 | tf_op jit(solution)/shard_map/ppermute | solution.py:338
  76.3 15.2 %collective-permute-start.15 = (bf16[2048,256]{1,0:T(8,128)(2,1)S(1)}, bf16[2048,256]{1,0:T(8,128)(2,1)S(1)}, u32[]{:S(2)}, u32[]{:S(2)}) collective-permute-start(bf16[2048,256]{1,0:T(8,128)(2,1)S(1)} %get-tuple-element.221), channel_id=1, source_target_pairs={{0,1},{1,0},{2,3},{3,2},{4,5},{5,4},{6,7},{7,6},{8,9},{9,8},{10,11... | collective-permute-start | bytes 3145736 | tf_op jit(solution)/shard_map/ppermute | solution.py:338
  76.4 18.6 %collective-permute-start.12 = (bf16[2048,256]{1,0:T(8,128)(2,1)S(1)}, bf16[2048,256]{1,0:T(8,128)(2,1)S(1)}, u32[]{:S(2)}, u32[]{:S(2)}) collective-permute-start(bf16[2048,256]{1,0:T(8,128)(2,1)S(1)} %get-tuple-element.206), channel_id=1, source_target_pairs={{0,1},{1,0},{2,3},{3,2},{4,5},{5,4},{6,7},{7,6},{8,9},{9,8},{10,11... | collective-permute-start | bytes 3145736 | tf_op jit(solution)/shard_map/ppermute | solution.py:338
  77.5 14.0 %collective-permute-start.14 = (bf16[256,256]{1,0:T(8,128)(2,1)S(1)}, bf16[256,256]{1,0:T(8,128)(2,1)S(1)}, u32[]{:S(2)}, u32[]{:S(2)}) collective-permute-start(bf16[256,256]{1,0:T(8,128)(2,1)S(1)} %add_convert_fusion.3), channel_id=1, source_target_pairs={{0,8},{4,12},{8,0},{12,4},{1,9},{5,13},{9,1},{13,5},{2,10},{6,14},... | collective-permute-start | bytes 393224 | tf_op jit(solution)/shard_map/ppermute | solution.py:338
  81.7 17.2 %collective-permute-start.23 = (bf16[256,512]{1,0:T(8,128)(2,1)S(1)}, bf16[256,512]{1,0:T(8,128)(2,1)S(1)}, u32[]{:S(2)}, u32[]{:S(2)}) collective-permute-start(bf16[256,512]{1,0:T(8,128)(2,1)S(1)} %get-tuple-element.256.refs_0_), channel_id=1, source_target_pairs={{0,8},{4,12},{8,0},{12,4},{1,9},{5,13},{9,1},{13,5},{2,10},{6,14},... | collective-permute-start | bytes 786440 | tf_op jit(solution)/shard_map/ppermute | solution.py:338
  83.0 17.4 %collective-permute-start.22 = (bf16[256,512]{1,0:T(8,128)(2,1)S(1)}, bf16[256,512]{1,0:T(8,128)(2,1)S(1)}, u32[]{:S(2)}, u32[]{:S(2)}) collective-permute-start(bf16[256,512]{1,0:T(8,128)(2,1)S(1)} %get-tuple-element.256.refs_0_), channel_id=1, source_target_pairs={{0,4},{4,0},{8,12},{12,8},{1,5},{5,1},{9,13},{13,9},{2,6},{6,2},{1... | collective-permute-start | bytes 786440 | tf_op jit(solution)/shard_map/ppermute | solution.py:338
  91.8 24.4 %collective-permute-start.19 = (bf16[2048,256]{1,0:T(8,128)(2,1)S(1)}, bf16[2048,256]{1,0:T(8,128)(2,1)S(1)}, u32[]{:S(2)}, u32[]{:S(2)}) collective-permute-start(bf16[2048,256]{1,0:T(8,128)(2,1)S(1)} %add_convert_fusion.1), channel_id=1, source_target_pairs={{0,2},{1,3},{2,0},{3,1},{4,6},{5,7},{6,4},{7,5},{8,10},{9,11},{10,... | collective-permute-start | bytes 3145736 | tf_op jit(solution)/shard_map/ppermute | solution.py:338
  95.0 8.4 %collective-permute-start.21 = (bf16[256,256]{1,0:T(8,128)(2,1)S(1)}, bf16[256,256]{1,0:T(8,128)(2,1)S(1)}, u32[]{:S(2)}, u32[]{:S(2)}) collective-permute-start(bf16[256,256]{1,0:T(8,128)(2,1)S(1)} %get-tuple-element.255.refs_0_), channel_id=1, source_target_pairs={{0,8},{4,12},{8,0},{12,4},{1,9},{5,13},{9,1},{13,5},{2,10},{6,14},... | collective-permute-start | bytes 393224 | tf_op jit(solution)/shard_map/ppermute | solution.py:338
  95.0 10.9 %collective-permute-start.20 = (bf16[256,256]{1,0:T(8,128)(2,1)S(1)}, bf16[256,256]{1,0:T(8,128)(2,1)S(1)}, u32[]{:S(2)}, u32[]{:S(2)}) collective-permute-start(bf16[256,256]{1,0:T(8,128)(2,1)S(1)} %collective-permute-done.10.refs_6_.refs_2_), channel_id=1, source_target_pairs={{0,4},{4,0},{8,12},{12,8},{1,5},{5,1},{9,13},{13,9},{2,6},{6,2},{1... | collective-permute-start | bytes 393224 | tf_op jit(solution)/shard_map/ppermute | solution.py:338
  98.9 21.0 %collective-permute-start.24 = (bf16[256,256]{1,0:T(8,128)(2,1)S(1)}, bf16[256,256]{1,0:T(8,128)(2,1)S(1)}, u32[]{:S(2)}, u32[]{:S(2)}) collective-permute-start(bf16[256,256]{1,0:T(8,128)(2,1)S(1)} %get-tuple-element.255.refs_0_), channel_id=1, source_target_pairs={{0,4},{4,0},{8,12},{12,8},{1,5},{5,1},{9,13},{13,9},{2,6},{6,2},{1... | collective-permute-start | bytes 393224 | tf_op jit(solution)/shard_map/ppermute | solution.py:338
  100.4 17.2 %collective-permute-start.26 = (bf16[256,512]{1,0:T(8,128)(2,1)S(1)}, bf16[256,512]{1,0:T(8,128)(2,1)S(1)}, u32[]{:S(2)}, u32[]{:S(2)}) collective-permute-start(bf16[256,512]{1,0:T(8,128)(2,1)S(1)} %collective-permute-done.23.refs_9_.refs_2_), channel_id=1, source_target_pairs={{0,4},{4,0},{8,12},{12,8},{1,5},{5,1},{9,13},{13,9},{2,6},{6,2},{1... | collective-permute-start | bytes 786440 | tf_op jit(solution)/shard_map/ppermute | solution.py:338
  103.4 16.5 %collective-permute-start.25 = (bf16[256,256]{1,0:T(8,128)(2,1)S(1)}, bf16[256,256]{1,0:T(8,128)(2,1)S(1)}, u32[]{:S(2)}, u32[]{:S(2)}) collective-permute-start(bf16[256,256]{1,0:T(8,128)(2,1)S(1)} %get-tuple-element.255.refs_0_), channel_id=1, source_target_pairs={{0,12},{4,8},{8,4},{12,0},{1,13},{5,9},{9,5},{13,1},{2,14},{6,10},... | collective-permute-start | bytes 393224 | tf_op jit(solution)/shard_map/ppermute | solution.py:338

commit v7 on v6

--- a/solution.py
+++ b/solution.py
@@ -13,11 +13,11 @@
 TILE = 256
 CHUNKS = (((0, 0), (1, 0)), ((0, 1), (1, 1), (2, 0), (3, 0)), ((2, 1), (3, 1)))
 SUMS = ("two", "tri", "two",)
-GATHERS = ("two", "two", "one",)
+GATHERS = ("two", "two", "two",)
 PLAN = (
     "h0", "b00", "b10", "t0", "b01", "m0", "b20", "b11", "r0", "a0", "b30", "t1", "g0",
-    "e0", "b21", "b31", "t2", "m1", "r1", "a1", "p0", "m2", "r2", "x0", "a2", "u0", "g1",
-    "e1", "g2", "l0", "x1", "l1", "l2",
+    "e0", "b21", "b31", "t2", "m1", "r1", "a1", "p0", "m2", "r2", "x0", "a2", "u0", "e1",
+    "g1", "e2", "g2", "l0", "q0", "l1", "x1", "l2", "q1", "q2",
 )
 ANYWHERE = pl.BlockSpec(memory_space=pl.ANY)
 INSIDE = pl.BlockSpec(memory_space=pltpu.VMEM)
@@ -25,7 +25,7 @@
 COSTS = {
     "h0": 40000000000, "t0": 10000000000, "a0": 10000000000, "t1": 40000000000,
     "t2": 6000000000, "a1": 10000000000, "p0": 3000000000, "a2": 6000000000, "l0": 4199999999,
-    "l1": 1000, "l2": 6000000000,
+    "q0": 3000000000, "l1": 1000, "l2": 80000000000, "q1": 3000000000, "q2": 3000000000,
 }
 
 

time: 122 us -> 119 us (0.975)
  starting transfers between devices: 35.9 us -> 30.7 us
  Pallas kernels: 35.6 us -> 40.8 us
  waiting for transfers between devices: 43.9 us -> 40.9 us
    ppermute x25, starting transfers between devices: 31.2 us -> 25.9 us  [swapped(): return lax.ppermute(value, axis, [(i, i ^ distance) for i in range(4)])]
    pallas_call x3 -> x6, Pallas kernels: 5.6 us -> 10.8 us  [place_rows(): pl.pallas_call(kernel, grid_spec=pltpu.PrefetchScalarGridSpec(num_scalar_...]
    ppermute x25, waiting for transfers between devices: 32.5 us -> 29.5 us  [swapped(): return lax.ppermute(value, axis, [(i, i ^ distance) for i in range(4)])]
  transfers between devices with their start and end apart: 27 -> 27, of which waited for: 12 -> 15; matrix products, arithmetic and copies ran while one was open for 2% -> 2% of each run, Pallas kernels for 28% -> 33%
where the time goes in v7:
time: 119 us
  waiting for transfers between devices  40.9 us (34%)
  Pallas kernels  40.8 us (34%)
  starting transfers between devices  30.7 us (26%)
  local copies, waits for them, and re-layouts  3.57 us (3%)
  other arithmetic  2.05 us (2%)
    ppermute x25, waiting for transfers between devices, swapped(): return lax.ppermute(value, axis, [(i, i ^ distance) for i in range(4)])  29.5 us
    ppermute x25, starting transfers between devices, swapped(): return lax.ppermute(value, axis, [(i, i ^ distance) for i in range(4)])  25.9 us
    pallas_call x1, Pallas kernels, partials(): pl.pallas_call(kernel, grid_spec=pltpu.PrefetchScalarGridSpec(num_scalar_...  11.9 us
    ppermute x2, waiting for transfers between devices, from_behind(): return lax.ppermute(block, axis, route)  11.5 us
    pallas_call x6, Pallas kernels, place_rows(): pl.pallas_call(kernel, grid_spec=pltpu.PrefetchScalarGridSpec(num_scalar_...  10.8 us
    pallas_call x3, Pallas kernels, terms(): pl.pallas_call(kernel, in_specs=[pl.BlockSpec(memory_space=pltpu.SMEM)] +...  7.22 us
    pallas_call x3, Pallas kernels, adam_chunk(): pl.pallas_call(kernel, grid_spec=pltpu.PrefetchScalarGridSpec(num_scalar_...  5.84 us
    pallas_call x1, Pallas kernels, prepare(): pl.pallas_call(kernel, grid=(tokens // TILE,), in_specs=[pl.BlockSpec((TI...  5.02 us
  transfers between devices with their start and end apart: 27, of which 15 were waited for; matrix products, arithmetic and copies ran while one was open for 2% of the time, Pallas kernels for 33%

profile of v7, /device:TPU:0, one launch (start us, length us, event | category | flops | bytes accessed | tf_op | source)
XLA Modules:
  0.0 118.8 jit_solution(6311269289547711416)
XLA Ops:
  1.9 3.0 %collective-permute-start = (bf16[2048,128]{1,0:T(8,128)(2,1)S(1)}, bf16[2048,128]{1,0:T(8,128)(2,1)S(1)}, u32[]{:S(2)}, u32[]{:S(2)}) collective-permute-start(bf16[2048,128]{1,0:T(8,128)(2,1)S(1)} %get-tuple-element.311), channel_id=1, source_target_pairs={{16,0},{0,16},{17,1},{1,17},{18,2},{2,18},{19,3},{3,19},{20,4},{4,... | collective-permute-start | bytes 1572872 | tf_op jit(solution)/shard_map/ppermute | solution.py:35
  5.3 2.2 %copy-done.2 = bf16[1,2048,1024]{2,1,0:T(8,128)(2,1)S(1)} copy-done((bf16[1,2048,1024]{2,1,0:T(8,128)(2,1)S(1)}, bf16[1,2048,1024]{2,1,0:T(8,128)(2,1)}, u32[]{:S(2)}) %copy-start.2) | copy-done | bytes 4194328
  7.4 5.0 %prepare.1 = (bf16[1024,2048]{1,0:T(8,128)(2,1)S(1)}, bf16[2048,1024]{1,0:T(8,128)(2,1)S(1)}, f32[8,128]{1,0:T(8,128)S(1)}) custom-call(bf16[2048,1024]{1,0:T(8,128)(2,1)S(1)} %bitcast.32, s32[4]{0:T(128)S(1)} %get-tuple-element.312.refs_0_.places_ref.rows_ref, s32[4]{0:T(128)S(1)} %get-tuple-element.313.refs_1_.places_ref, s32[1]{0:T(128)} %bitcast.14.refs_2_.rank_ref, ...), custom_call_target="tpu_custom_call" | custom-call | flops 40000000000 | bytes 1024 | tf_op jit(solution)/shard_map/prepare/pallas_call | solution.py:123
  12.5 4.4 %collective-permute-done.refs_0_.refs_4_ = bf16[2048,128]{1,0:T(8,128)(2,1)S(1)} collective-permute-done((bf16[2048,128]{1,0:T(8,128)(2,1)S(1)}, bf16[2048,128]{1,0:T(8,128)(2,1)S(1)}, u32[]{:S(2)}, u32[]{:S(2)}) %collective-permute-start) | collective-permute-done | bytes 524320 | tf_op jit(solution)/shard_map/ppermute | solution.py:35
  16.9 1.7 %collective-permute-start.4 = (bf16[2048,128]{1,0:T(8,128)(2,1)S(1)}, bf16[2048,128]{1,0:T(8,128)(2,1)S(1)}, u32[]{:S(2)}, u32[]{:S(2)}) collective-permute-start(bf16[2048,128]{1,0:T(8,128)(2,1)S(1)} %get-tuple-element.310), channel_id=1, source_target_pairs={{16,0},{0,16},{17,1},{1,17},{18,2},{2,18},{19,3},{3,19},{20,4},{4,... | collective-permute-start | bytes 1572872 | tf_op jit(solution)/shard_map/ppermute | solution.py:35
  18.8 2.0 %terms.3 = (bf16[256,256]{1,0:T(8,128)(2,1)S(1)}, bf16[256,256]{1,0:T(8,128)(2,1)S(1)}, bf16[512,256]{1,0:T(8,128)(2,1)S(1)}, f32[8,128]{1,0:T(8,128)S(1)}) custom-call(s32[4]{0:T(128)S(1)} %get-tuple-element.313.refs_1_.places_ref, bf16[1024,2048]{1,0:T(8,128)(2,1)S(1)} %get-tuple-element.161.hidden_ref, ...), custom_call_target="tpu_custom_call" | custom-call | flops 10000000000 | bytes 1024 | tf_op jit(solution)/shard_map/terms/pallas_call | solution.py:165
  20.8 1.9 %collective-permute-start.3 = (bf16[512,256]{1,0:T(8,128)(2,1)S(1)}, bf16[512,256]{1,0:T(8,128)(2,1)S(1)}, u32[]{:S(2)}, u32[]{:S(2)}) collective-permute-start(bf16[512,256]{1,0:T(8,128)(2,1)S(1)} %get-tuple-element.166), channel_id=1, source_target_pairs={{0,4},{4,0},{8,12},{12,8},{1,5},{5,1},{9,13},{13,9},{2,6},{6,2},{1... | collective-permute-start | bytes 786440 | tf_op jit(solution)/shard_map/ppermute | solution.py:338
  24.1 7.1 %collective-permute-done.4.refs_11_.refs_0_.refs_4_ = bf16[2048,128]{1,0:T(8,128)(2,1)S(1)} collective-permute-done((bf16[2048,128]{1,0:T(8,128)(2,1)S(1)}, bf16[2048,128]{1,0:T(8,128)(2,1)S(1)}, u32[]{:S(2)}, u32[]{:S(2)}) %collective-permute-start.4) | collective-permute-done | bytes 524320 | tf_op jit(solution)/shard_map/ppermute | solution.py:35
  31.2 2.9 %collective-permute-start.6 = (bf16[256,256]{1,0:T(8,128)(2,1)S(1)}, bf16[256,256]{1,0:T(8,128)(2,1)S(1)}, u32[]{:S(2)}, u32[]{:S(2)}) collective-permute-start(bf16[256,256]{1,0:T(8,128)(2,1)S(1)} %add_convert_fusion.4), channel_id=1, source_target_pairs={{0,8},{4,12},{8,0},{12,4},{1,9},{5,13},{9,1},{13,5},{2,10},{6,14},... | collective-permute-start | bytes 393224 | tf_op jit(solution)/shard_map/ppermute | solution.py:338
  36.3 4.8 %collective-permute-done.6.refs_1_.refs_15_ = bf16[256,256]{1,0:T(8,128)(2,1)S(1)} collective-permute-done((bf16[256,256]{1,0:T(8,128)(2,1)S(1)}, bf16[256,256]{1,0:T(8,128)(2,1)S(1)}, u32[]{:S(2)}, u32[]{:S(2)}) %collective-permute-start.6) | collective-permute-done | bytes 131104 | tf_op jit(solution)/shard_map/ppermute | solution.py:338
  41.1 1.7 %adam.3 = (bf16[256,256]{1,0:T(8,128)(2,1)S(1)}, f32[256,1024]{1,0:T(8,128)}, f32[256,1024]{1,0:T(8,128)}, f32[8,128]{1,0:T(8,128)S(1)}) custom-call(s32[2]{0:T(128)S(1)} %get-tuple-element.316.refs_5_.columns_ref, s32[1]{0:T(128)} %bitcast.14.refs_2_.rank_ref, bf16[256,256]{1,0:T(8,128)(2,1)S(1)} %get-tuple-element.174.refs_0_, ...), custom_call_target="tpu_custom_call" | custom-call | flops 10000000000 | bytes 1024 | tf_op jit(solution)/shard_map/adam/pallas_call | solution.py:203
  42.8 4.1 %collective-permute-start.9 = (bf16[256,256]{1,0:T(8,128)(2,1)S(1)}, bf16[256,256]{1,0:T(8,128)(2,1)S(1)}, u32[]{:S(2)}, u32[]{:S(2)}) collective-permute-start(bf16[256,256]{1,0:T(8,128)(2,1)S(1)} %get-tuple-element.203.refs_0_), channel_id=1, source_target_pairs={{0,4},{4,0},{8,12},{12,8},{1,5},{5,1},{9,13},{13,9},{2,6},{6,2},{1... | collective-permute-start | bytes 393224 | tf_op jit(solution)/shard_map/ppermute | solution.py:338
  46.9 3.3 %terms.4 = (bf16[256,512]{1,0:T(8,128)(2,1)S(1)}, bf16[256,512]{1,0:T(8,128)(2,1)S(1)}, bf16[256,512]{1,0:T(8,128)(2,1)S(1)}, bf16[256,512]{1,0:T(8,128)(2,1)S(1)}, f32[8,128]{1,0:T(8,128)S(1)}) custom-call(s32[4]{0:T(128)S(1)} %get-tuple-element.312.refs_0_.places_ref.rows_ref, bf16[1024,2048]{1,0:T(8,128)(2,1)S(1)} %get-tuple-element.161.hidden_ref, ...), custom_call_target="tpu_custom_call" | custom-call | flops 40000000000 | bytes 1024 | tf_op jit(solution)/shard_map/terms/pallas_call | solution.py:165
  52.1 1.9 %collective-permute-start.16 = (bf16[256,512]{1,0:T(8,128)(2,1)S(1)}, bf16[256,512]{1,0:T(8,128)(2,1)S(1)}, u32[]{:S(2)}, u32[]{:S(2)}) collective-permute-start(bf16[256,512]{1,0:T(8,128)(2,1)S(1)} %get-tuple-element.245), channel_id=1, source_target_pairs={{0,4},{4,0},{8,12},{12,8},{1,5},{5,1},{9,13},{13,9},{2,6},{6,2},{1... | collective-permute-start | bytes 786440 | tf_op jit(solution)/shard_map/ppermute | solution.py:338
  54.0 2.0 %terms.5 = (bf16[256,256]{1,0:T(8,128)(2,1)S(1)}, bf16[256,256]{1,0:T(8,128)(2,1)S(1)}, bf16[512,256]{1,0:T(8,128)(2,1)S(1)}, f32[8,128]{1,0:T(8,128)S(1)}) custom-call(s32[4]{0:T(128)S(1)} %get-tuple-element.313.refs_1_.places_ref, bf16[1024,2048]{1,0:T(8,128)(2,1)S(1)} %get-tuple-element.161.hidden_ref, ...), custom_call_target="tpu_custom_call" | custom-call | flops 6000000000 | bytes 1024 | tf_op jit(solution)/shard_map/terms/pallas_call | solution.py:165
  55.9 5.1 %collective-permute-done.17.refs_9_ = bf16[256,512]{1,0:T(8,128)(2,1)S(1)} collective-permute-done((bf16[256,512]{1,0:T(8,128)(2,1)S(1)}, bf16[256,512]{1,0:T(8,128)(2,1)S(1)}, u32[]{:S(2)}, u32[]{:S(2)}) %collective-permute-start.17) | collective-permute-done | bytes 262176 | tf_op jit(solution)/shard_map/ppermute | solution.py:338
  62.7 1.7 %collective-permute-start.13 = (bf16[512,256]{1,0:T(8,128)(2,1)S(1)}, bf16[512,256]{1,0:T(8,128)(2,1)S(1)}, u32[]{:S(2)}, u32[]{:S(2)}) collective-permute-start(bf16[512,256]{1,0:T(8,128)(2,1)S(1)} %get-tuple-element.229), channel_id=1, source_target_pairs={{0,4},{4,0},{8,12},{12,8},{1,5},{5,1},{9,13},{13,9},{2,6},{6,2},{1... | collective-permute-start | bytes 786440 | tf_op jit(solution)/shard_map/ppermute | solution.py:338
  64.4 11.9 %partials.1 = (bf16[2048,256]{1,0:T(8,128)(2,1)S(1)}, bf16[2048,256]{1,0:T(8,128)(2,1)S(1)}, bf16[2048,256]{1,0:T(8,128)(2,1)S(1)}, bf16[2048,256]{1,0:T(8,128)(2,1)S(1)}, f32[8,128]{1,0:T(8,128)S(1)}) custom-call(s32[8]{0:T(128)S(1)} %stack.89.refs_4_.where_ref, s32[4]{0:T(128)S(1)} %get-tuple-element.314.refs_3_.order_ref, ...), custom_call_target="tpu_custom_call" | custom-call | flops 3000000000 | bytes 1024 | tf_op jit(solution)/shard_map/partials/pallas_call | solution.py:299
  77.5 1.7 %collective-permute-start.14 = (bf16[256,256]{1,0:T(8,128)(2,1)S(1)}, bf16[256,256]{1,0:T(8,128)(2,1)S(1)}, u32[]{:S(2)}, u32[]{:S(2)}) collective-permute-start(bf16[256,256]{1,0:T(8,128)(2,1)S(1)} %add_convert_fusion.3), channel_id=1, source_target_pairs={{0,8},{4,12},{8,0},{12,4},{1,9},{5,13},{9,1},{13,5},{2,10},{6,14},... | collective-permute-start | bytes 393224 | tf_op jit(solution)/shard_map/ppermute | solution.py:338
  79.2 2.5 %adam.4 = (bf16[256,512]{1,0:T(8,128)(2,1)S(1)}, f32[256,1024]{1,0:T(8,128)}, f32[256,1024]{1,0:T(8,128)}, f32[8,128]{1,0:T(8,128)}) custom-call(s32[4]{0:T(128)S(1)} %get-tuple-element.315.refs_6_.columns_ref, s32[1]{0:T(128)} %bitcast.14.refs_2_.rank_ref, ...), custom_call_target="tpu_custom_call", output_to_operand_aliasing={{1}: (14, {}), {2}: (15, {})} | custom-call | flops 10000000000 | bytes 1024 | tf_op jit(solution)/shard_map/adam/pallas_call | solution.py:203
  83.4 3.3 %collective-permute-done.14.refs_1_.refs_10_ = bf16[256,256]{1,0:T(8,128)(2,1)S(1)} collective-permute-done((bf16[256,256]{1,0:T(8,128)(2,1)S(1)}, bf16[256,256]{1,0:T(8,128)(2,1)S(1)}, u32[]{:S(2)}, u32[]{:S(2)}) %collective-permute-start.14) | collective-permute-done | bytes 131104 | tf_op jit(solution)/shard_map/ppermute | solution.py:338
  88.5 1.7 %adam.5 = (bf16[256,256]{1,0:T(8,128)(2,1)S(1)}, f32[256,1024]{1,0:T(8,128)}, f32[256,1024]{1,0:T(8,128)}, f32[8,128]{1,0:T(8,128)S(1)}) custom-call(s32[2]{0:T(128)S(1)} %get-tuple-element.317.refs_7_.columns_ref, s32[1]{0:T(128)} %bitcast.14.refs_2_.rank_ref, ...), custom_call_target="tpu_custom_call", output_to_operand_aliasing={{1}: (14, {}), {2}: (15, {})} | custom-call | flops 6000000000 | bytes 1024 | tf_op jit(solution)/shard_map/adam/pallas_call | solution.py:203
  90.2 3.0 %collective-permute-start.23 = (bf16[256,256]{1,0:T(8,128)(2,1)S(1)}, bf16[256,256]{1,0:T(8,128)(2,1)S(1)}, u32[]{:S(2)}, u32[]{:S(2)}) collective-permute-start(bf16[256,256]{1,0:T(8,128)(2,1)S(1)} %get-tuple-element.275.refs_0_), channel_id=1, source_target_pairs={{0,8},{4,12},{8,0},{12,4},{1,9},{5,13},{9,1},{13,5},{2,10},{6,14},... | collective-permute-start | bytes 393224 | tf_op jit(solution)/shard_map/ppermute | solution.py:338
  93.2 4.0 %collective-permute-done.20.refs_9_.refs_1_ = bf16[256,512]{1,0:T(8,128)(2,1)S(1)} collective-permute-done((bf16[256,512]{1,0:T(8,128)(2,1)S(1)}, bf16[256,512]{1,0:T(8,128)(2,1)S(1)}, u32[]{:S(2)}, u32[]{:S(2)}) %collective-permute-start.20) | collective-permute-done | bytes 262176 | tf_op jit(solution)/shard_map/ppermute | solution.py:338
  97.2 3.6 %collective-permute-done.21.refs_10_.refs_2_ = bf16[256,512]{1,0:T(8,128)(2,1)S(1)} collective-permute-done((bf16[256,512]{1,0:T(8,128)(2,1)S(1)}, bf16[256,512]{1,0:T(8,128)(2,1)S(1)}, u32[]{:S(2)}, u32[]{:S(2)}) %collective-permute-start.21) | collective-permute-done | bytes 262176 | tf_op jit(solution)/shard_map/ppermute | solution.py:338
  100.8 2.5 %collective-permute-done.24.refs_11_.refs_1_ = bf16[256,256]{1,0:T(8,128)(2,1)S(1)} collective-permute-done((bf16[256,256]{1,0:T(8,128)(2,1)S(1)}, bf16[256,256]{1,0:T(8,128)(2,1)S(1)}, u32[]{:S(2)}, u32[]{:S(2)}) %collective-permute-start.24) | collective-permute-done | bytes 131104 | tf_op jit(solution)/shard_map/ppermute | solution.py:338
  103.5 1.9 %place.6 = (bf16[1024,1024]{1,0:T(8,128)(2,1)}, f32[8,128]{1,0:T(8,128)}) custom-call(s32[4]{0:T(128)S(1)} %get-tuple-element.312.refs_0_.places_ref.rows_ref, s32[2]{0:T(128)S(1)} %get-tuple-element.316.refs_5_.columns_ref, bf16[256,256]{1,0:T(8,128)(2,1)S(1)} %get-tuple-element.203.refs_0_, bf16[256,256]{1,0:T(8,128)(2,1)S(1)} %collective-permute-done.9.refs_7_.refs_1_, ...), custom_call_target="tpu_custom_call" | custom-call | flops 4200000000 | bytes 1024 | tf_op jit(solution)/shard_map/place/pallas_call | solution.py:255
  106.1 1.8 %place.7 = (bf16[1024,1024]{1,0:T(8,128)(2,1)}, f32[8,128]{1,0:T(8,128)}) custom-call(s32[4]{0:T(128)S(1)} %get-tuple-element.312.refs_0_.places_ref.rows_ref, s32[2]{0:T(128)S(1)} %get-tuple-element.316.refs_5_.columns_ref, bf16[256,256]{1,0:T(8,128)(2,1)S(1)} %collective-permute-done.22.refs_0_, ...), custom_call_target="tpu_custom_call", output_to_operand_aliasing={{0}: (3, {})} | custom-call | flops 3000000000 | bytes 1024 | tf_op jit(solution)/shard_map/place/pallas_call | solution.py:255
  109.5 2.3 %collective-permute-done.19.refs_4_ = bf16[2048,256]{1,0:T(8,128)(2,1)S(1)} collective-permute-done((bf16[2048,256]{1,0:T(8,128)(2,1)S(1)}, bf16[2048,256]{1,0:T(8,128)(2,1)S(1)}, u32[]{:S(2)}, u32[]{:S(2)}) %collective-permute-start.19) | collective-permute-done | bytes 1048608 | tf_op jit(solution)/shard_map/ppermute | solution.py:338
  111.8 1.9 %place.9 = (bf16[1024,1024]{1,0:T(8,128)(2,1)}, f32[8,128]{1,0:T(8,128)}) custom-call(s32[4]{0:T(128)S(1)} %get-tuple-element.312.refs_0_.places_ref.rows_ref, s32[2]{0:T(128)S(1)} %get-tuple-element.317.refs_7_.columns_ref, bf16[256,256]{1,0:T(8,128)(2,1)S(1)} %get-tuple-element.275.refs_0_, ...), custom_call_target="tpu_custom_call", output_to_operand_aliasing={{0}: (7, {})} | custom-call | flops 80000000000 | bytes 1024 | tf_op jit(solution)/shard_map/place/pallas_call | solution.py:255
  115.1 1.9 %place.10 = (bf16[1024,1024]{1,0:T(8,128)(2,1)}, f32[8,128]{1,0:T(8,128)}) custom-call(s32[4]{0:T(128)S(1)} %get-tuple-element.312.refs_0_.places_ref.rows_ref, s32[4]{0:T(128)S(1)} %get-tuple-element.315.refs_6_.columns_ref, bf16[256,512]{1,0:T(8,128)(2,1)S(1)} %collective-permute-done.26.refs_0_, ...), custom_call_target="tpu_custom_call", output_to_operand_aliasing={{0}: (3, {})} | custom-call | flops 3000000000 | bytes 1024 | tf_op jit(solution)/shard_map/place/pallas_call | solution.py:255
  117.0 1.8 %place.11 = (bf16[1024,1024]{1,0:T(8,128)(2,1)}, f32[8,128]{1,0:T(8,128)}) custom-call(s32[4]{0:T(128)S(1)} %get-tuple-element.312.refs_0_.places_ref.rows_ref, s32[2]{0:T(128)S(1)} %get-tuple-element.317.refs_7_.columns_ref, bf16[256,256]{1,0:T(8,128)(2,1)S(1)} %collective-permute-done.25.refs_0_, ...), custom_call_target="tpu_custom_call", output_to_operand_aliasing={{0}: (3, {})} | custom-call | flops 3000000000 | bytes 1024 | tf_op jit(solution)/shard_map/place/pallas_call | solution.py:255
  (56 shorter events, 17.6 us)
Async XLA Ops:
  1.9 15.0 %collective-permute-start = (bf16[2048,128]{1,0:T(8,128)(2,1)S(1)}, bf16[2048,128]{1,0:T(8,128)(2,1)S(1)}, u32[]{:S(2)}, u32[]{:S(2)}) collective-permute-start(bf16[2048,128]{1,0:T(8,128)(2,1)S(1)} %get-tuple-element.311), channel_id=1, source_target_pairs={{16,0},{0,16},{17,1},{1,17},{18,2},{2,18},{19,3},{3,19},{20,4},{4,... | collective-permute-start | bytes 1572872 | tf_op jit(solution)/shard_map/ppermute | solution.py:35
  5.3 2.2 %copy-start.2 = (bf16[1,2048,1024]{2,1,0:T(8,128)(2,1)S(1)}, bf16[1,2048,1024]{2,1,0:T(8,128)(2,1)}, u32[]{:S(2)}) copy-start(bf16[1,2048,1024]{2,1,0:T(8,128)(2,1)} %param.7) | copy-start | bytes 12582916
  16.9 1.9 %collective-permute-start.1 = (bf16[2048,128]{1,0:T(8,128)(2,1)S(1)}, bf16[2048,128]{1,0:T(8,128)(2,1)S(1)}, u32[]{:S(2)}, u32[]{:S(2)}) collective-permute-start(bf16[2048,128]{1,0:T(8,128)(2,1)S(1)} %collective-permute-done.refs_0_.refs_4_), channel_id=1, source_target_pairs={{0,1},{1,0},{2,3},{3,2},{4,5},{5,4},{6,7},{7,6},{8,9},{9,8},{10,11... | collective-permute-start | bytes 1572872 | tf_op jit(solution)/shard_map/ppermute | solution.py:338
  16.9 14.3 %collective-permute-start.4 = (bf16[2048,128]{1,0:T(8,128)(2,1)S(1)}, bf16[2048,128]{1,0:T(8,128)(2,1)S(1)}, u32[]{:S(2)}, u32[]{:S(2)}) collective-permute-start(bf16[2048,128]{1,0:T(8,128)(2,1)S(1)} %get-tuple-element.310), channel_id=1, source_target_pairs={{16,0},{0,16},{17,1},{1,17},{18,2},{2,18},{19,3},{3,19},{20,4},{4,... | collective-permute-start | bytes 1572872 | tf_op jit(solution)/shard_map/ppermute | solution.py:35
  18.8 22.3 %copy-start.1 = (bf16[1,1024,1024]{2,1,0:T(8,128)(2,1)S(1)}, bf16[1,1024,1024]{2,1,0:T(8,128)(2,1)}, u32[]{:S(2)}) copy-start(bf16[1,1024,1024]{2,1,0:T(8,128)(2,1)} %param.8) | copy-start | bytes 6291460
  18.8 22.3 %copy-start.3 = (f32[1,256,1024]{2,1,0:T(8,128)S(1)}, f32[1,256,1024]{2,1,0:T(8,128)}, u32[]{:S(2)}) copy-start(f32[1,256,1024]{2,1,0:T(8,128)} %param.10) | copy-start | bytes 3145732
  18.8 22.3 %copy-start.4 = (f32[1,256,1024]{2,1,0:T(8,128)S(1)}, f32[1,256,1024]{2,1,0:T(8,128)}, u32[]{:S(2)}) copy-start(f32[1,256,1024]{2,1,0:T(8,128)} %param.11) | copy-start | bytes 3145732
  20.8 10.4 %collective-permute-start.3 = (bf16[512,256]{1,0:T(8,128)(2,1)S(1)}, bf16[512,256]{1,0:T(8,128)(2,1)S(1)}, u32[]{:S(2)}, u32[]{:S(2)}) collective-permute-start(bf16[512,256]{1,0:T(8,128)(2,1)S(1)} %get-tuple-element.166), channel_id=1, source_target_pairs={{0,4},{4,0},{8,12},{12,8},{1,5},{5,1},{9,13},{13,9},{2,6},{6,2},{1... | collective-permute-start | bytes 786440 | tf_op jit(solution)/shard_map/ppermute | solution.py:338
  22.6 13.7 %collective-permute-start.2 = (bf16[2048,128]{1,0:T(8,128)(2,1)S(1)}, bf16[2048,128]{1,0:T(8,128)(2,1)S(1)}, u32[]{:S(2)}, u32[]{:S(2)}) collective-permute-start(bf16[2048,128]{1,0:T(8,128)(2,1)S(1)} %collective-permute-done.refs_0_.refs_4_), channel_id=1, source_target_pairs={{0,2},{1,3},{2,0},{3,1},{4,6},{5,7},{6,4},{7,5},{8,10},{9,11},{10,... | collective-permute-start | bytes 1572872 | tf_op jit(solution)/shard_map/ppermute | solution.py:338
  31.2 5.1 %collective-permute-start.7 = (bf16[2048,128]{1,0:T(8,128)(2,1)S(1)}, bf16[2048,128]{1,0:T(8,128)(2,1)S(1)}, u32[]{:S(2)}, u32[]{:S(2)}) collective-permute-start(bf16[2048,128]{1,0:T(8,128)(2,1)S(1)} %collective-permute-done.4.refs_11_.refs_0_.refs_4_), channel_id=1, source_target_pairs={{0,1},{1,0},{2,3},{3,2},{4,5},{5,4},{6,7},{7,6},{8,9},{9,8},{10,11... | collective-permute-start | bytes 1572872 | tf_op jit(solution)/shard_map/ppermute | solution.py:338
  31.2 9.9 %collective-permute-start.6 = (bf16[256,256]{1,0:T(8,128)(2,1)S(1)}, bf16[256,256]{1,0:T(8,128)(2,1)S(1)}, u32[]{:S(2)}, u32[]{:S(2)}) collective-permute-start(bf16[256,256]{1,0:T(8,128)(2,1)S(1)} %add_convert_fusion.4), channel_id=1, source_target_pairs={{0,8},{4,12},{8,0},{12,4},{1,9},{5,13},{9,1},{13,5},{2,10},{6,14},... | collective-permute-start | bytes 393224 | tf_op jit(solution)/shard_map/ppermute | solution.py:338
  34.1 17.8 %collective-permute-start.8 = (bf16[2048,128]{1,0:T(8,128)(2,1)S(1)}, bf16[2048,128]{1,0:T(8,128)(2,1)S(1)}, u32[]{:S(2)}, u32[]{:S(2)}) collective-permute-start(bf16[2048,128]{1,0:T(8,128)(2,1)S(1)} %collective-permute-done.4.refs_11_.refs_0_.refs_4_), channel_id=1, source_target_pairs={{0,2},{1,3},{2,0},{3,1},{4,6},{5,7},{6,4},{7,5},{8,10},{9,11},{10,... | collective-permute-start | bytes 1572872 | tf_op jit(solution)/shard_map/ppermute | solution.py:338
  36.3 10.6 %collective-permute-start.5 = (bf16[2048,128]{1,0:T(8,128)(2,1)S(1)}, bf16[2048,128]{1,0:T(8,128)(2,1)S(1)}, u32[]{:S(2)}, u32[]{:S(2)}) collective-permute-start(bf16[2048,128]{1,0:T(8,128)(2,1)S(1)} %collective-permute-done.2.refs_13_.refs_2_), channel_id=1, source_target_pairs={{0,1},{1,0},{2,3},{3,2},{4,5},{5,4},{6,7},{7,6},{8,9},{9,8},{10,11... | collective-permute-start | bytes 1572872 | tf_op jit(solution)/shard_map/ppermute | solution.py:338
  42.8 9.0 %collective-permute-start.10 = (bf16[256,256]{1,0:T(8,128)(2,1)S(1)}, bf16[256,256]{1,0:T(8,128)(2,1)S(1)}, u32[]{:S(2)}, u32[]{:S(2)}) collective-permute-start(bf16[256,256]{1,0:T(8,128)(2,1)S(1)} %get-tuple-element.203.refs_0_), channel_id=1, source_target_pairs={{0,8},{4,12},{8,0},{12,4},{1,9},{5,13},{9,1},{13,5},{2,10},{6,14},... | collective-permute-start | bytes 393224 | tf_op jit(solution)/shard_map/ppermute | solution.py:338
  42.8 9.1 %collective-permute-start.9 = (bf16[256,256]{1,0:T(8,128)(2,1)S(1)}, bf16[256,256]{1,0:T(8,128)(2,1)S(1)}, u32[]{:S(2)}, u32[]{:S(2)}) collective-permute-start(bf16[256,256]{1,0:T(8,128)(2,1)S(1)} %get-tuple-element.203.refs_0_), channel_id=1, source_target_pairs={{0,4},{4,0},{8,12},{12,8},{1,5},{5,1},{9,13},{13,9},{2,6},{6,2},{1... | collective-permute-start | bytes 393224 | tf_op jit(solution)/shard_map/ppermute | solution.py:338
  51.9 2.1 %collective-permute-start.11 = (bf16[2048,128]{1,0:T(8,128)(2,1)S(1)}, bf16[2048,128]{1,0:T(8,128)(2,1)S(1)}, u32[]{:S(2)}, u32[]{:S(2)}) collective-permute-start(bf16[2048,128]{1,0:T(8,128)(2,1)S(1)} %collective-permute-done.8.refs_6_.refs_0_.refs_8_), channel_id=1, source_target_pairs={{0,1},{1,0},{2,3},{3,2},{4,5},{5,4},{6,7},{7,6},{8,9},{9,8},{10,11... | collective-permute-start | bytes 1572872 | tf_op jit(solution)/shard_map/ppermute | solution.py:338
  51.9 9.1 %collective-permute-start.17 = (bf16[256,512]{1,0:T(8,128)(2,1)S(1)}, bf16[256,512]{1,0:T(8,128)(2,1)S(1)}, u32[]{:S(2)}, u32[]{:S(2)}) collective-permute-start(bf16[256,512]{1,0:T(8,128)(2,1)S(1)} %get-tuple-element.247), channel_id=1, source_target_pairs={{0,4},{4,0},{8,12},{12,8},{1,5},{5,1},{9,13},{13,9},{2,6},{6,2},{1... | collective-permute-start | bytes 786440 | tf_op jit(solution)/shard_map/ppermute | solution.py:338
  52.1 24.2 %collective-permute-start.16 = (bf16[256,512]{1,0:T(8,128)(2,1)S(1)}, bf16[256,512]{1,0:T(8,128)(2,1)S(1)}, u32[]{:S(2)}, u32[]{:S(2)}) collective-permute-start(bf16[256,512]{1,0:T(8,128)(2,1)S(1)} %get-tuple-element.245), channel_id=1, source_target_pairs={{0,4},{4,0},{8,12},{12,8},{1,5},{5,1},{9,13},{13,9},{2,6},{6,2},{1... | collective-permute-start | bytes 786440 | tf_op jit(solution)/shard_map/ppermute | solution.py:338
  54.0 10.5 %copy-start = (bf16[1,1024,1024]{2,1,0:T(8,128)(2,1)S(1)}, bf16[1,1024,1024]{2,1,0:T(8,128)(2,1)}, u32[]{:S(2)}) copy-start(bf16[1,1024,1024]{2,1,0:T(8,128)(2,1)} %param.9) | copy-start | bytes 6291460
  61.1 16.4 %collective-permute-start.18 = (bf16[256,512]{1,0:T(8,128)(2,1)S(1)}, bf16[256,512]{1,0:T(8,128)(2,1)S(1)}, u32[]{:S(2)}, u32[]{:S(2)}) collective-permute-start(bf16[256,512]{1,0:T(8,128)(2,1)S(1)} %add_convert_fusion.2), channel_id=1, source_target_pairs={{0,8},{4,12},{8,0},{12,4},{1,9},{5,13},{9,1},{13,5},{2,10},{6,14},... | collective-permute-start | bytes 786440 | tf_op jit(solution)/shard_map/ppermute | solution.py:338
  62.7 14.8 %collective-permute-start.13 = (bf16[512,256]{1,0:T(8,128)(2,1)S(1)}, bf16[512,256]{1,0:T(8,128)(2,1)S(1)}, u32[]{:S(2)}, u32[]{:S(2)}) collective-permute-start(bf16[512,256]{1,0:T(8,128)(2,1)S(1)} %get-tuple-element.229), channel_id=1, source_target_pairs={{0,4},{4,0},{8,12},{12,8},{1,5},{5,1},{9,13},{13,9},{2,6},{6,2},{1... | collective-permute-start | bytes 786440 | tf_op jit(solution)/shard_map/ppermute | solution.py:338
  76.3 10.4 %collective-permute-start.15 = (bf16[2048,256]{1,0:T(8,128)(2,1)S(1)}, bf16[2048,256]{1,0:T(8,128)(2,1)S(1)}, u32[]{:S(2)}, u32[]{:S(2)}) collective-permute-start(bf16[2048,256]{1,0:T(8,128)(2,1)S(1)} %get-tuple-element.234), channel_id=1, source_target_pairs={{0,1},{1,0},{2,3},{3,2},{4,5},{5,4},{6,7},{7,6},{8,9},{9,8},{10,11... | collective-permute-start | bytes 3145736 | tf_op jit(solution)/shard_map/ppermute | solution.py:338
  76.4 13.8 %collective-permute-start.12 = (bf16[2048,256]{1,0:T(8,128)(2,1)S(1)}, bf16[2048,256]{1,0:T(8,128)(2,1)S(1)}, u32[]{:S(2)}, u32[]{:S(2)}) collective-permute-start(bf16[2048,256]{1,0:T(8,128)(2,1)S(1)} %get-tuple-element.219), channel_id=1, source_target_pairs={{0,1},{1,0},{2,3},{3,2},{4,5},{5,4},{6,7},{7,6},{8,9},{9,8},{10,11... | collective-permute-start | bytes 3145736 | tf_op jit(solution)/shard_map/ppermute | solution.py:338
  77.5 9.2 %collective-permute-start.14 = (bf16[256,256]{1,0:T(8,128)(2,1)S(1)}, bf16[256,256]{1,0:T(8,128)(2,1)S(1)}, u32[]{:S(2)}, u32[]{:S(2)}) collective-permute-start(bf16[256,256]{1,0:T(8,128)(2,1)S(1)} %add_convert_fusion.3), channel_id=1, source_target_pairs={{0,8},{4,12},{8,0},{12,4},{1,9},{5,13},{9,1},{13,5},{2,10},{6,14},... | collective-permute-start | bytes 393224 | tf_op jit(solution)/shard_map/ppermute | solution.py:338
  81.7 15.5 %collective-permute-start.20 = (bf16[256,512]{1,0:T(8,128)(2,1)S(1)}, bf16[256,512]{1,0:T(8,128)(2,1)S(1)}, u32[]{:S(2)}, u32[]{:S(2)}) collective-permute-start(bf16[256,512]{1,0:T(8,128)(2,1)S(1)} %get-tuple-element.268.refs_0_), channel_id=1, source_target_pairs={{0,4},{4,0},{8,12},{12,8},{1,5},{5,1},{9,13},{13,9},{2,6},{6,2},{1... | collective-permute-start | bytes 786440 | tf_op jit(solution)/shard_map/ppermute | solution.py:338
  83.4 17.4 %collective-permute-start.21 = (bf16[256,512]{1,0:T(8,128)(2,1)S(1)}, bf16[256,512]{1,0:T(8,128)(2,1)S(1)}, u32[]{:S(2)}, u32[]{:S(2)}) collective-permute-start(bf16[256,512]{1,0:T(8,128)(2,1)S(1)} %get-tuple-element.268.refs_0_), channel_id=1, source_target_pairs={{0,8},{4,12},{8,0},{12,4},{1,9},{5,13},{9,1},{13,5},{2,10},{6,14},... | collective-permute-start | bytes 786440 | tf_op jit(solution)/shard_map/ppermute | solution.py:338
  87.0 24.8 %collective-permute-start.19 = (bf16[2048,256]{1,0:T(8,128)(2,1)S(1)}, bf16[2048,256]{1,0:T(8,128)(2,1)S(1)}, u32[]{:S(2)}, u32[]{:S(2)}) collective-permute-start(bf16[2048,256]{1,0:T(8,128)(2,1)S(1)} %add_convert_fusion.1), channel_id=1, source_target_pairs={{0,2},{1,3},{2,0},{3,1},{4,6},{5,7},{6,4},{7,5},{8,10},{9,11},{10,... | collective-permute-start | bytes 3145736 | tf_op jit(solution)/shard_map/ppermute | solution.py:338
  90.2 13.1 %collective-permute-start.24 = (bf16[256,256]{1,0:T(8,128)(2,1)S(1)}, bf16[256,256]{1,0:T(8,128)(2,1)S(1)}, u32[]{:S(2)}, u32[]{:S(2)}) collective-permute-start(bf16[256,256]{1,0:T(8,128)(2,1)S(1)} %get-tuple-element.275.refs_0_), channel_id=1, source_target_pairs={{0,4},{4,0},{8,12},{12,8},{1,5},{5,1},{9,13},{13,9},{2,6},{6,2},{1... | collective-permute-start | bytes 393224 | tf_op jit(solution)/shard_map/ppermute | solution.py:338
  90.2 13.1 %collective-permute-start.23 = (bf16[256,256]{1,0:T(8,128)(2,1)S(1)}, bf16[256,256]{1,0:T(8,128)(2,1)S(1)}, u32[]{:S(2)}, u32[]{:S(2)}) collective-permute-start(bf16[256,256]{1,0:T(8,128)(2,1)S(1)} %get-tuple-element.275.refs_0_), channel_id=1, source_target_pairs={{0,8},{4,12},{8,0},{12,4},{1,9},{5,13},{9,1},{13,5},{2,10},{6,14},... | collective-permute-start | bytes 393224 | tf_op jit(solution)/shard_map/ppermute | solution.py:338
  97.2 9.0 %collective-permute-start.22 = (bf16[256,256]{1,0:T(8,128)(2,1)S(1)}, bf16[256,256]{1,0:T(8,128)(2,1)S(1)}, u32[]{:S(2)}, u32[]{:S(2)}) collective-permute-start(bf16[256,256]{1,0:T(8,128)(2,1)S(1)} %collective-permute-done.10.refs_6_.refs_2_), channel_id=1, source_target_pairs={{0,4},{4,0},{8,12},{12,8},{1,5},{5,1},{9,13},{13,9},{2,6},{6,2},{1... | collective-permute-start | bytes 393224 | tf_op jit(solution)/shard_map/ppermute | solution.py:338
  100.8 14.3 %collective-permute-start.26 = (bf16[256,512]{1,0:T(8,128)(2,1)S(1)}, bf16[256,512]{1,0:T(8,128)(2,1)S(1)}, u32[]{:S(2)}, u32[]{:S(2)}) collective-permute-start(bf16[256,512]{1,0:T(8,128)(2,1)S(1)} %collective-permute-done.21.refs_10_.refs_2_), channel_id=1, source_target_pairs={{0,4},{4,0},{8,12},{12,8},{1,5},{5,1},{9,13},{13,9},{2,6},{6,2},{1... | collective-permute-start | bytes 786440 | tf_op jit(solution)/shard_map/ppermute | solution.py:338
  103.3 13.6 %collective-permute-start.25 = (bf16[256,256]{1,0:T(8,128)(2,1)S(1)}, bf16[256,256]{1,0:T(8,128)(2,1)S(1)}, u32[]{:S(2)}, u32[]{:S(2)}) collective-permute-start(bf16[256,256]{1,0:T(8,128)(2,1)S(1)} %collective-permute-done.23.refs_12_.refs_2_), channel_id=1, source_target_pairs={{0,4},{4,0},{8,12},{12,8},{1,5},{5,1},{9,13},{13,9},{2,6},{6,2},{1... | collective-permute-start | bytes 393224 | tf_op jit(solution)/shard_map/ppermute | solution.py:338

commit v8 on v7

--- a/solution.py
+++ b/solution.py
@@ -17,7 +17,7 @@
 PLAN = (
     "h0", "b00", "b10", "t0", "b01", "m0", "b20", "b11", "r0", "a0", "b30", "t1", "g0",
     "e0", "b21", "b31", "t2", "m1", "r1", "a1", "p0", "m2", "r2", "x0", "a2", "u0", "e1",
-    "g1", "e2", "g2", "l0", "q0", "l1", "x1", "l2", "q1", "q2",
+    "g1", "e2", "g2", "l0", "x1", "l12",
 )
 ANYWHERE = pl.BlockSpec(memory_space=pl.ANY)
 INSIDE = pl.BlockSpec(memory_space=pltpu.VMEM)
@@ -25,7 +25,7 @@
 COSTS = {
     "h0": 40000000000, "t0": 10000000000, "a0": 10000000000, "t1": 40000000000,
     "t2": 6000000000, "a1": 10000000000, "p0": 3000000000, "a2": 6000000000, "l0": 4199999999,
-    "q0": 3000000000, "l1": 1000, "l2": 80000000000, "q1": 3000000000, "q2": 3000000000,
+    "l12": 1000,
 }
 
 
@@ -226,47 +226,49 @@
     )(columns, rank, *shares, *near, moment, second, down, *after, *previous)
 
 
-def place_rows(shards, chosen, rows, columns, previous, total, width, after, item):
-    size, wide = shards[0].shape
-    count = wide // width
-    number = len(shards)
-
-    def kernel(rows_ref, columns_ref, *refs):
-        shard_refs, out_ref, token_ref, sems = refs[:number], refs[-3], refs[-2], refs[-1]
+def place_rows(groups, rows, columns, previous, total, width, after, item):
+    size = groups[0][0].shape[0]
+    counts = [group[0].shape[1] // width for group in groups]
+    shards = [shard for group in groups for shard in group]
+
+    def kernel(rows_ref, *refs):
+        columns_refs, refs = refs[: len(groups)], refs[len(groups) :]
+        out_ref, token_ref, sems = refs[-3:]
         token_ref[...] = jnp.zeros_like(token_ref)
         copies = []
-        for k in range(number):
-            for j in range(count):
-                copies.append(
-                    pltpu.make_async_copy(
-                        shard_refs[k].at[:, pl.ds(j * width, width)],
-                        out_ref.at[
-                            pl.ds(pl.multiple_of(rows_ref[chosen[k]] * size, size), size),
-                            pl.ds(pl.multiple_of(columns_ref[j] * width, width), width),
-                        ],
-                        sems.at[k, j],
+        for n, count in enumerate(counts):
+            for k in range(4):
+                for j in range(count):
+                    first_row = pl.multiple_of(rows_ref[k] * size, size)
+                    first_column = pl.multiple_of(columns_refs[n][j] * width, width)
+                    copies.append(
+                        pltpu.make_async_copy(
+                            refs[4 * n + k].at[:, pl.ds(j * width, width)],
+                            out_ref.at[pl.ds(first_row, size), pl.ds(first_column, width)],
+                            sems.at[n, k, j],
+                        )
                     )
-                )
         for copy in copies:
             copy.start()
         for copy in copies:
             copy.wait()
 
+    scalars = 1 + len(groups)
     return pl.pallas_call(
         kernel,
         grid_spec=pltpu.PrefetchScalarGridSpec(
-            num_scalar_prefetch=2,
+            num_scalar_prefetch=scalars,
             grid=(1,),
-            in_specs=[ANYWHERE] * (number + len(after) + len(previous)),
-            out_specs=[ANYWHERE, pl.BlockSpec((8, 128), lambda i, rows, columns: (0, 0))],
-            scratch_shapes=[pltpu.SemaphoreType.DMA((number, count))],
+            in_specs=[ANYWHERE] * (len(shards) + len(after) + len(previous)),
+            out_specs=[ANYWHERE, pl.BlockSpec((8, 128), lambda i, *scalars: (0, 0))],
+            scratch_shapes=[pltpu.SemaphoreType.DMA((len(groups), 4, max(counts)))],
         ),
         out_shape=[jax.ShapeDtypeStruct(total, BF16), TOKEN],
-        input_output_aliases={2 + number + len(after): 0} if previous else {},
+        input_output_aliases={scalars + len(shards) + len(after): 0} if previous else {},
         compiler_params=params(8),
         cost_estimate=cost(item),
         name="place",
-    )(rows, columns, *shards, *after, *previous)
+    )(rows, *columns, *shards, *after, *previous)
 
 
 def partials(pieces, where, order, slope, down, up, scale, after, item):
@@ -431,11 +433,12 @@
                 values["g3" + name[1]] = swapped(values["g2" + name[1]], "dp", 1)
         elif kind == "e":
             arrive("g1" + name[1])
-        elif kind in "lq":
-            chosen = [3] if kind == "q" else [0, 1, 2] + [3] * ("q" + name[1] not in PLAN)
-            gathered = [values["g%d%d" % (j, k)] for j in chosen]
+        elif kind == "l":
+            parts = [int(part) for part in name[1:]]
+            groups = [[values["g%d%d" % (j, part)] for j in range(4)] for part in parts]
             *new_down[:], values["token"] = place_rows(
-                gathered, chosen, shards, columns[k], new_down, down.shape, width, after(), name
+                groups, shards, [columns[part] for part in parts], new_down, down.shape, width,
+                after(), name,
             )
         elif kind == "p":
             pieces = [values["b%d%d" % key] for key in keys]

time: 119 us -> 117 us (0.983)
  Pallas kernels: 40.8 us -> 33.9 us
  waiting for transfers between devices: 40.9 us -> 45.8 us
    pallas_call x6 -> x2, Pallas kernels: 10.8 us -> 3.92 us  [place_rows(): pl.pallas_call(kernel, grid_spec=pltpu.PrefetchScalarGridSpec(num_scalar_...]
    ppermute x25, waiting for transfers between devices: 29.5 us -> 34.3 us  [swapped(): return lax.ppermute(value, axis, [(i, i ^ distance) for i in range(4)])]
  transfers between devices with their start and end apart: 27 -> 27, of which waited for: 15 -> 15; matrix products, arithmetic and copies ran while one was open for 2% -> 2% of each run, Pallas kernels for 33% -> 27%
where the time goes in v8:
time: 117 us
  waiting for transfers between devices  45.8 us (39%)
  Pallas kernels  33.9 us (29%)
  starting transfers between devices  30.9 us (26%)
  local copies, waits for them, and re-layouts  3.57 us (3%)
  other arithmetic  2.06 us (2%)
    ppermute x25, waiting for transfers between devices, swapped(): return lax.ppermute(value, axis, [(i, i ^ distance) for i in range(4)])  34.3 us
    ppermute x25, starting transfers between devices, swapped(): return lax.ppermute(value, axis, [(i, i ^ distance) for i in range(4)])  26.1 us
    pallas_call x1, Pallas kernels, partials(): pl.pallas_call(kernel, grid_spec=pltpu.PrefetchScalarGridSpec(num_scalar_...  11.9 us
    ppermute x2, waiting for transfers between devices, from_behind(): return lax.ppermute(block, axis, route)  11.5 us
    pallas_call x3, Pallas kernels, terms(): pl.pallas_call(kernel, in_specs=[pl.BlockSpec(memory_space=pltpu.SMEM)] +...  7.26 us
    pallas_call x3, Pallas kernels, adam_chunk(): pl.pallas_call(kernel, grid_spec=pltpu.PrefetchScalarGridSpec(num_scalar_...  5.83 us
    pallas_call x1, Pallas kernels, prepare(): pl.pallas_call(kernel, grid=(tokens // TILE,), in_specs=[pl.BlockSpec((TI...  5.02 us
    ppermute x2, starting transfers between devices, from_behind(): return lax.ppermute(block, axis, route)  4.77 us
  transfers between devices with their start and end apart: 27, of which 15 were waited for; matrix products, arithmetic and copies ran while one was open for 2% of the time, Pallas kernels for 27%

profile of v8, /device:TPU:0, one launch (start us, length us, event | category | flops | bytes accessed | tf_op | source)
XLA Modules:
  0.0 117.0 jit_solution(5589836897500207268)
XLA Ops:
  1.9 3.0 %collective-permute-start = (bf16[2048,128]{1,0:T(8,128)(2,1)S(1)}, bf16[2048,128]{1,0:T(8,128)(2,1)S(1)}, u32[]{:S(2)}, u32[]{:S(2)}) collective-permute-start(bf16[2048,128]{1,0:T(8,128)(2,1)S(1)} %get-tuple-element.303), channel_id=1, source_target_pairs={{16,0},{0,16},{17,1},{1,17},{18,2},{2,18},{19,3},{3,19},{20,4},{4,... | collective-permute-start | bytes 1572872 | tf_op jit(solution)/shard_map/ppermute | solution.py:35
  5.3 2.2 %copy-done.2 = bf16[1,2048,1024]{2,1,0:T(8,128)(2,1)S(1)} copy-done((bf16[1,2048,1024]{2,1,0:T(8,128)(2,1)S(1)}, bf16[1,2048,1024]{2,1,0:T(8,128)(2,1)}, u32[]{:S(2)}) %copy-start.2) | copy-done | bytes 4194328
  7.4 5.0 %prepare.1 = (bf16[1024,2048]{1,0:T(8,128)(2,1)S(1)}, bf16[2048,1024]{1,0:T(8,128)(2,1)S(1)}, f32[8,128]{1,0:T(8,128)S(1)}) custom-call(bf16[2048,1024]{1,0:T(8,128)(2,1)S(1)} %bitcast.32, s32[4]{0:T(128)S(1)} %get-tuple-element.304.refs_0_.places_ref.rows_ref, s32[4]{0:T(128)S(1)} %get-tuple-element.305.refs_1_.places_ref, s32[1]{0:T(128)} %bitcast.14.refs_2_.rank_ref, ...), custom_call_target="tpu_custom_call" | custom-call | flops 40000000000 | bytes 1024 | tf_op jit(solution)/shard_map/prepare/pallas_call | solution.py:123
  12.5 4.4 %collective-permute-done.refs_0_.refs_4_ = bf16[2048,128]{1,0:T(8,128)(2,1)S(1)} collective-permute-done((bf16[2048,128]{1,0:T(8,128)(2,1)S(1)}, bf16[2048,128]{1,0:T(8,128)(2,1)S(1)}, u32[]{:S(2)}, u32[]{:S(2)}) %collective-permute-start) | collective-permute-done | bytes 524320 | tf_op jit(solution)/shard_map/ppermute | solution.py:35
  16.9 1.7 %collective-permute-start.4 = (bf16[2048,128]{1,0:T(8,128)(2,1)S(1)}, bf16[2048,128]{1,0:T(8,128)(2,1)S(1)}, u32[]{:S(2)}, u32[]{:S(2)}) collective-permute-start(bf16[2048,128]{1,0:T(8,128)(2,1)S(1)} %get-tuple-element.302), channel_id=1, source_target_pairs={{16,0},{0,16},{17,1},{1,17},{18,2},{2,18},{19,3},{3,19},{20,4},{4,... | collective-permute-start | bytes 1572872 | tf_op jit(solution)/shard_map/ppermute | solution.py:35
  18.8 2.0 %terms.3 = (bf16[256,256]{1,0:T(8,128)(2,1)S(1)}, bf16[256,256]{1,0:T(8,128)(2,1)S(1)}, bf16[512,256]{1,0:T(8,128)(2,1)S(1)}, f32[8,128]{1,0:T(8,128)S(1)}) custom-call(s32[4]{0:T(128)S(1)} %get-tuple-element.305.refs_1_.places_ref, bf16[1024,2048]{1,0:T(8,128)(2,1)S(1)} %get-tuple-element.157.hidden_ref, ...), custom_call_target="tpu_custom_call" | custom-call | flops 10000000000 | bytes 1024 | tf_op jit(solution)/shard_map/terms/pallas_call | solution.py:165
  20.8 1.9 %collective-permute-start.3 = (bf16[512,256]{1,0:T(8,128)(2,1)S(1)}, bf16[512,256]{1,0:T(8,128)(2,1)S(1)}, u32[]{:S(2)}, u32[]{:S(2)}) collective-permute-start(bf16[512,256]{1,0:T(8,128)(2,1)S(1)} %get-tuple-element.162), channel_id=1, source_target_pairs={{0,4},{4,0},{8,12},{12,8},{1,5},{5,1},{9,13},{13,9},{2,6},{6,2},{1... | collective-permute-start | bytes 786440 | tf_op jit(solution)/shard_map/ppermute | solution.py:340
  24.1 7.1 %collective-permute-done.4.refs_11_.refs_0_.refs_4_ = bf16[2048,128]{1,0:T(8,128)(2,1)S(1)} collective-permute-done((bf16[2048,128]{1,0:T(8,128)(2,1)S(1)}, bf16[2048,128]{1,0:T(8,128)(2,1)S(1)}, u32[]{:S(2)}, u32[]{:S(2)}) %collective-permute-start.4) | collective-permute-done | bytes 524320 | tf_op jit(solution)/shard_map/ppermute | solution.py:35
  31.2 2.9 %collective-permute-start.6 = (bf16[256,256]{1,0:T(8,128)(2,1)S(1)}, bf16[256,256]{1,0:T(8,128)(2,1)S(1)}, u32[]{:S(2)}, u32[]{:S(2)}) collective-permute-start(bf16[256,256]{1,0:T(8,128)(2,1)S(1)} %add_convert_fusion.4), channel_id=1, source_target_pairs={{0,8},{4,12},{8,0},{12,4},{1,9},{5,13},{9,1},{13,5},{2,10},{6,14},... | collective-permute-start | bytes 393224 | tf_op jit(solution)/shard_map/ppermute | solution.py:340
  36.3 4.8 %collective-permute-done.6.refs_1_.refs_15_ = bf16[256,256]{1,0:T(8,128)(2,1)S(1)} collective-permute-done((bf16[256,256]{1,0:T(8,128)(2,1)S(1)}, bf16[256,256]{1,0:T(8,128)(2,1)S(1)}, u32[]{:S(2)}, u32[]{:S(2)}) %collective-permute-start.6) | collective-permute-done | bytes 131104 | tf_op jit(solution)/shard_map/ppermute | solution.py:340
  41.1 1.7 %adam.3 = (bf16[256,256]{1,0:T(8,128)(2,1)S(1)}, f32[256,1024]{1,0:T(8,128)}, f32[256,1024]{1,0:T(8,128)}, f32[8,128]{1,0:T(8,128)S(1)}) custom-call(s32[2]{0:T(128)S(1)} %get-tuple-element.308.refs_5_.columns_ref.refs_0_, s32[1]{0:T(128)} %bitcast.14.refs_2_.rank_ref, bf16[256,256]{1,0:T(8,128)(2,1)S(1)} %get-tuple-element.170.refs_0_, ...), custom_call_target="tpu_custom_call" | custom-call | flops 10000000000 | bytes 1024 | tf_op jit(solution)/shard_map/adam/pallas_call | solution.py:203
  42.8 4.1 %collective-permute-start.9 = (bf16[256,256]{1,0:T(8,128)(2,1)S(1)}, bf16[256,256]{1,0:T(8,128)(2,1)S(1)}, u32[]{:S(2)}, u32[]{:S(2)}) collective-permute-start(bf16[256,256]{1,0:T(8,128)(2,1)S(1)} %get-tuple-element.199.refs_1_), channel_id=1, source_target_pairs={{0,4},{4,0},{8,12},{12,8},{1,5},{5,1},{9,13},{13,9},{2,6},{6,2},{1... | collective-permute-start | bytes 393224 | tf_op jit(solution)/shard_map/ppermute | solution.py:340
  46.9 3.3 %terms.4 = (bf16[256,512]{1,0:T(8,128)(2,1)S(1)}, bf16[256,512]{1,0:T(8,128)(2,1)S(1)}, bf16[256,512]{1,0:T(8,128)(2,1)S(1)}, bf16[256,512]{1,0:T(8,128)(2,1)S(1)}, f32[8,128]{1,0:T(8,128)S(1)}) custom-call(s32[4]{0:T(128)S(1)} %get-tuple-element.304.refs_0_.places_ref.rows_ref, bf16[1024,2048]{1,0:T(8,128)(2,1)S(1)} %get-tuple-element.157.hidden_ref, ...), custom_call_target="tpu_custom_call" | custom-call | flops 40000000000 | bytes 1024 | tf_op jit(solution)/shard_map/terms/pallas_call | solution.py:165
  50.2 1.6 %collective-permute-done.10.refs_6_.refs_3_ = bf16[256,256]{1,0:T(8,128)(2,1)S(1)} collective-permute-done((bf16[256,256]{1,0:T(8,128)(2,1)S(1)}, bf16[256,256]{1,0:T(8,128)(2,1)S(1)}, u32[]{:S(2)}, u32[]{:S(2)}) %collective-permute-start.10) | collective-permute-done | bytes 131104 | tf_op jit(solution)/shard_map/ppermute | solution.py:340
  52.1 1.9 %collective-permute-start.16 = (bf16[256,512]{1,0:T(8,128)(2,1)S(1)}, bf16[256,512]{1,0:T(8,128)(2,1)S(1)}, u32[]{:S(2)}, u32[]{:S(2)}) collective-permute-start(bf16[256,512]{1,0:T(8,128)(2,1)S(1)} %get-tuple-element.241), channel_id=1, source_target_pairs={{0,4},{4,0},{8,12},{12,8},{1,5},{5,1},{9,13},{13,9},{2,6},{6,2},{1... | collective-permute-start | bytes 786440 | tf_op jit(solution)/shard_map/ppermute | solution.py:340
  54.0 2.0 %terms.5 = (bf16[256,256]{1,0:T(8,128)(2,1)S(1)}, bf16[256,256]{1,0:T(8,128)(2,1)S(1)}, bf16[512,256]{1,0:T(8,128)(2,1)S(1)}, f32[8,128]{1,0:T(8,128)S(1)}) custom-call(s32[4]{0:T(128)S(1)} %get-tuple-element.305.refs_1_.places_ref, bf16[1024,2048]{1,0:T(8,128)(2,1)S(1)} %get-tuple-element.157.hidden_ref, ...), custom_call_target="tpu_custom_call" | custom-call | flops 6000000000 | bytes 1024 | tf_op jit(solution)/shard_map/terms/pallas_call | solution.py:165
  56.0 5.1 %collective-permute-done.17.refs_9_ = bf16[256,512]{1,0:T(8,128)(2,1)S(1)} collective-permute-done((bf16[256,512]{1,0:T(8,128)(2,1)S(1)}, bf16[256,512]{1,0:T(8,128)(2,1)S(1)}, u32[]{:S(2)}, u32[]{:S(2)}) %collective-permute-start.17) | collective-permute-done | bytes 262176 | tf_op jit(solution)/shard_map/ppermute | solution.py:340
  61.1 1.6 %collective-permute-start.18 = (bf16[256,512]{1,0:T(8,128)(2,1)S(1)}, bf16[256,512]{1,0:T(8,128)(2,1)S(1)}, u32[]{:S(2)}, u32[]{:S(2)}) collective-permute-start(bf16[256,512]{1,0:T(8,128)(2,1)S(1)} %add_convert_fusion.2), channel_id=1, source_target_pairs={{0,8},{4,12},{8,0},{12,4},{1,9},{5,13},{9,1},{13,5},{2,10},{6,14},... | collective-permute-start | bytes 786440 | tf_op jit(solution)/shard_map/ppermute | solution.py:340
  62.7 1.7 %collective-permute-start.13 = (bf16[512,256]{1,0:T(8,128)(2,1)S(1)}, bf16[512,256]{1,0:T(8,128)(2,1)S(1)}, u32[]{:S(2)}, u32[]{:S(2)}) collective-permute-start(bf16[512,256]{1,0:T(8,128)(2,1)S(1)} %get-tuple-element.225), channel_id=1, source_target_pairs={{0,4},{4,0},{8,12},{12,8},{1,5},{5,1},{9,13},{13,9},{2,6},{6,2},{1... | collective-permute-start | bytes 786440 | tf_op jit(solution)/shard_map/ppermute | solution.py:340
  64.4 11.9 %partials.1 = (bf16[2048,256]{1,0:T(8,128)(2,1)S(1)}, bf16[2048,256]{1,0:T(8,128)(2,1)S(1)}, bf16[2048,256]{1,0:T(8,128)(2,1)S(1)}, bf16[2048,256]{1,0:T(8,128)(2,1)S(1)}, f32[8,128]{1,0:T(8,128)S(1)}) custom-call(s32[8]{0:T(128)S(1)} %stack.89.refs_4_.where_ref, s32[4]{0:T(128)S(1)} %get-tuple-element.306.refs_3_.order_ref, ...), custom_call_target="tpu_custom_call" | custom-call | flops 3000000000 | bytes 1024 | tf_op jit(solution)/shard_map/partials/pallas_call | solution.py:301
  77.5 1.7 %collective-permute-start.14 = (bf16[256,256]{1,0:T(8,128)(2,1)S(1)}, bf16[256,256]{1,0:T(8,128)(2,1)S(1)}, u32[]{:S(2)}, u32[]{:S(2)}) collective-permute-start(bf16[256,256]{1,0:T(8,128)(2,1)S(1)} %add_convert_fusion.3), channel_id=1, source_target_pairs={{0,8},{4,12},{8,0},{12,4},{1,9},{5,13},{9,1},{13,5},{2,10},{6,14},... | collective-permute-start | bytes 393224 | tf_op jit(solution)/shard_map/ppermute | solution.py:340
  79.2 2.5 %adam.4 = (bf16[256,512]{1,0:T(8,128)(2,1)S(1)}, f32[256,1024]{1,0:T(8,128)}, f32[256,1024]{1,0:T(8,128)}, f32[8,128]{1,0:T(8,128)}) custom-call(s32[4]{0:T(128)S(1)} %get-tuple-element.307.refs_6_.columns_ref.refs_0_, s32[1]{0:T(128)} %bitcast.14.refs_2_.rank_ref, ...), custom_call_target="tpu_custom_call", output_to_operand_aliasing={{1}: (14, {}), {2}: (15, {})} | custom-call | flops 10000000000 | bytes 1024 | tf_op jit(solution)/shard_map/adam/pallas_call | solution.py:203
  81.7 1.7 %collective-permute-start.24 = (bf16[256,512]{1,0:T(8,128)(2,1)S(1)}, bf16[256,512]{1,0:T(8,128)(2,1)S(1)}, u32[]{:S(2)}, u32[]{:S(2)}) collective-permute-start(bf16[256,512]{1,0:T(8,128)(2,1)S(1)} %get-tuple-element.265.refs_2_), channel_id=1, source_target_pairs={{0,4},{4,0},{8,12},{12,8},{1,5},{5,1},{9,13},{13,9},{2,6},{6,2},{1... | collective-permute-start | bytes 786440 | tf_op jit(solution)/shard_map/ppermute | solution.py:340
  83.4 3.3 %collective-permute-done.14.refs_1_.refs_10_ = bf16[256,256]{1,0:T(8,128)(2,1)S(1)} collective-permute-done((bf16[256,256]{1,0:T(8,128)(2,1)S(1)}, bf16[256,256]{1,0:T(8,128)(2,1)S(1)}, u32[]{:S(2)}, u32[]{:S(2)}) %collective-permute-start.14) | collective-permute-done | bytes 131104 | tf_op jit(solution)/shard_map/ppermute | solution.py:340
  87.0 1.6 %collective-permute-start.19 = (bf16[2048,256]{1,0:T(8,128)(2,1)S(1)}, bf16[2048,256]{1,0:T(8,128)(2,1)S(1)}, u32[]{:S(2)}, u32[]{:S(2)}) collective-permute-start(bf16[2048,256]{1,0:T(8,128)(2,1)S(1)} %add_convert_fusion.1), channel_id=1, source_target_pairs={{0,2},{1,3},{2,0},{3,1},{4,6},{5,7},{6,4},{7,5},{8,10},{9,11},{10,... | collective-permute-start | bytes 3145736 | tf_op jit(solution)/shard_map/ppermute | solution.py:340
  88.6 1.7 %adam.5 = (bf16[256,256]{1,0:T(8,128)(2,1)S(1)}, f32[256,1024]{1,0:T(8,128)}, f32[256,1024]{1,0:T(8,128)}, f32[8,128]{1,0:T(8,128)S(1)}) custom-call(s32[2]{0:T(128)S(1)} %get-tuple-element.309.refs_7_.columns_ref.refs_1_, s32[1]{0:T(128)} %bitcast.14.refs_2_.rank_ref, ...), custom_call_target="tpu_custom_call", output_to_operand_aliasing={{1}: (14, {}), {2}: (15, {})} | custom-call | flops 6000000000 | bytes 1024 | tf_op jit(solution)/shard_map/adam/pallas_call | solution.py:203
  90.2 7.0 %collective-permute-done.24.refs_11_.refs_3_ = bf16[256,512]{1,0:T(8,128)(2,1)S(1)} collective-permute-done((bf16[256,512]{1,0:T(8,128)(2,1)S(1)}, bf16[256,512]{1,0:T(8,128)(2,1)S(1)}, u32[]{:S(2)}, u32[]{:S(2)}) %collective-permute-start.24) | collective-permute-done | bytes 262176 | tf_op jit(solution)/shard_map/ppermute | solution.py:340
  97.8 2.7 %collective-permute-start.20 = (bf16[256,256]{1,0:T(8,128)(2,1)S(1)}, bf16[256,256]{1,0:T(8,128)(2,1)S(1)}, u32[]{:S(2)}, u32[]{:S(2)}) collective-permute-start(bf16[256,256]{1,0:T(8,128)(2,1)S(1)} %collective-permute-done.10.refs_6_.refs_3_), channel_id=1, source_target_pairs={{0,4},{4,0},{8,12},{12,8},{1,5},{5,1},{9,13},{13,9},{2,6},{6,2},{1... | collective-permute-start | bytes 393224 | tf_op jit(solution)/shard_map/ppermute | solution.py:340
  100.6 4.2 %collective-permute-done.21.refs_14_.refs_8_ = bf16[256,256]{1,0:T(8,128)(2,1)S(1)} collective-permute-done((bf16[256,256]{1,0:T(8,128)(2,1)S(1)}, bf16[256,256]{1,0:T(8,128)(2,1)S(1)}, u32[]{:S(2)}, u32[]{:S(2)}) %collective-permute-start.21) | collective-permute-done | bytes 131104 | tf_op jit(solution)/shard_map/ppermute | solution.py:340
  104.8 1.8 %collective-permute-done.20.refs_4_ = bf16[256,256]{1,0:T(8,128)(2,1)S(1)} collective-permute-done((bf16[256,256]{1,0:T(8,128)(2,1)S(1)}, bf16[256,256]{1,0:T(8,128)(2,1)S(1)}, u32[]{:S(2)}, u32[]{:S(2)}) %collective-permute-start.20) | collective-permute-done | bytes 131104 | tf_op jit(solution)/shard_map/ppermute | solution.py:340
  108.0 3.8 %collective-permute-done.19.refs_11_ = bf16[2048,256]{1,0:T(8,128)(2,1)S(1)} collective-permute-done((bf16[2048,256]{1,0:T(8,128)(2,1)S(1)}, bf16[2048,256]{1,0:T(8,128)(2,1)S(1)}, u32[]{:S(2)}, u32[]{:S(2)}) %collective-permute-start.19) | collective-permute-done | bytes 1048608 | tf_op jit(solution)/shard_map/ppermute | solution.py:340
  114.4 2.5 %place.3 = (bf16[1024,1024]{1,0:T(8,128)(2,1)}, f32[8,128]{1,0:T(8,128)}) custom-call(s32[4]{0:T(128)S(1)} %get-tuple-element.304.refs_0_.places_ref.rows_ref, s32[4]{0:T(128)S(1)} %get-tuple-element.307.refs_6_.columns_ref.refs_0_, s32[2]{0:T(128)S(1)} %get-tuple-element.309.refs_7_.columns_ref.refs_1_, ...), custom_call_target="tpu_custom_call", output_to_operand_aliasing={{0}: (13, {})} | custom-call | flops 1000 | bytes 1024 | tf_op jit(solution)/shard_map/place/pallas_call | solution.py:257
  (52 shorter events, 12.1 us)
Async XLA Ops:
  1.9 15.0 %collective-permute-start = (bf16[2048,128]{1,0:T(8,128)(2,1)S(1)}, bf16[2048,128]{1,0:T(8,128)(2,1)S(1)}, u32[]{:S(2)}, u32[]{:S(2)}) collective-permute-start(bf16[2048,128]{1,0:T(8,128)(2,1)S(1)} %get-tuple-element.303), channel_id=1, source_target_pairs={{16,0},{0,16},{17,1},{1,17},{18,2},{2,18},{19,3},{3,19},{20,4},{4,... | collective-permute-start | bytes 1572872 | tf_op jit(solution)/shard_map/ppermute | solution.py:35
  5.3 2.2 %copy-start.2 = (bf16[1,2048,1024]{2,1,0:T(8,128)(2,1)S(1)}, bf16[1,2048,1024]{2,1,0:T(8,128)(2,1)}, u32[]{:S(2)}) copy-start(bf16[1,2048,1024]{2,1,0:T(8,128)(2,1)} %param.7) | copy-start | bytes 12582916
  16.9 1.9 %collective-permute-start.1 = (bf16[2048,128]{1,0:T(8,128)(2,1)S(1)}, bf16[2048,128]{1,0:T(8,128)(2,1)S(1)}, u32[]{:S(2)}, u32[]{:S(2)}) collective-permute-start(bf16[2048,128]{1,0:T(8,128)(2,1)S(1)} %collective-permute-done.refs_0_.refs_4_), channel_id=1, source_target_pairs={{0,1},{1,0},{2,3},{3,2},{4,5},{5,4},{6,7},{7,6},{8,9},{9,8},{10,11... | collective-permute-start | bytes 1572872 | tf_op jit(solution)/shard_map/ppermute | solution.py:340
  16.9 14.3 %collective-permute-start.4 = (bf16[2048,128]{1,0:T(8,128)(2,1)S(1)}, bf16[2048,128]{1,0:T(8,128)(2,1)S(1)}, u32[]{:S(2)}, u32[]{:S(2)}) collective-permute-start(bf16[2048,128]{1,0:T(8,128)(2,1)S(1)} %get-tuple-element.302), channel_id=1, source_target_pairs={{16,0},{0,16},{17,1},{1,17},{18,2},{2,18},{19,3},{3,19},{20,4},{4,... | collective-permute-start | bytes 1572872 | tf_op jit(solution)/shard_map/ppermute | solution.py:35
  18.8 22.3 %copy-start.1 = (bf16[1,1024,1024]{2,1,0:T(8,128)(2,1)S(1)}, bf16[1,1024,1024]{2,1,0:T(8,128)(2,1)}, u32[]{:S(2)}) copy-start(bf16[1,1024,1024]{2,1,0:T(8,128)(2,1)} %param.8) | copy-start | bytes 6291460
  18.8 22.3 %copy-start.3 = (f32[1,256,1024]{2,1,0:T(8,128)S(1)}, f32[1,256,1024]{2,1,0:T(8,128)}, u32[]{:S(2)}) copy-start(f32[1,256,1024]{2,1,0:T(8,128)} %param.10) | copy-start | bytes 3145732
  18.8 22.3 %copy-start.4 = (f32[1,256,1024]{2,1,0:T(8,128)S(1)}, f32[1,256,1024]{2,1,0:T(8,128)}, u32[]{:S(2)}) copy-start(f32[1,256,1024]{2,1,0:T(8,128)} %param.11) | copy-start | bytes 3145732
  20.8 10.4 %collective-permute-start.3 = (bf16[512,256]{1,0:T(8,128)(2,1)S(1)}, bf16[512,256]{1,0:T(8,128)(2,1)S(1)}, u32[]{:S(2)}, u32[]{:S(2)}) collective-permute-start(bf16[512,256]{1,0:T(8,128)(2,1)S(1)} %get-tuple-element.162), channel_id=1, source_target_pairs={{0,4},{4,0},{8,12},{12,8},{1,5},{5,1},{9,13},{13,9},{2,6},{6,2},{1... | collective-permute-start | bytes 786440 | tf_op jit(solution)/shard_map/ppermute | solution.py:340
  22.6 13.7 %collective-permute-start.2 = (bf16[2048,128]{1,0:T(8,128)(2,1)S(1)}, bf16[2048,128]{1,0:T(8,128)(2,1)S(1)}, u32[]{:S(2)}, u32[]{:S(2)}) collective-permute-start(bf16[2048,128]{1,0:T(8,128)(2,1)S(1)} %collective-permute-done.refs_0_.refs_4_), channel_id=1, source_target_pairs={{0,2},{1,3},{2,0},{3,1},{4,6},{5,7},{6,4},{7,5},{8,10},{9,11},{10,... | collective-permute-start | bytes 1572872 | tf_op jit(solution)/shard_map/ppermute | solution.py:340
  31.2 5.1 %collective-permute-start.7 = (bf16[2048,128]{1,0:T(8,128)(2,1)S(1)}, bf16[2048,128]{1,0:T(8,128)(2,1)S(1)}, u32[]{:S(2)}, u32[]{:S(2)}) collective-permute-start(bf16[2048,128]{1,0:T(8,128)(2,1)S(1)} %collective-permute-done.4.refs_11_.refs_0_.refs_4_), channel_id=1, source_target_pairs={{0,1},{1,0},{2,3},{3,2},{4,5},{5,4},{6,7},{7,6},{8,9},{9,8},{10,11... | collective-permute-start | bytes 1572872 | tf_op jit(solution)/shard_map/ppermute | solution.py:340
  31.2 9.9 %collective-permute-start.6 = (bf16[256,256]{1,0:T(8,128)(2,1)S(1)}, bf16[256,256]{1,0:T(8,128)(2,1)S(1)}, u32[]{:S(2)}, u32[]{:S(2)}) collective-permute-start(bf16[256,256]{1,0:T(8,128)(2,1)S(1)} %add_convert_fusion.4), channel_id=1, source_target_pairs={{0,8},{4,12},{8,0},{12,4},{1,9},{5,13},{9,1},{13,5},{2,10},{6,14},... | collective-permute-start | bytes 393224 | tf_op jit(solution)/shard_map/ppermute | solution.py:340
  34.1 17.8 %collective-permute-start.8 = (bf16[2048,128]{1,0:T(8,128)(2,1)S(1)}, bf16[2048,128]{1,0:T(8,128)(2,1)S(1)}, u32[]{:S(2)}, u32[]{:S(2)}) collective-permute-start(bf16[2048,128]{1,0:T(8,128)(2,1)S(1)} %collective-permute-done.4.refs_11_.refs_0_.refs_4_), channel_id=1, source_target_pairs={{0,2},{1,3},{2,0},{3,1},{4,6},{5,7},{6,4},{7,5},{8,10},{9,11},{10,... | collective-permute-start | bytes 1572872 | tf_op jit(solution)/shard_map/ppermute | solution.py:340
  36.3 10.6 %collective-permute-start.5 = (bf16[2048,128]{1,0:T(8,128)(2,1)S(1)}, bf16[2048,128]{1,0:T(8,128)(2,1)S(1)}, u32[]{:S(2)}, u32[]{:S(2)}) collective-permute-start(bf16[2048,128]{1,0:T(8,128)(2,1)S(1)} %collective-permute-done.2.refs_13_.refs_2_), channel_id=1, source_target_pairs={{0,1},{1,0},{2,3},{3,2},{4,5},{5,4},{6,7},{7,6},{8,9},{9,8},{10,11... | collective-permute-start | bytes 1572872 | tf_op jit(solution)/shard_map/ppermute | solution.py:340
  42.8 9.0 %collective-permute-start.10 = (bf16[256,256]{1,0:T(8,128)(2,1)S(1)}, bf16[256,256]{1,0:T(8,128)(2,1)S(1)}, u32[]{:S(2)}, u32[]{:S(2)}) collective-permute-start(bf16[256,256]{1,0:T(8,128)(2,1)S(1)} %get-tuple-element.199.refs_1_), channel_id=1, source_target_pairs={{0,8},{4,12},{8,0},{12,4},{1,9},{5,13},{9,1},{13,5},{2,10},{6,14},... | collective-permute-start | bytes 393224 | tf_op jit(solution)/shard_map/ppermute | solution.py:340
  42.8 9.1 %collective-permute-start.9 = (bf16[256,256]{1,0:T(8,128)(2,1)S(1)}, bf16[256,256]{1,0:T(8,128)(2,1)S(1)}, u32[]{:S(2)}, u32[]{:S(2)}) collective-permute-start(bf16[256,256]{1,0:T(8,128)(2,1)S(1)} %get-tuple-element.199.refs_1_), channel_id=1, source_target_pairs={{0,4},{4,0},{8,12},{12,8},{1,5},{5,1},{9,13},{13,9},{2,6},{6,2},{1... | collective-permute-start | bytes 393224 | tf_op jit(solution)/shard_map/ppermute | solution.py:340
  51.9 2.1 %collective-permute-start.11 = (bf16[2048,128]{1,0:T(8,128)(2,1)S(1)}, bf16[2048,128]{1,0:T(8,128)(2,1)S(1)}, u32[]{:S(2)}, u32[]{:S(2)}) collective-permute-start(bf16[2048,128]{1,0:T(8,128)(2,1)S(1)} %collective-permute-done.8.refs_6_.refs_0_.refs_8_), channel_id=1, source_target_pairs={{0,1},{1,0},{2,3},{3,2},{4,5},{5,4},{6,7},{7,6},{8,9},{9,8},{10,11... | collective-permute-start | bytes 1572872 | tf_op jit(solution)/shard_map/ppermute | solution.py:340
  51.9 9.1 %collective-permute-start.17 = (bf16[256,512]{1,0:T(8,128)(2,1)S(1)}, bf16[256,512]{1,0:T(8,128)(2,1)S(1)}, u32[]{:S(2)}, u32[]{:S(2)}) collective-permute-start(bf16[256,512]{1,0:T(8,128)(2,1)S(1)} %get-tuple-element.243), channel_id=1, source_target_pairs={{0,4},{4,0},{8,12},{12,8},{1,5},{5,1},{9,13},{13,9},{2,6},{6,2},{1... | collective-permute-start | bytes 786440 | tf_op jit(solution)/shard_map/ppermute | solution.py:340
  52.1 24.2 %collective-permute-start.16 = (bf16[256,512]{1,0:T(8,128)(2,1)S(1)}, bf16[256,512]{1,0:T(8,128)(2,1)S(1)}, u32[]{:S(2)}, u32[]{:S(2)}) collective-permute-start(bf16[256,512]{1,0:T(8,128)(2,1)S(1)} %get-tuple-element.241), channel_id=1, source_target_pairs={{0,4},{4,0},{8,12},{12,8},{1,5},{5,1},{9,13},{13,9},{2,6},{6,2},{1... | collective-permute-start | bytes 786440 | tf_op jit(solution)/shard_map/ppermute | solution.py:340
  54.0 10.5 %copy-start = (bf16[1,1024,1024]{2,1,0:T(8,128)(2,1)S(1)}, bf16[1,1024,1024]{2,1,0:T(8,128)(2,1)}, u32[]{:S(2)}) copy-start(bf16[1,1024,1024]{2,1,0:T(8,128)(2,1)} %param.9) | copy-start | bytes 6291460
  61.1 16.4 %collective-permute-start.18 = (bf16[256,512]{1,0:T(8,128)(2,1)S(1)}, bf16[256,512]{1,0:T(8,128)(2,1)S(1)}, u32[]{:S(2)}, u32[]{:S(2)}) collective-permute-start(bf16[256,512]{1,0:T(8,128)(2,1)S(1)} %add_convert_fusion.2), channel_id=1, source_target_pairs={{0,8},{4,12},{8,0},{12,4},{1,9},{5,13},{9,1},{13,5},{2,10},{6,14},... | collective-permute-start | bytes 786440 | tf_op jit(solution)/shard_map/ppermute | solution.py:340
  62.7 14.8 %collective-permute-start.13 = (bf16[512,256]{1,0:T(8,128)(2,1)S(1)}, bf16[512,256]{1,0:T(8,128)(2,1)S(1)}, u32[]{:S(2)}, u32[]{:S(2)}) collective-permute-start(bf16[512,256]{1,0:T(8,128)(2,1)S(1)} %get-tuple-element.225), channel_id=1, source_target_pairs={{0,4},{4,0},{8,12},{12,8},{1,5},{5,1},{9,13},{13,9},{2,6},{6,2},{1... | collective-permute-start | bytes 786440 | tf_op jit(solution)/shard_map/ppermute | solution.py:340
  76.3 10.4 %collective-permute-start.15 = (bf16[2048,256]{1,0:T(8,128)(2,1)S(1)}, bf16[2048,256]{1,0:T(8,128)(2,1)S(1)}, u32[]{:S(2)}, u32[]{:S(2)}) collective-permute-start(bf16[2048,256]{1,0:T(8,128)(2,1)S(1)} %get-tuple-element.230), channel_id=1, source_target_pairs={{0,1},{1,0},{2,3},{3,2},{4,5},{5,4},{6,7},{7,6},{8,9},{9,8},{10,11... | collective-permute-start | bytes 3145736 | tf_op jit(solution)/shard_map/ppermute | solution.py:340
  76.4 21.4 %collective-permute-start.12 = (bf16[2048,256]{1,0:T(8,128)(2,1)S(1)}, bf16[2048,256]{1,0:T(8,128)(2,1)S(1)}, u32[]{:S(2)}, u32[]{:S(2)}) collective-permute-start(bf16[2048,256]{1,0:T(8,128)(2,1)S(1)} %get-tuple-element.215), channel_id=1, source_target_pairs={{0,1},{1,0},{2,3},{3,2},{4,5},{5,4},{6,7},{7,6},{8,9},{9,8},{10,11... | collective-permute-start | bytes 3145736 | tf_op jit(solution)/shard_map/ppermute | solution.py:340
  77.5 9.2 %collective-permute-start.14 = (bf16[256,256]{1,0:T(8,128)(2,1)S(1)}, bf16[256,256]{1,0:T(8,128)(2,1)S(1)}, u32[]{:S(2)}, u32[]{:S(2)}) collective-permute-start(bf16[256,256]{1,0:T(8,128)(2,1)S(1)} %add_convert_fusion.3), channel_id=1, source_target_pairs={{0,8},{4,12},{8,0},{12,4},{1,9},{5,13},{9,1},{13,5},{2,10},{6,14},... | collective-permute-start | bytes 393224 | tf_op jit(solution)/shard_map/ppermute | solution.py:340
  81.7 15.5 %collective-permute-start.24 = (bf16[256,512]{1,0:T(8,128)(2,1)S(1)}, bf16[256,512]{1,0:T(8,128)(2,1)S(1)}, u32[]{:S(2)}, u32[]{:S(2)}) collective-permute-start(bf16[256,512]{1,0:T(8,128)(2,1)S(1)} %get-tuple-element.265.refs_2_), channel_id=1, source_target_pairs={{0,4},{4,0},{8,12},{12,8},{1,5},{5,1},{9,13},{13,9},{2,6},{6,2},{1... | collective-permute-start | bytes 786440 | tf_op jit(solution)/shard_map/ppermute | solution.py:340
  83.4 17.2 %collective-permute-start.23 = (bf16[256,512]{1,0:T(8,128)(2,1)S(1)}, bf16[256,512]{1,0:T(8,128)(2,1)S(1)}, u32[]{:S(2)}, u32[]{:S(2)}) collective-permute-start(bf16[256,512]{1,0:T(8,128)(2,1)S(1)} %get-tuple-element.265.refs_2_), channel_id=1, source_target_pairs={{0,8},{4,12},{8,0},{12,4},{1,9},{5,13},{9,1},{13,5},{2,10},{6,14},... | collective-permute-start | bytes 786440 | tf_op jit(solution)/shard_map/ppermute | solution.py:340
  87.0 24.8 %collective-permute-start.19 = (bf16[2048,256]{1,0:T(8,128)(2,1)S(1)}, bf16[2048,256]{1,0:T(8,128)(2,1)S(1)}, u32[]{:S(2)}, u32[]{:S(2)}) collective-permute-start(bf16[2048,256]{1,0:T(8,128)(2,1)S(1)} %add_convert_fusion.1), channel_id=1, source_target_pairs={{0,2},{1,3},{2,0},{3,1},{4,6},{5,7},{6,4},{7,5},{8,10},{9,11},{10,... | collective-permute-start | bytes 3145736 | tf_op jit(solution)/shard_map/ppermute | solution.py:340
  90.2 10.4 %collective-permute-start.22 = (bf16[256,256]{1,0:T(8,128)(2,1)S(1)}, bf16[256,256]{1,0:T(8,128)(2,1)S(1)}, u32[]{:S(2)}, u32[]{:S(2)}) collective-permute-start(bf16[256,256]{1,0:T(8,128)(2,1)S(1)} %get-tuple-element.264.refs_6_), channel_id=1, source_target_pairs={{0,4},{4,0},{8,12},{12,8},{1,5},{5,1},{9,13},{13,9},{2,6},{6,2},{1... | collective-permute-start | bytes 393224 | tf_op jit(solution)/shard_map/ppermute | solution.py:340
  97.2 7.6 %collective-permute-start.21 = (bf16[256,256]{1,0:T(8,128)(2,1)S(1)}, bf16[256,256]{1,0:T(8,128)(2,1)S(1)}, u32[]{:S(2)}, u32[]{:S(2)}) collective-permute-start(bf16[256,256]{1,0:T(8,128)(2,1)S(1)} %get-tuple-element.264.refs_6_), channel_id=1, source_target_pairs={{0,8},{4,12},{8,0},{12,4},{1,9},{5,13},{9,1},{13,5},{2,10},{6,14},... | collective-permute-start | bytes 393224 | tf_op jit(solution)/shard_map/ppermute | solution.py:340
  97.8 8.8 %collective-permute-start.20 = (bf16[256,256]{1,0:T(8,128)(2,1)S(1)}, bf16[256,256]{1,0:T(8,128)(2,1)S(1)}, u32[]{:S(2)}, u32[]{:S(2)}) collective-permute-start(bf16[256,256]{1,0:T(8,128)(2,1)S(1)} %collective-permute-done.10.refs_6_.refs_3_), channel_id=1, source_target_pairs={{0,4},{4,0},{8,12},{12,8},{1,5},{5,1},{9,13},{13,9},{2,6},{6,2},{1... | collective-permute-start | bytes 393224 | tf_op jit(solution)/shard_map/ppermute | solution.py:340
  100.5 12.6 %collective-permute-start.25 = (bf16[256,512]{1,0:T(8,128)(2,1)S(1)}, bf16[256,512]{1,0:T(8,128)(2,1)S(1)}, u32[]{:S(2)}, u32[]{:S(2)}) collective-permute-start(bf16[256,512]{1,0:T(8,128)(2,1)S(1)} %collective-permute-done.23.refs_12_.refs_4_), channel_id=1, source_target_pairs={{0,4},{4,0},{8,12},{12,8},{1,5},{5,1},{9,13},{13,9},{2,6},{6,2},{1... | collective-permute-start | bytes 786440 | tf_op jit(solution)/shard_map/ppermute | solution.py:340
  104.8 9.6 %collective-permute-start.26 = (bf16[256,256]{1,0:T(8,128)(2,1)S(1)}, bf16[256,256]{1,0:T(8,128)(2,1)S(1)}, u32[]{:S(2)}, u32[]{:S(2)}) collective-permute-start(bf16[256,256]{1,0:T(8,128)(2,1)S(1)} %collective-permute-done.21.refs_14_.refs_8_), channel_id=1, source_target_pairs={{0,4},{4,0},{8,12},{12,8},{1,5},{5,1},{9,13},{13,9},{2,6},{6,2},{1... | collective-permute-start | bytes 393224 | tf_op jit(solution)/shard_map/ppermute | solution.py:340
